TPU v7x, 32 devices: a whole 2x2x4 slice. The times are simulated.
32 devices in a mesh: groups: 2 (over y), bond: 4 (over z), mpo: 4 (over x, core).
Axes of the slice: x: 2, y: 2, z: 4, core: 2. Of those that a mesh axis runs over, the one named last changes fastest.
Arguments:
- psi: bfloat16 [8, 16, 128, 128], P(('groups', 'bond'), 'mpo'), parts along dimension 0, may hold values from -24 to 24
- left_env: bfloat16 [20, 8, 128, 128], P('mpo', ('groups', 'bond')), parts along dimension 1, may hold values from -0.5 to 0.5
- right_env: bfloat16 [20, 8, 128, 128], P(None, ('groups', 'bond')), parts along dimension 1, may hold values from -0.125 to 0.125
- site_one: bfloat16 [40, 20, 4, 4], P('groups'), parts along dimension 0, may hold values from -0.625 to 0.625
- site_two: bfloat16 [40, 20, 4, 4], P('groups'), parts along dimension 0, may hold values from -0.625 to 0.625
- mpo_charge: int32 [20], replicated, may hold values from -1 to 1
- left_sizes: int32 [8], P('groups'), parts along dimension 0, may hold values from 64 to 128, as said below
- right_sizes: int32 [8], P('groups'), parts along dimension 0, may hold values from 64 to 128, as said below
Outputs:
- image: bfloat16 [8, 16, 128, 128], P(('groups', 'bond'), 'mpo'), parts along dimension 0
- correction_image: bfloat16 [8, 16, 128, 128], P(('groups', 'bond'), 'mpo'), parts along dimension 0
There are 2 independent parts, one for each index of `groups`. A program takes and returns all parts, laid end to end along the dimension named above; an argument that names none is the same for every part. Nothing has to cross between parts.
Inputs may be any that keep to these rules, and one draw needn't show every extreme that they name: `left_sizes`: live rows of a sector; some sector has 128 and some has 64. `right_sizes`: live rows of a sector; some sector has 128 and some has 64.
All inputs are finite; a program needn't handle non-finite values.
Results may differ from a plain program's by a relative error of at most 0.006.
The roundings to bfloat16 on the way count: a program that leaves them out, or rounds other values in their place, can miss the bound.
Values may be sent and summed in bfloat16 or wider, within the bound.
No kernel may reach another device: no remote copies, remote signals or barrier semaphores. Data moves between devices by JAX's collectives and lax.ppermute only.
A program may use at most 128 MiB of HBM per device.

v0:
```python
import jax
import jax.numpy as jnp
from jax import lax
from jax.sharding import PartitionSpec as P

EPSILON = 1e-06
STATE_CHARGES = (0, 1, 1, 2)


def from_behind(value, axis, steps):
    count = lax.axis_size(axis)
    initial, last = (max(0, -steps), min(count, count - steps))
    return lax.ppermute(value, axis, [(source, source + steps) for source in range(initial, last)])


def padded(block, sides, width):
    for axis, dim in sides:
        count = lax.axis_size(axis)
        forward = [(i, i + 1) for i in range(count - 1)]
        backward = [(target, source) for source, target in forward]
        low = lax.ppermute(
            lax.slice_in_dim(block, block.shape[dim] - width, None, axis=dim), axis, forward
        )
        high = lax.ppermute(lax.slice_in_dim(block, 0, width, axis=dim), axis, backward)
        block = jnp.concatenate([low, block, high], axis=dim)
    return block


def pair_charges():
    return [left + right for left in STATE_CHARGES for right in STATE_CHARGES]


def charge_allowed(weight, row_charge, column_charge):
    local_charge = jnp.array(STATE_CHARGES, jnp.int32)
    charge_step = local_charge[:, None] - local_charge[None, :]
    bond_step = column_charge[None, :] - row_charge[:, None]
    allowed = charge_step[None, None, :, :] == bond_step[:, :, None, None]
    return jnp.where(allowed, weight, jnp.zeros_like(weight))


def right_rim(block, distance):
    return from_behind(block, "bond", -distance)


def gathered_states(vector_mine):
    every_pair = lax.all_gather(vector_mine, "mpo", axis=1, tiled=True)
    return padded(every_pair, (("bond", 0),), 1)


def shifted_states(vector_mine):
    sectors_here = vector_mine.shape[0]
    rimmed = gathered_states(vector_mine)
    return jnp.stack(
        [rimmed[2 : sectors_here + 2], rimmed[1 : sectors_here + 1], rimmed[0:sectors_here]], 0
    )


def group_terms(shifted, left_group, charge_group, first_group, second_site):
    sectors_here = shifted.shape[1]
    site_states = second_site.shape[2]
    block_width = shifted.shape[3]
    mpo_width = second_site.shape[0]
    group_width = left_group.shape[0]
    pick_table = (charge_group[:, None] + 1 == jnp.arange(3, dtype=jnp.int32)[None, :]).astype(
        jnp.bfloat16
    )
    picked = jnp.einsum(
        "wc,cspkj->wspkj", pick_table, shifted, preferred_element_type=jnp.float32
    ).astype(jnp.bfloat16)
    left_done = jnp.einsum(
        "wsik,wspkj->wspij", left_group, picked, preferred_element_type=jnp.float32
    ).astype(jnp.bfloat16)
    left_done = left_done.reshape(
        group_width, sectors_here, site_states, site_states, block_width, block_width
    )
    middle = jnp.einsum(
        "wvxa,wsabij->vsxbij", first_group, left_done, preferred_element_type=jnp.float32
    ).astype(jnp.bfloat16)
    mpo_done = jnp.einsum(
        "vuyb,vsxbij->usxyij", second_site, middle, preferred_element_type=jnp.float32
    ).astype(jnp.bfloat16)
    return mpo_done.reshape(
        mpo_width, sectors_here, site_states * site_states, block_width, block_width
    )


def apply_split(
    vector_mine, left_env, right_pick, first_local, second_site, charge_here, live_mine
):
    shifted = shifted_states(vector_mine)
    mpo_done = group_terms(shifted, left_env, charge_here, first_local, second_site)
    partial_sum = jnp.einsum(
        "uspij,usplj->spil", mpo_done, right_pick, preferred_element_type=jnp.float32
    )
    summed = lax.psum_scatter(partial_sum, "mpo", scatter_dimension=1, tiled=True)
    return jnp.where(live_mine, summed, 0.0).astype(jnp.bfloat16)


def shards(psi, left_env, right_env, site_one, site_two, mpo_charge, left_sizes, right_sizes):
    sectors_here = psi.shape[0]
    pairs_here = psi.shape[1]
    block_width = psi.shape[2]
    mpo_local = left_env.shape[0]
    nsec_all = sectors_here * lax.axis_size("bond")
    sector_first = lax.axis_index("bond") * sectors_here
    pair_first = lax.axis_index("mpo") * pairs_here
    mpo_first = lax.axis_index("mpo") * mpo_local
    pair_list = pair_charges()
    occupancy = jnp.array(pair_list, jnp.int32)
    sectors = sector_first + jnp.arange(sectors_here, dtype=jnp.int32)
    target = sectors[:, None] + occupancy[None, :]
    every_sector = jnp.arange(nsec_all, dtype=jnp.int32)
    right_live = jnp.sum(
        jnp.where(target[:, :, None] == every_sector[None, None, :], right_sizes[None, None, :], 0),
        -1,
    )
    left_live = jnp.sum(
        jnp.where(sectors[:, None] == every_sector[None, :], left_sizes[None, :], 0), -1
    )
    rows = jnp.arange(block_width, dtype=jnp.int32)
    live_full = (
        (target < nsec_all)[:, :, None, None]
        & (rows[None, :] < left_live[:, None])[:, None, :, None]
        & (rows[None, None, :] < right_live[:, :, None])[:, :, None, :]
    )
    live_mine = lax.dynamic_slice_in_dim(live_full, pair_first, pairs_here, 1)
    second_site = charge_allowed(site_two, mpo_charge, mpo_charge)
    rim_sectors = 4
    blocks_list = [right_env]
    for distance in range(1, (rim_sectors + sectors_here - 1) // sectors_here + 1):
        blocks_list.append(right_rim(right_env, distance))
    extended = jnp.concatenate(blocks_list, 1)
    right_pick = jnp.stack([extended[:, charge : charge + sectors_here] for charge in pair_list], 2)
    charge_here = lax.dynamic_slice_in_dim(mpo_charge, mpo_first, mpo_local, 0)
    first_local = charge_allowed(
        lax.dynamic_slice_in_dim(site_one, mpo_first, mpo_local, 0), charge_here, mpo_charge
    )

    def hamiltonian(field):
        return apply_split(
            field, left_env, right_pick, first_local, second_site, charge_here, live_mine
        )

    vector_mine = jnp.where(live_mine, psi, jnp.zeros_like(psi))
    image = hamiltonian(vector_mine)
    vector_full = vector_mine.astype(jnp.float32)
    image_full = image.astype(jnp.float32)
    correlation, norm_sq = lax.psum(
        (jnp.sum(vector_full * image_full), jnp.sum(vector_full * vector_full)), ("bond", "mpo")
    )
    rayleigh = correlation / norm_sq
    residual = image_full - rayleigh * vector_full
    squares = lax.psum(jnp.sum(residual * residual), ("bond", "mpo"))
    count_all = nsec_all * len(pair_list) * block_width * block_width
    scale = lax.rsqrt(squares / count_all + EPSILON)
    correction = (residual * scale).astype(jnp.bfloat16)
    second = hamiltonian(correction)
    return (image, second)


def solution(mesh):
    in_specs = (
        P(("groups", "bond"), "mpo", None, None),
        P("mpo", ("groups", "bond"), None, None),
        P(None, ("groups", "bond"), None, None),
        P("groups", None, None, None),
        P("groups", None, None, None),
        P(),
        P("groups"),
        P("groups"),
    )
    out_specs = (P(("groups", "bond"), "mpo", None, None), P(("groups", "bond"), "mpo", None, None))
    return jax.shard_map(shards, mesh=mesh, in_specs=in_specs, out_specs=out_specs, check_vma=False)
```

profile of v0, /device:TPU:0, one launch (start us, length us, event | category | flops | bytes accessed | tf_op | source)
XLA Modules:
  0.0 325.5 jit_solution(2481142903238585637)
XLA Ops:
  12.5 8.6 %all_gather.6 = bf16[1,16,128,128]{3,2,0,1:T(8,128)(2,1)S(1)} all-gather(bf16[1,4,128,128]{3,2,0,1:T(8,128)(2,1)S(1)} %fusion.51), channel_id=1, replica_groups=mesh['groups'=2,'bond'=4,'mpo'=4] {'mpo'}, dimensions={1}, use_global_device_ids=true | all-gather | bytes 655360 | tf_op jit(solution)/shard_map/all_gather | solution.py:46
  21.1 3.5 %collective-permute-start.1 = (bf16[1,16,128,128]{3,2,1,0:T(8,128)(2,1)S(1)}, bf16[1,16,128,128]{3,2,1,0:T(8,128)(2,1)S(1)}, u32[]{:S(2)}, u32[]{:S(2)}) collective-permute-start(bf16[1,16,128,128]{3,2,1,0:T(8,128)(2,1)S(1)} %bitcast.154), channel_id=1, source_target_pairs={{0,4},{4,8},{8,12},{1,5},{5,9},{9,13},{2,6},{6,10},{10,14},{3,7},{... | collective-permute-start | bytes 1572872 | tf_op jit(solution)/shard_map/ppermute | solution.py:21
  41.4 4.3 %convolution_convert_fusion.1 = bf16[5,16,128,128]{3,0,2,1:T(8,128)(2,1)S(1)} fusion(bf16[1,1,16,128,128]{4,0,3,2,1:T(2,128)(2,1)S(1)} %copy.96, bf16[1,1,16,128,128]{4,0,3,2,1:T(2,128)(2,1)S(1)} %copy.95, bf16[1,1,16,128,128]{4,0,3,2,1:T(2,128)(2,1)S(1)} %copy.94, s32[5]{0:T(128)S(1)} %get-tuple-element.7), kind=kOutput, calls=%fused_computation.17 | convolution fusion | flops 13893647 | bytes 4194324 | tf_op jit(solution)/shard_map/wc,cspkj->wspkj/dot_general | solution.py:67
  45.7 2.5 fusion.28
  48.3 4.2 %copy.121 = bf16[5,4,4,128,128,1]{4,1,0,5,3,2:T(4,128)(2,1)S(1)} copy(bf16[5,4,4,128,128,1]{3,4,2,1,0,5:T(8,128)(2,1)} %bitcast.152) | data formatting | bytes 5242880 | tf_op jit(solution)/shard_map/reshape.23
  52.5 7.6 %fusion = bf16[20,4,4,128,128,1]{4,0,1,3,2,5:T(8,128)(2,1)} fusion(bf16[5,4,4,128,128,1]{4,1,0,5,3,2:T(4,128)(2,1)S(1)} %copy.121, bf16[20,20,4,4]{1,3,2,0:T(4,128)(2,1)} %param.14, s32[]{:T(128)S(6)} %select_n.46, s32[5,20]{1,0:T(8,128)S(1)} %broadcast_subtract_fusion.1, s32[4,4]{1,0:T(4,128)S(1)} %broadcast_add_fusion), kind=kOutput, calls=%fused_computation.4 | convolution fusion | flops 214961280 | bytes 13128148 | tf_op jit(solution)/shard_map/wvxa,wsabij->vsxbij/dot_general | solution.py:76
  60.1 13.6 %fusion.1 = bf16[20,1,4,4,128,128]{5,0,3,4,2,1:T(8,128)(2,1)} fusion(bf16[20,20,4,4,1,1]{0,1,3,2,5,4:T(8,128)(2,1)S(1)} %copy.125, bf16[20,4,4,128,128,1]{4,0,1,3,2,5:T(8,128)(2,1)} %fusion), kind=kOutput, calls=%fused_computation.5 | convolution fusion | flops 844103680 | bytes 20984320 | tf_op jit(solution)/shard_map/vuyb,vsxbij->usxyij/dot_general | solution.py:79
  73.8 11.7 %copy.102 = bf16[20,1,4,4,128,128]{5,4,3,2,0,1:T(8,128)(2,1)} copy(bf16[20,1,4,4,128,128]{5,0,3,4,2,1:T(8,128)(2,1)} %fusion.1) | data formatting | bytes 20971520 | tf_op jit(solution)/shard_map/convert_element_type | solution.py:81
  105.7 2.1 bitcast_dynamic-update-slice_fusion.4
  110.0 10.9 %fusion.34 = f32[1,16,128,128]{3,2,1,0:T(8,128)} fusion(bf16[20,16,128,128]{3,2,1,0:T(8,128)(2,1)} %bitcast.150, bf16[20,1,16,128,128]{4,3,2,0,1:T(8,128)(2,1)} %bitcast_dynamic-update-slice_fusion), kind=kOutput, calls=%fused_computation.34 | convolution fusion | flops 1342177280 | bytes 22020096 | tf_op jit(solution)/shard_map/uspij,usplj->spil/dot_general | solution.py:92
  120.9 35.1 %reduce-scatter.3.cloned.1.call-done = f32[1,4,128,128]{3,2,1,0:T(8,128)} async-done(((f32[1,16,128,128]{3,2,1,0:T(8,128)}), f32[1,4,128,128]{3,2,1,0:T(8,128)}) %reduce-scatter.3.cloned.1.call-update) | async-done | bytes 262160 | tf_op jit(solution)/shard_map/reduce_scatter | solution.py:95
  157.7 32.9 %all-reduce = (f32[]{:T(128)}, f32[]{:T(128)}) all-reduce(f32[]{:T(128)} %get-tuple-element.3, f32[]{:T(128)} %get-tuple-element.2), channel_id=1, replica_groups=mesh['groups'=2,'bond'=4,'mpo'=4] {'bond','mpo'}, use_global_device_ids=true, to_apply=%region_4.5 | all-reduce | flops 2 | bytes 16 | tf_op jit(solution)/shard_map/psum | solution.py:148
  192.8 30.1 %psum.23 = f32[]{:T(128)} all-reduce(f32[]{:T(128)} %multiply_reduce_fusion), channel_id=1, replica_groups=mesh['groups'=2,'bond'=4,'mpo'=4] {'bond','mpo'}, use_global_device_ids=true, to_apply=%region_8.9 | all-reduce | flops 1 | bytes 8 | tf_op jit(solution)/shard_map/psum | solution.py:153
  223.7 6.8 %all_gather.7 = bf16[1,16,128,128]{3,2,0,1:T(8,128)(2,1)S(1)} all-gather(bf16[1,4,128,128]{3,2,0,1:T(8,128)(2,1)S(1)} %fusion.46), channel_id=1, replica_groups=mesh['groups'=2,'bond'=4,'mpo'=4] {'mpo'}, dimensions={1}, use_global_device_ids=true | all-gather | bytes 655360 | tf_op jit(solution)/shard_map/all_gather | solution.py:46
  234.1 9.6 %collective-permute-done.7 = bf16[1,16,128,128]{3,2,1,0:T(8,128)(2,1)S(1)} collective-permute-done((bf16[1,16,128,128]{3,2,1,0:T(8,128)(2,1)S(1)}, bf16[1,16,128,128]{3,2,1,0:T(8,128)(2,1)S(1)}, u32[]{:S(2)}, u32[]{:S(2)}) %collective-permute-start.7) | collective-permute-done | bytes 524320 | tf_op jit(solution)/shard_map/ppermute | solution.py:21
  244.7 3.2 collective-permute-done.6
  248.9 4.6 %convolution_convert_fusion = bf16[5,16,128,128]{3,0,2,1:T(8,128)(2,1)S(1)} fusion(bf16[1,1,16,128,128]{4,0,3,2,1:T(2,128)(2,1)S(1)} %copy.112, bf16[1,1,16,128,128]{4,0,3,2,1:T(2,128)(2,1)S(1)} %copy.111, bf16[1,1,16,128,128]{4,0,3,2,1:T(2,128)(2,1)S(1)} %copy.110, s32[5]{0:T(128)S(1)} %copy-done.4), kind=kOutput, calls=%fused_computation.16 | convolution fusion | flops 13893647 | bytes 4194324 | tf_op jit(solution)/shard_map/wc,cspkj->wspkj/dot_general | solution.py:67
  253.5 2.5 fusion.31
  256.0 4.2 %copy.127 = bf16[5,4,4,128,128,1]{4,1,0,5,3,2:T(4,128)(2,1)S(1)} copy(bf16[5,4,4,128,128,1]{3,4,2,1,0,5:T(8,128)(2,1)} %bitcast.153) | data formatting | bytes 5242880 | tf_op jit(solution)/shard_map/reshape.35
  260.3 7.7 %fusion.2 = bf16[20,4,4,128,128,1]{4,0,1,3,2,5:T(8,128)(2,1)} fusion(bf16[5,4,4,128,128,1]{4,1,0,5,3,2:T(4,128)(2,1)S(1)} %copy.127, bf16[20,20,4,4]{1,3,2,0:T(4,128)(2,1)} %param.14, s32[]{:T(128)S(6)} %select_n.46, s32[5,20]{1,0:T(8,128)S(1)} %broadcast_subtract_fusion.1, s32[4,4]{1,0:T(4,128)S(1)} %broadcast_add_fusion), kind=kOutput, calls=%fused_computation.6 | convolution fusion | flops 214961280 | bytes 13128148 | tf_op jit(solution)/shard_map/wvxa,wsabij->vsxbij/dot_general | solution.py:76
  268.0 6.5 %fusion.3 = bf16[20,1,4,4,128,128]{5,0,3,4,2,1:T(8,128)(2,1)S(1)} fusion(bf16[20,20,4,4,1,1]{0,1,3,2,5,4:T(8,128)(2,1)S(1)} %copy.125, bf16[20,4,4,128,128,1]{4,0,1,3,2,5:T(8,128)(2,1)} %fusion.2), kind=kOutput, calls=%fused_computation.7 | convolution fusion | flops 844103680 | bytes 20984320 | tf_op jit(solution)/shard_map/vuyb,vsxbij->usxyij/dot_general | solution.py:79
  274.5 9.0 %copy.118 = bf16[20,1,4,4,128,128]{5,4,3,2,0,1:T(8,128)(2,1)} copy(bf16[20,1,4,4,128,128]{5,0,3,4,2,1:T(8,128)(2,1)S(1)} %fusion.3) | data formatting | bytes 20971520 | tf_op jit(solution)/shard_map/convert_element_type | solution.py:81
  283.5 10.8 %fusion.37 = f32[1,16,128,128]{3,2,1,0:T(8,128)} fusion(bf16[20,16,128,128]{3,2,1,0:T(8,128)(2,1)} %bitcast.151, bf16[20,1,16,128,128]{4,3,2,0,1:T(8,128)(2,1)} %bitcast_dynamic-update-slice_fusion), kind=kOutput, calls=%fused_computation.35 | convolution fusion | flops 1342177280 | bytes 22020096 | tf_op jit(solution)/shard_map/uspij,usplj->spil/dot_general | solution.py:92
  294.3 22.6 %reduce-scatter.5.cloned.1.call-done = f32[1,4,128,128]{3,2,1,0:T(8,128)} async-done(((f32[1,16,128,128]{3,2,1,0:T(8,128)}), f32[1,4,128,128]{3,2,1,0:T(8,128)}) %reduce-scatter.5.cloned.1.call-update) | async-done | bytes 262160 | tf_op jit(solution)/shard_map/reduce_scatter | solution.py:95
  (67 shorter events, 54.3 us)
Async XLA Ops:
  7.2 38.5 %copy-start = (bf16[5,1,128,128]{3,2,1,0:T(8,128)(2,1)S(1)}, bf16[5,1,128,128]{3,2,1,0:T(8,128)(2,1)}, u32[]{:S(2)}) copy-start(bf16[5,1,128,128]{3,2,1,0:T(8,128)(2,1)} %param.12) | copy-start | bytes 491524
  7.2 148.8 %reduce-scatter.3.cloned.1.call-start = ((), (), s32[]{:S(2)}) async-start(), calls=%async_computation.2 | async-start | bytes 1310720 | tf_op jit(solution)/shard_map/reduce_scatter | solution.py:95
  21.1 16.2 %collective-permute-start.1 = (bf16[1,16,128,128]{3,2,1,0:T(8,128)(2,1)S(1)}, bf16[1,16,128,128]{3,2,1,0:T(8,128)(2,1)S(1)}, u32[]{:S(2)}, u32[]{:S(2)}) collective-permute-start(bf16[1,16,128,128]{3,2,1,0:T(8,128)(2,1)S(1)} %bitcast.154), channel_id=1, source_target_pairs={{0,4},{4,8},{8,12},{1,5},{5,9},{9,13},{2,6},{6,10},{10,14},{3,7},{... | collective-permute-start | bytes 1572872 | tf_op jit(solution)/shard_map/ppermute | solution.py:21
  24.6 15.8 %collective-permute-start = (bf16[1,16,128,128]{3,2,1,0:T(8,128)(2,1)S(1)}, bf16[1,16,128,128]{3,2,1,0:T(8,128)(2,1)S(1)}, u32[]{:S(2)}, u32[]{:S(2)}) collective-permute-start(bf16[1,16,128,128]{3,2,1,0:T(8,128)(2,1)S(1)} %bitcast.155), channel_id=1, source_target_pairs={{4,0},{8,4},{12,8},{5,1},{9,5},{13,9},{6,2},{10,6},{14,10},{7,3},{... | collective-permute-start | bytes 1572872 | tf_op jit(solution)/shard_map/ppermute | solution.py:24
  25.9 81.9 %collective-permute-start.5 = (bf16[20,1,128,128]{3,2,0,1:T(8,128)(2,1)}, bf16[20,1,128,128]{3,2,0,1:T(8,128)(2,1)}, u32[]{:S(2)}, u32[]{:S(2)}) collective-permute-start(bf16[20,1,128,128]{3,2,0,1:T(8,128)(2,1)} %bitcast.160), channel_id=1, source_target_pairs={} | collective-permute-start | bytes 1966088 | tf_op jit(solution)/shard_map/ppermute | solution.py:13
  27.4 67.1 %collective-permute-start.4 = (bf16[20,1,128,128]{3,2,0,1:T(8,128)(2,1)}, bf16[20,1,128,128]{3,2,0,1:T(8,128)(2,1)}, u32[]{:S(2)}, u32[]{:S(2)}) collective-permute-start(bf16[20,1,128,128]{3,2,0,1:T(8,128)(2,1)} %bitcast.161), channel_id=1, source_target_pairs={{12,0},{13,1},{14,2},{15,3},{28,16},{29,17},{30,18},{31,19}} | collective-permute-start | bytes 1966088 | tf_op jit(solution)/shard_map/ppermute | solution.py:13
  28.7 60.9 %collective-permute-start.3 = (bf16[20,1,128,128]{3,2,0,1:T(8,128)(2,1)}, bf16[20,1,128,128]{3,2,0,1:T(8,128)(2,1)S(1)}, u32[]{:S(2)}, u32[]{:S(2)}) collective-permute-start(bf16[20,1,128,128]{3,2,0,1:T(8,128)(2,1)} %bitcast.162), channel_id=1, source_target_pairs={{8,0},{12,4},{9,1},{13,5},{10,2},{14,6},{11,3},{15,7},{24,16},{28,... | collective-permute-start | bytes 1966088 | tf_op jit(solution)/shard_map/ppermute | solution.py:13
  33.3 14.9 %copy-start.3 = (s32[5]{0:T(128)}, s32[5]{0:T(128)S(1)}, u32[]{:S(2)}) copy-start(s32[5]{0:T(128)S(1)} %get-tuple-element.7) | copy-start | bytes 64
  37.4 48.1 %collective-permute-start.2 = (bf16[20,1,128,128]{3,2,0,1:T(8,128)(2,1)}, bf16[20,1,128,128]{3,2,0,1:T(8,128)(2,1)}, u32[]{:S(2)}, u32[]{:S(2)}) collective-permute-start(bf16[20,1,128,128]{3,2,0,1:T(8,128)(2,1)} %bitcast.163), channel_id=1, source_target_pairs={{4,0},{8,4},{12,8},{5,1},{9,5},{13,9},{6,2},{10,6},{14,10},{7,3},{... | collective-permute-start | bytes 1966088 | tf_op jit(solution)/shard_map/ppermute | solution.py:13
  109.9 46.0 %copy-start.1 = (bf16[1,4,128,128]{3,2,1,0:T(8,128)(2,1)S(1)}, bf16[1,4,128,128]{3,2,1,0:T(8,128)(2,1)}, u32[]{:S(2)}) copy-start(bf16[1,4,128,128]{3,2,1,0:T(8,128)(2,1)} %param.11) | copy-start | bytes 393220
  109.9 138.9 %copy-start.4 = (s32[5]{0:T(128)S(1)}, s32[5]{0:T(128)}, u32[]{:S(2)}) copy-start(s32[5]{0:T(128)} %copy-done.3) | copy-start | bytes 64
  120.8 196.0 %reduce-scatter.5.cloned.1.call-start = ((), (), s32[]{:S(2)}) async-start(), calls=%async_computation.3 | async-start | bytes 1310720 | tf_op jit(solution)/shard_map/reduce_scatter | solution.py:95
  157.7 98.3 %copy-start.2 = (bf16[1,4,128,128]{3,2,1,0:T(8,128)(2,1)}, bf16[1,4,128,128]{3,2,1,0:T(8,128)(2,1)S(1)}, u32[]{:S(2)}) copy-start(bf16[1,4,128,128]{3,2,1,0:T(8,128)(2,1)S(1)} %get-tuple-element.6) | copy-start | bytes 393220
  230.5 13.2 %collective-permute-start.7 = (bf16[1,16,128,128]{3,2,1,0:T(8,128)(2,1)S(1)}, bf16[1,16,128,128]{3,2,1,0:T(8,128)(2,1)S(1)}, u32[]{:S(2)}, u32[]{:S(2)}) collective-permute-start(bf16[1,16,128,128]{3,2,1,0:T(8,128)(2,1)S(1)} %bitcast.157), channel_id=1, source_target_pairs={{0,4},{4,8},{8,12},{1,5},{5,9},{9,13},{2,6},{6,10},{10,14},{3,7},{... | collective-permute-start | bytes 1572872 | tf_op jit(solution)/shard_map/ppermute | solution.py:21
  231.8 16.1 %collective-permute-start.6 = (bf16[1,16,128,128]{3,2,1,0:T(8,128)(2,1)S(1)}, bf16[1,16,128,128]{3,2,1,0:T(8,128)(2,1)S(1)}, u32[]{:S(2)}, u32[]{:S(2)}) collective-permute-start(bf16[1,16,128,128]{3,2,1,0:T(8,128)(2,1)S(1)} %bitcast.158), channel_id=1, source_target_pairs={{4,0},{8,4},{12,8},{5,1},{9,5},{13,9},{6,2},{10,6},{14,10},{7,3},{... | collective-permute-start | bytes 1572872 | tf_op jit(solution)/shard_map/ppermute | solution.py:24
Sparse Core Ops, SparseCore 0:
  121.0 34.9 reduce-scatter.2
  294.4 22.4 reduce-scatter.4
where the time goes:
time: 327 us; the launch traced here: 325 us
  blocking collectives  78.5 us (24%)
  waiting for transfers between devices  71.1 us (22%)
  matrix products  71.1 us (22%)
  local copies, waits for them, and re-layouts  61.8 us (19%)
  between operations  16.3 us (5%)
  other arithmetic  13.6 us (4%)
  starting transfers between devices  13 us (4%)
    reduce_scatter x2, waiting for transfers between devices, apply_split(): lax.psum_scatter(partial_sum, 'mpo', scatter_dimension=1, tiled=True)  57.6 us
    psum x1, blocking collectives, shards(): lax.psum((jnp.sum(vector_full * image_full), jnp.sum(vector_full * vector...  32.9 us
    psum x1, blocking collectives, shards(): squares = lax.psum(jnp.sum(residual * residual), ('bond', 'mpo'))  30.1 us
    unnamed x25, local copies, waits for them, and re-layouts  24.5 us
    dot_general x2, matrix products, apply_split(): jnp.einsum('uspij,usplj->spil', mpo_done, right_pick, preferred_element_t...  21.7 us
    convert_element_type x2, local copies, waits for them, and re-layouts, group_terms(): mpo_done = jnp.einsum('vuyb,vsxbij->usxyij', second_site, middle, preferr...  20.7 us
    dot_general x2, matrix products, group_terms(): jnp.einsum('vuyb,vsxbij->usxyij', second_site, middle, preferred_element_...  20.1 us
    all_gather x2, blocking collectives, gathered_states(): every_pair = lax.all_gather(vector_mine, 'mpo', axis=1, tiled=True)  15.4 us
  transfers between devices with their start and end apart: 10, of which 5 were waited for; matrix products, arithmetic and copies ran while one was open for 24% of the time, Pallas kernels for 0%

commit v1 on v0

v1 whole, which is shorter than its diff:
```python
import functools

import jax
import jax.numpy as jnp
from jax import lax
from jax.experimental import pallas as pl
from jax.experimental.pallas import tpu as pltpu
from jax.sharding import PartitionSpec as P

EPSILON = 1e-06
STATE_CHARGES = (0, 1, 1, 2)
STATES = len(STATE_CHARGES)
PAIRS = STATES * STATES
RIM = 4
F32 = jnp.float32
BF16 = jnp.bfloat16
NT = (((1,), (1,)), ((), ()))


def pair_charges():
    return [left + right for left in STATE_CHARGES for right in STATE_CHARGES]


def round_up(value, step):
    return -(-value // step) * step


def charge_allowed(weight, row_charge, column_charge):
    local_charge = jnp.array(STATE_CHARGES, jnp.int32)
    charge_step = local_charge[:, None] - local_charge[None, :]
    bond_step = column_charge[None, :] - row_charge[:, None]
    allowed = charge_step[None, None, :, :] == bond_step[:, :, None, None]
    return jnp.where(allowed, weight, jnp.zeros_like(weight))


def from_bond(value, step):
    count = lax.axis_size("bond")
    pairs = [(i + step, i) for i in range(count) if 0 <= i + step < count]
    return lax.ppermute(value, "bond", pairs)


def from_mpo(value, flip):
    count = lax.axis_size("mpo")
    return lax.ppermute(value, "mpo", [(i ^ flip, i) for i in range(count)])


def mpo_bits():
    count = lax.axis_size("mpo")
    bits = []
    while count > 1:
        count //= 2
        bits.append(count)
    return bits


def spread(value):
    pieces = {0: value}
    for bit in mpo_bits():
        pieces.update({r ^ bit: from_mpo(piece, bit) for r, piece in list(pieces.items())})
    return [pieces[r] for r in range(len(pieces))]


def merged(one, two):
    a1, b1, c1 = one[0:1], one[1:2], one[2:3]
    a2, b2, c2 = two[0:1], two[1:2], two[2:3]
    both = b1 + b2
    ratio1 = jnp.where(b1 > 0, a1 / jnp.where(b1 > 0, b1, 1.0), 0.0)
    ratio2 = jnp.where(b2 > 0, a2 / jnp.where(b2 > 0, b2, 1.0), 0.0)
    share = jnp.where(both > 0, b1 / jnp.where(both > 0, both, 1.0), 0.0) * b2
    gap = ratio1 - ratio2
    rest = jnp.zeros((one.shape[0] - 3, one.shape[1]), F32)
    return jnp.concatenate([a1 + a2, both, c1 + c2 + gap * gap * share, rest], 0)


def sector_limits(sizes_ref, sector, count):
    inside = (sector >= 0) & (sector < count)
    return jnp.where(inside, sizes_ref[jnp.clip(sector, 0, count - 1)], 0)


def state_charge(state):
    return (state + 1) // 2


class Plan:
    def __init__(self, n_mpo, n_bond, width, mpo_width):
        self.n_mpo = n_mpo
        self.n_bond = n_bond
        self.width = width
        self.w = mpo_width
        self.w_here = mpo_width // n_mpo
        self.w_pad = round_up(mpo_width, 8)
        self.rows = width // n_mpo
        self.k = STATES * self.w_pad
        self.far = min(RIM, n_bond - 1)


def fill_left(plan, charge_ref, own_left, piece_refs, wide, ls):
    me = lax.axis_index("mpo")
    wide[...] = jnp.zeros_like(wide)
    for r in range(plan.n_mpo):
        owner = lax.bitwise_xor(me, r)
        for t in range(plan.w_here):
            w = owner * plan.w_here + t
            if r == 0:
                block = own_left[t, pl.ds(pl.multiple_of(me * plan.rows, plan.rows), plan.rows), :]
            else:
                block = piece_refs[r - 1][t]
            block = block.astype(F32)
            for c, charge in enumerate((0, 1, -1)):
                factor = jnp.where(charge_ref[w] == charge, 1.0, 0.0).astype(F32)
                wide[c, pl.ds(w, plan.rows, stride=plan.w_pad), :] = block * factor
    for c in range(3):
        ls[:, c * plan.width : (c + 1) * plan.width] = wide[c].astype(BF16)


def fill_vector(plan, left_ref, right_ref, psi_refs, fs):
    me = lax.axis_index("mpo")
    here = lax.axis_index("bond")
    row = lax.broadcasted_iota(jnp.int32, (plan.width, plan.width), 0)
    column = lax.broadcasted_iota(jnp.int32, (plan.width, plan.width), 1)
    for c, step in enumerate((0, -1, 1)):
        sector = here + step
        row_ok = row < sector_limits(left_ref, sector, plan.n_bond)
        for r in range(plan.n_mpo):
            first = lax.bitwise_xor(me, r)
            for second in range(STATES):
                target = sector + state_charge(first) + STATE_CHARGES[second]
                ok = row_ok & (column < sector_limits(right_ref, target, plan.n_bond))
                block = psi_refs[r * 3 + c][0, second].astype(F32)
                fs[first * STATES + second, c * plan.width : (c + 1) * plan.width, :] = jnp.where(
                    ok, block, 0.0
                ).astype(BF16)


def left_phase(plan, fs, ls, xs):
    def step(index, carry):
        p = index * 2
        both = jnp.concatenate([fs[p], fs[p + 1]], axis=1)
        done = jnp.dot(ls[...], both, preferred_element_type=F32)
        xs[p] = done[:, : plan.width]
        xs[p + 1] = done[:, plan.width :]
        return carry

    lax.fori_loop(0, PAIRS // 2, step, 0)


def middle_phase(plan, groups, xs, first_ref, second_ref, ys):
    pad = plan.w_pad
    first = first_ref[...]
    second = second_ref[...]

    def step(index, carry):
        middle = []
        for b in range(STATES):
            columns = []
            for one in range(2):
                start = pl.multiple_of((index * 2 + one) * pad, pad)
                columns.append(
                    jnp.concatenate([xs[a * STATES + b, pl.ds(start, pad), :] for a in range(STATES)], 0)
                )
            column = jnp.concatenate(columns, 1).astype(BF16)
            middle.append(jnp.dot(first, column, preferred_element_type=F32))
        for s1 in range(STATES):
            total = None
            for g in range(groups):
                at = g * plan.k + s1 * pad
                column = jnp.concatenate([z[at : at + pad] for z in middle], 0).astype(BF16)
                term = jnp.dot(second, column, preferred_element_type=F32)
                if groups > 1:
                    term = term.astype(BF16).astype(F32)
                total = term if total is None else total + term
            for s2 in range(STATES):
                for one in range(2):
                    ys[s1 * STATES + s2, pl.ds(index * 2 + one, plan.w, stride=plan.rows), :] = total[
                        s2 * pad : s2 * pad + plan.w, one * plan.width : (one + 1) * plan.width
                    ]
        return carry

    lax.fori_loop(0, plan.rows // 2, step, 0)


def right_phase(plan, split, ys, own_right, right_refs):
    me = lax.axis_index("mpo")
    result = [None] * PAIRS
    for n in range(plan.far + 1):
        members = [p for p, charge in enumerate(pair_charges()) if charge == n]
        total = None
        for r in range(plan.n_mpo):
            if n == 0:
                owner = r
                blocks = [own_right[owner * plan.w_here + t, 0] for t in range(plan.w_here)]
            else:
                owner = lax.bitwise_xor(me, r)
                blocks = [right_refs[r][(n - 1) * plan.w_here + t] for t in range(plan.w_here)]
            right = jnp.concatenate(blocks, 1)
            lines = []
            for p in members:
                parts = []
                for t in range(plan.w_here):
                    start = (owner * plan.w_here + t) * plan.rows
                    if n > 0:
                        start = pl.multiple_of(start, plan.rows)
                    parts.append(ys[p, pl.ds(start, plan.rows), :])
                lines.append(jnp.concatenate(parts, 1))
            field = jnp.concatenate(lines, 0)
            high = field.astype(BF16)
            if split:
                low = (field - high.astype(F32)).astype(BF16)
                high = jnp.concatenate([high, low], 0)
            term = lax.dot_general(high, right, NT, preferred_element_type=F32)
            total = term if total is None else total + term
        if split:
            half = total.shape[0] // 2
            total = total[:half] + total[half:]
        for place, p in enumerate(members):
            result[p] = total[place * plan.rows : (place + 1) * plan.rows]
    return result


def masked_rows(plan, left_ref, right_ref, result):
    me = lax.axis_index("mpo")
    here = lax.axis_index("bond")
    shape = (plan.rows, plan.width)
    row = lax.broadcasted_iota(jnp.int32, shape, 0) + me * plan.rows
    column = lax.broadcasted_iota(jnp.int32, shape, 1)
    row_ok = row < sector_limits(left_ref, here, plan.n_bond)
    blocks = []
    for p, charge in enumerate(pair_charges()):
        if result[p] is None:
            blocks.append(jnp.zeros(shape, BF16))
            continue
        ok = row_ok & (column < sector_limits(right_ref, here + charge, plan.n_bond))
        blocks.append(jnp.where(ok, result[p], 0.0).astype(BF16))
    return blocks


def whole_sum(values):
    return jnp.sum(jnp.sum(values, axis=1, keepdims=True), axis=0, keepdims=True)


def first_kernel(plan, *refs):
    charge_ref, left_ref, right_ref = refs[:3]
    psi_refs = refs[3 : 3 + 3 * plan.n_mpo]
    rest = refs[3 + 3 * plan.n_mpo :]
    own_left, rest = rest[0], rest[1:]
    piece_refs, rest = rest[: plan.n_mpo - 1], rest[plan.n_mpo - 1 :]
    first_ref, second_ref, ys, fs, ls, wide, xs = rest
    fill_left(plan, charge_ref, own_left, piece_refs, wide, ls)
    fill_vector(plan, left_ref, right_ref, psi_refs, fs)
    left_phase(plan, fs, ls, xs)
    middle_phase(plan, plan.n_mpo, xs, first_ref, second_ref, ys)


def image_kernel(plan, left_ref, right_ref, ys, fs, own_right, *refs):
    right_refs, (image, sums) = refs[: plan.n_mpo], refs[plan.n_mpo :]
    me = lax.axis_index("mpo")
    result = right_phase(plan, True, ys, own_right, right_refs)
    blocks = masked_rows(plan, left_ref, right_ref, result)
    rows_here = pl.ds(pl.multiple_of(me * plan.rows, plan.rows), plan.rows)
    along = jnp.zeros((plan.rows, plan.width), F32)
    norm = jnp.zeros((plan.rows, plan.width), F32)
    for p, block in enumerate(blocks):
        image[p] = block
        vector = fs[p, rows_here, :].astype(F32)
        along = along + vector * block.astype(F32)
        norm = norm + vector * vector
    along = whole_sum(along)
    norm = whole_sum(norm)
    ratio = jnp.where(norm > 0, along / jnp.where(norm > 0, norm, 1.0), 0.0)
    across = jnp.zeros((plan.rows, plan.width), F32)
    for p, block in enumerate(blocks):
        left_over = block.astype(F32) - ratio * fs[p, rows_here, :].astype(F32)
        across = across + left_over * left_over
    across = whole_sum(across)
    line = lax.broadcasted_iota(jnp.int32, sums.shape, 0)
    sums[...] = jnp.where(line == 0, along, jnp.where(line == 1, norm, jnp.where(line == 2, across, 0.0)))


def second_kernel(plan, count_all, *refs):
    left_ref, right_ref, sums = refs[:3]
    image_refs = refs[3 : 3 + 3 * plan.n_mpo]
    vector, ls, first_ref, second_ref, own_right = refs[3 + 3 * plan.n_mpo : 8 + 3 * plan.n_mpo]
    right_refs = refs[8 + 3 * plan.n_mpo : 8 + 4 * plan.n_mpo]
    out, fs, xs, ys = refs[8 + 4 * plan.n_mpo :]
    me = lax.axis_index("mpo")
    rayleigh = sums[0:1, :] / sums[1:2, :]
    scale = lax.rsqrt(sums[2:3, :] / count_all + EPSILON)
    for r in range(plan.n_mpo):
        start = lax.bitwise_xor(me, r) * plan.rows
        for c in range(3):
            where = pl.ds(pl.multiple_of(c * plan.width + start, plan.rows), plan.rows)
            for p in range(PAIRS):
                block = image_refs[r * 3 + c][p].astype(F32)
                residual = block - rayleigh * vector[p, where, :].astype(F32)
                fs[p, where, :] = (residual * scale).astype(BF16)
    left_phase(plan, fs, ls, xs)
    groups = first_ref.shape[0] // plan.k
    middle_phase(plan, groups, xs, first_ref, second_ref, ys)
    result = right_phase(plan, groups > 1, ys, own_right, right_refs)
    for p, block in enumerate(masked_rows(plan, left_ref, right_ref, result)):
        out[p] = block


VMEM = pl.BlockSpec(memory_space=pltpu.VMEM)
SMEM = pl.BlockSpec(memory_space=pltpu.SMEM)
PARAMS = pltpu.CompilerParams(vmem_limit_bytes=48 * 1024 * 1024)


def shape_of(shape, dtype):
    return jax.ShapeDtypeStruct(shape, dtype)


def shards(psi, left_env, right_env, site_one, site_two, mpo_charge, left_sizes, right_sizes):
    n_mpo = lax.axis_size("mpo")
    n_bond = lax.axis_size("bond")
    width = psi.shape[2]
    plan = Plan(n_mpo, n_bond, width, right_env.shape[0])
    me = lax.axis_index("mpo")

    neighbours = [psi, from_bond(psi, -1), from_bond(psi, 1)]
    by_sector = [spread(block) for block in neighbours]
    psi_pieces = [by_sector[c][r] for r in range(n_mpo) for c in range(3)]

    left_mine = left_env[:, 0]
    left_pieces = []
    for r in range(1, n_mpo):
        start = lax.bitwise_xor(me, r) * plan.rows
        left_pieces.append(from_mpo(lax.dynamic_slice_in_dim(left_mine, start, plan.rows, 1), r))

    quarter = lax.dynamic_slice_in_dim(right_env[:, 0], me * plan.w_here, plan.w_here, 0)
    right_far = jnp.concatenate([from_bond(quarter, d) for d in range(1, plan.far + 1)], 0)
    right_pieces = spread(right_far)

    pad = plan.w_pad - plan.w
    first = charge_allowed(site_one, mpo_charge, mpo_charge)
    first = jnp.transpose(first, (2, 1, 3, 0))
    first = jnp.pad(first, ((0, 0), (0, pad), (0, 0), (0, pad)))
    group_of = jnp.arange(plan.w_pad, dtype=jnp.int32) // plan.w_here
    groups = jnp.arange(n_mpo, dtype=jnp.int32)
    mine = (group_of[None, :] == groups[:, None])[:, None, None, None, :]
    first_wide = jnp.where(mine, first[None], jnp.zeros_like(first[None]))
    first_wide = first_wide.reshape(n_mpo * plan.k, plan.k)
    second = charge_allowed(site_two, mpo_charge, mpo_charge)
    second = jnp.transpose(second, (2, 1, 3, 0))
    second = jnp.pad(second, ((0, 0), (0, pad), (0, 0), (0, pad))).reshape(plan.k, plan.k)

    field_shape = (PAIRS, 3 * width, width)
    left_shape = (plan.rows * plan.w_pad, 3 * width)
    x_shape = (PAIRS, plan.rows * plan.w_pad, width)
    y_shape = (PAIRS, plan.rows * plan.w, width)
    row_shape = (PAIRS, plan.rows, width)

    ys, vector, left_rows = pl.pallas_call(
        functools.partial(first_kernel, plan),
        out_shape=(shape_of(y_shape, F32), shape_of(field_shape, BF16), shape_of(left_shape, BF16)),
        in_specs=[SMEM] * 3 + [VMEM] * (3 * n_mpo + n_mpo + 2),
        out_specs=(VMEM, VMEM, VMEM),
        scratch_shapes=[pltpu.VMEM((3, left_shape[0], width), F32), pltpu.VMEM(x_shape, F32)],
        compiler_params=PARAMS,
        name="states_of_vector",
    )(mpo_charge, left_sizes, right_sizes, *psi_pieces, left_mine, *left_pieces, first_wide, second)

    image_rows, sums = pl.pallas_call(
        functools.partial(image_kernel, plan),
        out_shape=(shape_of(row_shape, BF16), shape_of((8, width), F32)),
        in_specs=[SMEM] * 2 + [VMEM] * (3 + n_mpo),
        out_specs=(VMEM, VMEM),
        compiler_params=PARAMS,
        name="image_rows",
    )(left_sizes, right_sizes, ys, vector, right_env, *right_pieces)

    neighbours = [image_rows, from_bond(image_rows, -1), from_bond(image_rows, 1)]
    by_sector = [spread(block) for block in neighbours]
    image_pieces = [by_sector[c][r] for r in range(n_mpo) for c in range(3)]

    for bit in mpo_bits():
        sums = merged(sums, from_mpo(sums, bit))
    reach = 1
    while reach < n_bond:
        partner = [(i ^ reach, i) for i in range(n_bond)]
        sums = merged(sums, lax.ppermute(sums, "bond", partner))
        reach *= 2

    count_all = n_bond * PAIRS * width * width
    second_rows = pl.pallas_call(
        functools.partial(second_kernel, plan, float(count_all)),
        out_shape=shape_of(row_shape, BF16),
        in_specs=[SMEM] * 2 + [VMEM] * (1 + 3 * n_mpo + 5 + n_mpo),
        out_specs=VMEM,
        scratch_shapes=[
            pltpu.VMEM(field_shape, BF16),
            pltpu.VMEM(x_shape, F32),
            pltpu.VMEM(y_shape, F32),
        ],
        compiler_params=PARAMS,
        name="correction_image_rows",
    )(
        left_sizes, right_sizes, sums, *image_pieces, vector, left_rows, first_wide, second, right_env,
        *right_pieces,
    )

    image = jnp.zeros((STATES, width, width), BF16)
    for r in range(n_mpo):
        rows_of = lax.bitwise_xor(me, r)
        block = lax.dynamic_slice_in_dim(by_sector[0][r], me * STATES, STATES, 0)
        image = lax.dynamic_update_slice_in_dim(image, block, rows_of * plan.rows, 1)
    result = lax.all_to_all(
        second_rows.reshape(n_mpo, STATES, plan.rows, width), "mpo", 0, 0, tiled=False
    )
    result = jnp.transpose(result, (1, 0, 2, 3)).reshape(STATES, width, width)
    return (image[None], result[None])


def solution(mesh):
    in_specs = (
        P(("groups", "bond"), "mpo", None, None),
        P("mpo", ("groups", "bond"), None, None),
        P(None, ("groups", "bond"), None, None),
        P("groups", None, None, None),
        P("groups", None, None, None),
        P(),
        P("groups"),
        P("groups"),
    )
    out_specs = (P(("groups", "bond"), "mpo", None, None), P(("groups", "bond"), "mpo", None, None))
    return jax.shard_map(shards, mesh=mesh, in_specs=in_specs, out_specs=out_specs, check_vma=False)
```

time: 327 us -> 147 us (0.45)
  blocking collectives: 78.5 us -> 0 us
  matrix products: 71.1 us -> 0 us
  Pallas kernels: 0 us -> 44.7 us
  waiting for transfers between devices: 71.1 us -> 34.6 us
  local copies, waits for them, and re-layouts: 61.8 us -> 25.6 us
  starting transfers between devices: 13 us -> 36.3 us
  between operations: 16.3 us -> 1.09 us
  other arithmetic: 13.6 us -> 3.9 us
    dot_general x10 -> x0, matrix products: 71.1 us -> none  [the longest x2 21.7 us: apply_split(): jnp.einsum('uspij,usplj->spil', mpo_done, right_pick, preferred_element_t...]
    psum x2 -> x0, blocking collectives: 63 us -> none  [the longest x1 32.9 us: shards(): lax.psum((jnp.sum(vector_full * image_full), jnp.sum(vector_full * vector...]
    reduce_scatter x2 -> x0, waiting for transfers between devices: 57.6 us -> none  [apply_split(): lax.psum_scatter(partial_sum, 'mpo', scatter_dimension=1, tiled=True)]
    pallas_call x0 -> x3, Pallas kernels: none -> 44.7 us  [the longest x1 20.2 us: shards(): pl.pallas_call(functools.partial(second_kernel, plan, float(count_all)),...]
    convert_element_type x2 -> x0, local copies, waits for them, and re-layouts: 20.7 us -> none  [group_terms(): mpo_done = jnp.einsum('vuyb,vsxbij->usxyij', second_site, middle, preferr...]
    ppermute x8 -> x35, starting transfers between devices: 12.9 us -> 33 us  [the longest x26 15.5 us: from_mpo(): return lax.ppermute(value, 'mpo', [(i ^ flip, i) for i in range(count)])]
    ppermute x8 -> x35, waiting for transfers between devices: 13.4 us -> 31.4 us  [the longest x26 16.3 us: from_mpo(): return lax.ppermute(value, 'mpo', [(i ^ flip, i) for i in range(count)])]
    another operation x9 -> x1, local copies, waits for them, and re-layouts: 16.4 us -> 0.01 us
  transfers between devices with their start and end apart: 10 -> 36, of which waited for: 5 -> 13; matrix products, arithmetic and copies ran while one was open for 24% -> 7% of each run, Pallas kernels for 0% -> 13%
where the time goes in v1:
time: 147 us; the launch traced here: 146 us
  Pallas kernels  44.7 us (30%)
  starting transfers between devices  36.3 us (25%)
  waiting for transfers between devices  34.6 us (24%)
  local copies, waits for them, and re-layouts  25.6 us (17%)
  other arithmetic  3.9 us (3%)
    pallas_call x1, Pallas kernels, shards(): pl.pallas_call(functools.partial(second_kernel, plan, float(count_all)),...  20.2 us
    pallas_call x1, Pallas kernels, shards(): pl.pallas_call(functools.partial(first_kernel, plan), out_shape=(shape_of...  19.4 us
    unnamed x74, local copies, waits for them, and re-layouts  19.3 us
    ppermute x26, waiting for transfers between devices, from_mpo(): return lax.ppermute(value, 'mpo', [(i ^ flip, i) for i in range(count)])  16.3 us
    ppermute x26, starting transfers between devices, from_mpo(): return lax.ppermute(value, 'mpo', [(i ^ flip, i) for i in range(count)])  15.5 us
    ppermute x7, starting transfers between devices, from_bond(): return lax.ppermute(value, 'bond', pairs)  12.9 us
    ppermute x7, waiting for transfers between devices, from_bond(): return lax.ppermute(value, 'bond', pairs)  12.8 us
    pallas_call x1, Pallas kernels, shards(): pl.pallas_call(functools.partial(image_kernel, plan), out_shape=(shape_of...  5.14 us
  transfers between devices with their start and end apart: 36, of which 13 were waited for; matrix products, arithmetic and copies ran while one was open for 7% of the time, Pallas kernels for 13%

profile of v1, /device:TPU:0, one launch (start us, length us, event | category | flops | bytes accessed | tf_op | source)
XLA Modules:
  0.0 146.2 jit_solution(1507812723518554367)
XLA Ops:
  6.9 2.6 %collective-permute-start.12 = (bf16[5,32,128]{2,1,0:T(8,128)(2,1)S(1)}, bf16[5,32,128]{2,1,0:T(8,128)(2,1)S(1)}, u32[]{:S(2)}, u32[]{:S(2)}) collective-permute-start(bf16[5,32,128]{2,1,0:T(8,128)(2,1)S(1)} %get-tuple-element.20), channel_id=1, source_target_pairs={{2,0},{3,1},{0,2},{1,3},{6,4},{7,5},{4,6},{5,7},{10,8},{11,9},{8,1... | collective-permute-start | bytes 122888 | tf_op jit(solution)/shard_map/ppermute | solution.py:44
  11.0 11.5 %collective-permute-done.15 = bf16[5,128,128]{2,1,0:T(8,128)(2,1)S(1)} collective-permute-done((bf16[5,128,128]{2,1,0:T(8,128)(2,1)S(1)}, bf16[5,128,128]{2,1,0:T(8,128)(2,1)S(1)}, u32[]{:S(2)}, u32[]{:S(2)}) %collective-permute-start.15) | collective-permute-done | bytes 163872 | tf_op jit(solution)/shard_map/ppermute | solution.py:39
  23.8 1.6 %collective-permute-start.18 = (bf16[15,128,128]{2,1,0:T(8,128)(2,1)S(1)}, bf16[15,128,128]{2,1,0:T(8,128)(2,1)S(1)}, u32[]{:S(2)}, u32[]{:S(2)}) collective-permute-start(bf16[15,128,128]{2,1,0:T(8,128)(2,1)S(1)} %constant_dynamic-update-slice_fusion.refs_0_.refs_20_), channel_id=1, source_target_pairs={{2,0},{3,1},{0,2},{1,3},{6,4},{7,5},{4,6},{5,7},{10,8},{11,9},{8,1... | collective-permute-start | bytes 1474568 | tf_op jit(solution)/shard_map/ppermute | solution.py:44
  26.9 4.5 %collective-permute-start = (bf16[1,4,128,128]{3,2,1,0:T(8,128)(2,1)}, bf16[1,4,128,128]{3,2,1,0:T(8,128)(2,1)S(1)}, u32[]{:S(2)}, u32[]{:S(2)}) collective-permute-start(bf16[1,4,128,128]{3,2,1,0:T(8,128)(2,1)} %refs_3_.1), channel_id=1, source_target_pairs={{0,4},{4,8},{8,12},{1,5},{5,9},{9,13},{2,6},{6,10},{10,14},{3,7},{... | collective-permute-start | bytes 393224 | tf_op jit(solution)/shard_map/ppermute | solution.py:39
  32.7 1.5 %collective-permute-start.7 = (bf16[1,4,128,128]{3,2,1,0:T(8,128)(2,1)S(1)}, bf16[1,4,128,128]{3,2,1,0:T(8,128)(2,1)S(1)}, u32[]{:S(2)}, u32[]{:S(2)}) collective-permute-start(bf16[1,4,128,128]{3,2,1,0:T(8,128)(2,1)S(1)} %collective-permute-done.1.refs_5_), channel_id=1, source_target_pairs={{2,0},{3,1},{0,2},{1,3},{6,4},{7,5},{4,6},{5,7},{10,8},{11,9},{8,1... | collective-permute-start | bytes 393224 | tf_op jit(solution)/shard_map/ppermute | solution.py:44
  34.2 1.7 %fusion.1 = (bf16[4,20,4,20]{1,2,0,3:T(4,128)(2,1)}, bf16[4,20,4,20]{1,2,0,3:T(4,128)(2,1)S(1)}) fusion(bf16[20,20,4,4]{1,3,2,0:T(4,128)(2,1)} %param.14, s32[20,20]{1,0:T(8,128)S(1)} %broadcast_subtract_fusion, s32[4,4]{1,0:T(4,128)S(1)} %broadcast_add_fusion, bf16[20,20,4,4]{1,3,2,0:T(4,128)(2,1)} %param.13), kind=kLoop, calls=%fused_computation.5 | loop fusion | flops 19200 | bytes 52864 | tf_op jit(solution)/shard_map/transpose | solution.py:344
  36.2 1.9 %collective-permute-done.18.refs_2_.refs_22_ = bf16[15,128,128]{2,1,0:T(8,128)(2,1)S(1)} collective-permute-done((bf16[15,128,128]{2,1,0:T(8,128)(2,1)S(1)}, bf16[15,128,128]{2,1,0:T(8,128)(2,1)S(1)}, u32[]{:S(2)}, u32[]{:S(2)}) %collective-permute-start.18) | collective-permute-done | bytes 491552 | tf_op jit(solution)/shard_map/ppermute | solution.py:44
  38.2 2.0 %collective-permute-done.5.refs_9_ = bf16[1,4,128,128]{3,2,1,0:T(8,128)(2,1)S(1)} collective-permute-done((bf16[1,4,128,128]{3,2,1,0:T(8,128)(2,1)}, bf16[1,4,128,128]{3,2,1,0:T(8,128)(2,1)S(1)}, u32[]{:S(2)}, u32[]{:S(2)}) %collective-permute-start.5) | collective-permute-done | bytes 131104 | tf_op jit(solution)/shard_map/ppermute | solution.py:44
  40.2 1.5 %collective-permute-start.6 = (bf16[1,4,128,128]{3,2,1,0:T(8,128)(2,1)S(1)}, bf16[1,4,128,128]{3,2,1,0:T(8,128)(2,1)S(1)}, u32[]{:S(2)}, u32[]{:S(2)}) collective-permute-start(bf16[1,4,128,128]{3,2,1,0:T(8,128)(2,1)S(1)} %collective-permute-done.refs_4_), channel_id=1, source_target_pairs={{2,0},{3,1},{0,2},{1,3},{6,4},{7,5},{4,6},{5,7},{10,8},{11,9},{8,1... | collective-permute-start | bytes 393224 | tf_op jit(solution)/shard_map/ppermute | solution.py:44
  42.3 2.9 %collective-permute-done.6.refs_10_ = bf16[1,4,128,128]{3,2,1,0:T(8,128)(2,1)S(1)} collective-permute-done((bf16[1,4,128,128]{3,2,1,0:T(8,128)(2,1)S(1)}, bf16[1,4,128,128]{3,2,1,0:T(8,128)(2,1)S(1)}, u32[]{:S(2)}, u32[]{:S(2)}) %collective-permute-start.6) | collective-permute-done | bytes 131104 | tf_op jit(solution)/shard_map/ppermute | solution.py:44
  65.0 19.4 %states_of_vector.1 = (f32[16,640,128]{2,1,0:T(8,128)}, bf16[16,384,128]{2,1,0:T(8,128)(2,1)S(1)}, bf16[768,384]{1,0:T(8,128)(2,1)S(1)}) custom-call(s32[20]{0:T(128)S(1)} %copy-done.33, s32[4]{0:T(128)S(1)} %copy-done.29, s32[4]{0:T(128)S(1)} %copy-done.31, bf16[1,4,128,128]{3,2,1,0:T(8,128)(2,1)S(1)} %copy-done.6, bf16[1,4,128,128]{3,2,1,0:T(8,128)(2,1)S(1)} %copy-done.8, ...), custom_call_target="tpu_custom_call" | custom-call | tf_op jit(solution)/shard_map/states_of_vector/pallas_call | solution.py:353
  85.3 5.1 %image_rows.1 = (bf16[16,32,128]{2,1,0:T(8,128)(2,1)S(1)}, f32[8,128]{1,0:T(8,128)S(1)}) custom-call(s32[4]{0:T(128)S(1)} %copy-done.29, s32[4]{0:T(128)S(1)} %copy-done.31, f32[16,640,128]{2,1,0:T(8,128)} %get-tuple-element.7.ys, bf16[16,384,128]{2,1,0:T(8,128)(2,1)S(1)} %get-tuple-element.8.fs.refs_15_, bf16[20,1,128,128]{3,2,1,0:T(8,128)(2,1)S(1)} %copy-done.1, ...), custom_call_target="tpu_custom_call" | custom-call | tf_op jit(solution)/shard_map/image_rows/pallas_call | solution.py:363
  90.4 1.6 %collective-permute-start.23 = (f32[8,128]{1,0:T(8,128)S(1)}, f32[8,128]{1,0:T(8,128)S(1)}, u32[]{:S(2)}, u32[]{:S(2)}) collective-permute-start(f32[8,128]{1,0:T(8,128)S(1)} %get-tuple-element.10), channel_id=1, source_target_pairs={{2,0},{3,1},{0,2},{1,3},{6,4},{7,5},{4,6},{5,7},{10,8},{11,9},{8,1... | collective-permute-start | bytes 12296 | tf_op jit(solution)/shard_map/ppermute | solution.py:44
  92.1 2.0 %collective-permute-done.23 = f32[8,128]{1,0:T(8,128)S(1)} collective-permute-done((f32[8,128]{1,0:T(8,128)S(1)}, f32[8,128]{1,0:T(8,128)S(1)}, u32[]{:S(2)}, u32[]{:S(2)}) %collective-permute-start.23) | collective-permute-done | bytes 4128 | tf_op jit(solution)/shard_map/ppermute | solution.py:44
  95.5 2.4 %collective-permute-start.25 = (f32[8,128]{1,0:T(8,128)S(1)}, f32[8,128]{1,0:T(8,128)S(1)}, u32[]{:S(2)}, u32[]{:S(2)}) collective-permute-start(f32[8,128]{1,0:T(8,128)S(1)} %maximum_maximum_fusion.1), channel_id=1, source_target_pairs={{4,0},{0,4},{12,8},{8,12},{5,1},{1,5},{13,9},{9,13},{6,2},{2,6},{1... | collective-permute-start | bytes 12296 | tf_op jit(solution)/shard_map/ppermute | solution.py:381
  97.8 1.9 %collective-permute-start.27 = (bf16[16,32,128]{2,1,0:T(8,128)(2,1)S(1)}, bf16[16,32,128]{2,1,0:T(8,128)(2,1)S(1)}, u32[]{:S(2)}, u32[]{:S(2)}) collective-permute-start(bf16[16,32,128]{2,1,0:T(8,128)(2,1)S(1)} %get-tuple-element.9.refs_3_), channel_id=1, source_target_pairs={{0,4},{4,8},{8,12},{1,5},{5,9},{9,13},{2,6},{6,10},{10,14},{3,7},{... | collective-permute-start | bytes 393224 | tf_op jit(solution)/shard_map/ppermute | solution.py:39
  101.1 1.6 %collective-permute-start.21 = (bf16[16,32,128]{2,1,0:T(8,128)(2,1)S(1)}, bf16[16,32,128]{2,1,0:T(8,128)(2,1)S(1)}, u32[]{:S(2)}, u32[]{:S(2)}) collective-permute-start(bf16[16,32,128]{2,1,0:T(8,128)(2,1)S(1)} %get-tuple-element.9.refs_3_), channel_id=1, source_target_pairs={{2,0},{3,1},{0,2},{1,3},{6,4},{7,5},{4,6},{5,7},{10,8},{11,9},{8,1... | collective-permute-start | bytes 393224 | tf_op jit(solution)/shard_map/ppermute | solution.py:44
  102.7 2.2 %collective-permute-start.26 = (f32[8,128]{1,0:T(8,128)S(1)}, f32[8,128]{1,0:T(8,128)S(1)}, u32[]{:S(2)}, u32[]{:S(2)}) collective-permute-start(f32[8,128]{1,0:T(8,128)S(1)} %maximum_maximum_fusion.2), channel_id=1, source_target_pairs={{8,0},{12,4},{0,8},{4,12},{9,1},{13,5},{1,9},{5,13},{10,2},{14,6},... | collective-permute-start | bytes 12296 | tf_op jit(solution)/shard_map/ppermute | solution.py:381
  104.9 2.3 %collective-permute-done.26 = f32[8,128]{1,0:T(8,128)S(1)} collective-permute-done((f32[8,128]{1,0:T(8,128)S(1)}, f32[8,128]{1,0:T(8,128)S(1)}, u32[]{:S(2)}, u32[]{:S(2)}) %collective-permute-start.26) | collective-permute-done | bytes 4128 | tf_op jit(solution)/shard_map/ppermute | solution.py:381
  110.0 3.6 %collective-permute-done.31.refs_10_ = bf16[16,32,128]{2,1,0:T(8,128)(2,1)S(1)} collective-permute-done((bf16[16,32,128]{2,1,0:T(8,128)(2,1)S(1)}, bf16[16,32,128]{2,1,0:T(8,128)(2,1)S(1)}, u32[]{:S(2)}, u32[]{:S(2)}) %collective-permute-start.31) | collective-permute-done | bytes 131104 | tf_op jit(solution)/shard_map/ppermute | solution.py:44
  113.6 1.4 collective-permute-done.32.refs_11_
  117.4 20.2 %correction_image_rows.1 = bf16[16,32,128]{2,1,0:T(8,128)(2,1)} custom-call(s32[4]{0:T(128)S(1)} %copy-done.30, s32[4]{0:T(128)S(1)} %copy-done.32, f32[8,128]{1,0:T(8,128)S(1)} %maximum_maximum_fusion.3.refs_2_, bf16[16,32,128]{2,1,0:T(8,128)(2,1)S(1)} %get-tuple-element.9.refs_3_, bf16[16,32,128]{2,1,0:T(8,128)(2,1)S(1)} %collective-permute-done.27.refs_4_, ...), custom_call_target="tpu_custom_call" | custom-call | tf_op jit(solution)/shard_map/correction_image_rows/pallas_call | solution.py:385
  137.6 3.3 %all-to-all-start = ((bf16[4,4,32,128]{3,2,1,0:T(8,128)(2,1)}), bf16[4,4,32,128]{3,2,1,0:T(8,128)(2,1)S(1)}, u32[]{:S(2)}, u32[]{:S(2)}) async-start(bf16[4,4,32,128]{3,2,1,0:T(8,128)(2,1)} %bitcast.11), calls=%async_computation | async-start | bytes 262144 | tf_op jit(solution)/shard_map/all_to_all | solution.py:407
  142.4 3.2 %all-to-all-done = bf16[4,4,32,128]{3,2,1,0:T(8,128)(2,1)S(1)} async-done(((bf16[4,4,32,128]{3,2,1,0:T(8,128)(2,1)}), bf16[4,4,32,128]{3,2,1,0:T(8,128)(2,1)S(1)}, u32[]{:S(2)}, u32[]{:S(2)}) %all-to-all-start) | async-done | bytes 131104 | tf_op jit(solution)/shard_map/all_to_all | solution.py:407
  (155 shorter events, 43.4 us)
Async XLA Ops:
  1.6 9.1 %collective-permute-start.14 = (bf16[5,128,128]{2,1,0:T(8,128)(2,1)S(1)}, bf16[5,128,128]{2,1,0:T(8,128)(2,1)S(1)}, u32[]{:S(2)}, u32[]{:S(2)}) collective-permute-start(bf16[5,128,128]{2,1,0:T(8,128)(2,1)S(1)} %dynamic-slice_bitcast_fusion), channel_id=1, source_target_pairs={{4,0},{8,4},{12,8},{5,1},{9,5},{13,9},{6,2},{10,6},{14,10},{7,3},{... | collective-permute-start | bytes 491528 | tf_op jit(solution)/shard_map/ppermute | solution.py:39
  2.9 19.5 %collective-permute-start.15 = (bf16[5,128,128]{2,1,0:T(8,128)(2,1)S(1)}, bf16[5,128,128]{2,1,0:T(8,128)(2,1)S(1)}, u32[]{:S(2)}, u32[]{:S(2)}) collective-permute-start(bf16[5,128,128]{2,1,0:T(8,128)(2,1)S(1)} %dynamic-slice_bitcast_fusion), channel_id=1, source_target_pairs={{8,0},{12,4},{9,1},{13,5},{10,2},{14,6},{11,3},{15,7},{24,16},{28,... | collective-permute-start | bytes 491528 | tf_op jit(solution)/shard_map/ppermute | solution.py:39
  4.2 19.5 %collective-permute-start.16 = (bf16[5,128,128]{2,1,0:T(8,128)(2,1)S(1)}, bf16[5,128,128]{2,1,0:T(8,128)(2,1)S(1)}, u32[]{:S(2)}, u32[]{:S(2)}) collective-permute-start(bf16[5,128,128]{2,1,0:T(8,128)(2,1)S(1)} %dynamic-slice_bitcast_fusion), channel_id=1, source_target_pairs={{12,0},{13,1},{14,2},{15,3},{28,16},{29,17},{30,18},{31,19}} | collective-permute-start | bytes 491528 | tf_op jit(solution)/shard_map/ppermute | solution.py:39
  6.4 20.5 %collective-permute-start.11 = (bf16[5,32,128]{2,1,0:T(8,128)(2,1)S(1)}, bf16[5,32,128]{2,1,0:T(8,128)(2,1)S(1)}, u32[]{:S(2)}, u32[]{:S(2)}) collective-permute-start(bf16[5,32,128]{2,1,0:T(8,128)(2,1)S(1)} %get-tuple-element.19), channel_id=1, source_target_pairs={{1,0},{0,1},{3,2},{2,3},{5,4},{4,5},{7,6},{6,7},{9,8},{8,9},{11,10... | collective-permute-start | bytes 122888 | tf_op jit(solution)/shard_map/ppermute | solution.py:44
  6.9 24.6 %collective-permute-start.12 = (bf16[5,32,128]{2,1,0:T(8,128)(2,1)S(1)}, bf16[5,32,128]{2,1,0:T(8,128)(2,1)S(1)}, u32[]{:S(2)}, u32[]{:S(2)}) collective-permute-start(bf16[5,32,128]{2,1,0:T(8,128)(2,1)S(1)} %get-tuple-element.20), channel_id=1, source_target_pairs={{2,0},{3,1},{0,2},{1,3},{6,4},{7,5},{4,6},{5,7},{10,8},{11,9},{8,1... | collective-permute-start | bytes 122888 | tf_op jit(solution)/shard_map/ppermute | solution.py:44
  10.8 21.3 %collective-permute-start.13 = (bf16[5,32,128]{2,1,0:T(8,128)(2,1)S(1)}, bf16[5,32,128]{2,1,0:T(8,128)(2,1)S(1)}, u32[]{:S(2)}, u32[]{:S(2)}) collective-permute-start(bf16[5,32,128]{2,1,0:T(8,128)(2,1)S(1)} %get-tuple-element.18), channel_id=1, source_target_pairs={{3,0},{2,1},{1,2},{0,3},{7,4},{6,5},{5,6},{4,7},{11,8},{10,9},{9,1... | collective-permute-start | bytes 122888 | tf_op jit(solution)/shard_map/ppermute | solution.py:44
  22.5 10.3 %collective-permute-start.1 = (bf16[1,4,128,128]{3,2,1,0:T(8,128)(2,1)}, bf16[1,4,128,128]{3,2,1,0:T(8,128)(2,1)S(1)}, u32[]{:S(2)}, u32[]{:S(2)}) collective-permute-start(bf16[1,4,128,128]{3,2,1,0:T(8,128)(2,1)} %refs_3_.1), channel_id=1, source_target_pairs={{4,0},{8,4},{12,8},{5,1},{9,5},{13,9},{6,2},{10,6},{14,10},{7,3},{... | collective-permute-start | bytes 393224 | tf_op jit(solution)/shard_map/ppermute | solution.py:39
  23.8 14.2 %collective-permute-start.18 = (bf16[15,128,128]{2,1,0:T(8,128)(2,1)S(1)}, bf16[15,128,128]{2,1,0:T(8,128)(2,1)S(1)}, u32[]{:S(2)}, u32[]{:S(2)}) collective-permute-start(bf16[15,128,128]{2,1,0:T(8,128)(2,1)S(1)} %constant_dynamic-update-slice_fusion.refs_0_.refs_20_), channel_id=1, source_target_pairs={{2,0},{3,1},{0,2},{1,3},{6,4},{7,5},{4,6},{5,7},{10,8},{11,9},{8,1... | collective-permute-start | bytes 1474568 | tf_op jit(solution)/shard_map/ppermute | solution.py:44
  26.9 9.0 %collective-permute-start = (bf16[1,4,128,128]{3,2,1,0:T(8,128)(2,1)}, bf16[1,4,128,128]{3,2,1,0:T(8,128)(2,1)S(1)}, u32[]{:S(2)}, u32[]{:S(2)}) collective-permute-start(bf16[1,4,128,128]{3,2,1,0:T(8,128)(2,1)} %refs_3_.1), channel_id=1, source_target_pairs={{0,4},{4,8},{8,12},{1,5},{5,9},{9,13},{2,6},{6,10},{10,14},{3,7},{... | collective-permute-start | bytes 393224 | tf_op jit(solution)/shard_map/ppermute | solution.py:39
  31.5 8.7 %collective-permute-start.5 = (bf16[1,4,128,128]{3,2,1,0:T(8,128)(2,1)}, bf16[1,4,128,128]{3,2,1,0:T(8,128)(2,1)S(1)}, u32[]{:S(2)}, u32[]{:S(2)}) collective-permute-start(bf16[1,4,128,128]{3,2,1,0:T(8,128)(2,1)} %refs_3_.1), channel_id=1, source_target_pairs={{2,0},{3,1},{0,2},{1,3},{6,4},{7,5},{4,6},{5,7},{10,8},{11,9},{8,1... | collective-permute-start | bytes 393224 | tf_op jit(solution)/shard_map/ppermute | solution.py:44
  32.7 9.0 %collective-permute-start.2 = (bf16[1,4,128,128]{3,2,1,0:T(8,128)(2,1)}, bf16[1,4,128,128]{3,2,1,0:T(8,128)(2,1)S(1)}, u32[]{:S(2)}, u32[]{:S(2)}) collective-permute-start(bf16[1,4,128,128]{3,2,1,0:T(8,128)(2,1)} %refs_3_.1), channel_id=1, source_target_pairs={{1,0},{0,1},{3,2},{2,3},{5,4},{4,5},{7,6},{6,7},{9,8},{8,9},{11,10... | collective-permute-start | bytes 393224 | tf_op jit(solution)/shard_map/ppermute | solution.py:44
  32.7 9.1 %collective-permute-start.7 = (bf16[1,4,128,128]{3,2,1,0:T(8,128)(2,1)S(1)}, bf16[1,4,128,128]{3,2,1,0:T(8,128)(2,1)S(1)}, u32[]{:S(2)}, u32[]{:S(2)}) collective-permute-start(bf16[1,4,128,128]{3,2,1,0:T(8,128)(2,1)S(1)} %collective-permute-done.1.refs_5_), channel_id=1, source_target_pairs={{2,0},{3,1},{0,2},{1,3},{6,4},{7,5},{4,6},{5,7},{10,8},{11,9},{8,1... | collective-permute-start | bytes 393224 | tf_op jit(solution)/shard_map/ppermute | solution.py:44
  35.9 49.3 %collective-permute-start.17 = (bf16[15,128,128]{2,1,0:T(8,128)(2,1)S(1)}, bf16[15,128,128]{2,1,0:T(8,128)(2,1)}, u32[]{:S(2)}, u32[]{:S(2)}) collective-permute-start(bf16[15,128,128]{2,1,0:T(8,128)(2,1)S(1)} %constant_dynamic-update-slice_fusion.refs_0_.refs_20_), channel_id=1, source_target_pairs={{1,0},{0,1},{3,2},{2,3},{5,4},{4,5},{7,6},{6,7},{9,8},{8,9},{11,10... | collective-permute-start | bytes 1474568 | tf_op jit(solution)/shard_map/ppermute | solution.py:44
  38.1 47.2 %collective-permute-start.19 = (bf16[15,128,128]{2,1,0:T(8,128)(2,1)S(1)}, bf16[15,128,128]{2,1,0:T(8,128)(2,1)}, u32[]{:S(2)}, u32[]{:S(2)}) collective-permute-start(bf16[15,128,128]{2,1,0:T(8,128)(2,1)S(1)} %collective-permute-done.18.refs_2_.refs_22_), channel_id=1, source_target_pairs={{1,0},{0,1},{3,2},{2,3},{5,4},{4,5},{7,6},{6,7},{9,8},{8,9},{11,10... | collective-permute-start | bytes 1474568 | tf_op jit(solution)/shard_map/ppermute | solution.py:44
  95.5 7.2 %collective-permute-start.25 = (f32[8,128]{1,0:T(8,128)S(1)}, f32[8,128]{1,0:T(8,128)S(1)}, u32[]{:S(2)}, u32[]{:S(2)}) collective-permute-start(f32[8,128]{1,0:T(8,128)S(1)} %maximum_maximum_fusion.1), channel_id=1, source_target_pairs={{4,0},{0,4},{12,8},{8,12},{5,1},{1,5},{13,9},{9,13},{6,2},{2,6},{1... | collective-permute-start | bytes 12296 | tf_op jit(solution)/shard_map/ppermute | solution.py:381
  97.8 9.4 %collective-permute-start.27 = (bf16[16,32,128]{2,1,0:T(8,128)(2,1)S(1)}, bf16[16,32,128]{2,1,0:T(8,128)(2,1)S(1)}, u32[]{:S(2)}, u32[]{:S(2)}) collective-permute-start(bf16[16,32,128]{2,1,0:T(8,128)(2,1)S(1)} %get-tuple-element.9.refs_3_), channel_id=1, source_target_pairs={{0,4},{4,8},{8,12},{1,5},{5,9},{9,13},{2,6},{6,10},{10,14},{3,7},{... | collective-permute-start | bytes 393224 | tf_op jit(solution)/shard_map/ppermute | solution.py:39
  99.8 8.7 %collective-permute-start.28 = (bf16[16,32,128]{2,1,0:T(8,128)(2,1)S(1)}, bf16[16,32,128]{2,1,0:T(8,128)(2,1)S(1)}, u32[]{:S(2)}, u32[]{:S(2)}) collective-permute-start(bf16[16,32,128]{2,1,0:T(8,128)(2,1)S(1)} %get-tuple-element.9.refs_3_), channel_id=1, source_target_pairs={{4,0},{8,4},{12,8},{5,1},{9,5},{13,9},{6,2},{10,6},{14,10},{7,3},{... | collective-permute-start | bytes 393224 | tf_op jit(solution)/shard_map/ppermute | solution.py:39
  101.1 8.4 %collective-permute-start.21 = (bf16[16,32,128]{2,1,0:T(8,128)(2,1)S(1)}, bf16[16,32,128]{2,1,0:T(8,128)(2,1)S(1)}, u32[]{:S(2)}, u32[]{:S(2)}) collective-permute-start(bf16[16,32,128]{2,1,0:T(8,128)(2,1)S(1)} %get-tuple-element.9.refs_3_), channel_id=1, source_target_pairs={{2,0},{3,1},{0,2},{1,3},{6,4},{7,5},{4,6},{5,7},{10,8},{11,9},{8,1... | collective-permute-start | bytes 393224 | tf_op jit(solution)/shard_map/ppermute | solution.py:44
  102.6 7.3 %collective-permute-start.20 = (bf16[16,32,128]{2,1,0:T(8,128)(2,1)S(1)}, bf16[16,32,128]{2,1,0:T(8,128)(2,1)S(1)}, u32[]{:S(2)}, u32[]{:S(2)}) collective-permute-start(bf16[16,32,128]{2,1,0:T(8,128)(2,1)S(1)} %get-tuple-element.9.refs_3_), channel_id=1, source_target_pairs={{1,0},{0,1},{3,2},{2,3},{5,4},{4,5},{7,6},{6,7},{9,8},{8,9},{11,10... | collective-permute-start | bytes 393224 | tf_op jit(solution)/shard_map/ppermute | solution.py:44
  107.3 6.3 %collective-permute-start.31 = (bf16[16,32,128]{2,1,0:T(8,128)(2,1)S(1)}, bf16[16,32,128]{2,1,0:T(8,128)(2,1)S(1)}, u32[]{:S(2)}, u32[]{:S(2)}) collective-permute-start(bf16[16,32,128]{2,1,0:T(8,128)(2,1)S(1)} %collective-permute-done.27.refs_4_), channel_id=1, source_target_pairs={{2,0},{3,1},{0,2},{1,3},{6,4},{7,5},{4,6},{5,7},{10,8},{11,9},{8,1... | collective-permute-start | bytes 393224 | tf_op jit(solution)/shard_map/ppermute | solution.py:44
  108.4 6.5 %collective-permute-start.32 = (bf16[16,32,128]{2,1,0:T(8,128)(2,1)S(1)}, bf16[16,32,128]{2,1,0:T(8,128)(2,1)S(1)}, u32[]{:S(2)}, u32[]{:S(2)}) collective-permute-start(bf16[16,32,128]{2,1,0:T(8,128)(2,1)S(1)} %collective-permute-done.28.refs_5_), channel_id=1, source_target_pairs={{2,0},{3,1},{0,2},{1,3},{6,4},{7,5},{4,6},{5,7},{10,8},{11,9},{8,1... | collective-permute-start | bytes 393224 | tf_op jit(solution)/shard_map/ppermute | solution.py:44
  109.4 5.6 %collective-permute-start.29 = (bf16[16,32,128]{2,1,0:T(8,128)(2,1)S(1)}, bf16[16,32,128]{2,1,0:T(8,128)(2,1)S(1)}, u32[]{:S(2)}, u32[]{:S(2)}) collective-permute-start(bf16[16,32,128]{2,1,0:T(8,128)(2,1)S(1)} %collective-permute-done.27.refs_4_), channel_id=1, source_target_pairs={{1,0},{0,1},{3,2},{2,3},{5,4},{4,5},{7,6},{6,7},{9,8},{8,9},{11,10... | collective-permute-start | bytes 393224 | tf_op jit(solution)/shard_map/ppermute | solution.py:44
  109.5 5.6 %collective-permute-start.30 = (bf16[16,32,128]{2,1,0:T(8,128)(2,1)S(1)}, bf16[16,32,128]{2,1,0:T(8,128)(2,1)S(1)}, u32[]{:S(2)}, u32[]{:S(2)}) collective-permute-start(bf16[16,32,128]{2,1,0:T(8,128)(2,1)S(1)} %collective-permute-done.28.refs_5_), channel_id=1, source_target_pairs={{1,0},{0,1},{3,2},{2,3},{5,4},{4,5},{7,6},{6,7},{9,8},{8,9},{11,10... | collective-permute-start | bytes 393224 | tf_op jit(solution)/shard_map/ppermute | solution.py:44
  137.6 7.9 %all-to-all-start = ((bf16[4,4,32,128]{3,2,1,0:T(8,128)(2,1)}), bf16[4,4,32,128]{3,2,1,0:T(8,128)(2,1)S(1)}, u32[]{:S(2)}, u32[]{:S(2)}) async-start(bf16[4,4,32,128]{3,2,1,0:T(8,128)(2,1)} %bitcast.11), calls=%async_computation | async-start | bytes 262144 | tf_op jit(solution)/shard_map/all_to_all | solution.py:407
  (47 other events, 339.0 us)

commit v2 on v1

v2 whole, which is shorter than its diff:
```python
import functools

import jax
import jax.numpy as jnp
from jax import lax
from jax.experimental import pallas as pl
from jax.experimental.pallas import tpu as pltpu
from jax.sharding import PartitionSpec as P

EPSILON = 1e-06
STATE_CHARGES = (0, 1, 1, 2)
STATES = len(STATE_CHARGES)
PAIRS = STATES * STATES
RIM = 4
F32 = jnp.float32
BF16 = jnp.bfloat16
NT = (((1,), (1,)), ((), ()))


def pair_charges():
    return [left + right for left in STATE_CHARGES for right in STATE_CHARGES]


def round_up(value, step):
    return -(-value // step) * step


def charge_allowed(weight, row_charge, column_charge):
    local_charge = jnp.array(STATE_CHARGES, jnp.int32)
    charge_step = local_charge[:, None] - local_charge[None, :]
    bond_step = column_charge[None, :] - row_charge[:, None]
    allowed = charge_step[None, None, :, :] == bond_step[:, :, None, None]
    return jnp.where(allowed, weight, jnp.zeros_like(weight))


def from_near(value, step, flip):
    n_bond, n_mpo = lax.axis_size("bond"), lax.axis_size("mpo")
    pairs = [
        ((i + step) * n_mpo + (j ^ flip), i * n_mpo + j)
        for i in range(n_bond)
        for j in range(n_mpo)
        if 0 <= i + step < n_bond
    ]
    return lax.ppermute(value, ("bond", "mpo"), pairs)


def mpo_bits():
    count = lax.axis_size("mpo")
    bits = []
    while count > 1:
        count //= 2
        bits.append(count)
    return bits


def spread(value, steps):
    pieces = {(step, 0): from_near(value, step, 0) if step else value for step in steps}
    for bit in mpo_bits():
        pieces.update({(step, r ^ bit): from_near(piece, 0, bit) for (step, r), piece in list(pieces.items())})
    return pieces


def merged(parts):
    along = sum(part[0:1] for part in parts)
    norm = sum(part[1:2] for part in parts)
    ratio = jnp.where(norm > 0, along / jnp.where(norm > 0, norm, 1.0), 0.0)
    across = jnp.zeros_like(along)
    for part in parts:
        own = jnp.where(part[1:2] > 0, part[0:1] / jnp.where(part[1:2] > 0, part[1:2], 1.0), 0.0)
        gap = own - ratio
        across = across + part[2:3] + gap * gap * part[1:2]
    rest = jnp.zeros((parts[0].shape[0] - 3, parts[0].shape[1]), F32)
    return jnp.concatenate([along, norm, across, rest], 0)


def summed_over_bond(sums):
    n_bond = lax.axis_size("bond")
    reach, parts = 1, [sums]
    while reach < n_bond:
        if reach > 1:
            parts = [merged(parts)]
        radix = min(4, n_bond // reach)
        parts = parts + [
            lax.ppermute(parts[0], "bond", [(i ^ (reach * k), i) for i in range(n_bond)])
            for k in range(1, radix)
        ]
        reach *= radix
    return parts


def sector_limits(sizes_ref, sector, count):
    inside = (sector >= 0) & (sector < count)
    return jnp.where(inside, sizes_ref[jnp.clip(sector, 0, count - 1)], 0)


def state_charge(state):
    return (state + 1) // 2


class Plan:
    def __init__(self, n_mpo, n_bond, width, mpo_width):
        self.n_mpo = n_mpo
        self.n_bond = n_bond
        self.width = width
        self.w = mpo_width
        self.w_here = mpo_width // n_mpo
        self.w_pad = round_up(mpo_width, 8)
        self.rows = width // n_mpo
        self.k = STATES * self.w_pad
        self.y_step = self.rows + 8
        self.far = min(RIM, n_bond - 1)


def fill_left(plan, charge_ref, left_near, wide, ls):
    me = lax.axis_index("mpo")
    wide[...] = jnp.zeros_like(wide)
    for r in range(plan.n_mpo):
        owner = lax.bitwise_xor(me, r)
        for t in range(plan.w_here):
            w = owner * plan.w_here + t
            block = left_near[r, t].astype(F32)
            for c, charge in enumerate((0, 1, -1)):
                factor = jnp.where(charge_ref[w] == charge, 1.0, 0.0).astype(F32)
                wide[c, pl.ds(w, plan.rows, stride=plan.w_pad), :] = block * factor
    for c in range(3):
        ls[:, c * plan.width : (c + 1) * plan.width] = wide[c].astype(BF16)


def fill_vector(plan, left_ref, right_ref, psi_near, fs):
    me = lax.axis_index("mpo")
    here = lax.axis_index("bond")
    row = lax.broadcasted_iota(jnp.int32, (plan.width, plan.width), 0)
    column = lax.broadcasted_iota(jnp.int32, (plan.width, plan.width), 1)
    for c, step in enumerate((0, -1, 1)):
        sector = here + step
        row_ok = row < sector_limits(left_ref, sector, plan.n_bond)
        for r in range(plan.n_mpo):
            first = lax.bitwise_xor(me, r)
            for second in range(STATES):
                target = sector + state_charge(first) + STATE_CHARGES[second]
                ok = row_ok & (column < sector_limits(right_ref, target, plan.n_bond))
                block = psi_near[r * 3 + c, second].astype(F32)
                fs[first * STATES + second, c * plan.width : (c + 1) * plan.width, :] = jnp.where(
                    ok, block, 0.0
                ).astype(BF16)


def left_phase(plan, fs, ls, xs):
    def step(index, carry):
        p = index * 2
        both = jnp.concatenate([fs[p], fs[p + 1]], axis=1)
        done = jnp.dot(ls[...], both, preferred_element_type=F32)
        xs[p] = done[:, : plan.width]
        xs[p + 1] = done[:, plan.width :]
        return carry

    lax.fori_loop(0, PAIRS // 2, step, 0, unroll=2)


def middle_phase(plan, groups, xs, first_ref, second_ref, ys):
    pad = plan.w_pad
    first = first_ref[...]
    second = second_ref[...]

    def step(index, carry):
        middle = []
        for b in range(STATES):
            columns = []
            for one in range(2):
                start = pl.multiple_of((index * 2 + one) * pad, pad)
                columns.append(
                    jnp.concatenate([xs[a * STATES + b, pl.ds(start, pad), :] for a in range(STATES)], 0)
                )
            column = jnp.concatenate(columns, 1).astype(BF16)
            middle.append(jnp.dot(first, column, preferred_element_type=F32))
        for s1 in range(STATES):
            total = None
            for g in range(groups):
                at = g * plan.k + s1 * pad
                column = jnp.concatenate([z[at : at + pad] for z in middle], 0).astype(BF16)
                term = jnp.dot(second, column, preferred_element_type=F32)
                if groups > 1:
                    term = term.astype(BF16).astype(F32)
                total = term if total is None else total + term
            for s2 in range(STATES):
                for one in range(2):
                    ys[s1 * STATES + s2, pl.ds(index * 2 + one, plan.w, stride=plan.y_step), :] = total[
                        s2 * pad : s2 * pad + plan.w, one * plan.width : (one + 1) * plan.width
                    ]
        return carry

    lax.fori_loop(0, plan.rows // 2, step, 0, unroll=2)


def right_phase(plan, split, ys, right_near, ready):
    result = [None] * PAIRS
    for n in range(plan.far + 1):
        ready(n)
        members = [p for p, charge in enumerate(pair_charges()) if charge == n]
        total = None
        for first in range(0, plan.w, plan.w_here):
            group = range(first, first + plan.w_here)
            right = jnp.concatenate([right_near[n, u] for u in group], 1)
            lines = []
            for p in members:
                parts = [ys[p, pl.ds(u * plan.y_step, plan.rows), :] for u in group]
                lines.append(jnp.concatenate(parts, 1))
            field = jnp.concatenate(lines, 0)
            high = field.astype(BF16)
            if split:
                low = (field - high.astype(F32)).astype(BF16)
                high = jnp.concatenate([high, low], 0)
            term = lax.dot_general(high, right, NT, preferred_element_type=F32)
            total = term if total is None else total + term
        if split:
            half = total.shape[0] // 2
            total = total[:half] + total[half:]
        for place, p in enumerate(members):
            result[p] = total[place * plan.rows : (place + 1) * plan.rows]
    return result


def right_copies(plan, own_ref, far_refs, right_near, sems):
    half = plan.w // 2
    core = lax.rem(lax.axis_index("mpo"), 2)
    copies = [[pltpu.make_async_copy(own_ref.at[:, 0], right_near.at[0], sems.at[0])]]
    for d in range(1, plan.far + 1):
        pair = []
        for other in range(2):
            start = lax.bitwise_xor(core, other) * half
            place = 2 * (d - 1) + other
            pair.append(
                pltpu.make_async_copy(
                    far_refs[place], right_near.at[d, pl.ds(start, half)], sems.at[1 + place]
                )
            )
        copies.append(pair)
    return copies


def masked_rows(plan, left_ref, right_ref, result):
    me = lax.axis_index("mpo")
    here = lax.axis_index("bond")
    shape = (plan.rows, plan.width)
    row = lax.broadcasted_iota(jnp.int32, shape, 0) + me * plan.rows
    column = lax.broadcasted_iota(jnp.int32, shape, 1)
    row_ok = row < sector_limits(left_ref, here, plan.n_bond)
    blocks = []
    for p, charge in enumerate(pair_charges()):
        if result[p] is None:
            blocks.append(jnp.zeros(shape, BF16))
            continue
        ok = row_ok & (column < sector_limits(right_ref, here + charge, plan.n_bond))
        blocks.append(jnp.where(ok, result[p], 0.0).astype(BF16))
    return blocks


def whole_sum(values):
    return jnp.sum(jnp.sum(values, axis=1, keepdims=True), axis=0, keepdims=True)


def first_kernel(plan, *refs):
    charge_ref, left_ref, right_ref = refs[:3]
    psi_refs = refs[3 : 3 + 3 * plan.n_mpo]
    left_refs = refs[3 + 3 * plan.n_mpo : 3 + 4 * plan.n_mpo]
    first_ref, second_ref, ys, fs_out, ls_out, fs, ls, wide, xs, left_near, psi_near, left_sem, psi_sem, out_sem = refs[
        3 + 4 * plan.n_mpo :
    ]
    me = lax.axis_index("mpo")
    rows_here = pl.ds(pl.multiple_of(me * plan.rows, plan.rows), plan.rows)
    left_copies = []
    for r, source in enumerate(left_refs):
        source = source.at[:, rows_here, :] if r == 0 else source
        left_copies.append(pltpu.make_async_copy(source, left_near.at[r], left_sem.at[r]))
    psi_copies = [
        pltpu.make_async_copy(source, psi_near.at[pl.ds(place, 1)], psi_sem.at[place])
        for place, source in enumerate(psi_refs)
    ]
    for copy in left_copies + psi_copies:
        copy.start()
    for copy in left_copies:
        copy.wait()
    fill_left(plan, charge_ref, left_near, wide, ls)
    ls_copy = pltpu.make_async_copy(ls, ls_out, out_sem.at[0])
    ls_copy.start()
    for copy in psi_copies:
        copy.wait()
    fill_vector(plan, left_ref, right_ref, psi_near, fs)
    fs_copy = pltpu.make_async_copy(fs, fs_out, out_sem.at[1])
    fs_copy.start()
    left_phase(plan, fs, ls, xs)
    middle_phase(plan, plan.n_mpo, xs, first_ref, second_ref, ys)
    ls_copy.wait()
    fs_copy.wait()


def image_kernel(plan, left_ref, right_ref, ys_ref, vector_ref, own_ref, *refs):
    far_refs, (image, ys, right_near, vector, y_sem, right_sem, v_sem) = refs[: 2 * plan.far], refs[2 * plan.far :]
    me = lax.axis_index("mpo")
    rows_here = pl.ds(pl.multiple_of(me * plan.rows, plan.rows), plan.rows)
    charges = pair_charges()
    y_copies = {
        p: pltpu.make_async_copy(ys_ref.at[p], ys.at[p], y_sem.at[p]) for p in range(PAIRS) if charges[p] <= plan.far
    }
    r_copies = right_copies(plan, own_ref, far_refs, right_near, right_sem)
    v_copy = pltpu.make_async_copy(vector_ref.at[:, rows_here, :], vector, v_sem)
    for n in range(plan.far + 1):
        for copy in r_copies[n] + [y_copies[p] for p in range(PAIRS) if charges[p] == n]:
            copy.start()
    v_copy.start()

    def ready(n):
        for copy in r_copies[n] + [y_copies[p] for p in range(PAIRS) if charges[p] == n]:
            copy.wait()

    result = right_phase(plan, True, ys, right_near, ready)
    blocks = masked_rows(plan, left_ref, right_ref, result)
    v_copy.wait()
    along = jnp.zeros((plan.rows, plan.width), F32)
    norm = jnp.zeros((plan.rows, plan.width), F32)
    for p, block in enumerate(blocks):
        image[p] = block
        field = vector[p].astype(F32)
        along = along + field * block.astype(F32)
        norm = norm + field * field
    along = whole_sum(along)
    norm = whole_sum(norm)
    ratio = jnp.where(norm > 0, along / jnp.where(norm > 0, norm, 1.0), 0.0)
    across = jnp.zeros((plan.rows, plan.width), F32)
    for p, block in enumerate(blocks):
        left_over = block.astype(F32) - ratio * vector[p].astype(F32)
        across = across + left_over * left_over
    across = whole_sum(across)
    line = lax.broadcasted_iota(jnp.int32, (8, plan.width), 0)
    sums = jnp.where(line == 0, along, jnp.where(line == 1, norm, jnp.where(line == 2, across, 0.0)))
    parts = []
    for _ in range(3):
        parts.append(sums.astype(BF16).astype(F32))
        sums = sums - parts[-1]
    parts.append(jnp.zeros((plan.rows - 24, plan.width), F32))
    image[PAIRS] = jnp.concatenate(parts, 0).astype(BF16)


def sums_of(piece):
    block = piece[PAIRS].astype(F32)
    return block[0:8] + block[8:16] + block[16:24]


def second_kernel(plan, count_all, n_parts, *refs):
    left_ref, right_ref = refs[:2]
    parts, refs = refs[2 : 2 + n_parts], refs[2 + n_parts :]
    image_refs, refs = refs[: 3 * plan.n_mpo], refs[3 * plan.n_mpo :]
    vector_ref, ls_ref, first_ref, second_ref, own_ref = refs[:5]
    far_refs, refs = refs[5 : 5 + 2 * plan.far], refs[5 + 2 * plan.far :]
    out, fs, xs, ys, image_near, vector, ls, right_near, image_sem, field_sem, right_sem = refs
    me = lax.axis_index("mpo")
    image_copies = [
        pltpu.make_async_copy(source.at[pl.ds(0, PAIRS)], image_near.at[place], image_sem.at[place])
        for place, source in enumerate(image_refs)
    ]
    v_copy = pltpu.make_async_copy(vector_ref, vector, field_sem.at[0])
    l_copy = pltpu.make_async_copy(ls_ref, ls, field_sem.at[1])
    r_copies = right_copies(plan, own_ref, far_refs, right_near, right_sem)
    for copy in [v_copy] + image_copies + [l_copy] + [copy for some in r_copies for copy in some]:
        copy.start()
    sums = merged([part[...] for part in parts])
    rayleigh = sums[0:1, :] / sums[1:2, :]
    scale = lax.rsqrt(sums[2:3, :] / count_all + EPSILON)
    v_copy.wait()
    for r in range(plan.n_mpo):
        start = lax.bitwise_xor(me, r) * plan.rows
        for c in range(3):
            image_copies[r * 3 + c].wait()
            where = pl.ds(pl.multiple_of(c * plan.width + start, plan.rows), plan.rows)
            for p in range(PAIRS):
                block = image_near[r * 3 + c, p].astype(F32)
                residual = block - rayleigh * vector[p, where, :].astype(F32)
                fs[p, where, :] = (residual * scale).astype(BF16)
    l_copy.wait()
    left_phase(plan, fs, ls, xs)
    middle_phase(plan, 1, xs, first_ref, second_ref, ys)

    def ready(n):
        for copy in r_copies[n]:
            copy.wait()

    result = right_phase(plan, False, ys, right_near, ready)
    for p, block in enumerate(masked_rows(plan, left_ref, right_ref, result)):
        out[p] = block


COST_A = 12_000_000_000
COST_B = 4_000_000_000
VMEM = pl.BlockSpec(memory_space=pltpu.VMEM)
ANY = pl.BlockSpec(memory_space=pl.ANY)
SMEM = pl.BlockSpec(memory_space=pltpu.SMEM)
PARAMS = pltpu.CompilerParams(vmem_limit_bytes=60 * 1024 * 1024)


def shape_of(shape, dtype):
    return jax.ShapeDtypeStruct(shape, dtype)


def shards(psi, left_env, right_env, site_one, site_two, mpo_charge, left_sizes, right_sizes):
    n_mpo = lax.axis_size("mpo")
    n_bond = lax.axis_size("bond")
    width = psi.shape[2]
    plan = Plan(n_mpo, n_bond, width, right_env.shape[0])
    me = lax.axis_index("mpo")

    steps = (0, -1, 1)
    by_sector = spread(psi, steps)
    psi_pieces = [by_sector[step, r] for r in range(n_mpo) for step in steps]

    left_mine = left_env[:, 0]
    left_pieces = []
    for r in range(1, n_mpo):
        start = lax.bitwise_xor(me, r) * plan.rows
        left_pieces.append(from_near(lax.dynamic_slice_in_dim(left_mine, start, plan.rows, 1), 0, r))

    half = plan.w // 2
    here = lax.dynamic_slice_in_dim(right_env[:, 0], lax.rem(me, 2) * half, half, 0)
    right_far = []
    for d in range(1, plan.far + 1):
        here = from_near(here, 1, 0)
        right_far.append(here)
    pad = plan.w_pad - plan.w
    first = charge_allowed(site_one, mpo_charge, mpo_charge)
    first = jnp.transpose(first, (2, 1, 3, 0))
    first = jnp.pad(first, ((0, 0), (0, pad), (0, 0), (0, pad)))
    group_of = jnp.arange(plan.w_pad, dtype=jnp.int32) // plan.w_here
    groups = jnp.arange(n_mpo, dtype=jnp.int32)
    mine = (group_of[None, :] == groups[:, None])[:, None, None, None, :]
    first_whole = first.reshape(plan.k, plan.k)
    first_wide = jnp.where(mine, first[None], jnp.zeros_like(first[None]))
    first_wide = first_wide.reshape(n_mpo * plan.k, plan.k)
    second = charge_allowed(site_two, mpo_charge, mpo_charge)
    second = jnp.transpose(second, (2, 1, 3, 0))
    second = jnp.pad(second, ((0, 0), (0, pad), (0, 0), (0, pad))).reshape(plan.k, plan.k)

    field_shape = (PAIRS, 3 * width, width)
    left_shape = (plan.rows * plan.w_pad, 3 * width)
    x_shape = (PAIRS, plan.rows * plan.w_pad, width)
    y_shape = (PAIRS, plan.y_step * plan.w, width)
    row_shape = (PAIRS, plan.rows, width)

    ys, vector, left_rows = pl.pallas_call(
        functools.partial(first_kernel, plan),
        out_shape=(shape_of(y_shape, F32), shape_of(field_shape, BF16), shape_of(left_shape, BF16)),
        in_specs=[SMEM] * 3 + [ANY] * (4 * n_mpo) + [VMEM] * 2,
        out_specs=(VMEM, ANY, ANY),
        scratch_shapes=[
            pltpu.VMEM(field_shape, BF16),
            pltpu.VMEM(left_shape, BF16),
            pltpu.VMEM((3, left_shape[0], width), F32),
            pltpu.VMEM(x_shape, F32),
            pltpu.VMEM((n_mpo, plan.w_here, plan.rows, width), BF16),
            pltpu.VMEM((3 * n_mpo,) + psi.shape[1:], BF16),
            pltpu.SemaphoreType.DMA((n_mpo,)),
            pltpu.SemaphoreType.DMA((3 * n_mpo,)),
            pltpu.SemaphoreType.DMA((2,)),
        ],
        compiler_params=PARAMS,
        cost_estimate=pl.CostEstimate(flops=COST_A, bytes_accessed=0, transcendentals=0),
        name="states_of_vector",
    )(mpo_charge, left_sizes, right_sizes, *psi_pieces, left_mine, *left_pieces, first_wide, second)

    right_pieces = [piece for far in right_far for piece in (far, from_near(far, 0, 1))]
    right_scratch = pltpu.VMEM((plan.far + 1, plan.w, width, width), BF16)
    image_shape = (PAIRS + 1,) + row_shape[1:]
    image_rows = pl.pallas_call(
        functools.partial(image_kernel, plan),
        out_shape=shape_of(image_shape, BF16),
        in_specs=[SMEM] * 2 + [ANY] * (3 + 2 * plan.far),
        out_specs=VMEM,
        scratch_shapes=[
            pltpu.VMEM(y_shape, F32),
            right_scratch,
            pltpu.VMEM(row_shape, BF16),
            pltpu.SemaphoreType.DMA((PAIRS,)),
            pltpu.SemaphoreType.DMA((1 + 2 * plan.far,)),
            pltpu.SemaphoreType.DMA,
        ],
        compiler_params=PARAMS,
        cost_estimate=pl.CostEstimate(flops=COST_B, bytes_accessed=0, transcendentals=0),
        name="image_rows",
    )(left_sizes, right_sizes, ys, vector, right_env, *right_pieces)

    by_sector = spread(image_rows, steps)
    image_pieces = [by_sector[step, r] for r in range(n_mpo) for step in steps]
    sums = summed_over_bond(merged([sums_of(by_sector[0, r]) for r in range(n_mpo)]))

    count_all = n_bond * PAIRS * width * width
    second_rows = pl.pallas_call(
        functools.partial(second_kernel, plan, float(count_all), len(sums)),
        out_shape=shape_of(row_shape, BF16),
        in_specs=[SMEM] * 2 + [VMEM] * len(sums) + [ANY] * (3 * n_mpo + 2) + [VMEM] * 2 + [ANY] * (1 + 2 * plan.far),
        out_specs=VMEM,
        scratch_shapes=[
            pltpu.VMEM(field_shape, BF16),
            pltpu.VMEM(x_shape, F32),
            pltpu.VMEM(y_shape, F32),
            pltpu.VMEM((3 * n_mpo,) + row_shape, BF16),
            pltpu.VMEM(field_shape, BF16),
            pltpu.VMEM(left_shape, BF16),
            right_scratch,
            pltpu.SemaphoreType.DMA((3 * n_mpo,)),
            pltpu.SemaphoreType.DMA((2,)),
            pltpu.SemaphoreType.DMA((1 + 2 * plan.far,)),
        ],
        compiler_params=PARAMS,
        cost_estimate=pl.CostEstimate(flops=COST_A, bytes_accessed=0, transcendentals=0),
        name="correction_image_rows",
    )(
        left_sizes, right_sizes, *sums, *image_pieces, vector, left_rows, first_whole, second, right_env,
        *right_pieces,
    )

    image = jnp.zeros((STATES, width, width), BF16)
    for r in range(n_mpo):
        rows_of = lax.bitwise_xor(me, r)
        block = lax.dynamic_slice_in_dim(by_sector[0, r], me * STATES, STATES, 0)
        image = lax.dynamic_update_slice_in_dim(image, block, rows_of * plan.rows, 1)
    result = lax.all_to_all(
        second_rows.reshape(n_mpo, STATES, plan.rows, width), "mpo", 0, 0, tiled=False
    )
    result = jnp.transpose(result, (1, 0, 2, 3)).reshape(STATES, width, width)
    return (image[None], result[None])


def solution(mesh):
    in_specs = (
        P(("groups", "bond"), "mpo", None, None),
        P("mpo", ("groups", "bond"), None, None),
        P(None, ("groups", "bond"), None, None),
        P("groups", None, None, None),
        P("groups", None, None, None),
        P(),
        P("groups"),
        P("groups"),
    )
    out_specs = (P(("groups", "bond"), "mpo", None, None), P(("groups", "bond"), "mpo", None, None))
    return jax.shard_map(shards, mesh=mesh, in_specs=in_specs, out_specs=out_specs, check_vma=False)
```

time: 147 us -> 120 us (0.82)
  local copies, waits for them, and re-layouts: 25.6 us -> 8.84 us
  Pallas kernels: 44.7 us -> 36.8 us
  starting transfers between devices: 36.3 us -> 33.3 us
    unnamed x74 -> x63, local copies, waits for them, and re-layouts: 19.3 us -> 1.8 us
    pallas_call x2, Pallas kernels: 25.3 us -> 19.4 us  [the longest x1 13.1 us: shards(): pl.pallas_call(functools.partial(second_kernel, plan, float(count_all), l...]
    ppermute x35 -> x34, starting transfers between devices: 33 us -> 30 us  [the longest x31 25.6 us: from_near(): return lax.ppermute(value, ('bond', 'mpo'), pairs)]
    pallas_call x1, Pallas kernels: 19.4 us -> 17.4 us  [shards(): pl.pallas_call(functools.partial(first_kernel, plan), out_shape=(shape_of...]
    ppermute x35 -> x34, waiting for transfers between devices: 31.4 us -> 31.1 us  [the longest x31 26.6 us: from_near(): return lax.ppermute(value, ('bond', 'mpo'), pairs)]
  transfers between devices with their start and end apart: 36 -> 35, of which waited for: 13 -> 11; matrix products, arithmetic and copies ran while one was open for 7% -> 9% of each run, Pallas kernels for 13% -> 15%
where the time goes in v2:
time: 120 us; the launch traced here: 119 us
  Pallas kernels  36.8 us (31%)
  waiting for transfers between devices  35 us (29%)
  starting transfers between devices  33.3 us (28%)
  local copies, waits for them, and re-layouts  8.84 us (7%)
  other arithmetic  3.77 us (3%)
  between operations  1.27 us (1%)
    ppermute x31, waiting for transfers between devices, from_near(): return lax.ppermute(value, ('bond', 'mpo'), pairs)  26.6 us
    ppermute x31, starting transfers between devices, from_near(): return lax.ppermute(value, ('bond', 'mpo'), pairs)  25.6 us
    pallas_call x1, Pallas kernels, shards(): pl.pallas_call(functools.partial(first_kernel, plan), out_shape=(shape_of...  17.4 us
    pallas_call x1, Pallas kernels, shards(): pl.pallas_call(functools.partial(second_kernel, plan, float(count_all), l...  13.1 us
    pallas_call x1, Pallas kernels, shards(): pl.pallas_call(functools.partial(image_kernel, plan), out_shape=shape_of(...  6.31 us
    ppermute x3, waiting for transfers between devices, summed_over_bond(): lax.ppermute(parts[0], 'bond', [(i ^ reach * k, i) for i in range(n_bond)])  4.57 us
    ppermute x3, starting transfers between devices, summed_over_bond(): lax.ppermute(parts[0], 'bond', [(i ^ reach * k, i) for i in range(n_bond)])  4.4 us
    all_to_all x1, waiting for transfers between devices, shards(): lax.all_to_all(second_rows.reshape(n_mpo, STATES, plan.rows, width), 'mpo...  3.82 us
  transfers between devices with their start and end apart: 35, of which 11 were waited for; matrix products, arithmetic and copies ran while one was open for 9% of the time, Pallas kernels for 15%

profile of v2, /device:TPU:0, one launch (start us, length us, event | category | flops | bytes accessed | tf_op | source)
XLA Modules:
  0.0 119.0 jit_solution(12920617914599391620)
XLA Ops:
  1.9 5.6 %collective-permute-start = (bf16[1,4,128,128]{3,2,1,0:T(8,128)(2,1)}, bf16[1,4,128,128]{3,2,1,0:T(8,128)(2,1)S(1)}, u32[]{:S(2)}, u32[]{:S(2)}) collective-permute-start(bf16[1,4,128,128]{3,2,1,0:T(8,128)(2,1)} %refs_3_.1), channel_id=1, source_target_pairs={{0,4},{1,5},{2,6},{3,7},{4,8},{5,9},{6,10},{7,11},{8,12},{9,13},{1... | collective-permute-start | bytes 393224 | tf_op jit(solution)/shard_map/ppermute | solution.py:44
  7.5 2.0 %collective-permute-start.5 = (bf16[1,4,128,128]{3,2,1,0:T(8,128)(2,1)}, bf16[1,4,128,128]{3,2,1,0:T(8,128)(2,1)S(1)}, u32[]{:S(2)}, u32[]{:S(2)}) collective-permute-start(bf16[1,4,128,128]{3,2,1,0:T(8,128)(2,1)} %refs_3_.1), channel_id=1, source_target_pairs={{2,0},{3,1},{0,2},{1,3},{6,4},{7,5},{4,6},{5,7},{10,8},{11,9},{8,1... | collective-permute-start | bytes 393224 | tf_op jit(solution)/shard_map/ppermute | solution.py:44
  11.4 1.3 %collective-permute-start.14 = (bf16[10,128,128]{2,1,0:T(8,128)(2,1)S(1)}, bf16[10,128,128]{2,1,0:T(8,128)(2,1)S(1)}, u32[]{:S(2)}, u32[]{:S(2)}) collective-permute-start(bf16[10,128,128]{2,1,0:T(8,128)(2,1)S(1)} %dynamic-slice_bitcast_fusion), channel_id=1, source_target_pairs={{4,0},{5,1},{6,2},{7,3},{8,4},{9,5},{10,6},{11,7},{12,8},{13,9},{1... | collective-permute-start | bytes 983048 | tf_op jit(solution)/shard_map/ppermute | solution.py:44
  14.4 9.0 %collective-permute-done.14.refs_0_.refs_23_ = bf16[10,128,128]{2,1,0:T(8,128)(2,1)S(1)} collective-permute-done((bf16[10,128,128]{2,1,0:T(8,128)(2,1)S(1)}, bf16[10,128,128]{2,1,0:T(8,128)(2,1)S(1)}, u32[]{:S(2)}, u32[]{:S(2)}) %collective-permute-start.14) | collective-permute-done | bytes 327712 | tf_op jit(solution)/shard_map/ppermute | solution.py:44
  25.9 3.7 %collective-permute-done.13.refs_18_ = bf16[5,32,128]{2,1,0:T(8,128)(2,1)S(1)} collective-permute-done((bf16[5,32,128]{2,1,0:T(8,128)(2,1)S(1)}, bf16[5,32,128]{2,1,0:T(8,128)(2,1)S(1)}, u32[]{:S(2)}, u32[]{:S(2)}) %collective-permute-start.13) | collective-permute-done | bytes 40992 | tf_op jit(solution)/shard_map/ppermute | solution.py:44
  30.3 1.6 %collective-permute-start.7 = (bf16[1,4,128,128]{3,2,1,0:T(8,128)(2,1)S(1)}, bf16[1,4,128,128]{3,2,1,0:T(8,128)(2,1)}, u32[]{:S(2)}, u32[]{:S(2)}) collective-permute-start(bf16[1,4,128,128]{3,2,1,0:T(8,128)(2,1)S(1)} %collective-permute-done.1.refs_5_), channel_id=1, source_target_pairs={{2,0},{3,1},{0,2},{1,3},{6,4},{7,5},{4,6},{5,7},{10,8},{11,9},{8,1... | collective-permute-start | bytes 393224 | tf_op jit(solution)/shard_map/ppermute | solution.py:44
  31.9 2.7 %collective-permute-done.16.refs_2_.refs_25_ = bf16[10,128,128]{2,1,0:T(8,128)(2,1)S(1)} collective-permute-done((bf16[10,128,128]{2,1,0:T(8,128)(2,1)S(1)}, bf16[10,128,128]{2,1,0:T(8,128)(2,1)S(1)}, u32[]{:S(2)}, u32[]{:S(2)}) %collective-permute-start.16) | collective-permute-done | bytes 327712 | tf_op jit(solution)/shard_map/ppermute | solution.py:44
  36.4 2.1 %collective-permute-done.7.refs_11_ = bf16[1,4,128,128]{3,2,1,0:T(8,128)(2,1)} collective-permute-done((bf16[1,4,128,128]{3,2,1,0:T(8,128)(2,1)S(1)}, bf16[1,4,128,128]{3,2,1,0:T(8,128)(2,1)}, u32[]{:S(2)}, u32[]{:S(2)}) %collective-permute-start.7) | collective-permute-done | bytes 131104 | tf_op jit(solution)/shard_map/ppermute | solution.py:44
  42.8 2.1 %collective-permute-done.18.refs_4_.refs_27_ = bf16[10,128,128]{2,1,0:T(8,128)(2,1)S(1)} collective-permute-done((bf16[10,128,128]{2,1,0:T(8,128)(2,1)S(1)}, bf16[10,128,128]{2,1,0:T(8,128)(2,1)S(1)}, u32[]{:S(2)}, u32[]{:S(2)}) %collective-permute-start.18) | collective-permute-done | bytes 327712 | tf_op jit(solution)/shard_map/ppermute | solution.py:44
  45.0 17.4 %states_of_vector.1 = (f32[16,800,128]{2,1,0:T(8,128)}, bf16[16,384,128]{2,1,0:T(8,128)(2,1)}, bf16[768,384]{1,0:T(8,128)(2,1)}) custom-call(s32[20]{0:T(128)} %refs_0_.2, s32[4]{0:T(128)} %refs_0_.3, s32[4]{0:T(128)} %refs_1_.3, bf16[1,4,128,128]{3,2,1,0:T(8,128)(2,1)} %refs_3_.1, bf16[1,4,128,128]{3,2,1,0:T(8,128)(2,1)} %copy-done.20, ...), custom_call_target="tpu_custom_call" | custom-call | flops 12000000000 | tf_op jit(solution)/shard_map/states_of_vector/pallas_call | solution.py:447
  63.4 6.3 %image_rows.1.refs_6_ = bf16[17,32,128]{2,1,0:T(8,128)(2,1)} custom-call(s32[4]{0:T(128)} %refs_0_.3, s32[4]{0:T(128)} %refs_1_.3, f32[16,800,128]{2,1,0:T(8,128)} %get-tuple-element.5.ys_ref, bf16[16,384,128]{2,1,0:T(8,128)(2,1)} %get-tuple-element.6.vector_ref.refs_18_, bf16[20,1,128,128]{3,2,1,0:T(8,128)(2,1)} %refs_22_.1, ...), custom_call_target="tpu_custom_call" | custom-call | flops 4000000000 | tf_op jit(solution)/shard_map/image_rows/pallas_call | solution.py:471
  71.5 3.2 %collective-permute-start.26 = (bf16[17,32,128]{2,1,0:T(8,128)(2,1)}, bf16[17,32,128]{2,1,0:T(8,128)(2,1)S(1)}, u32[]{:S(2)}, u32[]{:S(2)}) collective-permute-start(bf16[17,32,128]{2,1,0:T(8,128)(2,1)} %image_rows.1.refs_6_), channel_id=1, source_target_pairs={{0,4},{1,5},{2,6},{3,7},{4,8},{5,9},{6,10},{7,11},{8,12},{9,13},{1... | collective-permute-start | bytes 417800 | tf_op jit(solution)/shard_map/ppermute | solution.py:44
  77.0 1.4 %collective-permute-done.26.refs_7_ = bf16[17,32,128]{2,1,0:T(8,128)(2,1)S(1)} collective-permute-done((bf16[17,32,128]{2,1,0:T(8,128)(2,1)}, bf16[17,32,128]{2,1,0:T(8,128)(2,1)S(1)}, u32[]{:S(2)}, u32[]{:S(2)}) %collective-permute-start.26) | collective-permute-done | bytes 139296 | tf_op jit(solution)/shard_map/ppermute | solution.py:44
  78.4 1.5 %collective-permute-start.30 = (bf16[17,32,128]{2,1,0:T(8,128)(2,1)S(1)}, bf16[17,32,128]{2,1,0:T(8,128)(2,1)S(1)}, u32[]{:S(2)}, u32[]{:S(2)}) collective-permute-start(bf16[17,32,128]{2,1,0:T(8,128)(2,1)S(1)} %collective-permute-done.26.refs_7_), channel_id=1, source_target_pairs={{2,0},{3,1},{0,2},{1,3},{6,4},{7,5},{4,6},{5,7},{10,8},{11,9},{8,1... | collective-permute-start | bytes 417800 | tf_op jit(solution)/shard_map/ppermute | solution.py:44
  79.9 2.5 %collective-permute-done.27.refs_8_ = bf16[17,32,128]{2,1,0:T(8,128)(2,1)S(1)} collective-permute-done((bf16[17,32,128]{2,1,0:T(8,128)(2,1)}, bf16[17,32,128]{2,1,0:T(8,128)(2,1)S(1)}, u32[]{:S(2)}, u32[]{:S(2)}) %collective-permute-start.27) | collective-permute-done | bytes 139296 | tf_op jit(solution)/shard_map/ppermute | solution.py:44
  82.4 1.5 %collective-permute-start.31 = (bf16[17,32,128]{2,1,0:T(8,128)(2,1)S(1)}, bf16[17,32,128]{2,1,0:T(8,128)(2,1)S(1)}, u32[]{:S(2)}, u32[]{:S(2)}) collective-permute-start(bf16[17,32,128]{2,1,0:T(8,128)(2,1)S(1)} %collective-permute-done.27.refs_8_), channel_id=1, source_target_pairs={{2,0},{3,1},{0,2},{1,3},{6,4},{7,5},{4,6},{5,7},{10,8},{11,9},{8,1... | collective-permute-start | bytes 417800 | tf_op jit(solution)/shard_map/ppermute | solution.py:44
  84.6 2.9 %collective-permute-done.31.refs_14_ = bf16[17,32,128]{2,1,0:T(8,128)(2,1)S(1)} collective-permute-done((bf16[17,32,128]{2,1,0:T(8,128)(2,1)S(1)}, bf16[17,32,128]{2,1,0:T(8,128)(2,1)S(1)}, u32[]{:S(2)}, u32[]{:S(2)}) %collective-permute-start.31) | collective-permute-done | bytes 139296 | tf_op jit(solution)/shard_map/ppermute | solution.py:44
  87.6 1.6 %collective-permute-start.23 = (f32[8,128]{1,0:T(8,128)S(1)}, f32[8,128]{1,0:T(8,128)S(1)}, u32[]{:S(2)}, u32[]{:S(2)}) collective-permute-start(f32[8,128]{1,0:T(8,128)S(1)} %maximum_maximum_fusion.refs_2_), channel_id=1, source_target_pairs={{4,0},{0,4},{12,8},{8,12},{5,1},{1,5},{13,9},{9,13},{6,2},{2,6},{1... | collective-permute-start | bytes 12296 | tf_op jit(solution)/shard_map/ppermute | solution.py:84
  89.2 2.0 %collective-permute-start.24 = (f32[8,128]{1,0:T(8,128)S(1)}, f32[8,128]{1,0:T(8,128)S(1)}, u32[]{:S(2)}, u32[]{:S(2)}) collective-permute-start(f32[8,128]{1,0:T(8,128)S(1)} %maximum_maximum_fusion.refs_2_), channel_id=1, source_target_pairs={{8,0},{12,4},{0,8},{4,12},{9,1},{13,5},{1,9},{5,13},{10,2},{14,6},... | collective-permute-start | bytes 12296 | tf_op jit(solution)/shard_map/ppermute | solution.py:84
  92.0 1.7 %collective-permute-done.24.refs_4_ = f32[8,128]{1,0:T(8,128)S(1)} collective-permute-done((f32[8,128]{1,0:T(8,128)S(1)}, f32[8,128]{1,0:T(8,128)S(1)}, u32[]{:S(2)}, u32[]{:S(2)}) %collective-permute-start.24) | collective-permute-done | bytes 4128 | tf_op jit(solution)/shard_map/ppermute | solution.py:84
  93.7 2.9 %collective-permute-done.25.refs_5_ = f32[8,128]{1,0:T(8,128)S(1)} collective-permute-done((f32[8,128]{1,0:T(8,128)S(1)}, f32[8,128]{1,0:T(8,128)S(1)}, u32[]{:S(2)}, u32[]{:S(2)}) %collective-permute-start.25) | collective-permute-done | bytes 4128 | tf_op jit(solution)/shard_map/ppermute | solution.py:84
  97.3 13.1 %correction_image_rows.1 = bf16[16,32,128]{2,1,0:T(8,128)(2,1)} custom-call(s32[4]{0:T(128)} %refs_0_.3, s32[4]{0:T(128)} %refs_1_.3, f32[8,128]{1,0:T(8,128)} %copy-done.4, f32[8,128]{1,0:T(8,128)} %copy-done.28, f32[8,128]{1,0:T(8,128)} %copy-done.29, f32[8,128]{1,0:T(8,128)} %copy-done.30, bf16[17,32,128]{2,1,0:T(8,128)(2,1)} %image_rows.1.refs_6_, ...), custom_call_target="tpu_custom_call" | custom-call | flops 12000000000 | tf_op jit(solution)/shard_map/correction_image_rows/pallas_call | solution.py:494
  110.4 3.3 %all-to-all-start = ((bf16[4,4,32,128]{3,2,1,0:T(8,128)(2,1)}), bf16[4,4,32,128]{3,2,1,0:T(8,128)(2,1)S(1)}, u32[]{:S(2)}, u32[]{:S(2)}) async-start(bf16[4,4,32,128]{3,2,1,0:T(8,128)(2,1)} %bitcast.115), calls=%async_computation | async-start | bytes 262144 | tf_op jit(solution)/shard_map/all_to_all | solution.py:524
  114.5 3.8 %all-to-all-done = bf16[4,4,32,128]{3,2,1,0:T(8,128)(2,1)S(1)} async-done(((bf16[4,4,32,128]{3,2,1,0:T(8,128)(2,1)}), bf16[4,4,32,128]{3,2,1,0:T(8,128)(2,1)S(1)}, u32[]{:S(2)}, u32[]{:S(2)}) %all-to-all-start) | async-done | bytes 131104 | tf_op jit(solution)/shard_map/all_to_all | solution.py:524
  (146 shorter events, 22.4 us)
Async XLA Ops:
  0.6 29.6 %collective-permute-start.1 = (bf16[1,4,128,128]{3,2,1,0:T(8,128)(2,1)}, bf16[1,4,128,128]{3,2,1,0:T(8,128)(2,1)S(1)}, u32[]{:S(2)}, u32[]{:S(2)}) collective-permute-start(bf16[1,4,128,128]{3,2,1,0:T(8,128)(2,1)} %refs_3_.1), channel_id=1, source_target_pairs={{4,0},{5,1},{6,2},{7,3},{8,4},{9,5},{10,6},{11,7},{12,8},{13,9},{1... | collective-permute-start | bytes 393224 | tf_op jit(solution)/shard_map/ppermute | solution.py:44
  1.9 27.7 %collective-permute-start = (bf16[1,4,128,128]{3,2,1,0:T(8,128)(2,1)}, bf16[1,4,128,128]{3,2,1,0:T(8,128)(2,1)S(1)}, u32[]{:S(2)}, u32[]{:S(2)}) collective-permute-start(bf16[1,4,128,128]{3,2,1,0:T(8,128)(2,1)} %refs_3_.1), channel_id=1, source_target_pairs={{0,4},{1,5},{2,6},{3,7},{4,8},{5,9},{6,10},{7,11},{8,12},{9,13},{1... | collective-permute-start | bytes 393224 | tf_op jit(solution)/shard_map/ppermute | solution.py:44
  7.5 22.8 %collective-permute-start.5 = (bf16[1,4,128,128]{3,2,1,0:T(8,128)(2,1)}, bf16[1,4,128,128]{3,2,1,0:T(8,128)(2,1)S(1)}, u32[]{:S(2)}, u32[]{:S(2)}) collective-permute-start(bf16[1,4,128,128]{3,2,1,0:T(8,128)(2,1)} %refs_3_.1), channel_id=1, source_target_pairs={{2,0},{3,1},{0,2},{1,3},{6,4},{7,5},{4,6},{5,7},{10,8},{11,9},{8,1... | collective-permute-start | bytes 393224 | tf_op jit(solution)/shard_map/ppermute | solution.py:44
  11.4 12.0 %collective-permute-start.14 = (bf16[10,128,128]{2,1,0:T(8,128)(2,1)S(1)}, bf16[10,128,128]{2,1,0:T(8,128)(2,1)S(1)}, u32[]{:S(2)}, u32[]{:S(2)}) collective-permute-start(bf16[10,128,128]{2,1,0:T(8,128)(2,1)S(1)} %dynamic-slice_bitcast_fusion), channel_id=1, source_target_pairs={{4,0},{5,1},{6,2},{7,3},{8,4},{9,5},{10,6},{11,7},{12,8},{13,9},{1... | collective-permute-start | bytes 983048 | tf_op jit(solution)/shard_map/ppermute | solution.py:44
  14.3 11.5 %collective-permute-start.12 = (bf16[5,32,128]{2,1,0:T(8,128)(2,1)S(1)}, bf16[5,32,128]{2,1,0:T(8,128)(2,1)S(1)}, u32[]{:S(2)}, u32[]{:S(2)}) collective-permute-start(bf16[5,32,128]{2,1,0:T(8,128)(2,1)S(1)} %get-tuple-element.13), channel_id=1, source_target_pairs={{2,0},{3,1},{0,2},{1,3},{6,4},{7,5},{4,6},{5,7},{10,8},{11,9},{8,1... | collective-permute-start | bytes 122888 | tf_op jit(solution)/shard_map/ppermute | solution.py:44
  23.4 11.2 %collective-permute-start.16 = (bf16[10,128,128]{2,1,0:T(8,128)(2,1)S(1)}, bf16[10,128,128]{2,1,0:T(8,128)(2,1)S(1)}, u32[]{:S(2)}, u32[]{:S(2)}) collective-permute-start(bf16[10,128,128]{2,1,0:T(8,128)(2,1)S(1)} %collective-permute-done.14.refs_0_.refs_23_), channel_id=1, source_target_pairs={{4,0},{5,1},{6,2},{7,3},{8,4},{9,5},{10,6},{11,7},{12,8},{13,9},{1... | collective-permute-start | bytes 983048 | tf_op jit(solution)/shard_map/ppermute | solution.py:44
  29.6 6.6 %collective-permute-start.2 = (bf16[1,4,128,128]{3,2,1,0:T(8,128)(2,1)}, bf16[1,4,128,128]{3,2,1,0:T(8,128)(2,1)S(1)}, u32[]{:S(2)}, u32[]{:S(2)}) collective-permute-start(bf16[1,4,128,128]{3,2,1,0:T(8,128)(2,1)} %refs_3_.1), channel_id=1, source_target_pairs={{1,0},{0,1},{3,2},{2,3},{5,4},{4,5},{7,6},{6,7},{9,8},{8,9},{11,10... | collective-permute-start | bytes 393224 | tf_op jit(solution)/shard_map/ppermute | solution.py:44
  29.7 8.8 %collective-permute-start.6 = (bf16[1,4,128,128]{3,2,1,0:T(8,128)(2,1)S(1)}, bf16[1,4,128,128]{3,2,1,0:T(8,128)(2,1)S(1)}, u32[]{:S(2)}, u32[]{:S(2)}) collective-permute-start(bf16[1,4,128,128]{3,2,1,0:T(8,128)(2,1)S(1)} %collective-permute-done.refs_4_), channel_id=1, source_target_pairs={{2,0},{3,1},{0,2},{1,3},{6,4},{7,5},{4,6},{5,7},{10,8},{11,9},{8,1... | collective-permute-start | bytes 393224 | tf_op jit(solution)/shard_map/ppermute | solution.py:44
  30.3 8.7 %collective-permute-start.3 = (bf16[1,4,128,128]{3,2,1,0:T(8,128)(2,1)S(1)}, bf16[1,4,128,128]{3,2,1,0:T(8,128)(2,1)S(1)}, u32[]{:S(2)}, u32[]{:S(2)}) collective-permute-start(bf16[1,4,128,128]{3,2,1,0:T(8,128)(2,1)S(1)} %collective-permute-done.refs_4_), channel_id=1, source_target_pairs={{1,0},{0,1},{3,2},{2,3},{5,4},{4,5},{7,6},{6,7},{9,8},{8,9},{11,10... | collective-permute-start | bytes 393224 | tf_op jit(solution)/shard_map/ppermute | solution.py:44
  30.3 8.2 %collective-permute-start.7 = (bf16[1,4,128,128]{3,2,1,0:T(8,128)(2,1)S(1)}, bf16[1,4,128,128]{3,2,1,0:T(8,128)(2,1)}, u32[]{:S(2)}, u32[]{:S(2)}) collective-permute-start(bf16[1,4,128,128]{3,2,1,0:T(8,128)(2,1)S(1)} %collective-permute-done.1.refs_5_), channel_id=1, source_target_pairs={{2,0},{3,1},{0,2},{1,3},{6,4},{7,5},{4,6},{5,7},{10,8},{11,9},{8,1... | collective-permute-start | bytes 393224 | tf_op jit(solution)/shard_map/ppermute | solution.py:44
  34.6 10.3 %collective-permute-start.18 = (bf16[10,128,128]{2,1,0:T(8,128)(2,1)S(1)}, bf16[10,128,128]{2,1,0:T(8,128)(2,1)S(1)}, u32[]{:S(2)}, u32[]{:S(2)}) collective-permute-start(bf16[10,128,128]{2,1,0:T(8,128)(2,1)S(1)} %collective-permute-done.16.refs_2_.refs_25_), channel_id=1, source_target_pairs={{4,0},{5,1},{6,2},{7,3},{8,4},{9,5},{10,6},{11,7},{12,8},{13,9},{1... | collective-permute-start | bytes 983048 | tf_op jit(solution)/shard_map/ppermute | solution.py:44
  38.5 6.4 %collective-permute-start.10 = (bf16[1,4,128,128]{3,2,1,0:T(8,128)(2,1)}, bf16[1,4,128,128]{3,2,1,0:T(8,128)(2,1)}, u32[]{:S(2)}, u32[]{:S(2)}) collective-permute-start(bf16[1,4,128,128]{3,2,1,0:T(8,128)(2,1)} %collective-permute-done.7.refs_11_), channel_id=1, source_target_pairs={{1,0},{0,1},{3,2},{2,3},{5,4},{4,5},{7,6},{6,7},{9,8},{8,9},{11,10... | collective-permute-start | bytes 393224 | tf_op jit(solution)/shard_map/ppermute | solution.py:44
  42.3 20.2 %collective-permute-start.15 = (bf16[10,128,128]{2,1,0:T(8,128)(2,1)S(1)}, bf16[10,128,128]{2,1,0:T(8,128)(2,1)S(1)}, u32[]{:S(2)}, u32[]{:S(2)}) collective-permute-start(bf16[10,128,128]{2,1,0:T(8,128)(2,1)S(1)} %collective-permute-done.14.refs_0_.refs_23_), channel_id=1, source_target_pairs={{1,0},{0,1},{3,2},{2,3},{5,4},{4,5},{7,6},{6,7},{9,8},{8,9},{11,10... | collective-permute-start | bytes 983048 | tf_op jit(solution)/shard_map/ppermute | solution.py:44
  42.7 19.8 %collective-permute-start.17 = (bf16[10,128,128]{2,1,0:T(8,128)(2,1)S(1)}, bf16[10,128,128]{2,1,0:T(8,128)(2,1)S(1)}, u32[]{:S(2)}, u32[]{:S(2)}) collective-permute-start(bf16[10,128,128]{2,1,0:T(8,128)(2,1)S(1)} %collective-permute-done.16.refs_2_.refs_25_), channel_id=1, source_target_pairs={{1,0},{0,1},{3,2},{2,3},{5,4},{4,5},{7,6},{6,7},{9,8},{8,9},{11,10... | collective-permute-start | bytes 983048 | tf_op jit(solution)/shard_map/ppermute | solution.py:44
  44.9 17.6 %collective-permute-start.19 = (bf16[10,128,128]{2,1,0:T(8,128)(2,1)S(1)}, bf16[10,128,128]{2,1,0:T(8,128)(2,1)S(1)}, u32[]{:S(2)}, u32[]{:S(2)}) collective-permute-start(bf16[10,128,128]{2,1,0:T(8,128)(2,1)S(1)} %collective-permute-done.18.refs_4_.refs_27_), channel_id=1, source_target_pairs={{1,0},{0,1},{3,2},{2,3},{5,4},{4,5},{7,6},{6,7},{9,8},{8,9},{11,10... | collective-permute-start | bytes 983048 | tf_op jit(solution)/shard_map/ppermute | solution.py:44
  69.7 7.1 %collective-permute-start.21 = (bf16[17,32,128]{2,1,0:T(8,128)(2,1)}, bf16[17,32,128]{2,1,0:T(8,128)(2,1)S(1)}, u32[]{:S(2)}, u32[]{:S(2)}) collective-permute-start(bf16[17,32,128]{2,1,0:T(8,128)(2,1)} %image_rows.1.refs_6_), channel_id=1, source_target_pairs={{2,0},{3,1},{0,2},{1,3},{6,4},{7,5},{4,6},{5,7},{10,8},{11,9},{8,1... | collective-permute-start | bytes 417800 | tf_op jit(solution)/shard_map/ppermute | solution.py:44
  71.5 6.9 %collective-permute-start.26 = (bf16[17,32,128]{2,1,0:T(8,128)(2,1)}, bf16[17,32,128]{2,1,0:T(8,128)(2,1)S(1)}, u32[]{:S(2)}, u32[]{:S(2)}) collective-permute-start(bf16[17,32,128]{2,1,0:T(8,128)(2,1)} %image_rows.1.refs_6_), channel_id=1, source_target_pairs={{0,4},{1,5},{2,6},{3,7},{4,8},{5,9},{6,10},{7,11},{8,12},{9,13},{1... | collective-permute-start | bytes 417800 | tf_op jit(solution)/shard_map/ppermute | solution.py:44
  74.7 7.7 %collective-permute-start.27 = (bf16[17,32,128]{2,1,0:T(8,128)(2,1)}, bf16[17,32,128]{2,1,0:T(8,128)(2,1)S(1)}, u32[]{:S(2)}, u32[]{:S(2)}) collective-permute-start(bf16[17,32,128]{2,1,0:T(8,128)(2,1)} %image_rows.1.refs_6_), channel_id=1, source_target_pairs={{4,0},{5,1},{6,2},{7,3},{8,4},{9,5},{10,6},{11,7},{12,8},{13,9},{1... | collective-permute-start | bytes 417800 | tf_op jit(solution)/shard_map/ppermute | solution.py:44
  76.8 7.1 %collective-permute-start.22 = (bf16[17,32,128]{2,1,0:T(8,128)(2,1)S(1)}, bf16[17,32,128]{2,1,0:T(8,128)(2,1)S(1)}, u32[]{:S(2)}, u32[]{:S(2)}) collective-permute-start(bf16[17,32,128]{2,1,0:T(8,128)(2,1)S(1)} %collective-permute-done.21.refs_12_), channel_id=1, source_target_pairs={{1,0},{0,1},{3,2},{2,3},{5,4},{4,5},{7,6},{6,7},{9,8},{8,9},{11,10... | collective-permute-start | bytes 417800 | tf_op jit(solution)/shard_map/ppermute | solution.py:44
  79.9 9.2 %collective-permute-start.28 = (bf16[17,32,128]{2,1,0:T(8,128)(2,1)S(1)}, bf16[17,32,128]{2,1,0:T(8,128)(2,1)S(1)}, u32[]{:S(2)}, u32[]{:S(2)}) collective-permute-start(bf16[17,32,128]{2,1,0:T(8,128)(2,1)S(1)} %collective-permute-done.26.refs_7_), channel_id=1, source_target_pairs={{1,0},{0,1},{3,2},{2,3},{5,4},{4,5},{7,6},{6,7},{9,8},{8,9},{11,10... | collective-permute-start | bytes 417800 | tf_op jit(solution)/shard_map/ppermute | solution.py:44
  83.9 7.2 %collective-permute-start.29 = (bf16[17,32,128]{2,1,0:T(8,128)(2,1)S(1)}, bf16[17,32,128]{2,1,0:T(8,128)(2,1)S(1)}, u32[]{:S(2)}, u32[]{:S(2)}) collective-permute-start(bf16[17,32,128]{2,1,0:T(8,128)(2,1)S(1)} %collective-permute-done.27.refs_8_), channel_id=1, source_target_pairs={{1,0},{0,1},{3,2},{2,3},{5,4},{4,5},{7,6},{6,7},{9,8},{8,9},{11,10... | collective-permute-start | bytes 417800 | tf_op jit(solution)/shard_map/ppermute | solution.py:44
  84.0 12.6 %collective-permute-start.32 = (bf16[17,32,128]{2,1,0:T(8,128)(2,1)S(1)}, bf16[17,32,128]{2,1,0:T(8,128)(2,1)S(1)}, u32[]{:S(2)}, u32[]{:S(2)}) collective-permute-start(bf16[17,32,128]{2,1,0:T(8,128)(2,1)S(1)} %collective-permute-done.30.refs_13_), channel_id=1, source_target_pairs={{1,0},{0,1},{3,2},{2,3},{5,4},{4,5},{7,6},{6,7},{9,8},{8,9},{11,10... | collective-permute-start | bytes 417800 | tf_op jit(solution)/shard_map/ppermute | solution.py:44
  87.5 9.1 %collective-permute-start.33 = (bf16[17,32,128]{2,1,0:T(8,128)(2,1)S(1)}, bf16[17,32,128]{2,1,0:T(8,128)(2,1)S(1)}, u32[]{:S(2)}, u32[]{:S(2)}) collective-permute-start(bf16[17,32,128]{2,1,0:T(8,128)(2,1)S(1)} %collective-permute-done.31.refs_14_), channel_id=1, source_target_pairs={{1,0},{0,1},{3,2},{2,3},{5,4},{4,5},{7,6},{6,7},{9,8},{8,9},{11,10... | collective-permute-start | bytes 417800 | tf_op jit(solution)/shard_map/ppermute | solution.py:44
  110.4 7.9 %all-to-all-start = ((bf16[4,4,32,128]{3,2,1,0:T(8,128)(2,1)}), bf16[4,4,32,128]{3,2,1,0:T(8,128)(2,1)S(1)}, u32[]{:S(2)}, u32[]{:S(2)}) async-start(bf16[4,4,32,128]{3,2,1,0:T(8,128)(2,1)} %bitcast.115), calls=%async_computation | async-start | bytes 262144 | tf_op jit(solution)/shard_map/all_to_all | solution.py:524
  (42 other events, 415.9 us)

commit v3 on v2

--- a/solution.py
+++ b/solution.py
@@ -23,14 +23,6 @@
 
 def round_up(value, step):
     return -(-value // step) * step
-
-
-def charge_allowed(weight, row_charge, column_charge):
-    local_charge = jnp.array(STATE_CHARGES, jnp.int32)
-    charge_step = local_charge[:, None] - local_charge[None, :]
-    bond_step = column_charge[None, :] - row_charge[:, None]
-    allowed = charge_step[None, None, :, :] == bond_step[:, :, None, None]
-    return jnp.where(allowed, weight, jnp.zeros_like(weight))
 
 
 def from_near(value, step, flip):
@@ -53,11 +45,81 @@
     return bits
 
 
-def spread(value, steps):
-    pieces = {(step, 0): from_near(value, step, 0) if step else value for step in steps}
-    for bit in mpo_bits():
-        pieces.update({(step, r ^ bit): from_near(piece, 0, bit) for (step, r), piece in list(pieces.items())})
-    return pieces
+def exchange(own, direct):
+    n_bond, n_mpo = lax.axis_size("bond"), lax.axis_size("mpo")
+    here = {0: own, 1: from_near(own, 0, 1)}
+    both = jnp.stack([here[0], here[1]])
+    pairs = [
+        (i * n_mpo + j, (i + 1 - 2 * (j % 2)) * n_mpo + j)
+        for i in range(n_bond)
+        for j in range(n_mpo)
+        if 0 <= i + 1 - 2 * (j % 2) < n_bond
+    ]
+    mine = {0: lax.ppermute(both, ("bond", "mpo"), pairs)}
+    for bit in mpo_bits()[:-1]:
+        for r in range(0, n_mpo, 2):
+            if r in mine and r ^ bit not in mine:
+                here[r ^ bit] = from_near(here[r], 0, bit)
+                if direct:
+                    cross = [(i, (j // n_mpo) * n_mpo + ((j % n_mpo) ^ bit)) for i, j in pairs]
+                    mine[r ^ bit] = lax.ppermute(both, ("bond", "mpo"), cross)
+                else:
+                    mine[r ^ bit] = from_near(mine[r], 0, bit)
+    for r in range(2, n_mpo, 2):
+        here[r ^ 1] = from_near(here[r], 0, 1)
+    other = {r: from_near(pair, 0, 1) for r, pair in mine.items()}
+    return here, mine, other
+
+
+def by_place(here, mine, other):
+    evens = sorted(mine)
+    return [here[r] for r in sorted(here)] + [mine[r] for r in evens] + [other[r] for r in evens]
+
+
+def block_places(n_mpo):
+    places = [(r, None, r, 0) for r in range(n_mpo)]
+    for kind in (1, 2):
+        for r in range(0, n_mpo, 2):
+            array = n_mpo + (kind - 1) * (n_mpo // 2) + r // 2
+            order = (r, r ^ 1) if kind == 1 else (r ^ 1, r)
+            places += [(array, index, member, kind) for index, member in enumerate(order)]
+    return places
+
+
+def sector_of(kind):
+    odd = lax.rem(lax.axis_index("mpo"), 2)
+    if kind == 0:
+        return 0, 0
+    above = odd if kind == 1 else 1 - odd
+    return 1 + above, 2 * above - 1
+
+
+def right_exchange(own, far):
+    n_bond, n_mpo = lax.axis_size("bond"), lax.axis_size("mpo")
+    arrays = []
+    for first in range(1, far + 1, 2):
+        pairs = [
+            ((i + first + j % 2) * n_mpo + j, i * n_mpo + j)
+            for i in range(n_bond)
+            for j in range(n_mpo)
+            if first + j % 2 <= far and i + first + j % 2 < n_bond
+        ]
+        arrays.append(lax.ppermute(own, ("bond", "mpo"), pairs))
+    return arrays
+
+
+def handed_over(arrays, far):
+    n_bond, n_mpo = lax.axis_size("bond"), lax.axis_size("mpo")
+    result = []
+    for place, array in enumerate(arrays):
+        pairs = [
+            (i * n_mpo + j, i * n_mpo + (j ^ 1))
+            for i in range(n_bond)
+            for j in range(n_mpo)
+            if 1 + 2 * place + j % 2 <= far
+        ]
+        result += [array, lax.ppermute(array, ("bond", "mpo"), pairs)]
+    return result
 
 
 def merged(parts):
@@ -109,6 +171,7 @@
         self.k = STATES * self.w_pad
         self.y_step = self.rows + 8
         self.far = min(RIM, n_bond - 1)
+        self.n_far = 2 * ((self.far + 1) // 2)
 
 
 def fill_left(plan, charge_ref, left_near, wide, ls):
@@ -131,18 +194,17 @@
     here = lax.axis_index("bond")
     row = lax.broadcasted_iota(jnp.int32, (plan.width, plan.width), 0)
     column = lax.broadcasted_iota(jnp.int32, (plan.width, plan.width), 1)
-    for c, step in enumerate((0, -1, 1)):
+    for place, (_, _, r, kind) in enumerate(block_places(plan.n_mpo)):
+        slot, step = sector_of(kind)
         sector = here + step
+        first = lax.bitwise_xor(me, r)
         row_ok = row < sector_limits(left_ref, sector, plan.n_bond)
-        for r in range(plan.n_mpo):
-            first = lax.bitwise_xor(me, r)
-            for second in range(STATES):
-                target = sector + state_charge(first) + STATE_CHARGES[second]
-                ok = row_ok & (column < sector_limits(right_ref, target, plan.n_bond))
-                block = psi_near[r * 3 + c, second].astype(F32)
-                fs[first * STATES + second, c * plan.width : (c + 1) * plan.width, :] = jnp.where(
-                    ok, block, 0.0
-                ).astype(BF16)
+        where = pl.ds(pl.multiple_of(slot * plan.width, plan.width), plan.width)
+        for second in range(STATES):
+            target = sector + state_charge(first) + STATE_CHARGES[second]
+            ok = row_ok & (column < sector_limits(right_ref, target, plan.n_bond))
+            block = psi_near[place, second].astype(F32)
+            fs[first * STATES + second, where, :] = jnp.where(ok, block, 0.0).astype(BF16)
 
 
 def left_phase(plan, fs, ls, xs):
@@ -154,13 +216,24 @@
         xs[p + 1] = done[:, plan.width :]
         return carry
 
-    lax.fori_loop(0, PAIRS // 2, step, 0, unroll=2)
-
-
-def middle_phase(plan, groups, xs, first_ref, second_ref, ys):
+    lax.fori_loop(0, PAIRS // 2, step, 0, unroll=4)
+
+
+def middle_phase(plan, groups, xs, sites_ref, ys):
     pad = plan.w_pad
-    first = first_ref[...]
-    second = second_ref[...]
+    first = sites_ref[0]
+    second = sites_ref[1]
+    if groups > 1:
+        column = lax.broadcasted_iota(jnp.int32, first.shape, 1)
+        wide = first.astype(F32)
+        rows = []
+        for g in range(groups):
+            ok = jnp.zeros(first.shape, jnp.bool_)
+            for a in range(STATES):
+                start = a * pad + g * plan.w_here
+                ok = ok | ((column >= start) & (column < start + plan.w_here))
+            rows.append(jnp.where(ok, wide, 0.0))
+        first = jnp.concatenate(rows, 0).astype(BF16)
 
     def step(index, carry):
         middle = []
@@ -189,7 +262,7 @@
                     ]
         return carry
 
-    lax.fori_loop(0, plan.rows // 2, step, 0, unroll=2)
+    lax.fori_loop(0, plan.rows // 2, step, 0, unroll=4)
 
 
 def right_phase(plan, split, ys, right_near, ready):
@@ -221,20 +294,13 @@
 
 
 def right_copies(plan, own_ref, far_refs, right_near, sems):
-    half = plan.w // 2
-    core = lax.rem(lax.axis_index("mpo"), 2)
-    copies = [[pltpu.make_async_copy(own_ref.at[:, 0], right_near.at[0], sems.at[0])]]
-    for d in range(1, plan.far + 1):
-        pair = []
-        for other in range(2):
-            start = lax.bitwise_xor(core, other) * half
-            place = 2 * (d - 1) + other
-            pair.append(
-                pltpu.make_async_copy(
-                    far_refs[place], right_near.at[d, pl.ds(start, half)], sems.at[1 + place]
-                )
-            )
-        copies.append(pair)
+    odd = lax.rem(lax.axis_index("mpo"), 2)
+    copies = [[] for _ in range(plan.far + 1)]
+    copies[0].append(pltpu.make_async_copy(own_ref.at[:, 0], right_near.at[0], sems.at[0]))
+    for place, source in enumerate(far_refs):
+        first, other = 1 + 2 * (place // 2), place % 2
+        slot = first + (1 - odd if other else odd)
+        copies[first].append(pltpu.make_async_copy(source.at[:, 0], right_near.at[slot], sems.at[1 + place]))
     return copies
 
 
@@ -259,23 +325,28 @@
     return jnp.sum(jnp.sum(values, axis=1, keepdims=True), axis=0, keepdims=True)
 
 
+def near_copies(plan, refs, near, sems, count):
+    copies = []
+    for place, (array, index, _, _) in enumerate(block_places(plan.n_mpo)):
+        source = refs[array] if index is None else refs[array].at[index]
+        copies.append(pltpu.make_async_copy(source.at[pl.ds(0, count)], near.at[place], sems.at[place]))
+    return copies
+
+
 def first_kernel(plan, *refs):
     charge_ref, left_ref, right_ref = refs[:3]
-    psi_refs = refs[3 : 3 + 3 * plan.n_mpo]
-    left_refs = refs[3 + 3 * plan.n_mpo : 3 + 4 * plan.n_mpo]
-    first_ref, second_ref, ys, fs_out, ls_out, fs, ls, wide, xs, left_near, psi_near, left_sem, psi_sem, out_sem = refs[
-        3 + 4 * plan.n_mpo :
+    psi_refs = refs[3 : 3 + 2 * plan.n_mpo]
+    left_refs = refs[3 + 2 * plan.n_mpo : 3 + 3 * plan.n_mpo]
+    sites_ref, ys, fs_out, ls_out, fs, ls, wide, xs, left_near, psi_near, left_sem, psi_sem, out_sem = refs[
+        3 + 3 * plan.n_mpo :
     ]
     me = lax.axis_index("mpo")
     rows_here = pl.ds(pl.multiple_of(me * plan.rows, plan.rows), plan.rows)
-    left_copies = []
-    for r, source in enumerate(left_refs):
-        source = source.at[:, rows_here, :] if r == 0 else source
-        left_copies.append(pltpu.make_async_copy(source, left_near.at[r], left_sem.at[r]))
-    psi_copies = [
-        pltpu.make_async_copy(source, psi_near.at[pl.ds(place, 1)], psi_sem.at[place])
-        for place, source in enumerate(psi_refs)
+    left_copies = [
+        pltpu.make_async_copy(source.at[:, rows_here, :], left_near.at[r], left_sem.at[r])
+        for r, source in enumerate(left_refs)
     ]
+    psi_copies = near_copies(plan, psi_refs, psi_near, psi_sem, STATES)
     for copy in left_copies + psi_copies:
         copy.start()
     for copy in left_copies:
@@ -289,13 +360,13 @@
     fs_copy = pltpu.make_async_copy(fs, fs_out, out_sem.at[1])
     fs_copy.start()
     left_phase(plan, fs, ls, xs)
-    middle_phase(plan, plan.n_mpo, xs, first_ref, second_ref, ys)
+    middle_phase(plan, plan.n_mpo, xs, sites_ref, ys)
     ls_copy.wait()
     fs_copy.wait()
 
 
 def image_kernel(plan, left_ref, right_ref, ys_ref, vector_ref, own_ref, *refs):
-    far_refs, (image, ys, right_near, vector, y_sem, right_sem, v_sem) = refs[: 2 * plan.far], refs[2 * plan.far :]
+    far_refs, (image, ys, right_near, vector, y_sem, right_sem, v_sem) = refs[: plan.n_far], refs[plan.n_far :]
     me = lax.axis_index("mpo")
     rows_here = pl.ds(pl.multiple_of(me * plan.rows, plan.rows), plan.rows)
     charges = pair_charges()
@@ -349,15 +420,13 @@
 def second_kernel(plan, count_all, n_parts, *refs):
     left_ref, right_ref = refs[:2]
     parts, refs = refs[2 : 2 + n_parts], refs[2 + n_parts :]
-    image_refs, refs = refs[: 3 * plan.n_mpo], refs[3 * plan.n_mpo :]
-    vector_ref, ls_ref, first_ref, second_ref, own_ref = refs[:5]
-    far_refs, refs = refs[5 : 5 + 2 * plan.far], refs[5 + 2 * plan.far :]
-    out, fs, xs, ys, image_near, vector, ls, right_near, image_sem, field_sem, right_sem = refs
+    image_refs, refs = refs[: 2 * plan.n_mpo], refs[2 * plan.n_mpo :]
+    vector_ref, ls_ref, sites_ref, own_ref = refs[:4]
+    far_refs, refs = refs[4 : 4 + plan.n_far], refs[4 + plan.n_far :]
+    outs, image_out = refs[: plan.n_mpo], refs[plan.n_mpo]
+    fs, xs, ys, image_near, vector, ls, right_near, image_sem, field_sem, right_sem, out_sem = refs[plan.n_mpo + 1 :]
     me = lax.axis_index("mpo")
-    image_copies = [
-        pltpu.make_async_copy(source.at[pl.ds(0, PAIRS)], image_near.at[place], image_sem.at[place])
-        for place, source in enumerate(image_refs)
-    ]
+    image_copies = near_copies(plan, image_refs, image_near, image_sem, PAIRS)
     v_copy = pltpu.make_async_copy(vector_ref, vector, field_sem.at[0])
     l_copy = pltpu.make_async_copy(ls_ref, ls, field_sem.at[1])
     r_copies = right_copies(plan, own_ref, far_refs, right_near, right_sem)
@@ -367,29 +436,47 @@
     rayleigh = sums[0:1, :] / sums[1:2, :]
     scale = lax.rsqrt(sums[2:3, :] / count_all + EPSILON)
     v_copy.wait()
-    for r in range(plan.n_mpo):
-        start = lax.bitwise_xor(me, r) * plan.rows
-        for c in range(3):
-            image_copies[r * 3 + c].wait()
-            where = pl.ds(pl.multiple_of(c * plan.width + start, plan.rows), plan.rows)
-            for p in range(PAIRS):
-                block = image_near[r * 3 + c, p].astype(F32)
-                residual = block - rayleigh * vector[p, where, :].astype(F32)
-                fs[p, where, :] = (residual * scale).astype(BF16)
+    for place, (_, _, r, kind) in enumerate(block_places(plan.n_mpo)):
+        image_copies[place].wait()
+        slot, _ = sector_of(kind)
+        start = slot * plan.width + lax.bitwise_xor(me, r) * plan.rows
+        where = pl.ds(pl.multiple_of(start, plan.rows), plan.rows)
+        for p in range(PAIRS):
+            block = image_near[place, p].astype(F32)
+            residual = block - rayleigh * vector[p, where, :].astype(F32)
+            fs[p, where, :] = (residual * scale).astype(BF16)
+    out_copies = []
+    pairs_here = pl.ds(me * STATES, STATES)
+    for place, (_, _, r, kind) in enumerate(block_places(plan.n_mpo)):
+        if kind == 0:
+            start = lax.bitwise_xor(me, r) * plan.rows
+            rows = pl.ds(pl.multiple_of(start, plan.rows), plan.rows)
+            out_copies.append(
+                pltpu.make_async_copy(image_near.at[place, pairs_here], image_out.at[0, :, rows, :], out_sem.at[r])
+            )
+    for copy in out_copies:
+        copy.start()
     l_copy.wait()
     left_phase(plan, fs, ls, xs)
-    middle_phase(plan, 1, xs, first_ref, second_ref, ys)
+    middle_phase(plan, 1, xs, sites_ref, ys)
 
     def ready(n):
         for copy in r_copies[n]:
             copy.wait()
 
     result = right_phase(plan, False, ys, right_near, ready)
-    for p, block in enumerate(masked_rows(plan, left_ref, right_ref, result)):
-        out[p] = block
-
-
-COST_A = 12_000_000_000
+    rows = masked_rows(plan, left_ref, right_ref, result)
+    for p in range(PAIRS):
+        ys[p, : plan.rows, :] = rows[p].astype(F32)
+    for r, out in enumerate(outs):
+        first = lax.bitwise_xor(me, r) * STATES
+        for second in range(STATES):
+            out[second] = ys[first + second, : plan.rows, :].astype(BF16)
+    for copy in out_copies:
+        copy.wait()
+
+
+COST_A = 2_000_000_000
 COST_B = 4_000_000_000
 VMEM = pl.BlockSpec(memory_space=pltpu.VMEM)
 ANY = pl.BlockSpec(memory_space=pl.ANY)
@@ -408,35 +495,23 @@
     plan = Plan(n_mpo, n_bond, width, right_env.shape[0])
     me = lax.axis_index("mpo")
 
-    steps = (0, -1, 1)
-    by_sector = spread(psi, steps)
-    psi_pieces = [by_sector[step, r] for r in range(n_mpo) for step in steps]
+    psi_here, psi_mine, psi_other = exchange(psi[0], False)
 
     left_mine = left_env[:, 0]
-    left_pieces = []
-    for r in range(1, n_mpo):
-        start = lax.bitwise_xor(me, r) * plan.rows
-        left_pieces.append(from_near(lax.dynamic_slice_in_dim(left_mine, start, plan.rows, 1), 0, r))
-
-    half = plan.w // 2
-    here = lax.dynamic_slice_in_dim(right_env[:, 0], lax.rem(me, 2) * half, half, 0)
-    right_far = []
-    for d in range(1, plan.far + 1):
-        here = from_near(here, 1, 0)
-        right_far.append(here)
+    left_here = {0: left_mine}
+    for bit in mpo_bits():
+        left_here.update({r ^ bit: from_near(block, 0, bit) for r, block in list(left_here.items())})
+    left_pieces = [left_here[r] for r in range(n_mpo)]
+
+    right_far = right_exchange(right_env, plan.far)
+
     pad = plan.w_pad - plan.w
-    first = charge_allowed(site_one, mpo_charge, mpo_charge)
-    first = jnp.transpose(first, (2, 1, 3, 0))
-    first = jnp.pad(first, ((0, 0), (0, pad), (0, 0), (0, pad)))
-    group_of = jnp.arange(plan.w_pad, dtype=jnp.int32) // plan.w_here
-    groups = jnp.arange(n_mpo, dtype=jnp.int32)
-    mine = (group_of[None, :] == groups[:, None])[:, None, None, None, :]
-    first_whole = first.reshape(plan.k, plan.k)
-    first_wide = jnp.where(mine, first[None], jnp.zeros_like(first[None]))
-    first_wide = first_wide.reshape(n_mpo * plan.k, plan.k)
-    second = charge_allowed(site_two, mpo_charge, mpo_charge)
-    second = jnp.transpose(second, (2, 1, 3, 0))
-    second = jnp.pad(second, ((0, 0), (0, pad), (0, 0), (0, pad))).reshape(plan.k, plan.k)
+    charge_step = jnp.array(STATE_CHARGES, jnp.int32)
+    charge_step = charge_step[:, None, None, None] - charge_step[None, None, :, None]
+    bond_step = mpo_charge[None, :, None, None] - mpo_charge[None, None, None, :]
+    sites = jnp.transpose(jnp.stack([site_one, site_two]), (0, 3, 2, 4, 1))
+    sites = jnp.where((charge_step == bond_step)[None], sites, jnp.zeros_like(sites))
+    sites = jnp.pad(sites, ((0, 0), (0, 0), (0, pad), (0, 0), (0, pad))).reshape(2, plan.k, plan.k)
 
     field_shape = (PAIRS, 3 * width, width)
     left_shape = (plan.rows * plan.w_pad, 3 * width)
@@ -447,7 +522,7 @@
     ys, vector, left_rows = pl.pallas_call(
         functools.partial(first_kernel, plan),
         out_shape=(shape_of(y_shape, F32), shape_of(field_shape, BF16), shape_of(left_shape, BF16)),
-        in_specs=[SMEM] * 3 + [ANY] * (4 * n_mpo) + [VMEM] * 2,
+        in_specs=[SMEM] * 3 + [ANY] * (3 * n_mpo) + [VMEM],
         out_specs=(VMEM, ANY, ANY),
         scratch_shapes=[
             pltpu.VMEM(field_shape, BF16),
@@ -463,22 +538,25 @@
         compiler_params=PARAMS,
         cost_estimate=pl.CostEstimate(flops=COST_A, bytes_accessed=0, transcendentals=0),
         name="states_of_vector",
-    )(mpo_charge, left_sizes, right_sizes, *psi_pieces, left_mine, *left_pieces, first_wide, second)
-
-    right_pieces = [piece for far in right_far for piece in (far, from_near(far, 0, 1))]
-    right_scratch = pltpu.VMEM((plan.far + 1, plan.w, width, width), BF16)
+    )(
+        mpo_charge, left_sizes, right_sizes, *by_place(psi_here, psi_mine, psi_other), *left_pieces, sites,
+    )
+
+    right_far, ys = lax.optimization_barrier((right_far, ys))
+    right_pieces = handed_over(right_far, plan.far)
+    right_scratch = pltpu.VMEM((plan.n_far + 1, plan.w, width, width), BF16)
     image_shape = (PAIRS + 1,) + row_shape[1:]
     image_rows = pl.pallas_call(
         functools.partial(image_kernel, plan),
         out_shape=shape_of(image_shape, BF16),
-        in_specs=[SMEM] * 2 + [ANY] * (3 + 2 * plan.far),
+        in_specs=[SMEM] * 2 + [ANY] * (3 + plan.n_far),
         out_specs=VMEM,
         scratch_shapes=[
             pltpu.VMEM(y_shape, F32),
             right_scratch,
             pltpu.VMEM(row_shape, BF16),
             pltpu.SemaphoreType.DMA((PAIRS,)),
-            pltpu.SemaphoreType.DMA((1 + 2 * plan.far,)),
+            pltpu.SemaphoreType.DMA((1 + plan.n_far,)),
             pltpu.SemaphoreType.DMA,
         ],
         compiler_params=PARAMS,
@@ -486,16 +564,16 @@
         name="image_rows",
     )(left_sizes, right_sizes, ys, vector, right_env, *right_pieces)
 
-    by_sector = spread(image_rows, steps)
-    image_pieces = [by_sector[step, r] for r in range(n_mpo) for step in steps]
-    sums = summed_over_bond(merged([sums_of(by_sector[0, r]) for r in range(n_mpo)]))
+    image_here, image_mine, image_other = exchange(image_rows, True)
+    blocks, _ = lax.optimization_barrier((image_here, image_mine[0]))
+    sums = summed_over_bond(merged([sums_of(blocks[r]) for r in range(n_mpo)]))
 
     count_all = n_bond * PAIRS * width * width
-    second_rows = pl.pallas_call(
+    *second_rows, image = pl.pallas_call(
         functools.partial(second_kernel, plan, float(count_all), len(sums)),
-        out_shape=shape_of(row_shape, BF16),
-        in_specs=[SMEM] * 2 + [VMEM] * len(sums) + [ANY] * (3 * n_mpo + 2) + [VMEM] * 2 + [ANY] * (1 + 2 * plan.far),
-        out_specs=VMEM,
+        out_shape=(shape_of((STATES,) + row_shape[1:], BF16),) * n_mpo + (shape_of(psi.shape, BF16),),
+        in_specs=[SMEM] * 2 + [VMEM] * len(sums) + [ANY] * (2 * n_mpo + 2) + [VMEM] + [ANY] * (1 + plan.n_far),
+        out_specs=(VMEM,) * n_mpo + (ANY,),
         scratch_shapes=[
             pltpu.VMEM(field_shape, BF16),
             pltpu.VMEM(x_shape, F32),
@@ -506,26 +584,23 @@
             right_scratch,
             pltpu.SemaphoreType.DMA((3 * n_mpo,)),
             pltpu.SemaphoreType.DMA((2,)),
-            pltpu.SemaphoreType.DMA((1 + 2 * plan.far,)),
+            pltpu.SemaphoreType.DMA((1 + plan.n_far,)),
+            pltpu.SemaphoreType.DMA((n_mpo,)),
         ],
         compiler_params=PARAMS,
         cost_estimate=pl.CostEstimate(flops=COST_A, bytes_accessed=0, transcendentals=0),
         name="correction_image_rows",
     )(
-        left_sizes, right_sizes, *sums, *image_pieces, vector, left_rows, first_whole, second, right_env,
-        *right_pieces,
+        left_sizes, right_sizes, *sums, *by_place(image_here, image_mine, image_other), vector, left_rows, sites,
+        right_env, *right_pieces,
     )
 
-    image = jnp.zeros((STATES, width, width), BF16)
-    for r in range(n_mpo):
-        rows_of = lax.bitwise_xor(me, r)
-        block = lax.dynamic_slice_in_dim(by_sector[0, r], me * STATES, STATES, 0)
-        image = lax.dynamic_update_slice_in_dim(image, block, rows_of * plan.rows, 1)
-    result = lax.all_to_all(
-        second_rows.reshape(n_mpo, STATES, plan.rows, width), "mpo", 0, 0, tiled=False
-    )
-    result = jnp.transpose(result, (1, 0, 2, 3)).reshape(STATES, width, width)
-    return (image[None], result[None])
+    result = jnp.zeros((STATES, width, width), BF16)
+    for r, block in enumerate(second_rows):
+        block = from_near(block, 0, r) if r else block
+        start = lax.bitwise_xor(me, r) * plan.rows
+        result = lax.dynamic_update_slice_in_dim(result, block, start, 1)
+    return (image, result[None])
 
 
 def solution(mesh):

time: 120 us -> 100 us (0.83)
  waiting for transfers between devices: 35 us -> 18 us
  local copies, waits for them, and re-layouts: 8.84 us -> 5.77 us
  other arithmetic: 3.77 us -> 5.62 us
  Pallas kernels: 36.8 us -> 35.3 us
    ppermute x0 -> x7, starting transfers between devices: none -> 19.4 us  [the longest x2 8.51 us: exchange(): mine = {0: lax.ppermute(both, ('bond', 'mpo'), pairs)}]
    ppermute x31 -> x17, waiting for transfers between devices: 26.6 us -> 7.5 us  [from_near(): return lax.ppermute(value, ('bond', 'mpo'), pairs)]
    ppermute x31 -> x17, starting transfers between devices: 25.6 us -> 9.19 us  [from_near(): return lax.ppermute(value, ('bond', 'mpo'), pairs)]
    ppermute x0 -> x7, waiting for transfers between devices: none -> 7.05 us  [the longest x1 4.92 us: exchange(): mine[r ^ bit] = lax.ppermute(both, ('bond', 'mpo'), cross)]
    all_to_all x1 -> x0, waiting for transfers between devices: 3.82 us -> none  [shards(): lax.all_to_all(second_rows.reshape(n_mpo, STATES, plan.rows, width), 'mpo...]
    all_to_all x1 -> x0, starting transfers between devices: 3.34 us -> none  [shards(): lax.all_to_all(second_rows.reshape(n_mpo, STATES, plan.rows, width), 'mpo...]
    unnamed x63 -> x51, local copies, waits for them, and re-layouts: 1.8 us -> 4.01 us
    another operation x0 -> x2, other arithmetic: none -> 1.96 us  [exchange(): both = jnp.stack([here[0], here[1]])]
  transfers between devices with their start and end apart: 35 -> 27, of which waited for: 11 -> 9; matrix products, arithmetic and copies ran while one was open for 9% -> 7% of each run, Pallas kernels for 15% -> 16%
where the time goes in v3:
time: 100 us; the launch traced here: 99.9 us
  Pallas kernels  35.3 us (35%)
  starting transfers between devices  34.1 us (34%)
  waiting for transfers between devices  18 us (18%)
  local copies, waits for them, and re-layouts  5.77 us (6%)
  other arithmetic  5.62 us (6%)
  between operations  1.09 us (1%)
    pallas_call x1, Pallas kernels, shards(): pl.pallas_call(functools.partial(first_kernel, plan), out_shape=(shape_of...  16.4 us
    pallas_call x1, Pallas kernels, shards(): pl.pallas_call(functools.partial(second_kernel, plan, float(count_all), l...  12.2 us
    ppermute x17, starting transfers between devices, from_near(): return lax.ppermute(value, ('bond', 'mpo'), pairs)  9.19 us
    ppermute x2, starting transfers between devices, exchange(): mine = {0: lax.ppermute(both, ('bond', 'mpo'), pairs)}  8.51 us
    ppermute x17, waiting for transfers between devices, from_near(): return lax.ppermute(value, ('bond', 'mpo'), pairs)  7.5 us
    pallas_call x1, Pallas kernels, shards(): pl.pallas_call(functools.partial(image_kernel, plan), out_shape=shape_of(...  6.73 us
    ppermute x3, starting transfers between devices, summed_over_bond(): lax.ppermute(parts[0], 'bond', [(i ^ reach * k, i) for i in range(n_bond)])  5.48 us
    ppermute x1, waiting for transfers between devices, exchange(): mine[r ^ bit] = lax.ppermute(both, ('bond', 'mpo'), cross)  4.92 us
  transfers between devices with their start and end apart: 27, of which 9 were waited for; matrix products, arithmetic and copies ran while one was open for 7% of the time, Pallas kernels for 16%

profile of v3, /device:TPU:0, one launch (start us, length us, event | category | flops | bytes accessed | tf_op | source)
XLA Modules:
  0.0 99.9 jit_solution(14073265913286714815)
XLA Ops:
  1.1 1.2 %collective-permute-done.2.refs_4_ = bf16[4,128,128]{2,1,0:T(8,128)(2,1)S(1)} collective-permute-done((bf16[4,128,128]{2,1,0:T(8,128)(2,1)}, bf16[4,128,128]{2,1,0:T(8,128)(2,1)S(1)}, u32[]{:S(2)}, u32[]{:S(2)}) %collective-permute-start.2) | collective-permute-done | bytes 131104 | tf_op jit(solution)/shard_map/ppermute | solution.py:36
  3.3 4.9 %collective-permute-start.5 = (bf16[2,4,128,128]{3,2,1,0:T(8,128)(2,1)S(1)}, bf16[2,4,128,128]{3,2,1,0:T(8,128)(2,1)S(1)}, u32[]{:S(2)}, u32[]{:S(2)}) collective-permute-start(bf16[2,4,128,128]{3,2,1,0:T(8,128)(2,1)S(1)} %pad_maximum_fusion.1), channel_id=1, source_target_pairs={{0,4},{2,6},{4,8},{5,1},{6,10},{7,3},{8,12},{9,5},{10,14},{11,7},{... | collective-permute-start | bytes 786440 | tf_op jit(solution)/shard_map/ppermute | solution.py:58
  8.2 1.6 %collective-permute-start.3 = (bf16[4,128,128]{2,1,0:T(8,128)(2,1)}, bf16[4,128,128]{2,1,0:T(8,128)(2,1)S(1)}, u32[]{:S(2)}, u32[]{:S(2)}) collective-permute-start(bf16[4,128,128]{2,1,0:T(8,128)(2,1)} %bitcast.110), channel_id=1, source_target_pairs={{2,0},{3,1},{0,2},{1,3},{6,4},{7,5},{4,6},{5,7},{10,8},{11,9},{8,1... | collective-permute-start | bytes 393224 | tf_op jit(solution)/shard_map/ppermute | solution.py:36
  10.3 1.3 %collective-permute-start = (bf16[20,1,128,128]{3,2,1,0:T(8,128)(2,1)}, bf16[20,1,128,128]{3,2,1,0:T(8,128)(2,1)S(1)}, u32[]{:S(2)}, u32[]{:S(2)}) collective-permute-start(bf16[20,1,128,128]{3,2,1,0:T(8,128)(2,1)} %refs_17_.1), channel_id=1, source_target_pairs={{4,0},{9,1},{6,2},{11,3},{8,4},{13,5},{10,6},{15,7},{12,8},{14,10}... | collective-permute-start | bytes 1966088 | tf_op jit(solution)/shard_map/ppermute | solution.py:107
  12.0 1.5 %collective-permute-start.6 = (bf16[2,4,128,128]{3,2,1,0:T(8,128)(2,1)S(1)}, bf16[2,4,128,128]{3,2,1,0:T(8,128)(2,1)S(1)}, u32[]{:S(2)}, u32[]{:S(2)}) collective-permute-start(bf16[2,4,128,128]{3,2,1,0:T(8,128)(2,1)S(1)} %collective-permute-done.5.refs_7_), channel_id=1, source_target_pairs={{2,0},{3,1},{0,2},{1,3},{6,4},{7,5},{4,6},{5,7},{10,8},{11,9},{8,1... | collective-permute-start | bytes 786440 | tf_op jit(solution)/shard_map/ppermute | solution.py:36
  14.3 1.3 %collective-permute-start.1 = (bf16[20,1,128,128]{3,2,1,0:T(8,128)(2,1)}, bf16[20,1,128,128]{3,2,1,0:T(8,128)(2,1)S(1)}, u32[]{:S(2)}, u32[]{:S(2)}) collective-permute-start(bf16[20,1,128,128]{3,2,1,0:T(8,128)(2,1)} %refs_17_.1), channel_id=1, source_target_pairs={{12,0},{14,2},{28,16},{30,18}} | collective-permute-start | bytes 1966088 | tf_op jit(solution)/shard_map/ppermute | solution.py:107
  16.9 4.0 %collective-permute-done.6.refs_8_ = bf16[2,4,128,128]{3,2,1,0:T(8,128)(2,1)S(1)} collective-permute-done((bf16[2,4,128,128]{3,2,1,0:T(8,128)(2,1)S(1)}, bf16[2,4,128,128]{3,2,1,0:T(8,128)(2,1)S(1)}, u32[]{:S(2)}, u32[]{:S(2)}) %collective-permute-start.6) | collective-permute-done | bytes 262176 | tf_op jit(solution)/shard_map/ppermute | solution.py:36
  21.6 1.1 %fusion = bf16[2,4,20,4,20]{2,3,1,4,0:T(4,128)(2,1)S(1)} fusion(bf16[1,20,20,4,4]{2,4,3,1,0:T(4,128)(2,1)} %bitcast.113, bf16[1,20,20,4,4]{2,4,3,1,0:T(4,128)(2,1)} %bitcast.114, pred[4,20,4,20]{1,2,0,3:T(4,128)(4,1)S(1)} %broadcast_compare_fusion), kind=kLoop, calls=%fused_computation.3 | loop fusion | flops 25600 | bytes 57600 | tf_op jit(solution)/shard_map/jit(_where)/select_n | solution.py:513
  25.4 16.4 %states_of_vector.1 = (f32[16,800,128]{2,1,0:T(8,128)}, bf16[16,384,128]{2,1,0:T(8,128)(2,1)}, bf16[768,384]{1,0:T(8,128)(2,1)}) custom-call(s32[20]{0:T(128)} %refs_0_.2, s32[4]{0:T(128)} %refs_0_.3, s32[4]{0:T(128)} %refs_1_.3, bf16[4,128,128]{2,1,0:T(8,128)(2,1)} %bitcast.111, bf16[4,128,128]{2,1,0:T(8,128)(2,1)} %copy-done.2, ...), custom_call_target="tpu_custom_call" | custom-call | flops 2000000000 | tf_op jit(solution)/shard_map/states_of_vector/pallas_call | solution.py:522
  41.9 2.0 %collective-permute-start.12 = (bf16[20,1,128,128]{3,2,1,0:T(8,128)(2,1)S(1)}, bf16[20,1,128,128]{3,2,1,0:T(8,128)(2,1)S(1)}, u32[]{:S(2)}, u32[]{:S(2)}) collective-permute-start(bf16[20,1,128,128]{3,2,1,0:T(8,128)(2,1)S(1)} %collective-permute-done.refs_0_.refs_18_), channel_id=1, source_target_pairs={{0,1},{1,0},{2,3},{3,2},{4,5},{5,4},{6,7},{7,6},{8,9},{9,8},{10,11... | collective-permute-start | bytes 1966088 | tf_op jit(solution)/shard_map/ppermute | solution.py:121
  43.8 2.0 %collective-permute-start.13 = (bf16[20,1,128,128]{3,2,1,0:T(8,128)(2,1)S(1)}, bf16[20,1,128,128]{3,2,1,0:T(8,128)(2,1)S(1)}, u32[]{:S(2)}, u32[]{:S(2)}) collective-permute-start(bf16[20,1,128,128]{3,2,1,0:T(8,128)(2,1)S(1)} %collective-permute-done.1.refs_2_.refs_20_), channel_id=1, source_target_pairs={{0,1},{2,3},{4,5},{6,7},{8,9},{10,11},{12,13},{14,15},{16,17},{18,... | collective-permute-start | bytes 1966088 | tf_op jit(solution)/shard_map/ppermute | solution.py:121
  45.8 1.6 %collective-permute-done.13.refs_3_.refs_21_ = bf16[20,1,128,128]{3,2,1,0:T(8,128)(2,1)S(1)} collective-permute-done((bf16[20,1,128,128]{3,2,1,0:T(8,128)(2,1)S(1)}, bf16[20,1,128,128]{3,2,1,0:T(8,128)(2,1)S(1)}, u32[]{:S(2)}, u32[]{:S(2)}) %collective-permute-start.13) | collective-permute-done | bytes 655392 | tf_op jit(solution)/shard_map/ppermute | solution.py:121
  48.3 6.7 %image_rows.1.refs_6_ = bf16[17,32,128]{2,1,0:T(8,128)(2,1)} custom-call(s32[4]{0:T(128)} %refs_0_.3, s32[4]{0:T(128)} %refs_1_.3, f32[16,800,128]{2,1,0:T(8,128)} %get-tuple-element.18.ys_ref, bf16[16,384,128]{2,1,0:T(8,128)(2,1)} %get-tuple-element.19.vector_ref.refs_14_, bf16[20,1,128,128]{3,2,1,0:T(8,128)(2,1)} %refs_17_.1, ...), custom_call_target="tpu_custom_call" | custom-call | flops 4000000000 | tf_op jit(solution)/shard_map/image_rows/pallas_call | solution.py:549
  55.5 1.5 %collective-permute-start.15 = (bf16[17,32,128]{2,1,0:T(8,128)(2,1)}, bf16[17,32,128]{2,1,0:T(8,128)(2,1)S(1)}, u32[]{:S(2)}, u32[]{:S(2)}) collective-permute-start(bf16[17,32,128]{2,1,0:T(8,128)(2,1)} %image_rows.1.refs_6_), channel_id=1, source_target_pairs={{2,0},{3,1},{0,2},{1,3},{6,4},{7,5},{4,6},{5,7},{10,8},{11,9},{8,1... | collective-permute-start | bytes 417800 | tf_op jit(solution)/shard_map/ppermute | solution.py:36
  58.0 3.7 %collective-permute-start.17 = (bf16[2,17,32,128]{3,2,1,0:T(8,128)(2,1)S(1)}, bf16[2,17,32,128]{3,2,1,0:T(8,128)(2,1)S(1)}, u32[]{:S(2)}, u32[]{:S(2)}) collective-permute-start(bf16[2,17,32,128]{3,2,1,0:T(8,128)(2,1)S(1)} %pad_maximum_fusion), channel_id=1, source_target_pairs={{0,4},{2,6},{4,8},{5,1},{6,10},{7,3},{8,12},{9,5},{10,14},{11,7},{... | collective-permute-start | bytes 835592 | tf_op jit(solution)/shard_map/ppermute | solution.py:58
  61.9 4.4 %collective-permute-start.21 = (bf16[2,17,32,128]{3,2,1,0:T(8,128)(2,1)S(1)}, bf16[2,17,32,128]{3,2,1,0:T(8,128)(2,1)S(1)}, u32[]{:S(2)}, u32[]{:S(2)}) collective-permute-start(bf16[2,17,32,128]{3,2,1,0:T(8,128)(2,1)S(1)} %pad_maximum_fusion), channel_id=1, source_target_pairs={{0,6},{2,4},{4,10},{5,3},{6,8},{7,1},{8,14},{9,7},{10,12},{11,5},{... | collective-permute-start | bytes 835592 | tf_op jit(solution)/shard_map/ppermute | solution.py:65
  67.2 4.9 %collective-permute-done.21.refs_11_ = bf16[2,17,32,128]{3,2,1,0:T(8,128)(2,1)S(1)} collective-permute-done((bf16[2,17,32,128]{3,2,1,0:T(8,128)(2,1)S(1)}, bf16[2,17,32,128]{3,2,1,0:T(8,128)(2,1)S(1)}, u32[]{:S(2)}, u32[]{:S(2)}) %collective-permute-start.21) | collective-permute-done | bytes 278560 | tf_op jit(solution)/shard_map/ppermute | solution.py:65
  72.2 3.0 %collective-permute-start.18 = (f32[8,128]{1,0:T(8,128)S(1)}, f32[8,128]{1,0:T(8,128)S(1)}, u32[]{:S(2)}, u32[]{:S(2)}) collective-permute-start(f32[8,128]{1,0:T(8,128)S(1)} %maximum_maximum_fusion.refs_2_), channel_id=1, source_target_pairs={{4,0},{0,4},{12,8},{8,12},{5,1},{1,5},{13,9},{9,13},{6,2},{2,6},{1... | collective-permute-start | bytes 12296 | tf_op jit(solution)/shard_map/ppermute | solution.py:146
  75.7 2.0 %collective-permute-start.20 = (f32[8,128]{1,0:T(8,128)S(1)}, f32[8,128]{1,0:T(8,128)S(1)}, u32[]{:S(2)}, u32[]{:S(2)}) collective-permute-start(f32[8,128]{1,0:T(8,128)S(1)} %maximum_maximum_fusion.refs_2_), channel_id=1, source_target_pairs={{12,0},{8,4},{4,8},{0,12},{13,1},{9,5},{5,9},{1,13},{14,2},{10,6},... | collective-permute-start | bytes 12296 | tf_op jit(solution)/shard_map/ppermute | solution.py:146
  77.7 2.1 %collective-permute-done.19.refs_4_ = f32[8,128]{1,0:T(8,128)S(1)} collective-permute-done((f32[8,128]{1,0:T(8,128)S(1)}, f32[8,128]{1,0:T(8,128)S(1)}, u32[]{:S(2)}, u32[]{:S(2)}) %collective-permute-start.19) | collective-permute-done | bytes 4128 | tf_op jit(solution)/shard_map/ppermute | solution.py:146
  79.8 1.4 %collective-permute-done.20.refs_5_ = f32[8,128]{1,0:T(8,128)S(1)} collective-permute-done((f32[8,128]{1,0:T(8,128)S(1)}, f32[8,128]{1,0:T(8,128)S(1)}, u32[]{:S(2)}, u32[]{:S(2)}) %collective-permute-start.20) | collective-permute-done | bytes 4128 | tf_op jit(solution)/shard_map/ppermute | solution.py:146
  82.0 12.2 %correction_image_rows.1 = (bf16[4,32,128]{2,1,0:T(8,128)(2,1)}, bf16[4,32,128]{2,1,0:T(8,128)(2,1)}, bf16[4,32,128]{2,1,0:T(8,128)(2,1)}, bf16[4,32,128]{2,1,0:T(8,128)(2,1)}, bf16[1,4,128,128]{3,2,1,0:T(8,128)(2,1)}) custom-call(s32[4]{0:T(128)} %refs_0_.3, s32[4]{0:T(128)} %refs_1_.3, f32[8,128]{1,0:T(8,128)} %copy-done.3, f32[8,128]{1,0:T(8,128)} %copy-done.22, ...), custom_call_target="tpu_custom_call" | custom-call | flops 2000000000 | tf_op jit(solution)/shard_map/correction_image_rows/pallas_call | solution.py:572
  94.2 1.4 %collective-permute-start.25 = (bf16[4,32,128]{2,1,0:T(8,128)(2,1)}, bf16[4,32,128]{2,1,0:T(8,128)(2,1)S(1)}, u32[]{:S(2)}, u32[]{:S(2)}) collective-permute-start(bf16[4,32,128]{2,1,0:T(8,128)(2,1)} %get-tuple-element.30), channel_id=1, source_target_pairs={{2,0},{3,1},{0,2},{1,3},{6,4},{7,5},{4,6},{5,7},{10,8},{11,9},{8,1... | collective-permute-start | bytes 98312 | tf_op jit(solution)/shard_map/ppermute | solution.py:36
  96.9 1.5 %collective-permute-done.25 = bf16[4,32,128]{2,1,0:T(8,128)(2,1)S(1)} collective-permute-done((bf16[4,32,128]{2,1,0:T(8,128)(2,1)}, bf16[4,32,128]{2,1,0:T(8,128)(2,1)S(1)}, u32[]{:S(2)}, u32[]{:S(2)}) %collective-permute-start.25) | collective-permute-done | bytes 32800 | tf_op jit(solution)/shard_map/ppermute | solution.py:36
  (107 shorter events, 15.2 us)
Async XLA Ops:
  3.3 8.7 %collective-permute-start.5 = (bf16[2,4,128,128]{3,2,1,0:T(8,128)(2,1)S(1)}, bf16[2,4,128,128]{3,2,1,0:T(8,128)(2,1)S(1)}, u32[]{:S(2)}, u32[]{:S(2)}) collective-permute-start(bf16[2,4,128,128]{3,2,1,0:T(8,128)(2,1)S(1)} %pad_maximum_fusion.1), channel_id=1, source_target_pairs={{0,4},{2,6},{4,8},{5,1},{6,10},{7,3},{8,12},{9,5},{10,14},{11,7},{... | collective-permute-start | bytes 786440 | tf_op jit(solution)/shard_map/ppermute | solution.py:58
  8.2 6.2 %collective-permute-start.3 = (bf16[4,128,128]{2,1,0:T(8,128)(2,1)}, bf16[4,128,128]{2,1,0:T(8,128)(2,1)S(1)}, u32[]{:S(2)}, u32[]{:S(2)}) collective-permute-start(bf16[4,128,128]{2,1,0:T(8,128)(2,1)} %bitcast.110), channel_id=1, source_target_pairs={{2,0},{3,1},{0,2},{1,3},{6,4},{7,5},{4,6},{5,7},{10,8},{11,9},{8,1... | collective-permute-start | bytes 393224 | tf_op jit(solution)/shard_map/ppermute | solution.py:36
  9.7 6.6 %collective-permute-start.10 = (bf16[5,128,128]{2,1,0:T(8,128)(2,1)}, bf16[5,128,128]{2,1,0:T(8,128)(2,1)S(1)}, u32[]{:S(2)}, u32[]{:S(2)}) collective-permute-start(bf16[5,128,128]{2,1,0:T(8,128)(2,1)} %bitcast.115), channel_id=1, source_target_pairs={{2,0},{3,1},{0,2},{1,3},{6,4},{7,5},{4,6},{5,7},{10,8},{11,9},{8,1... | collective-permute-start | bytes 491528 | tf_op jit(solution)/shard_map/ppermute | solution.py:36
  10.3 6.1 %collective-permute-start.9 = (bf16[5,128,128]{2,1,0:T(8,128)(2,1)}, bf16[5,128,128]{2,1,0:T(8,128)(2,1)S(1)}, u32[]{:S(2)}, u32[]{:S(2)}) collective-permute-start(bf16[5,128,128]{2,1,0:T(8,128)(2,1)} %bitcast.116), channel_id=1, source_target_pairs={{1,0},{0,1},{3,2},{2,3},{5,4},{4,5},{7,6},{6,7},{9,8},{8,9},{11,10... | collective-permute-start | bytes 491528 | tf_op jit(solution)/shard_map/ppermute | solution.py:36
  10.3 31.5 %collective-permute-start = (bf16[20,1,128,128]{3,2,1,0:T(8,128)(2,1)}, bf16[20,1,128,128]{3,2,1,0:T(8,128)(2,1)S(1)}, u32[]{:S(2)}, u32[]{:S(2)}) collective-permute-start(bf16[20,1,128,128]{3,2,1,0:T(8,128)(2,1)} %refs_17_.1), channel_id=1, source_target_pairs={{4,0},{9,1},{6,2},{11,3},{8,4},{13,5},{10,6},{15,7},{12,8},{14,10}... | collective-permute-start | bytes 1966088 | tf_op jit(solution)/shard_map/ppermute | solution.py:107
  12.0 8.8 %collective-permute-start.6 = (bf16[2,4,128,128]{3,2,1,0:T(8,128)(2,1)S(1)}, bf16[2,4,128,128]{3,2,1,0:T(8,128)(2,1)S(1)}, u32[]{:S(2)}, u32[]{:S(2)}) collective-permute-start(bf16[2,4,128,128]{3,2,1,0:T(8,128)(2,1)S(1)} %collective-permute-done.5.refs_7_), channel_id=1, source_target_pairs={{2,0},{3,1},{0,2},{1,3},{6,4},{7,5},{4,6},{5,7},{10,8},{11,9},{8,1... | collective-permute-start | bytes 786440 | tf_op jit(solution)/shard_map/ppermute | solution.py:36
  14.3 27.5 %collective-permute-start.1 = (bf16[20,1,128,128]{3,2,1,0:T(8,128)(2,1)}, bf16[20,1,128,128]{3,2,1,0:T(8,128)(2,1)S(1)}, u32[]{:S(2)}, u32[]{:S(2)}) collective-permute-start(bf16[20,1,128,128]{3,2,1,0:T(8,128)(2,1)} %refs_17_.1), channel_id=1, source_target_pairs={{12,0},{14,2},{28,16},{30,18}} | collective-permute-start | bytes 1966088 | tf_op jit(solution)/shard_map/ppermute | solution.py:107
  16.4 4.6 %collective-permute-start.4 = (bf16[4,128,128]{2,1,0:T(8,128)(2,1)S(1)}, bf16[4,128,128]{2,1,0:T(8,128)(2,1)}, u32[]{:S(2)}, u32[]{:S(2)}) collective-permute-start(bf16[4,128,128]{2,1,0:T(8,128)(2,1)S(1)} %collective-permute-done.3.refs_5_), channel_id=1, source_target_pairs={{1,0},{0,1},{3,2},{2,3},{5,4},{4,5},{7,6},{6,7},{9,8},{8,9},{11,10... | collective-permute-start | bytes 393224 | tf_op jit(solution)/shard_map/ppermute | solution.py:36
  16.4 7.5 %collective-permute-start.7 = (bf16[2,4,128,128]{3,2,1,0:T(8,128)(2,1)S(1)}, bf16[2,4,128,128]{3,2,1,0:T(8,128)(2,1)S(1)}, u32[]{:S(2)}, u32[]{:S(2)}) collective-permute-start(bf16[2,4,128,128]{3,2,1,0:T(8,128)(2,1)S(1)} %collective-permute-done.5.refs_7_), channel_id=1, source_target_pairs={{1,0},{0,1},{3,2},{2,3},{5,4},{4,5},{7,6},{6,7},{9,8},{8,9},{11,10... | collective-permute-start | bytes 786440 | tf_op jit(solution)/shard_map/ppermute | solution.py:36
  20.9 3.1 %collective-permute-start.8 = (bf16[2,4,128,128]{3,2,1,0:T(8,128)(2,1)S(1)}, bf16[2,4,128,128]{3,2,1,0:T(8,128)(2,1)S(1)}, u32[]{:S(2)}, u32[]{:S(2)}) collective-permute-start(bf16[2,4,128,128]{3,2,1,0:T(8,128)(2,1)S(1)} %collective-permute-done.6.refs_8_), channel_id=1, source_target_pairs={{1,0},{0,1},{3,2},{2,3},{5,4},{4,5},{7,6},{6,7},{9,8},{8,9},{11,10... | collective-permute-start | bytes 786440 | tf_op jit(solution)/shard_map/ppermute | solution.py:36
  21.0 2.9 %collective-permute-start.11 = (bf16[5,128,128]{2,1,0:T(8,128)(2,1)S(1)}, bf16[5,128,128]{2,1,0:T(8,128)(2,1)S(1)}, u32[]{:S(2)}, u32[]{:S(2)}) collective-permute-start(bf16[5,128,128]{2,1,0:T(8,128)(2,1)S(1)} %collective-permute-done.10.refs_13_), channel_id=1, source_target_pairs={{1,0},{0,1},{3,2},{2,3},{5,4},{4,5},{7,6},{6,7},{9,8},{8,9},{11,10... | collective-permute-start | bytes 491528 | tf_op jit(solution)/shard_map/ppermute | solution.py:36
  41.9 4.0 %collective-permute-start.12 = (bf16[20,1,128,128]{3,2,1,0:T(8,128)(2,1)S(1)}, bf16[20,1,128,128]{3,2,1,0:T(8,128)(2,1)S(1)}, u32[]{:S(2)}, u32[]{:S(2)}) collective-permute-start(bf16[20,1,128,128]{3,2,1,0:T(8,128)(2,1)S(1)} %collective-permute-done.refs_0_.refs_18_), channel_id=1, source_target_pairs={{0,1},{1,0},{2,3},{3,2},{4,5},{5,4},{6,7},{7,6},{8,9},{9,8},{10,11... | collective-permute-start | bytes 1966088 | tf_op jit(solution)/shard_map/ppermute | solution.py:121
  43.8 3.6 %collective-permute-start.13 = (bf16[20,1,128,128]{3,2,1,0:T(8,128)(2,1)S(1)}, bf16[20,1,128,128]{3,2,1,0:T(8,128)(2,1)S(1)}, u32[]{:S(2)}, u32[]{:S(2)}) collective-permute-start(bf16[20,1,128,128]{3,2,1,0:T(8,128)(2,1)S(1)} %collective-permute-done.1.refs_2_.refs_20_), channel_id=1, source_target_pairs={{0,1},{2,3},{4,5},{6,7},{8,9},{10,11},{12,13},{14,15},{16,17},{18,... | collective-permute-start | bytes 1966088 | tf_op jit(solution)/shard_map/ppermute | solution.py:121
  55.5 6.2 %collective-permute-start.15 = (bf16[17,32,128]{2,1,0:T(8,128)(2,1)}, bf16[17,32,128]{2,1,0:T(8,128)(2,1)S(1)}, u32[]{:S(2)}, u32[]{:S(2)}) collective-permute-start(bf16[17,32,128]{2,1,0:T(8,128)(2,1)} %image_rows.1.refs_6_), channel_id=1, source_target_pairs={{2,0},{3,1},{0,2},{1,3},{6,4},{7,5},{4,6},{5,7},{10,8},{11,9},{8,1... | collective-permute-start | bytes 417800 | tf_op jit(solution)/shard_map/ppermute | solution.py:36
  58.0 8.3 %collective-permute-start.17 = (bf16[2,17,32,128]{3,2,1,0:T(8,128)(2,1)S(1)}, bf16[2,17,32,128]{3,2,1,0:T(8,128)(2,1)S(1)}, u32[]{:S(2)}, u32[]{:S(2)}) collective-permute-start(bf16[2,17,32,128]{3,2,1,0:T(8,128)(2,1)S(1)} %pad_maximum_fusion), channel_id=1, source_target_pairs={{0,4},{2,6},{4,8},{5,1},{6,10},{7,3},{8,12},{9,5},{10,14},{11,7},{... | collective-permute-start | bytes 835592 | tf_op jit(solution)/shard_map/ppermute | solution.py:58
  61.7 4.6 %collective-permute-start.16 = (bf16[17,32,128]{2,1,0:T(8,128)(2,1)S(1)}, bf16[17,32,128]{2,1,0:T(8,128)(2,1)S(1)}, u32[]{:S(2)}, u32[]{:S(2)}) collective-permute-start(bf16[17,32,128]{2,1,0:T(8,128)(2,1)S(1)} %collective-permute-done.15.refs_8_), channel_id=1, source_target_pairs={{1,0},{0,1},{3,2},{2,3},{5,4},{4,5},{7,6},{6,7},{9,8},{8,9},{11,10... | collective-permute-start | bytes 417800 | tf_op jit(solution)/shard_map/ppermute | solution.py:36
  61.9 10.2 %collective-permute-start.21 = (bf16[2,17,32,128]{3,2,1,0:T(8,128)(2,1)S(1)}, bf16[2,17,32,128]{3,2,1,0:T(8,128)(2,1)S(1)}, u32[]{:S(2)}, u32[]{:S(2)}) collective-permute-start(bf16[2,17,32,128]{3,2,1,0:T(8,128)(2,1)S(1)} %pad_maximum_fusion), channel_id=1, source_target_pairs={{0,6},{2,4},{4,10},{5,3},{6,8},{7,1},{8,14},{9,7},{10,12},{11,5},{... | collective-permute-start | bytes 835592 | tf_op jit(solution)/shard_map/ppermute | solution.py:65
  67.1 14.0 %collective-permute-start.22 = (bf16[2,17,32,128]{3,2,1,0:T(8,128)(2,1)S(1)}, bf16[2,17,32,128]{3,2,1,0:T(8,128)(2,1)S(1)}, u32[]{:S(2)}, u32[]{:S(2)}) collective-permute-start(bf16[2,17,32,128]{3,2,1,0:T(8,128)(2,1)S(1)} %collective-permute-done.17.refs_10_), channel_id=1, source_target_pairs={{1,0},{0,1},{3,2},{2,3},{5,4},{4,5},{7,6},{6,7},{9,8},{8,9},{11,10... | collective-permute-start | bytes 835592 | tf_op jit(solution)/shard_map/ppermute | solution.py:36
  72.1 9.0 %collective-permute-start.23 = (bf16[2,17,32,128]{3,2,1,0:T(8,128)(2,1)S(1)}, bf16[2,17,32,128]{3,2,1,0:T(8,128)(2,1)S(1)}, u32[]{:S(2)}, u32[]{:S(2)}) collective-permute-start(bf16[2,17,32,128]{3,2,1,0:T(8,128)(2,1)S(1)} %collective-permute-done.21.refs_11_), channel_id=1, source_target_pairs={{1,0},{0,1},{3,2},{2,3},{5,4},{4,5},{7,6},{6,7},{9,8},{8,9},{11,10... | collective-permute-start | bytes 835592 | tf_op jit(solution)/shard_map/ppermute | solution.py:36
  72.2 5.5 %collective-permute-start.18 = (f32[8,128]{1,0:T(8,128)S(1)}, f32[8,128]{1,0:T(8,128)S(1)}, u32[]{:S(2)}, u32[]{:S(2)}) collective-permute-start(f32[8,128]{1,0:T(8,128)S(1)} %maximum_maximum_fusion.refs_2_), channel_id=1, source_target_pairs={{4,0},{0,4},{12,8},{8,12},{5,1},{1,5},{13,9},{9,13},{6,2},{2,6},{1... | collective-permute-start | bytes 12296 | tf_op jit(solution)/shard_map/ppermute | solution.py:146
  75.2 4.5 %collective-permute-start.19 = (f32[8,128]{1,0:T(8,128)S(1)}, f32[8,128]{1,0:T(8,128)S(1)}, u32[]{:S(2)}, u32[]{:S(2)}) collective-permute-start(f32[8,128]{1,0:T(8,128)S(1)} %maximum_maximum_fusion.refs_2_), channel_id=1, source_target_pairs={{8,0},{12,4},{0,8},{4,12},{9,1},{13,5},{1,9},{5,13},{10,2},{14,6},... | collective-permute-start | bytes 12296 | tf_op jit(solution)/shard_map/ppermute | solution.py:146
  75.7 5.4 %collective-permute-start.20 = (f32[8,128]{1,0:T(8,128)S(1)}, f32[8,128]{1,0:T(8,128)S(1)}, u32[]{:S(2)}, u32[]{:S(2)}) collective-permute-start(f32[8,128]{1,0:T(8,128)S(1)} %maximum_maximum_fusion.refs_2_), channel_id=1, source_target_pairs={{12,0},{8,4},{4,8},{0,12},{13,1},{9,5},{5,9},{1,13},{14,2},{10,6},... | collective-permute-start | bytes 12296 | tf_op jit(solution)/shard_map/ppermute | solution.py:146
  94.2 4.2 %collective-permute-start.25 = (bf16[4,32,128]{2,1,0:T(8,128)(2,1)}, bf16[4,32,128]{2,1,0:T(8,128)(2,1)S(1)}, u32[]{:S(2)}, u32[]{:S(2)}) collective-permute-start(bf16[4,32,128]{2,1,0:T(8,128)(2,1)} %get-tuple-element.30), channel_id=1, source_target_pairs={{2,0},{3,1},{0,2},{1,3},{6,4},{7,5},{4,6},{5,7},{10,8},{11,9},{8,1... | collective-permute-start | bytes 98312 | tf_op jit(solution)/shard_map/ppermute | solution.py:36
  95.6 3.6 %collective-permute-start.26 = (bf16[4,32,128]{2,1,0:T(8,128)(2,1)}, bf16[4,32,128]{2,1,0:T(8,128)(2,1)S(1)}, u32[]{:S(2)}, u32[]{:S(2)}) collective-permute-start(bf16[4,32,128]{2,1,0:T(8,128)(2,1)} %get-tuple-element.31), channel_id=1, source_target_pairs={{3,0},{2,1},{1,2},{0,3},{7,4},{6,5},{5,6},{4,7},{11,8},{10,9},{9,1... | collective-permute-start | bytes 98312 | tf_op jit(solution)/shard_map/ppermute | solution.py:36
  (28 other events, 183.1 us)

commit v4 on v3

--- a/solution.py
+++ b/solution.py
@@ -45,30 +45,31 @@
     return bits
 
 
-def exchange(own, direct):
+def exchange(own, cross_last):
     n_bond, n_mpo = lax.axis_size("bond"), lax.axis_size("mpo")
-    here = {0: own, 1: from_near(own, 0, 1)}
-    both = jnp.stack([here[0], here[1]])
     pairs = [
         (i * n_mpo + j, (i + 1 - 2 * (j % 2)) * n_mpo + j)
         for i in range(n_bond)
         for j in range(n_mpo)
         if 0 <= i + 1 - 2 * (j % 2) < n_bond
     ]
-    mine = {0: lax.ppermute(both, ("bond", "mpo"), pairs)}
+    here = {0: own, 1: from_near(own, 0, 1)}
     for bit in mpo_bits()[:-1]:
-        for r in range(0, n_mpo, 2):
-            if r in mine and r ^ bit not in mine:
-                here[r ^ bit] = from_near(here[r], 0, bit)
-                if direct:
-                    cross = [(i, (j // n_mpo) * n_mpo + ((j % n_mpo) ^ bit)) for i, j in pairs]
-                    mine[r ^ bit] = lax.ppermute(both, ("bond", "mpo"), cross)
-                else:
-                    mine[r ^ bit] = from_near(mine[r], 0, bit)
+        here.update({r ^ bit: from_near(here[r], 0, bit) for r in sorted(here) if r % 2 == 0})
     for r in range(2, n_mpo, 2):
         here[r ^ 1] = from_near(here[r], 0, 1)
-    other = {r: from_near(pair, 0, 1) for r, pair in mine.items()}
-    return here, mine, other
+    mine = {}
+    for r in range(0, n_mpo, 2):
+        if r == 0 or not cross_last:
+            mine[r] = lax.ppermute(jnp.stack([here[r], here[r ^ 1]]), ("bond", "mpo"), pairs)
+    if cross_last:
+        for bit in mpo_bits()[:-1]:
+            mine.update({r ^ bit: from_near(pair, 0, bit) for r, pair in list(mine.items())})
+    return here, mine
+
+
+def handed_pairs(mine):
+    return {r: from_near(pair, 0, 1) for r, pair in mine.items()}
 
 
 def by_place(here, mine, other):
@@ -168,7 +169,6 @@
         self.w_here = mpo_width // n_mpo
         self.w_pad = round_up(mpo_width, 8)
         self.rows = width // n_mpo
-        self.k = STATES * self.w_pad
         self.y_step = self.rows + 8
         self.far = min(RIM, n_bond - 1)
         self.n_far = 2 * ((self.far + 1) // 2)
@@ -219,19 +219,50 @@
     lax.fori_loop(0, PAIRS // 2, step, 0, unroll=4)
 
 
-def middle_phase(plan, groups, xs, sites_ref, ys):
-    pad = plan.w_pad
-    first = sites_ref[0]
-    second = sites_ref[1]
+def site_matrices(plan, charge_ref, sites_ref, first_out, second_out):
+    w, pad = plan.w, plan.w_pad
+    size = STATES * w
+
+    def index(shape, axis):
+        return lax.broadcasted_iota(jnp.int32, shape, axis)
+
+    def charges(bond):
+        total = jnp.zeros(bond.shape, jnp.int32)
+        for v in range(w):
+            total = jnp.where(bond == v, charge_ref[v], total)
+        return total
+
+    row, column = index((size, size), 0), index((size, size), 1)
+    local_step = state_charge(row // w) - state_charge(column // w)
+    allowed = local_step == charges(row % w) - charges(column % w)
+    first = jnp.where(allowed, sites_ref[0].astype(F32), 0.0).astype(BF16)
+    second = jnp.where(allowed, sites_ref[1].astype(F32), 0.0).astype(BF16)
+
+    into = (size, STATES * pad)
+    spread_w = (index(into, 0) // w == index(into, 1) // pad) & (index(into, 0) % w == index(into, 1) % pad)
+    first = jnp.dot(first, jnp.where(spread_w, 1.0, 0.0).astype(BF16), preferred_element_type=F32)
+    first_out[...] = first.astype(BF16)
+
+    into = (size, 2 * size)
+    of, to = index(into, 0), index(into, 1)
+    halves = []
+    for k in range(2):
+        spread_v = to == (of // w) * 2 * w + k * w + of % w
+        halves.append(jnp.dot(second, jnp.where(spread_v, 1.0, 0.0).astype(BF16), preferred_element_type=F32))
+    second_out[...] = jnp.concatenate(halves, 0).astype(BF16)
+
+
+def middle_phase(plan, groups, block, unroll, xs, first_ref, second_ref, ys, done):
+    w, pad = plan.w, plan.w_pad
+    first = first_ref[...]
+    second = second_ref[...]
+    size = STATES * w
     if groups > 1:
-        column = lax.broadcasted_iota(jnp.int32, first.shape, 1)
+        column = lax.broadcasted_iota(jnp.int32, first.shape, 1) % pad
         wide = first.astype(F32)
         rows = []
         for g in range(groups):
-            ok = jnp.zeros(first.shape, jnp.bool_)
-            for a in range(STATES):
-                start = a * pad + g * plan.w_here
-                ok = ok | ((column >= start) & (column < start + plan.w_here))
+            ok = (column >= g * plan.w_here) & (column < (g + 1) * plan.w_here)
             rows.append(jnp.where(ok, wide, 0.0))
         first = jnp.concatenate(rows, 0).astype(BF16)
 
@@ -239,33 +270,37 @@
         middle = []
         for b in range(STATES):
             columns = []
-            for one in range(2):
-                start = pl.multiple_of((index * 2 + one) * pad, pad)
+            for one in range(block):
+                start = pl.multiple_of((index * block + one) * pad, pad)
                 columns.append(
                     jnp.concatenate([xs[a * STATES + b, pl.ds(start, pad), :] for a in range(STATES)], 0)
                 )
             column = jnp.concatenate(columns, 1).astype(BF16)
             middle.append(jnp.dot(first, column, preferred_element_type=F32))
-        for s1 in range(STATES):
+        for half in range(STATES // 2):
             total = None
             for g in range(groups):
-                at = g * plan.k + s1 * pad
-                column = jnp.concatenate([z[at : at + pad] for z in middle], 0).astype(BF16)
+                at = g * size + half * 2 * w
+                column = jnp.concatenate([z[at : at + 2 * w] for z in middle], 0).astype(BF16)
                 term = jnp.dot(second, column, preferred_element_type=F32)
                 if groups > 1:
                     term = term.astype(BF16).astype(F32)
                 total = term if total is None else total + term
-            for s2 in range(STATES):
-                for one in range(2):
-                    ys[s1 * STATES + s2, pl.ds(index * 2 + one, plan.w, stride=plan.y_step), :] = total[
-                        s2 * pad : s2 * pad + plan.w, one * plan.width : (one + 1) * plan.width
-                    ]
+            for k in range(2):
+                for s2 in range(STATES):
+                    at = k * size + s2 * w
+                    for one in range(block):
+                        rows = pl.ds(index * block + one, w, stride=plan.y_step)
+                        ys[(2 * half + k) * STATES + s2, rows, :] = total[
+                            at : at + w, one * plan.width : (one + 1) * plan.width
+                        ]
+        done(index)
         return carry
 
-    lax.fori_loop(0, plan.rows // 2, step, 0, unroll=4)
-
-
-def right_phase(plan, split, ys, right_near, ready):
+    lax.fori_loop(0, plan.rows // block, step, 0, unroll=unroll)
+
+
+def right_phase(plan, split, ys, y_step, right_near, ready):
     result = [None] * PAIRS
     for n in range(plan.far + 1):
         ready(n)
@@ -276,7 +311,7 @@
             right = jnp.concatenate([right_near[n, u] for u in group], 1)
             lines = []
             for p in members:
-                parts = [ys[p, pl.ds(u * plan.y_step, plan.rows), :] for u in group]
+                parts = [ys[p, pl.ds(u * y_step, plan.rows), :] for u in group]
                 lines.append(jnp.concatenate(parts, 1))
             field = jnp.concatenate(lines, 0)
             high = field.astype(BF16)
@@ -337,9 +372,9 @@
     charge_ref, left_ref, right_ref = refs[:3]
     psi_refs = refs[3 : 3 + 2 * plan.n_mpo]
     left_refs = refs[3 + 2 * plan.n_mpo : 3 + 3 * plan.n_mpo]
-    sites_ref, ys, fs_out, ls_out, fs, ls, wide, xs, left_near, psi_near, left_sem, psi_sem, out_sem = refs[
-        3 + 3 * plan.n_mpo :
-    ]
+    refs = refs[3 + 3 * plan.n_mpo :]
+    sites_ref, ys_out, fs_out, ls_out, first_out, second_out = refs[:6]
+    fs, ls, wide, xs, ys, left_near, psi_near, left_sem, psi_sem, out_sem, y_sem = refs[6:]
     me = lax.axis_index("mpo")
     rows_here = pl.ds(pl.multiple_of(me * plan.rows, plan.rows), plan.rows)
     left_copies = [
@@ -349,6 +384,7 @@
     psi_copies = near_copies(plan, psi_refs, psi_near, psi_sem, STATES)
     for copy in left_copies + psi_copies:
         copy.start()
+    site_matrices(plan, charge_ref, sites_ref, first_out, second_out)
     for copy in left_copies:
         copy.wait()
     fill_left(plan, charge_ref, left_near, wide, ls)
@@ -360,7 +396,17 @@
     fs_copy = pltpu.make_async_copy(fs, fs_out, out_sem.at[1])
     fs_copy.start()
     left_phase(plan, fs, ls, xs)
-    middle_phase(plan, plan.n_mpo, xs, sites_ref, ys)
+    tiles = ys.reshape(PAIRS, plan.w, plan.y_step, plan.width)
+
+    def out_copy(index):
+        rows = pl.ds(pl.multiple_of(index * Y_BLOCK, Y_BLOCK), Y_BLOCK)
+        return pltpu.make_async_copy(tiles.at[:, :, rows, :], ys_out.at[:, :, rows, :], y_sem.at[index])
+
+    middle_phase(
+        plan, plan.n_mpo, Y_BLOCK, 2, xs, first_out, second_out, ys, lambda index: out_copy(index).start()
+    )
+    for index in range(plan.rows // Y_BLOCK):
+        out_copy(index).wait()
     ls_copy.wait()
     fs_copy.wait()
 
@@ -384,7 +430,7 @@
         for copy in r_copies[n] + [y_copies[p] for p in range(PAIRS) if charges[p] == n]:
             copy.wait()
 
-    result = right_phase(plan, True, ys, right_near, ready)
+    result = right_phase(plan, True, ys, plan.rows, right_near, ready)
     blocks = masked_rows(plan, left_ref, right_ref, result)
     v_copy.wait()
     along = jnp.zeros((plan.rows, plan.width), F32)
@@ -421,8 +467,8 @@
     left_ref, right_ref = refs[:2]
     parts, refs = refs[2 : 2 + n_parts], refs[2 + n_parts :]
     image_refs, refs = refs[: 2 * plan.n_mpo], refs[2 * plan.n_mpo :]
-    vector_ref, ls_ref, sites_ref, own_ref = refs[:4]
-    far_refs, refs = refs[4 : 4 + plan.n_far], refs[4 + plan.n_far :]
+    vector_ref, ls_ref, first_ref, second_ref, own_ref = refs[:5]
+    far_refs, refs = refs[5 : 5 + plan.n_far], refs[5 + plan.n_far :]
     outs, image_out = refs[: plan.n_mpo], refs[plan.n_mpo]
     fs, xs, ys, image_near, vector, ls, right_near, image_sem, field_sem, right_sem, out_sem = refs[plan.n_mpo + 1 :]
     me = lax.axis_index("mpo")
@@ -458,13 +504,13 @@
         copy.start()
     l_copy.wait()
     left_phase(plan, fs, ls, xs)
-    middle_phase(plan, 1, xs, sites_ref, ys)
+    middle_phase(plan, 1, 2 * Y_BLOCK, 2, xs, first_ref, second_ref, ys, lambda index: None)
 
     def ready(n):
         for copy in r_copies[n]:
             copy.wait()
 
-    result = right_phase(plan, False, ys, right_near, ready)
+    result = right_phase(plan, False, ys, plan.y_step, right_near, ready)
     rows = masked_rows(plan, left_ref, right_ref, result)
     for p in range(PAIRS):
         ys[p, : plan.rows, :] = rows[p].astype(F32)
@@ -476,6 +522,7 @@
         copy.wait()
 
 
+Y_BLOCK = 8
 COST_A = 2_000_000_000
 COST_B = 4_000_000_000
 VMEM = pl.BlockSpec(memory_space=pltpu.VMEM)
@@ -495,7 +542,8 @@
     plan = Plan(n_mpo, n_bond, width, right_env.shape[0])
     me = lax.axis_index("mpo")
 
-    psi_here, psi_mine, psi_other = exchange(psi[0], False)
+    psi_here, psi_mine = exchange(psi[0], True)
+    psi_other = handed_pairs(psi_mine)
 
     left_mine = left_env[:, 0]
     left_here = {0: left_mine}
@@ -505,13 +553,8 @@
 
     right_far = right_exchange(right_env, plan.far)
 
-    pad = plan.w_pad - plan.w
-    charge_step = jnp.array(STATE_CHARGES, jnp.int32)
-    charge_step = charge_step[:, None, None, None] - charge_step[None, None, :, None]
-    bond_step = mpo_charge[None, :, None, None] - mpo_charge[None, None, None, :]
     sites = jnp.transpose(jnp.stack([site_one, site_two]), (0, 3, 2, 4, 1))
-    sites = jnp.where((charge_step == bond_step)[None], sites, jnp.zeros_like(sites))
-    sites = jnp.pad(sites, ((0, 0), (0, 0), (0, pad), (0, 0), (0, pad))).reshape(2, plan.k, plan.k)
+    sites = sites.reshape(2, STATES * plan.w, STATES * plan.w)
 
     field_shape = (PAIRS, 3 * width, width)
     left_shape = (plan.rows * plan.w_pad, 3 * width)
@@ -519,21 +562,32 @@
     y_shape = (PAIRS, plan.y_step * plan.w, width)
     row_shape = (PAIRS, plan.rows, width)
 
-    ys, vector, left_rows = pl.pallas_call(
+    first_shape = (STATES * plan.w, STATES * plan.w_pad)
+    second_shape = (2 * STATES * plan.w,) * 2
+    y_out_shape = (PAIRS, plan.w, plan.rows, width)
+    ys, vector, left_rows, first, second = pl.pallas_call(
         functools.partial(first_kernel, plan),
-        out_shape=(shape_of(y_shape, F32), shape_of(field_shape, BF16), shape_of(left_shape, BF16)),
+        out_shape=(
+            shape_of(y_out_shape, F32),
+            shape_of(field_shape, BF16),
+            shape_of(left_shape, BF16),
+            shape_of(first_shape, BF16),
+            shape_of(second_shape, BF16),
+        ),
         in_specs=[SMEM] * 3 + [ANY] * (3 * n_mpo) + [VMEM],
-        out_specs=(VMEM, ANY, ANY),
+        out_specs=(ANY, ANY, ANY, VMEM, VMEM),
         scratch_shapes=[
             pltpu.VMEM(field_shape, BF16),
             pltpu.VMEM(left_shape, BF16),
             pltpu.VMEM((3, left_shape[0], width), F32),
             pltpu.VMEM(x_shape, F32),
+            pltpu.VMEM(y_shape, F32),
             pltpu.VMEM((n_mpo, plan.w_here, plan.rows, width), BF16),
             pltpu.VMEM((3 * n_mpo,) + psi.shape[1:], BF16),
             pltpu.SemaphoreType.DMA((n_mpo,)),
             pltpu.SemaphoreType.DMA((3 * n_mpo,)),
             pltpu.SemaphoreType.DMA((2,)),
+            pltpu.SemaphoreType.DMA((plan.rows // Y_BLOCK,)),
         ],
         compiler_params=PARAMS,
         cost_estimate=pl.CostEstimate(flops=COST_A, bytes_accessed=0, transcendentals=0),
@@ -552,7 +606,7 @@
         in_specs=[SMEM] * 2 + [ANY] * (3 + plan.n_far),
         out_specs=VMEM,
         scratch_shapes=[
-            pltpu.VMEM(y_shape, F32),
+            pltpu.VMEM((PAIRS, plan.w * plan.rows, width), F32),
             right_scratch,
             pltpu.VMEM(row_shape, BF16),
             pltpu.SemaphoreType.DMA((PAIRS,)),
@@ -562,17 +616,18 @@
         compiler_params=PARAMS,
         cost_estimate=pl.CostEstimate(flops=COST_B, bytes_accessed=0, transcendentals=0),
         name="image_rows",
-    )(left_sizes, right_sizes, ys, vector, right_env, *right_pieces)
-
-    image_here, image_mine, image_other = exchange(image_rows, True)
-    blocks, _ = lax.optimization_barrier((image_here, image_mine[0]))
-    sums = summed_over_bond(merged([sums_of(blocks[r]) for r in range(n_mpo)]))
+    )(left_sizes, right_sizes, ys.reshape(PAIRS, plan.w * plan.rows, width), vector, right_env, *right_pieces)
+
+    image_here, image_mine = exchange(image_rows, False)
+    sums = summed_over_bond(merged([sums_of(image_here[r]) for r in range(n_mpo)]))
+    image_mine, sums = lax.optimization_barrier((image_mine, sums))
+    image_other = handed_pairs(image_mine)
 
     count_all = n_bond * PAIRS * width * width
     *second_rows, image = pl.pallas_call(
         functools.partial(second_kernel, plan, float(count_all), len(sums)),
         out_shape=(shape_of((STATES,) + row_shape[1:], BF16),) * n_mpo + (shape_of(psi.shape, BF16),),
-        in_specs=[SMEM] * 2 + [VMEM] * len(sums) + [ANY] * (2 * n_mpo + 2) + [VMEM] + [ANY] * (1 + plan.n_far),
+        in_specs=[SMEM] * 2 + [VMEM] * len(sums) + [ANY] * (2 * n_mpo + 2) + [VMEM] * 2 + [ANY] * (1 + plan.n_far),
         out_specs=(VMEM,) * n_mpo + (ANY,),
         scratch_shapes=[
             pltpu.VMEM(field_shape, BF16),
@@ -591,8 +646,8 @@
         cost_estimate=pl.CostEstimate(flops=COST_A, bytes_accessed=0, transcendentals=0),
         name="correction_image_rows",
     )(
-        left_sizes, right_sizes, *sums, *by_place(image_here, image_mine, image_other), vector, left_rows, sites,
-        right_env, *right_pieces,
+        left_sizes, right_sizes, *sums, *by_place(image_here, image_mine, image_other), vector, left_rows,
+        first, second, right_env, *right_pieces,
     )
 
     result = jnp.zeros((STATES, width, width), BF16)

time: 100 us -> 96.8 us (0.968)
  waiting for transfers between devices: 18 us -> 24.4 us
  Pallas kernels: 35.3 us -> 29.6 us
  starting transfers between devices: 34.1 us -> 31.7 us
  other arithmetic: 5.62 us -> 3.92 us
    ppermute x17, waiting for transfers between devices: 7.5 us -> 18.5 us  [from_near(): return lax.ppermute(value, ('bond', 'mpo'), pairs)]
    pallas_call x1, Pallas kernels: 16.4 us -> 13.3 us  [shards(): pl.pallas_call(functools.partial(first_kernel, plan), out_shape=(shape_of...]
    ppermute x3, waiting for transfers between devices: 5.39 us -> 2.31 us  [exchange(): lax.ppermute(jnp.stack([here[r], here[r ^ 1]]), ('bond', 'mpo'), pairs)]
    pallas_call x1, Pallas kernels: 12.2 us -> 9.95 us  [shards(): pl.pallas_call(functools.partial(second_kernel, plan, float(count_all), l...]
    ppermute x3, starting transfers between devices: 12.9 us -> 11.3 us  [exchange(): lax.ppermute(jnp.stack([here[r], here[r ^ 1]]), ('bond', 'mpo'), pairs)]
    sub x2 -> x0, other arithmetic: 1.55 us -> none  [the longest x1 0.8 us: shards(): mpo_charge[None, :, None, None] - mpo_charge[None, None, None, :]]
    ppermute x3, waiting for transfers between devices: 3.43 us -> 1.94 us  [summed_over_bond(): lax.ppermute(parts[0], 'bond', [(i ^ reach * k, i) for i in range(n_bond)])]
    ppermute x2, starting transfers between devices: 3.96 us -> 5.44 us  [handed_over(): result += [array, lax.ppermute(array, ('bond', 'mpo'), pairs)]]
  transfers between devices with their start and end apart: 27 -> 27, of which waited for: 9 -> 12; matrix products, arithmetic and copies ran while one was open for 7% -> 4% of each run, Pallas kernels for 16% -> 14%
where the time goes in v4:
time: 96.8 us; the launch traced here: 96.2 us
  starting transfers between devices  31.7 us (33%)
  Pallas kernels  29.6 us (31%)
  waiting for transfers between devices  24.4 us (25%)
  local copies, waits for them, and re-layouts  5.63 us (6%)
  other arithmetic  3.92 us (4%)
  between operations  1 us (1%)
    ppermute x17, waiting for transfers between devices, from_near(): return lax.ppermute(value, ('bond', 'mpo'), pairs)  18.5 us
    pallas_call x1, Pallas kernels, shards(): pl.pallas_call(functools.partial(first_kernel, plan), out_shape=(shape_of...  13.3 us
    ppermute x3, starting transfers between devices, exchange(): lax.ppermute(jnp.stack([here[r], here[r ^ 1]]), ('bond', 'mpo'), pairs)  11.3 us
    pallas_call x1, Pallas kernels, shards(): pl.pallas_call(functools.partial(second_kernel, plan, float(count_all), l...  9.95 us
    ppermute x17, starting transfers between devices, from_near(): return lax.ppermute(value, ('bond', 'mpo'), pairs)  8 us
    pallas_call x1, Pallas kernels, shards(): pl.pallas_call(functools.partial(image_kernel, plan), out_shape=shape_of(...  6.4 us
    ppermute x2, starting transfers between devices, handed_over(): result += [array, lax.ppermute(array, ('bond', 'mpo'), pairs)]  5.44 us
    ppermute x3, starting transfers between devices, summed_over_bond(): lax.ppermute(parts[0], 'bond', [(i ^ reach * k, i) for i in range(n_bond)])  4.41 us
  transfers between devices with their start and end apart: 27, of which 12 were waited for; matrix products, arithmetic and copies ran while one was open for 4% of the time, Pallas kernels for 14%

profile of v4, /device:TPU:0, one launch (start us, length us, event | category | flops | bytes accessed | tf_op | source)
XLA Modules:
  0.0 96.2 jit_solution(7000050825304071883)
XLA Ops:
  1.1 1.2 %collective-permute-done.2.refs_4_ = bf16[4,128,128]{2,1,0:T(8,128)(2,1)S(1)} collective-permute-done((bf16[4,128,128]{2,1,0:T(8,128)(2,1)}, bf16[4,128,128]{2,1,0:T(8,128)(2,1)S(1)}, u32[]{:S(2)}, u32[]{:S(2)}) %collective-permute-start.2) | collective-permute-done | bytes 131104 | tf_op jit(solution)/shard_map/ppermute | solution.py:36
  3.3 4.9 %collective-permute-start.5 = (bf16[2,4,128,128]{3,2,1,0:T(8,128)(2,1)S(1)}, bf16[2,4,128,128]{3,2,1,0:T(8,128)(2,1)S(1)}, u32[]{:S(2)}, u32[]{:S(2)}) collective-permute-start(bf16[2,4,128,128]{3,2,1,0:T(8,128)(2,1)S(1)} %pad_maximum_fusion.2), channel_id=1, source_target_pairs={{0,4},{2,6},{4,8},{5,1},{6,10},{7,3},{8,12},{9,5},{10,14},{11,7},{... | collective-permute-start | bytes 786440 | tf_op jit(solution)/shard_map/ppermute | solution.py:64
  8.2 1.6 %collective-permute-start.3 = (bf16[4,128,128]{2,1,0:T(8,128)(2,1)}, bf16[4,128,128]{2,1,0:T(8,128)(2,1)S(1)}, u32[]{:S(2)}, u32[]{:S(2)}) collective-permute-start(bf16[4,128,128]{2,1,0:T(8,128)(2,1)} %bitcast.113), channel_id=1, source_target_pairs={{2,0},{3,1},{0,2},{1,3},{6,4},{7,5},{4,6},{5,7},{10,8},{11,9},{8,1... | collective-permute-start | bytes 393224 | tf_op jit(solution)/shard_map/ppermute | solution.py:36
  9.7 2.3 %collective-permute-done.5.refs_7_ = bf16[2,4,128,128]{3,2,1,0:T(8,128)(2,1)S(1)} collective-permute-done((bf16[2,4,128,128]{3,2,1,0:T(8,128)(2,1)S(1)}, bf16[2,4,128,128]{3,2,1,0:T(8,128)(2,1)S(1)}, u32[]{:S(2)}, u32[]{:S(2)}) %collective-permute-start.5) | collective-permute-done | bytes 262176 | tf_op jit(solution)/shard_map/ppermute | solution.py:64
  12.0 1.5 %collective-permute-start.6 = (bf16[2,4,128,128]{3,2,1,0:T(8,128)(2,1)S(1)}, bf16[2,4,128,128]{3,2,1,0:T(8,128)(2,1)S(1)}, u32[]{:S(2)}, u32[]{:S(2)}) collective-permute-start(bf16[2,4,128,128]{3,2,1,0:T(8,128)(2,1)S(1)} %collective-permute-done.5.refs_7_), channel_id=1, source_target_pairs={{2,0},{3,1},{0,2},{1,3},{6,4},{7,5},{4,6},{5,7},{10,8},{11,9},{8,1... | collective-permute-start | bytes 786440 | tf_op jit(solution)/shard_map/ppermute | solution.py:36
  13.5 1.3 %collective-permute-start = (bf16[20,1,128,128]{3,2,1,0:T(8,128)(2,1)}, bf16[20,1,128,128]{3,2,1,0:T(8,128)(2,1)S(1)}, u32[]{:S(2)}, u32[]{:S(2)}) collective-permute-start(bf16[20,1,128,128]{3,2,1,0:T(8,128)(2,1)} %refs_18_.1), channel_id=1, source_target_pairs={{4,0},{9,1},{6,2},{11,3},{8,4},{13,5},{10,6},{15,7},{12,8},{14,10}... | collective-permute-start | bytes 1966088 | tf_op jit(solution)/shard_map/ppermute | solution.py:108
  14.8 1.3 %collective-permute-start.1 = (bf16[20,1,128,128]{3,2,1,0:T(8,128)(2,1)}, bf16[20,1,128,128]{3,2,1,0:T(8,128)(2,1)S(1)}, u32[]{:S(2)}, u32[]{:S(2)}) collective-permute-start(bf16[20,1,128,128]{3,2,1,0:T(8,128)(2,1)} %refs_18_.1), channel_id=1, source_target_pairs={{12,0},{14,2},{28,16},{30,18}} | collective-permute-start | bytes 1966088 | tf_op jit(solution)/shard_map/ppermute | solution.py:108
  16.7 7.0 %collective-permute-done.10.refs_13_ = bf16[5,128,128]{2,1,0:T(8,128)(2,1)S(1)} collective-permute-done((bf16[5,128,128]{2,1,0:T(8,128)(2,1)}, bf16[5,128,128]{2,1,0:T(8,128)(2,1)S(1)}, u32[]{:S(2)}, u32[]{:S(2)}) %collective-permute-start.10) | collective-permute-done | bytes 163872 | tf_op jit(solution)/shard_map/ppermute | solution.py:36
  25.3 1.1 %maximum_bitcast_fusion = bf16[2,4,20,4,20]{2,3,1,4,0:T(4,128)(2,1)S(1)} fusion(bf16[1,20,20,4,4]{2,4,3,1,0:T(4,128)(2,1)} %bitcast.116, bf16[1,20,20,4,4]{2,4,3,1,0:T(4,128)(2,1)} %bitcast.117), kind=kLoop, calls=%fused_computation.3 | loop fusion | flops 12800 | bytes 51200 | tf_op jit(solution)/shard_map/transpose | solution.py:556
  29.0 13.3 %states_of_vector.1 = (f32[16,20,32,128]{3,2,1,0:T(8,128)}, bf16[16,384,128]{2,1,0:T(8,128)(2,1)}, bf16[768,384]{1,0:T(8,128)(2,1)}, bf16[80,96]{1,0:T(8,128)(2,1)}, bf16[160,160]{1,0:T(8,128)(2,1)}) custom-call(s32[20]{0:T(128)} %refs_0_.2, s32[4]{0:T(128)} %refs_0_.3, s32[4]{0:T(128)} %refs_1_.3, bf16[4,128,128]{2,1,0:T(8,128)(2,1)} %bitcast.114, ...), custom_call_target="tpu_custom_call" | custom-call | flops 2000000000 | tf_op jit(solution)/shard_map/states_of_vector/pallas_call | solution.py:568
  42.4 3.5 %collective-permute-start.12 = (bf16[20,1,128,128]{3,2,1,0:T(8,128)(2,1)S(1)}, bf16[20,1,128,128]{3,2,1,0:T(8,128)(2,1)S(1)}, u32[]{:S(2)}, u32[]{:S(2)}) collective-permute-start(bf16[20,1,128,128]{3,2,1,0:T(8,128)(2,1)S(1)} %collective-permute-done.refs_0_.refs_19_), channel_id=1, source_target_pairs={{0,1},{1,0},{2,3},{3,2},{4,5},{5,4},{6,7},{7,6},{8,9},{9,8},{10,11... | collective-permute-start | bytes 1966088 | tf_op jit(solution)/shard_map/ppermute | solution.py:122
  45.8 2.0 %collective-permute-start.13 = (bf16[20,1,128,128]{3,2,1,0:T(8,128)(2,1)S(1)}, bf16[20,1,128,128]{3,2,1,0:T(8,128)(2,1)S(1)}, u32[]{:S(2)}, u32[]{:S(2)}) collective-permute-start(bf16[20,1,128,128]{3,2,1,0:T(8,128)(2,1)S(1)} %collective-permute-done.1.refs_2_.refs_21_), channel_id=1, source_target_pairs={{0,1},{2,3},{4,5},{6,7},{8,9},{10,11},{12,13},{14,15},{16,17},{18,... | collective-permute-start | bytes 1966088 | tf_op jit(solution)/shard_map/ppermute | solution.py:122
  47.9 1.6 %collective-permute-done.13.refs_3_.refs_22_ = bf16[20,1,128,128]{3,2,1,0:T(8,128)(2,1)S(1)} collective-permute-done((bf16[20,1,128,128]{3,2,1,0:T(8,128)(2,1)S(1)}, bf16[20,1,128,128]{3,2,1,0:T(8,128)(2,1)S(1)}, u32[]{:S(2)}, u32[]{:S(2)}) %collective-permute-start.13) | collective-permute-done | bytes 655392 | tf_op jit(solution)/shard_map/ppermute | solution.py:122
  50.3 6.4 %image_rows.1.refs_6_ = bf16[17,32,128]{2,1,0:T(8,128)(2,1)} custom-call(s32[4]{0:T(128)} %refs_0_.3, s32[4]{0:T(128)} %refs_1_.3, f32[16,640,128]{2,1,0:T(8,128)} %bitcast.121, bf16[16,384,128]{2,1,0:T(8,128)(2,1)} %get-tuple-element.23.vector_ref.refs_14_, bf16[20,1,128,128]{3,2,1,0:T(8,128)(2,1)} %refs_18_.1, bf16[20,1,128,128]{3,2,1,0:T(8,128)(2,1)} %copy-done.6, ...), custom_call_target="tpu_custom_call" | custom-call | flops 4000000000 | tf_op jit(solution)/shard_map/image_rows/pallas_call | solution.py:603
  58.0 5.0 %collective-permute-done.16.refs_8_ = bf16[17,32,128]{2,1,0:T(8,128)(2,1)S(1)} collective-permute-done((bf16[17,32,128]{2,1,0:T(8,128)(2,1)}, bf16[17,32,128]{2,1,0:T(8,128)(2,1)S(1)}, u32[]{:S(2)}, u32[]{:S(2)}) %collective-permute-start.16) | collective-permute-done | bytes 139296 | tf_op jit(solution)/shard_map/ppermute | solution.py:36
  64.0 4.3 %collective-permute-start.15 = (bf16[2,17,32,128]{3,2,1,0:T(8,128)(2,1)S(1)}, bf16[2,17,32,128]{3,2,1,0:T(8,128)(2,1)S(1)}, u32[]{:S(2)}, u32[]{:S(2)}) collective-permute-start(bf16[2,17,32,128]{3,2,1,0:T(8,128)(2,1)S(1)} %pad_maximum_fusion), channel_id=1, source_target_pairs={{0,4},{2,6},{4,8},{5,1},{6,10},{7,3},{8,12},{9,5},{10,14},{11,7},{... | collective-permute-start | bytes 835592 | tf_op jit(solution)/shard_map/ppermute | solution.py:64
  68.5 1.3 %collective-permute-done.17.refs_9_ = bf16[17,32,128]{2,1,0:T(8,128)(2,1)S(1)} collective-permute-done((bf16[17,32,128]{2,1,0:T(8,128)(2,1)S(1)}, bf16[17,32,128]{2,1,0:T(8,128)(2,1)S(1)}, u32[]{:S(2)}, u32[]{:S(2)}) %collective-permute-start.17) | collective-permute-done | bytes 139296 | tf_op jit(solution)/shard_map/ppermute | solution.py:36
  69.8 2.1 %collective-permute-start.18 = (bf16[2,17,32,128]{3,2,1,0:T(8,128)(2,1)S(1)}, bf16[2,17,32,128]{3,2,1,0:T(8,128)(2,1)S(1)}, u32[]{:S(2)}, u32[]{:S(2)}) collective-permute-start(bf16[2,17,32,128]{3,2,1,0:T(8,128)(2,1)S(1)} %pad_maximum_fusion.1), channel_id=1, source_target_pairs={{0,4},{2,6},{4,8},{5,1},{6,10},{7,3},{8,12},{9,5},{10,14},{11,7},{... | collective-permute-start | bytes 835592 | tf_op jit(solution)/shard_map/ppermute | solution.py:64
  73.0 3.5 %collective-permute-start.21 = (f32[8,128]{1,0:T(8,128)S(1)}, f32[8,128]{1,0:T(8,128)S(1)}, u32[]{:S(2)}, u32[]{:S(2)}) collective-permute-start(f32[8,128]{1,0:T(8,128)S(1)} %maximum_maximum_fusion.refs_2_), channel_id=1, source_target_pairs={{12,0},{8,4},{4,8},{0,12},{13,1},{9,5},{5,9},{1,13},{14,2},{10,6},... | collective-permute-start | bytes 12296 | tf_op jit(solution)/shard_map/ppermute | solution.py:147
  76.4 1.0 %collective-permute-done.20.refs_4_ = f32[8,128]{1,0:T(8,128)S(1)} collective-permute-done((f32[8,128]{1,0:T(8,128)S(1)}, f32[8,128]{1,0:T(8,128)S(1)}, u32[]{:S(2)}, u32[]{:S(2)}) %collective-permute-start.20) | collective-permute-done | bytes 4128 | tf_op jit(solution)/shard_map/ppermute | solution.py:147
  79.0 1.0 %collective-permute-done.22.refs_12_ = bf16[2,17,32,128]{3,2,1,0:T(8,128)(2,1)S(1)} collective-permute-done((bf16[2,17,32,128]{3,2,1,0:T(8,128)(2,1)S(1)}, bf16[2,17,32,128]{3,2,1,0:T(8,128)(2,1)S(1)}, u32[]{:S(2)}, u32[]{:S(2)}) %collective-permute-start.22) | collective-permute-done | bytes 278560 | tf_op jit(solution)/shard_map/ppermute | solution.py:36
  81.1 9.9 %correction_image_rows.1 = (bf16[4,32,128]{2,1,0:T(8,128)(2,1)}, bf16[4,32,128]{2,1,0:T(8,128)(2,1)}, bf16[4,32,128]{2,1,0:T(8,128)(2,1)}, bf16[4,32,128]{2,1,0:T(8,128)(2,1)}, bf16[1,4,128,128]{3,2,1,0:T(8,128)(2,1)}) custom-call(s32[4]{0:T(128)} %refs_0_.3, s32[4]{0:T(128)} %refs_1_.3, f32[8,128]{1,0:T(8,128)} %copy-done.5, f32[8,128]{1,0:T(8,128)} %copy-done.22, ...), custom_call_target="tpu_custom_call" | custom-call | flops 2000000000 | tf_op jit(solution)/shard_map/correction_image_rows/pallas_call | solution.py:627
  91.6 1.4 %collective-permute-start.26 = (bf16[4,32,128]{2,1,0:T(8,128)(2,1)}, bf16[4,32,128]{2,1,0:T(8,128)(2,1)S(1)}, u32[]{:S(2)}, u32[]{:S(2)}) collective-permute-start(bf16[4,32,128]{2,1,0:T(8,128)(2,1)} %get-tuple-element.39), channel_id=1, source_target_pairs={{3,0},{2,1},{1,2},{0,3},{7,4},{6,5},{5,6},{4,7},{11,8},{10,9},{9,1... | collective-permute-start | bytes 98312 | tf_op jit(solution)/shard_map/ppermute | solution.py:36
  93.8 1.7 %collective-permute-done.25 = bf16[4,32,128]{2,1,0:T(8,128)(2,1)S(1)} collective-permute-done((bf16[4,32,128]{2,1,0:T(8,128)(2,1)}, bf16[4,32,128]{2,1,0:T(8,128)(2,1)S(1)}, u32[]{:S(2)}, u32[]{:S(2)}) %collective-permute-start.25) | collective-permute-done | bytes 32800 | tf_op jit(solution)/shard_map/ppermute | solution.py:36
  (106 shorter events, 15.2 us)
Async XLA Ops:
  0.6 1.7 %collective-permute-start.2 = (bf16[4,128,128]{2,1,0:T(8,128)(2,1)}, bf16[4,128,128]{2,1,0:T(8,128)(2,1)S(1)}, u32[]{:S(2)}, u32[]{:S(2)}) collective-permute-start(bf16[4,128,128]{2,1,0:T(8,128)(2,1)} %bitcast.112), channel_id=1, source_target_pairs={{1,0},{0,1},{3,2},{2,3},{5,4},{4,5},{7,6},{6,7},{9,8},{8,9},{11,10... | collective-permute-start | bytes 393224 | tf_op jit(solution)/shard_map/ppermute | solution.py:36
  3.3 8.7 %collective-permute-start.5 = (bf16[2,4,128,128]{3,2,1,0:T(8,128)(2,1)S(1)}, bf16[2,4,128,128]{3,2,1,0:T(8,128)(2,1)S(1)}, u32[]{:S(2)}, u32[]{:S(2)}) collective-permute-start(bf16[2,4,128,128]{3,2,1,0:T(8,128)(2,1)S(1)} %pad_maximum_fusion.2), channel_id=1, source_target_pairs={{0,4},{2,6},{4,8},{5,1},{6,10},{7,3},{8,12},{9,5},{10,14},{11,7},{... | collective-permute-start | bytes 786440 | tf_op jit(solution)/shard_map/ppermute | solution.py:64
  8.2 8.5 %collective-permute-start.3 = (bf16[4,128,128]{2,1,0:T(8,128)(2,1)}, bf16[4,128,128]{2,1,0:T(8,128)(2,1)S(1)}, u32[]{:S(2)}, u32[]{:S(2)}) collective-permute-start(bf16[4,128,128]{2,1,0:T(8,128)(2,1)} %bitcast.113), channel_id=1, source_target_pairs={{2,0},{3,1},{0,2},{1,3},{6,4},{7,5},{4,6},{5,7},{10,8},{11,9},{8,1... | collective-permute-start | bytes 393224 | tf_op jit(solution)/shard_map/ppermute | solution.py:36
  12.0 12.2 %collective-permute-start.6 = (bf16[2,4,128,128]{3,2,1,0:T(8,128)(2,1)S(1)}, bf16[2,4,128,128]{3,2,1,0:T(8,128)(2,1)S(1)}, u32[]{:S(2)}, u32[]{:S(2)}) collective-permute-start(bf16[2,4,128,128]{3,2,1,0:T(8,128)(2,1)S(1)} %collective-permute-done.5.refs_7_), channel_id=1, source_target_pairs={{2,0},{3,1},{0,2},{1,3},{6,4},{7,5},{4,6},{5,7},{10,8},{11,9},{8,1... | collective-permute-start | bytes 786440 | tf_op jit(solution)/shard_map/ppermute | solution.py:36
  13.5 28.8 %collective-permute-start = (bf16[20,1,128,128]{3,2,1,0:T(8,128)(2,1)}, bf16[20,1,128,128]{3,2,1,0:T(8,128)(2,1)S(1)}, u32[]{:S(2)}, u32[]{:S(2)}) collective-permute-start(bf16[20,1,128,128]{3,2,1,0:T(8,128)(2,1)} %refs_18_.1), channel_id=1, source_target_pairs={{4,0},{9,1},{6,2},{11,3},{8,4},{13,5},{10,6},{15,7},{12,8},{14,10}... | collective-permute-start | bytes 1966088 | tf_op jit(solution)/shard_map/ppermute | solution.py:108
  14.8 27.5 %collective-permute-start.1 = (bf16[20,1,128,128]{3,2,1,0:T(8,128)(2,1)}, bf16[20,1,128,128]{3,2,1,0:T(8,128)(2,1)S(1)}, u32[]{:S(2)}, u32[]{:S(2)}) collective-permute-start(bf16[20,1,128,128]{3,2,1,0:T(8,128)(2,1)} %refs_18_.1), channel_id=1, source_target_pairs={{12,0},{14,2},{28,16},{30,18}} | collective-permute-start | bytes 1966088 | tf_op jit(solution)/shard_map/ppermute | solution.py:108
  16.1 7.6 %collective-permute-start.10 = (bf16[5,128,128]{2,1,0:T(8,128)(2,1)}, bf16[5,128,128]{2,1,0:T(8,128)(2,1)S(1)}, u32[]{:S(2)}, u32[]{:S(2)}) collective-permute-start(bf16[5,128,128]{2,1,0:T(8,128)(2,1)} %bitcast.118), channel_id=1, source_target_pairs={{2,0},{3,1},{0,2},{1,3},{6,4},{7,5},{4,6},{5,7},{10,8},{11,9},{8,1... | collective-permute-start | bytes 491528 | tf_op jit(solution)/shard_map/ppermute | solution.py:36
  16.7 7.0 %collective-permute-start.9 = (bf16[5,128,128]{2,1,0:T(8,128)(2,1)}, bf16[5,128,128]{2,1,0:T(8,128)(2,1)S(1)}, u32[]{:S(2)}, u32[]{:S(2)}) collective-permute-start(bf16[5,128,128]{2,1,0:T(8,128)(2,1)} %bitcast.119), channel_id=1, source_target_pairs={{1,0},{0,1},{3,2},{2,3},{5,4},{4,5},{7,6},{6,7},{9,8},{8,9},{11,10... | collective-permute-start | bytes 491528 | tf_op jit(solution)/shard_map/ppermute | solution.py:36
  23.7 3.8 %collective-permute-start.7 = (bf16[2,4,128,128]{3,2,1,0:T(8,128)(2,1)S(1)}, bf16[2,4,128,128]{3,2,1,0:T(8,128)(2,1)S(1)}, u32[]{:S(2)}, u32[]{:S(2)}) collective-permute-start(bf16[2,4,128,128]{3,2,1,0:T(8,128)(2,1)S(1)} %collective-permute-done.5.refs_7_), channel_id=1, source_target_pairs={{1,0},{0,1},{3,2},{2,3},{5,4},{4,5},{7,6},{6,7},{9,8},{8,9},{11,10... | collective-permute-start | bytes 786440 | tf_op jit(solution)/shard_map/ppermute | solution.py:36
  24.2 3.3 %collective-permute-start.8 = (bf16[2,4,128,128]{3,2,1,0:T(8,128)(2,1)S(1)}, bf16[2,4,128,128]{3,2,1,0:T(8,128)(2,1)S(1)}, u32[]{:S(2)}, u32[]{:S(2)}) collective-permute-start(bf16[2,4,128,128]{3,2,1,0:T(8,128)(2,1)S(1)} %collective-permute-done.6.refs_8_), channel_id=1, source_target_pairs={{1,0},{0,1},{3,2},{2,3},{5,4},{4,5},{7,6},{6,7},{9,8},{8,9},{11,10... | collective-permute-start | bytes 786440 | tf_op jit(solution)/shard_map/ppermute | solution.py:36
  25.2 2.3 %collective-permute-start.11 = (bf16[5,128,128]{2,1,0:T(8,128)(2,1)S(1)}, bf16[5,128,128]{2,1,0:T(8,128)(2,1)S(1)}, u32[]{:S(2)}, u32[]{:S(2)}) collective-permute-start(bf16[5,128,128]{2,1,0:T(8,128)(2,1)S(1)} %collective-permute-done.10.refs_13_), channel_id=1, source_target_pairs={{1,0},{0,1},{3,2},{2,3},{5,4},{4,5},{7,6},{6,7},{9,8},{8,9},{11,10... | collective-permute-start | bytes 491528 | tf_op jit(solution)/shard_map/ppermute | solution.py:36
  42.4 5.5 %collective-permute-start.12 = (bf16[20,1,128,128]{3,2,1,0:T(8,128)(2,1)S(1)}, bf16[20,1,128,128]{3,2,1,0:T(8,128)(2,1)S(1)}, u32[]{:S(2)}, u32[]{:S(2)}) collective-permute-start(bf16[20,1,128,128]{3,2,1,0:T(8,128)(2,1)S(1)} %collective-permute-done.refs_0_.refs_19_), channel_id=1, source_target_pairs={{0,1},{1,0},{2,3},{3,2},{4,5},{5,4},{6,7},{7,6},{8,9},{9,8},{10,11... | collective-permute-start | bytes 1966088 | tf_op jit(solution)/shard_map/ppermute | solution.py:122
  45.8 3.6 %collective-permute-start.13 = (bf16[20,1,128,128]{3,2,1,0:T(8,128)(2,1)S(1)}, bf16[20,1,128,128]{3,2,1,0:T(8,128)(2,1)S(1)}, u32[]{:S(2)}, u32[]{:S(2)}) collective-permute-start(bf16[20,1,128,128]{3,2,1,0:T(8,128)(2,1)S(1)} %collective-permute-done.1.refs_2_.refs_21_), channel_id=1, source_target_pairs={{0,1},{2,3},{4,5},{6,7},{8,9},{10,11},{12,13},{14,15},{16,17},{18,... | collective-permute-start | bytes 1966088 | tf_op jit(solution)/shard_map/ppermute | solution.py:122
  56.7 6.2 %collective-permute-start.16 = (bf16[17,32,128]{2,1,0:T(8,128)(2,1)}, bf16[17,32,128]{2,1,0:T(8,128)(2,1)S(1)}, u32[]{:S(2)}, u32[]{:S(2)}) collective-permute-start(bf16[17,32,128]{2,1,0:T(8,128)(2,1)} %image_rows.1.refs_6_), channel_id=1, source_target_pairs={{2,0},{3,1},{0,2},{1,3},{6,4},{7,5},{4,6},{5,7},{10,8},{11,9},{8,1... | collective-permute-start | bytes 417800 | tf_op jit(solution)/shard_map/ppermute | solution.py:36
  56.9 6.1 %collective-permute-start.14 = (bf16[17,32,128]{2,1,0:T(8,128)(2,1)}, bf16[17,32,128]{2,1,0:T(8,128)(2,1)S(1)}, u32[]{:S(2)}, u32[]{:S(2)}) collective-permute-start(bf16[17,32,128]{2,1,0:T(8,128)(2,1)} %image_rows.1.refs_6_), channel_id=1, source_target_pairs={{1,0},{0,1},{3,2},{2,3},{5,4},{4,5},{7,6},{6,7},{9,8},{8,9},{11,10... | collective-permute-start | bytes 417800 | tf_op jit(solution)/shard_map/ppermute | solution.py:36
  64.0 14.4 %collective-permute-start.15 = (bf16[2,17,32,128]{3,2,1,0:T(8,128)(2,1)S(1)}, bf16[2,17,32,128]{3,2,1,0:T(8,128)(2,1)S(1)}, u32[]{:S(2)}, u32[]{:S(2)}) collective-permute-start(bf16[2,17,32,128]{3,2,1,0:T(8,128)(2,1)S(1)} %pad_maximum_fusion), channel_id=1, source_target_pairs={{0,4},{2,6},{4,8},{5,1},{6,10},{7,3},{8,12},{9,5},{10,14},{11,7},{... | collective-permute-start | bytes 835592 | tf_op jit(solution)/shard_map/ppermute | solution.py:64
  69.8 8.6 %collective-permute-start.18 = (bf16[2,17,32,128]{3,2,1,0:T(8,128)(2,1)S(1)}, bf16[2,17,32,128]{3,2,1,0:T(8,128)(2,1)S(1)}, u32[]{:S(2)}, u32[]{:S(2)}) collective-permute-start(bf16[2,17,32,128]{3,2,1,0:T(8,128)(2,1)S(1)} %pad_maximum_fusion.1), channel_id=1, source_target_pairs={{0,4},{2,6},{4,8},{5,1},{6,10},{7,3},{8,12},{9,5},{10,14},{11,7},{... | collective-permute-start | bytes 835592 | tf_op jit(solution)/shard_map/ppermute | solution.py:64
  72.0 4.4 %collective-permute-start.19 = (f32[8,128]{1,0:T(8,128)S(1)}, f32[8,128]{1,0:T(8,128)S(1)}, u32[]{:S(2)}, u32[]{:S(2)}) collective-permute-start(f32[8,128]{1,0:T(8,128)S(1)} %maximum_maximum_fusion.refs_2_), channel_id=1, source_target_pairs={{4,0},{0,4},{12,8},{8,12},{5,1},{1,5},{13,9},{9,13},{6,2},{2,6},{1... | collective-permute-start | bytes 12296 | tf_op jit(solution)/shard_map/ppermute | solution.py:147
  73.0 4.5 %collective-permute-start.20 = (f32[8,128]{1,0:T(8,128)S(1)}, f32[8,128]{1,0:T(8,128)S(1)}, u32[]{:S(2)}, u32[]{:S(2)}) collective-permute-start(f32[8,128]{1,0:T(8,128)S(1)} %maximum_maximum_fusion.refs_2_), channel_id=1, source_target_pairs={{8,0},{12,4},{0,8},{4,12},{9,1},{13,5},{1,9},{5,13},{10,2},{14,6},... | collective-permute-start | bytes 12296 | tf_op jit(solution)/shard_map/ppermute | solution.py:147
  73.0 5.4 %collective-permute-start.21 = (f32[8,128]{1,0:T(8,128)S(1)}, f32[8,128]{1,0:T(8,128)S(1)}, u32[]{:S(2)}, u32[]{:S(2)}) collective-permute-start(f32[8,128]{1,0:T(8,128)S(1)} %maximum_maximum_fusion.refs_2_), channel_id=1, source_target_pairs={{12,0},{8,4},{4,8},{0,12},{13,1},{9,5},{5,9},{1,13},{14,2},{10,6},... | collective-permute-start | bytes 12296 | tf_op jit(solution)/shard_map/ppermute | solution.py:147
  78.6 1.8 %collective-permute-start.23 = (bf16[2,17,32,128]{3,2,1,0:T(8,128)(2,1)S(1)}, bf16[2,17,32,128]{3,2,1,0:T(8,128)(2,1)S(1)}, u32[]{:S(2)}, u32[]{:S(2)}) collective-permute-start(bf16[2,17,32,128]{3,2,1,0:T(8,128)(2,1)S(1)} %collective-permute-done.18.refs_11_), channel_id=1, source_target_pairs={{1,0},{0,1},{3,2},{2,3},{5,4},{4,5},{7,6},{6,7},{9,8},{8,9},{11,10... | collective-permute-start | bytes 835592 | tf_op jit(solution)/shard_map/ppermute | solution.py:36
  91.1 2.7 %collective-permute-start.24 = (bf16[4,32,128]{2,1,0:T(8,128)(2,1)}, bf16[4,32,128]{2,1,0:T(8,128)(2,1)S(1)}, u32[]{:S(2)}, u32[]{:S(2)}) collective-permute-start(bf16[4,32,128]{2,1,0:T(8,128)(2,1)} %get-tuple-element.37), channel_id=1, source_target_pairs={{1,0},{0,1},{3,2},{2,3},{5,4},{4,5},{7,6},{6,7},{9,8},{8,9},{11,10... | collective-permute-start | bytes 98312 | tf_op jit(solution)/shard_map/ppermute | solution.py:36
  91.3 4.2 %collective-permute-start.25 = (bf16[4,32,128]{2,1,0:T(8,128)(2,1)}, bf16[4,32,128]{2,1,0:T(8,128)(2,1)S(1)}, u32[]{:S(2)}, u32[]{:S(2)}) collective-permute-start(bf16[4,32,128]{2,1,0:T(8,128)(2,1)} %get-tuple-element.38), channel_id=1, source_target_pairs={{2,0},{3,1},{0,2},{1,3},{6,4},{7,5},{4,6},{5,7},{10,8},{11,9},{8,1... | collective-permute-start | bytes 98312 | tf_op jit(solution)/shard_map/ppermute | solution.py:36
  91.6 3.9 %collective-permute-start.26 = (bf16[4,32,128]{2,1,0:T(8,128)(2,1)}, bf16[4,32,128]{2,1,0:T(8,128)(2,1)S(1)}, u32[]{:S(2)}, u32[]{:S(2)}) collective-permute-start(bf16[4,32,128]{2,1,0:T(8,128)(2,1)} %get-tuple-element.39), channel_id=1, source_target_pairs={{3,0},{2,1},{1,2},{0,3},{7,4},{6,5},{5,6},{4,7},{11,8},{10,9},{9,1... | collective-permute-start | bytes 98312 | tf_op jit(solution)/shard_map/ppermute | solution.py:36
  (28 other events, 155.5 us)

commit v5 on v4

--- a/solution.py
+++ b/solution.py
@@ -216,7 +216,7 @@
         xs[p + 1] = done[:, plan.width :]
         return carry
 
-    lax.fori_loop(0, PAIRS // 2, step, 0, unroll=4)
+    lax.fori_loop(0, PAIRS // 2, step, 0, unroll=8)
 
 
 def site_matrices(plan, charge_ref, sites_ref, first_out, second_out):
@@ -377,8 +377,9 @@
     fs, ls, wide, xs, ys, left_near, psi_near, left_sem, psi_sem, out_sem, y_sem = refs[6:]
     me = lax.axis_index("mpo")
     rows_here = pl.ds(pl.multiple_of(me * plan.rows, plan.rows), plan.rows)
+    odd_rows = pl.ds(pl.multiple_of(lax.rem(me, 2) * plan.rows, plan.rows), plan.rows)
     left_copies = [
-        pltpu.make_async_copy(source.at[:, rows_here, :], left_near.at[r], left_sem.at[r])
+        pltpu.make_async_copy(source.at[:, odd_rows if r > 1 else rows_here, :], left_near.at[r], left_sem.at[r])
         for r, source in enumerate(left_refs)
     ]
     psi_copies = near_copies(plan, psi_refs, psi_near, psi_sem, STATES)
@@ -476,7 +477,7 @@
     v_copy = pltpu.make_async_copy(vector_ref, vector, field_sem.at[0])
     l_copy = pltpu.make_async_copy(ls_ref, ls, field_sem.at[1])
     r_copies = right_copies(plan, own_ref, far_refs, right_near, right_sem)
-    for copy in [v_copy] + image_copies + [l_copy] + [copy for some in r_copies for copy in some]:
+    for copy in [v_copy] + image_copies + [l_copy]:
         copy.start()
     sums = merged([part[...] for part in parts])
     rayleigh = sums[0:1, :] / sums[1:2, :]
@@ -500,7 +501,7 @@
             out_copies.append(
                 pltpu.make_async_copy(image_near.at[place, pairs_here], image_out.at[0, :, rows, :], out_sem.at[r])
             )
-    for copy in out_copies:
+    for copy in out_copies + [copy for some in r_copies for copy in some]:
         copy.start()
     l_copy.wait()
     left_phase(plan, fs, ls, xs)
@@ -523,12 +524,12 @@
 
 
 Y_BLOCK = 8
-COST_A = 2_000_000_000
+COST_A = 1_000
 COST_B = 4_000_000_000
 VMEM = pl.BlockSpec(memory_space=pltpu.VMEM)
 ANY = pl.BlockSpec(memory_space=pl.ANY)
 SMEM = pl.BlockSpec(memory_space=pltpu.SMEM)
-PARAMS = pltpu.CompilerParams(vmem_limit_bytes=60 * 1024 * 1024)
+PARAMS = pltpu.CompilerParams(vmem_limit_bytes=59 * 1024 * 1024)
 
 
 def shape_of(shape, dtype):
@@ -542,19 +543,21 @@
     plan = Plan(n_mpo, n_bond, width, right_env.shape[0])
     me = lax.axis_index("mpo")
 
-    psi_here, psi_mine = exchange(psi[0], True)
-    psi_other = handed_pairs(psi_mine)
-
-    left_mine = left_env[:, 0]
-    left_here = {0: left_mine}
-    for bit in mpo_bits():
-        left_here.update({r ^ bit: from_near(block, 0, bit) for r, block in list(left_here.items())})
-    left_pieces = [left_here[r] for r in range(n_mpo)]
-
-    right_far = right_exchange(right_env, plan.far)
-
     sites = jnp.transpose(jnp.stack([site_one, site_two]), (0, 3, 2, 4, 1))
     sites = sites.reshape(2, STATES * plan.w, STATES * plan.w)
+
+    psi_here, psi_mine = exchange(psi[0], True)
+    psi_mine, sites = lax.optimization_barrier((psi_mine, sites))
+    psi_other = handed_pairs(psi_mine)
+
+    left_mine = left_env[:, 0]
+    left_pieces = [left_mine, from_near(left_mine, 0, 1)]
+    for r in range(2, n_mpo, 2):
+        start = lax.bitwise_xor(me - lax.rem(me, 2), r) * plan.rows
+        both = from_near(lax.dynamic_slice_in_dim(left_mine, start, 2 * plan.rows, 1), 0, r)
+        left_pieces += [both, from_near(both, 0, 1)]
+
+    right_far = right_exchange(right_env, plan.far)
 
     field_shape = (PAIRS, 3 * width, width)
     left_shape = (plan.rows * plan.w_pad, 3 * width)
@@ -619,8 +622,10 @@
     )(left_sizes, right_sizes, ys.reshape(PAIRS, plan.w * plan.rows, width), vector, right_env, *right_pieces)
 
     image_here, image_mine = exchange(image_rows, False)
-    sums = summed_over_bond(merged([sums_of(image_here[r]) for r in range(n_mpo)]))
-    image_mine, sums = lax.optimization_barrier((image_mine, sums))
+    blocks, _ = lax.optimization_barrier((image_here, image_mine[0]))
+    sums = summed_over_bond(merged([sums_of(blocks[r]) for r in range(n_mpo)]))
+    last = max(image_mine)
+    image_mine[last], sums = lax.optimization_barrier((image_mine[last], sums))
     image_other = handed_pairs(image_mine)
 
     count_all = n_bond * PAIRS * width * width

time: 96.8 us -> 92.8 us (0.959)
  waiting for transfers between devices: 24.4 us -> 20.7 us
    ppermute x17, waiting for transfers between devices: 18.5 us -> 14.4 us  [from_near(): return lax.ppermute(value, ('bond', 'mpo'), pairs)]
    ppermute x2, starting transfers between devices: 5.44 us -> 2.51 us  [handed_over(): result += [array, lax.ppermute(array, ('bond', 'mpo'), pairs)]]
    ppermute x3, waiting for transfers between devices: 1.94 us -> 3.41 us  [summed_over_bond(): lax.ppermute(parts[0], 'bond', [(i ^ reach * k, i) for i in range(n_bond)])]
    ppermute x3, starting transfers between devices: 11.3 us -> 12.7 us  [exchange(): lax.ppermute(jnp.stack([here[r], here[r ^ 1]]), ('bond', 'mpo'), pairs)]
    ppermute x17, starting transfers between devices: 8 us -> 9.11 us  [from_near(): return lax.ppermute(value, ('bond', 'mpo'), pairs)]
    ppermute x3, waiting for transfers between devices: 2.31 us -> 1.26 us  [exchange(): lax.ppermute(jnp.stack([here[r], here[r ^ 1]]), ('bond', 'mpo'), pairs)]
    unnamed x50 -> x52, local copies, waits for them, and re-layouts: 3.63 us -> 3.65 us
  transfers between devices with their start and end apart: 27 -> 27, of which waited for: 12 -> 11; matrix products, arithmetic and copies ran while one was open for 4% -> 6% of each run, Pallas kernels for 14% -> 14%
where the time goes in v5:
time: 92.8 us; the launch traced here: 92.1 us
  starting transfers between devices  31.3 us (34%)
  Pallas kernels  28.7 us (31%)
  waiting for transfers between devices  20.7 us (22%)
  local copies, waits for them, and re-layouts  6.53 us (7%)
  other arithmetic  3.9 us (4%)
  between operations  1.06 us (1%)
    ppermute x17, waiting for transfers between devices, from_near(): return lax.ppermute(value, ('bond', 'mpo'), pairs)  14.4 us
    pallas_call x1, Pallas kernels, shards(): pl.pallas_call(functools.partial(first_kernel, plan), out_shape=(shape_of...  13 us
    ppermute x3, starting transfers between devices, exchange(): lax.ppermute(jnp.stack([here[r], here[r ^ 1]]), ('bond', 'mpo'), pairs)  12.7 us
    pallas_call x1, Pallas kernels, shards(): pl.pallas_call(functools.partial(second_kernel, plan, float(count_all), l...  9.3 us
    ppermute x17, starting transfers between devices, from_near(): return lax.ppermute(value, ('bond', 'mpo'), pairs)  9.11 us
    pallas_call x1, Pallas kernels, shards(): pl.pallas_call(functools.partial(image_kernel, plan), out_shape=shape_of(...  6.4 us
    ppermute x3, starting transfers between devices, summed_over_bond(): lax.ppermute(parts[0], 'bond', [(i ^ reach * k, i) for i in range(n_bond)])  4.41 us
    unnamed x52, local copies, waits for them, and re-layouts  3.65 us
  transfers between devices with their start and end apart: 27, of which 11 were waited for; matrix products, arithmetic and copies ran while one was open for 6% of the time, Pallas kernels for 14%

profile of v5, /device:TPU:0, one launch (start us, length us, event | category | flops | bytes accessed | tf_op | source)
XLA Modules:
  0.0 92.1 jit_solution(15828847284813381720)
XLA Ops:
  3.3 4.9 %collective-permute-start.5 = (bf16[2,4,128,128]{3,2,1,0:T(8,128)(2,1)S(1)}, bf16[2,4,128,128]{3,2,1,0:T(8,128)(2,1)S(1)}, u32[]{:S(2)}, u32[]{:S(2)}) collective-permute-start(bf16[2,4,128,128]{3,2,1,0:T(8,128)(2,1)S(1)} %pad_maximum_fusion.2), channel_id=1, source_target_pairs={{0,4},{2,6},{4,8},{5,1},{6,10},{7,3},{8,12},{9,5},{10,14},{11,7},{... | collective-permute-start | bytes 786440 | tf_op jit(solution)/shard_map/ppermute | solution.py:64
  8.2 1.3 %collective-permute-start = (bf16[20,1,128,128]{3,2,1,0:T(8,128)(2,1)}, bf16[20,1,128,128]{3,2,1,0:T(8,128)(2,1)S(1)}, u32[]{:S(2)}, u32[]{:S(2)}) collective-permute-start(bf16[20,1,128,128]{3,2,1,0:T(8,128)(2,1)} %refs_18_.1), channel_id=1, source_target_pairs={{4,0},{9,1},{6,2},{11,3},{8,4},{13,5},{10,6},{15,7},{12,8},{14,10}... | collective-permute-start | bytes 1966088 | tf_op jit(solution)/shard_map/ppermute | solution.py:108
  9.5 1.3 %collective-permute-start.1 = (bf16[20,1,128,128]{3,2,1,0:T(8,128)(2,1)}, bf16[20,1,128,128]{3,2,1,0:T(8,128)(2,1)S(1)}, u32[]{:S(2)}, u32[]{:S(2)}) collective-permute-start(bf16[20,1,128,128]{3,2,1,0:T(8,128)(2,1)} %refs_18_.1), channel_id=1, source_target_pairs={{12,0},{14,2},{28,16},{30,18}} | collective-permute-start | bytes 1966088 | tf_op jit(solution)/shard_map/ppermute | solution.py:108
  10.8 1.3 %collective-permute-done.5.refs_7_ = bf16[2,4,128,128]{3,2,1,0:T(8,128)(2,1)S(1)} collective-permute-done((bf16[2,4,128,128]{3,2,1,0:T(8,128)(2,1)S(1)}, bf16[2,4,128,128]{3,2,1,0:T(8,128)(2,1)S(1)}, u32[]{:S(2)}, u32[]{:S(2)}) %collective-permute-start.5) | collective-permute-done | bytes 262176 | tf_op jit(solution)/shard_map/ppermute | solution.py:64
  12.0 1.5 %collective-permute-start.6 = (bf16[2,4,128,128]{3,2,1,0:T(8,128)(2,1)S(1)}, bf16[2,4,128,128]{3,2,1,0:T(8,128)(2,1)S(1)}, u32[]{:S(2)}, u32[]{:S(2)}) collective-permute-start(bf16[2,4,128,128]{3,2,1,0:T(8,128)(2,1)S(1)} %collective-permute-done.5.refs_7_), channel_id=1, source_target_pairs={{2,0},{3,1},{0,2},{1,3},{6,4},{7,5},{4,6},{5,7},{10,8},{11,9},{8,1... | collective-permute-start | bytes 786440 | tf_op jit(solution)/shard_map/ppermute | solution.py:36
  15.0 1.5 %collective-permute-start.3 = (bf16[4,128,128]{2,1,0:T(8,128)(2,1)}, bf16[4,128,128]{2,1,0:T(8,128)(2,1)S(1)}, u32[]{:S(2)}, u32[]{:S(2)}) collective-permute-start(bf16[4,128,128]{2,1,0:T(8,128)(2,1)} %bitcast.115), channel_id=1, source_target_pairs={{2,0},{3,1},{0,2},{1,3},{6,4},{7,5},{4,6},{5,7},{10,8},{11,9},{8,1... | collective-permute-start | bytes 393224 | tf_op jit(solution)/shard_map/ppermute | solution.py:36
  16.5 6.6 %collective-permute-done.10.refs_13_ = bf16[5,64,128]{2,1,0:T(8,128)(2,1)S(1)} collective-permute-done((bf16[5,64,128]{2,1,0:T(8,128)(2,1)S(1)}, bf16[5,64,128]{2,1,0:T(8,128)(2,1)S(1)}, u32[]{:S(2)}, u32[]{:S(2)}) %collective-permute-start.10) | collective-permute-done | bytes 81952 | tf_op jit(solution)/shard_map/ppermute | solution.py:36
  26.3 1.5 %collective-permute-done.4.refs_6_ = bf16[4,128,128]{2,1,0:T(8,128)(2,1)S(1)} collective-permute-done((bf16[4,128,128]{2,1,0:T(8,128)(2,1)S(1)}, bf16[4,128,128]{2,1,0:T(8,128)(2,1)S(1)}, u32[]{:S(2)}, u32[]{:S(2)}) %collective-permute-start.4) | collective-permute-done | bytes 131104 | tf_op jit(solution)/shard_map/ppermute | solution.py:36
  29.3 13.0 %states_of_vector.1 = (f32[16,20,32,128]{3,2,1,0:T(8,128)}, bf16[16,384,128]{2,1,0:T(8,128)(2,1)}, bf16[768,384]{1,0:T(8,128)(2,1)}, bf16[80,96]{1,0:T(8,128)(2,1)}, bf16[160,160]{1,0:T(8,128)(2,1)}) custom-call(s32[20]{0:T(128)} %refs_0_.2, s32[4]{0:T(128)} %refs_0_.3, s32[4]{0:T(128)} %refs_1_.3, bf16[4,128,128]{2,1,0:T(8,128)(2,1)} %bitcast.116, ...), custom_call_target="tpu_custom_call" | custom-call | flops 1000 | tf_op jit(solution)/shard_map/states_of_vector/pallas_call | solution.py:571
  42.6 2.3 %collective-permute-start.13 = (bf16[20,1,128,128]{3,2,1,0:T(8,128)(2,1)S(1)}, bf16[20,1,128,128]{3,2,1,0:T(8,128)(2,1)S(1)}, u32[]{:S(2)}, u32[]{:S(2)}) collective-permute-start(bf16[20,1,128,128]{3,2,1,0:T(8,128)(2,1)S(1)} %collective-permute-done.1.refs_2_.refs_21_), channel_id=1, source_target_pairs={{0,1},{2,3},{4,5},{6,7},{8,9},{10,11},{12,13},{14,15},{16,17},{18,... | collective-permute-start | bytes 1966088 | tf_op jit(solution)/shard_map/ppermute | solution.py:122
  44.9 1.6 %collective-permute-done.13.refs_3_.refs_22_ = bf16[20,1,128,128]{3,2,1,0:T(8,128)(2,1)S(1)} collective-permute-done((bf16[20,1,128,128]{3,2,1,0:T(8,128)(2,1)S(1)}, bf16[20,1,128,128]{3,2,1,0:T(8,128)(2,1)S(1)}, u32[]{:S(2)}, u32[]{:S(2)}) %collective-permute-start.13) | collective-permute-done | bytes 655392 | tf_op jit(solution)/shard_map/ppermute | solution.py:122
  47.4 6.4 %image_rows.1.refs_6_ = bf16[17,32,128]{2,1,0:T(8,128)(2,1)} custom-call(s32[4]{0:T(128)} %refs_0_.3, s32[4]{0:T(128)} %refs_1_.3, f32[16,640,128]{2,1,0:T(8,128)} %bitcast.122, bf16[16,384,128]{2,1,0:T(8,128)(2,1)} %get-tuple-element.32.vector_ref.refs_14_, bf16[20,1,128,128]{3,2,1,0:T(8,128)(2,1)} %refs_18_.1, bf16[20,1,128,128]{3,2,1,0:T(8,128)(2,1)} %copy-done, ...), custom_call_target="tpu_custom_call" | custom-call | flops 4000000000 | tf_op jit(solution)/shard_map/image_rows/pallas_call | solution.py:606
  54.2 1.5 %collective-permute-start.14 = (bf16[17,32,128]{2,1,0:T(8,128)(2,1)}, bf16[17,32,128]{2,1,0:T(8,128)(2,1)S(1)}, u32[]{:S(2)}, u32[]{:S(2)}) collective-permute-start(bf16[17,32,128]{2,1,0:T(8,128)(2,1)} %image_rows.1.refs_6_), channel_id=1, source_target_pairs={{2,0},{3,1},{0,2},{1,3},{6,4},{7,5},{4,6},{5,7},{10,8},{11,9},{8,1... | collective-permute-start | bytes 417800 | tf_op jit(solution)/shard_map/ppermute | solution.py:36
  56.7 4.1 %collective-permute-start.18 = (bf16[2,17,32,128]{3,2,1,0:T(8,128)(2,1)S(1)}, bf16[2,17,32,128]{3,2,1,0:T(8,128)(2,1)S(1)}, u32[]{:S(2)}, u32[]{:S(2)}) collective-permute-start(bf16[2,17,32,128]{3,2,1,0:T(8,128)(2,1)S(1)} %pad_maximum_fusion.1), channel_id=1, source_target_pairs={{0,4},{2,6},{4,8},{5,1},{6,10},{7,3},{8,12},{9,5},{10,14},{11,7},{... | collective-permute-start | bytes 835592 | tf_op jit(solution)/shard_map/ppermute | solution.py:64
  61.0 1.3 %collective-permute-done.15.refs_9_ = bf16[17,32,128]{2,1,0:T(8,128)(2,1)S(1)} collective-permute-done((bf16[17,32,128]{2,1,0:T(8,128)(2,1)S(1)}, bf16[17,32,128]{2,1,0:T(8,128)(2,1)S(1)}, u32[]{:S(2)}, u32[]{:S(2)}) %collective-permute-start.15) | collective-permute-done | bytes 139296 | tf_op jit(solution)/shard_map/ppermute | solution.py:36
  62.3 3.7 %collective-permute-start.16 = (bf16[2,17,32,128]{3,2,1,0:T(8,128)(2,1)S(1)}, bf16[2,17,32,128]{3,2,1,0:T(8,128)(2,1)S(1)}, u32[]{:S(2)}, u32[]{:S(2)}) collective-permute-start(bf16[2,17,32,128]{3,2,1,0:T(8,128)(2,1)S(1)} %pad_maximum_fusion), channel_id=1, source_target_pairs={{0,4},{2,6},{4,8},{5,1},{6,10},{7,3},{8,12},{9,5},{10,14},{11,7},{... | collective-permute-start | bytes 835592 | tf_op jit(solution)/shard_map/ppermute | solution.py:64
  66.9 1.4 %collective-permute-start.19 = (f32[8,128]{1,0:T(8,128)S(1)}, f32[8,128]{1,0:T(8,128)S(1)}, u32[]{:S(2)}, u32[]{:S(2)}) collective-permute-start(f32[8,128]{1,0:T(8,128)S(1)} %maximum_maximum_fusion.refs_2_), channel_id=1, source_target_pairs={{4,0},{0,4},{12,8},{8,12},{5,1},{1,5},{13,9},{9,13},{6,2},{2,6},{1... | collective-permute-start | bytes 12296 | tf_op jit(solution)/shard_map/ppermute | solution.py:147
  69.3 2.0 %collective-permute-start.21 = (f32[8,128]{1,0:T(8,128)S(1)}, f32[8,128]{1,0:T(8,128)S(1)}, u32[]{:S(2)}, u32[]{:S(2)}) collective-permute-start(f32[8,128]{1,0:T(8,128)S(1)} %maximum_maximum_fusion.refs_2_), channel_id=1, source_target_pairs={{12,0},{8,4},{4,8},{0,12},{13,1},{9,5},{5,9},{1,13},{14,2},{10,6},... | collective-permute-start | bytes 12296 | tf_op jit(solution)/shard_map/ppermute | solution.py:147
  71.3 1.5 %collective-permute-done.20.refs_4_ = f32[8,128]{1,0:T(8,128)S(1)} collective-permute-done((f32[8,128]{1,0:T(8,128)S(1)}, f32[8,128]{1,0:T(8,128)S(1)}, u32[]{:S(2)}, u32[]{:S(2)}) %collective-permute-start.20) | collective-permute-done | bytes 4128 | tf_op jit(solution)/shard_map/ppermute | solution.py:147
  72.8 1.9 %collective-permute-done.21.refs_5_ = f32[8,128]{1,0:T(8,128)S(1)} collective-permute-done((f32[8,128]{1,0:T(8,128)S(1)}, f32[8,128]{1,0:T(8,128)S(1)}, u32[]{:S(2)}, u32[]{:S(2)}) %collective-permute-start.21) | collective-permute-done | bytes 4128 | tf_op jit(solution)/shard_map/ppermute | solution.py:147
  74.8 1.5 %collective-permute-done.23.refs_13_ = bf16[2,17,32,128]{3,2,1,0:T(8,128)(2,1)S(1)} collective-permute-done((bf16[2,17,32,128]{3,2,1,0:T(8,128)(2,1)S(1)}, bf16[2,17,32,128]{3,2,1,0:T(8,128)(2,1)S(1)}, u32[]{:S(2)}, u32[]{:S(2)}) %collective-permute-start.23) | collective-permute-done | bytes 278560 | tf_op jit(solution)/shard_map/ppermute | solution.py:36
  77.0 9.3 %correction_image_rows.1 = (bf16[4,32,128]{2,1,0:T(8,128)(2,1)}, bf16[4,32,128]{2,1,0:T(8,128)(2,1)}, bf16[4,32,128]{2,1,0:T(8,128)(2,1)}, bf16[4,32,128]{2,1,0:T(8,128)(2,1)}, bf16[1,4,128,128]{3,2,1,0:T(8,128)(2,1)}) custom-call(s32[4]{0:T(128)} %refs_0_.3, s32[4]{0:T(128)} %refs_1_.3, f32[8,128]{1,0:T(8,128)} %copy-done.22, f32[8,128]{1,0:T(8,128)} %copy-done.23, ...), custom_call_target="tpu_custom_call" | custom-call | flops 1000 | tf_op jit(solution)/shard_map/correction_image_rows/pallas_call | solution.py:632
  86.6 1.2 %collective-permute-start.25 = (bf16[4,32,128]{2,1,0:T(8,128)(2,1)}, bf16[4,32,128]{2,1,0:T(8,128)(2,1)S(1)}, u32[]{:S(2)}, u32[]{:S(2)}) collective-permute-start(bf16[4,32,128]{2,1,0:T(8,128)(2,1)} %get-tuple-element.50), channel_id=1, source_target_pairs={{2,0},{3,1},{0,2},{1,3},{6,4},{7,5},{4,6},{5,7},{10,8},{11,9},{8,1... | collective-permute-start | bytes 98312 | tf_op jit(solution)/shard_map/ppermute | solution.py:36
  89.1 1.6 %collective-permute-done.25 = bf16[4,32,128]{2,1,0:T(8,128)(2,1)S(1)} collective-permute-done((bf16[4,32,128]{2,1,0:T(8,128)(2,1)}, bf16[4,32,128]{2,1,0:T(8,128)(2,1)S(1)}, u32[]{:S(2)}, u32[]{:S(2)}) %collective-permute-start.25) | collective-permute-done | bytes 32800 | tf_op jit(solution)/shard_map/ppermute | solution.py:36
  (107 shorter events, 17.0 us)
Async XLA Ops:
  0.6 1.7 %collective-permute-start.2 = (bf16[4,128,128]{2,1,0:T(8,128)(2,1)}, bf16[4,128,128]{2,1,0:T(8,128)(2,1)S(1)}, u32[]{:S(2)}, u32[]{:S(2)}) collective-permute-start(bf16[4,128,128]{2,1,0:T(8,128)(2,1)} %bitcast.114), channel_id=1, source_target_pairs={{1,0},{0,1},{3,2},{2,3},{5,4},{4,5},{7,6},{6,7},{9,8},{8,9},{11,10... | collective-permute-start | bytes 393224 | tf_op jit(solution)/shard_map/ppermute | solution.py:36
  3.3 8.7 %collective-permute-start.5 = (bf16[2,4,128,128]{3,2,1,0:T(8,128)(2,1)S(1)}, bf16[2,4,128,128]{3,2,1,0:T(8,128)(2,1)S(1)}, u32[]{:S(2)}, u32[]{:S(2)}) collective-permute-start(bf16[2,4,128,128]{3,2,1,0:T(8,128)(2,1)S(1)} %pad_maximum_fusion.2), channel_id=1, source_target_pairs={{0,4},{2,6},{4,8},{5,1},{6,10},{7,3},{8,12},{9,5},{10,14},{11,7},{... | collective-permute-start | bytes 786440 | tf_op jit(solution)/shard_map/ppermute | solution.py:64
  8.2 34.1 %collective-permute-start = (bf16[20,1,128,128]{3,2,1,0:T(8,128)(2,1)}, bf16[20,1,128,128]{3,2,1,0:T(8,128)(2,1)S(1)}, u32[]{:S(2)}, u32[]{:S(2)}) collective-permute-start(bf16[20,1,128,128]{3,2,1,0:T(8,128)(2,1)} %refs_18_.1), channel_id=1, source_target_pairs={{4,0},{9,1},{6,2},{11,3},{8,4},{13,5},{10,6},{15,7},{12,8},{14,10}... | collective-permute-start | bytes 1966088 | tf_op jit(solution)/shard_map/ppermute | solution.py:108
  9.5 32.9 %collective-permute-start.1 = (bf16[20,1,128,128]{3,2,1,0:T(8,128)(2,1)}, bf16[20,1,128,128]{3,2,1,0:T(8,128)(2,1)S(1)}, u32[]{:S(2)}, u32[]{:S(2)}) collective-permute-start(bf16[20,1,128,128]{3,2,1,0:T(8,128)(2,1)} %refs_18_.1), channel_id=1, source_target_pairs={{12,0},{14,2},{28,16},{30,18}} | collective-permute-start | bytes 1966088 | tf_op jit(solution)/shard_map/ppermute | solution.py:108
  12.0 11.0 %collective-permute-start.6 = (bf16[2,4,128,128]{3,2,1,0:T(8,128)(2,1)S(1)}, bf16[2,4,128,128]{3,2,1,0:T(8,128)(2,1)S(1)}, u32[]{:S(2)}, u32[]{:S(2)}) collective-permute-start(bf16[2,4,128,128]{3,2,1,0:T(8,128)(2,1)S(1)} %collective-permute-done.5.refs_7_), channel_id=1, source_target_pairs={{2,0},{3,1},{0,2},{1,3},{6,4},{7,5},{4,6},{5,7},{10,8},{11,9},{8,1... | collective-permute-start | bytes 786440 | tf_op jit(solution)/shard_map/ppermute | solution.py:36
  14.4 8.6 %collective-permute-start.10 = (bf16[5,64,128]{2,1,0:T(8,128)(2,1)S(1)}, bf16[5,64,128]{2,1,0:T(8,128)(2,1)S(1)}, u32[]{:S(2)}, u32[]{:S(2)}) collective-permute-start(bf16[5,64,128]{2,1,0:T(8,128)(2,1)S(1)} %dynamic-slice_bitcast_fusion), channel_id=1, source_target_pairs={{2,0},{3,1},{0,2},{1,3},{6,4},{7,5},{4,6},{5,7},{10,8},{11,9},{8,1... | collective-permute-start | bytes 245768 | tf_op jit(solution)/shard_map/ppermute | solution.py:36
  15.0 10.7 %collective-permute-start.3 = (bf16[4,128,128]{2,1,0:T(8,128)(2,1)}, bf16[4,128,128]{2,1,0:T(8,128)(2,1)S(1)}, u32[]{:S(2)}, u32[]{:S(2)}) collective-permute-start(bf16[4,128,128]{2,1,0:T(8,128)(2,1)} %bitcast.115), channel_id=1, source_target_pairs={{2,0},{3,1},{0,2},{1,3},{6,4},{7,5},{4,6},{5,7},{10,8},{11,9},{8,1... | collective-permute-start | bytes 393224 | tf_op jit(solution)/shard_map/ppermute | solution.py:36
  23.0 3.2 %collective-permute-start.9 = (bf16[5,128,128]{2,1,0:T(8,128)(2,1)}, bf16[5,128,128]{2,1,0:T(8,128)(2,1)S(1)}, u32[]{:S(2)}, u32[]{:S(2)}) collective-permute-start(bf16[5,128,128]{2,1,0:T(8,128)(2,1)} %bitcast.118), channel_id=1, source_target_pairs={{1,0},{0,1},{3,2},{2,3},{5,4},{4,5},{7,6},{6,7},{9,8},{8,9},{11,10... | collective-permute-start | bytes 491528 | tf_op jit(solution)/shard_map/ppermute | solution.py:36
  23.0 2.8 %collective-permute-start.11 = (bf16[5,64,128]{2,1,0:T(8,128)(2,1)S(1)}, bf16[5,64,128]{2,1,0:T(8,128)(2,1)S(1)}, u32[]{:S(2)}, u32[]{:S(2)}) collective-permute-start(bf16[5,64,128]{2,1,0:T(8,128)(2,1)S(1)} %collective-permute-done.10.refs_13_), channel_id=1, source_target_pairs={{1,0},{0,1},{3,2},{2,3},{5,4},{4,5},{7,6},{6,7},{9,8},{8,9},{11,10... | collective-permute-start | bytes 245768 | tf_op jit(solution)/shard_map/ppermute | solution.py:36
  25.7 2.1 %collective-permute-start.7 = (bf16[2,4,128,128]{3,2,1,0:T(8,128)(2,1)S(1)}, bf16[2,4,128,128]{3,2,1,0:T(8,128)(2,1)S(1)}, u32[]{:S(2)}, u32[]{:S(2)}) collective-permute-start(bf16[2,4,128,128]{3,2,1,0:T(8,128)(2,1)S(1)} %collective-permute-done.5.refs_7_), channel_id=1, source_target_pairs={{1,0},{0,1},{3,2},{2,3},{5,4},{4,5},{7,6},{6,7},{9,8},{8,9},{11,10... | collective-permute-start | bytes 786440 | tf_op jit(solution)/shard_map/ppermute | solution.py:36
  25.8 2.0 %collective-permute-start.8 = (bf16[2,4,128,128]{3,2,1,0:T(8,128)(2,1)S(1)}, bf16[2,4,128,128]{3,2,1,0:T(8,128)(2,1)S(1)}, u32[]{:S(2)}, u32[]{:S(2)}) collective-permute-start(bf16[2,4,128,128]{3,2,1,0:T(8,128)(2,1)S(1)} %collective-permute-done.6.refs_8_), channel_id=1, source_target_pairs={{1,0},{0,1},{3,2},{2,3},{5,4},{4,5},{7,6},{6,7},{9,8},{8,9},{11,10... | collective-permute-start | bytes 786440 | tf_op jit(solution)/shard_map/ppermute | solution.py:36
  42.4 2.5 %collective-permute-start.12 = (bf16[20,1,128,128]{3,2,1,0:T(8,128)(2,1)S(1)}, bf16[20,1,128,128]{3,2,1,0:T(8,128)(2,1)S(1)}, u32[]{:S(2)}, u32[]{:S(2)}) collective-permute-start(bf16[20,1,128,128]{3,2,1,0:T(8,128)(2,1)S(1)} %collective-permute-done.refs_0_.refs_19_), channel_id=1, source_target_pairs={{0,1},{1,0},{2,3},{3,2},{4,5},{5,4},{6,7},{7,6},{8,9},{9,8},{10,11... | collective-permute-start | bytes 1966088 | tf_op jit(solution)/shard_map/ppermute | solution.py:122
  42.6 4.0 %collective-permute-start.13 = (bf16[20,1,128,128]{3,2,1,0:T(8,128)(2,1)S(1)}, bf16[20,1,128,128]{3,2,1,0:T(8,128)(2,1)S(1)}, u32[]{:S(2)}, u32[]{:S(2)}) collective-permute-start(bf16[20,1,128,128]{3,2,1,0:T(8,128)(2,1)S(1)} %collective-permute-done.1.refs_2_.refs_21_), channel_id=1, source_target_pairs={{0,1},{2,3},{4,5},{6,7},{8,9},{10,11},{12,13},{14,15},{16,17},{18,... | collective-permute-start | bytes 1966088 | tf_op jit(solution)/shard_map/ppermute | solution.py:122
  53.8 1.9 %collective-permute-start.17 = (bf16[17,32,128]{2,1,0:T(8,128)(2,1)}, bf16[17,32,128]{2,1,0:T(8,128)(2,1)S(1)}, u32[]{:S(2)}, u32[]{:S(2)}) collective-permute-start(bf16[17,32,128]{2,1,0:T(8,128)(2,1)} %image_rows.1.refs_6_), channel_id=1, source_target_pairs={{1,0},{0,1},{3,2},{2,3},{5,4},{4,5},{7,6},{6,7},{9,8},{8,9},{11,10... | collective-permute-start | bytes 417800 | tf_op jit(solution)/shard_map/ppermute | solution.py:36
  54.2 6.6 %collective-permute-start.14 = (bf16[17,32,128]{2,1,0:T(8,128)(2,1)}, bf16[17,32,128]{2,1,0:T(8,128)(2,1)S(1)}, u32[]{:S(2)}, u32[]{:S(2)}) collective-permute-start(bf16[17,32,128]{2,1,0:T(8,128)(2,1)} %image_rows.1.refs_6_), channel_id=1, source_target_pairs={{2,0},{3,1},{0,2},{1,3},{6,4},{7,5},{4,6},{5,7},{10,8},{11,9},{8,1... | collective-permute-start | bytes 417800 | tf_op jit(solution)/shard_map/ppermute | solution.py:36
  56.7 9.3 %collective-permute-start.18 = (bf16[2,17,32,128]{3,2,1,0:T(8,128)(2,1)S(1)}, bf16[2,17,32,128]{3,2,1,0:T(8,128)(2,1)S(1)}, u32[]{:S(2)}, u32[]{:S(2)}) collective-permute-start(bf16[2,17,32,128]{3,2,1,0:T(8,128)(2,1)S(1)} %pad_maximum_fusion.1), channel_id=1, source_target_pairs={{0,4},{2,6},{4,8},{5,1},{6,10},{7,3},{8,12},{9,5},{10,14},{11,7},{... | collective-permute-start | bytes 835592 | tf_op jit(solution)/shard_map/ppermute | solution.py:64
  62.3 12.4 %collective-permute-start.16 = (bf16[2,17,32,128]{3,2,1,0:T(8,128)(2,1)S(1)}, bf16[2,17,32,128]{3,2,1,0:T(8,128)(2,1)S(1)}, u32[]{:S(2)}, u32[]{:S(2)}) collective-permute-start(bf16[2,17,32,128]{3,2,1,0:T(8,128)(2,1)S(1)} %pad_maximum_fusion), channel_id=1, source_target_pairs={{0,4},{2,6},{4,8},{5,1},{6,10},{7,3},{8,12},{9,5},{10,14},{11,7},{... | collective-permute-start | bytes 835592 | tf_op jit(solution)/shard_map/ppermute | solution.py:64
  66.9 4.4 %collective-permute-start.19 = (f32[8,128]{1,0:T(8,128)S(1)}, f32[8,128]{1,0:T(8,128)S(1)}, u32[]{:S(2)}, u32[]{:S(2)}) collective-permute-start(f32[8,128]{1,0:T(8,128)S(1)} %maximum_maximum_fusion.refs_2_), channel_id=1, source_target_pairs={{4,0},{0,4},{12,8},{8,12},{5,1},{1,5},{13,9},{9,13},{6,2},{2,6},{1... | collective-permute-start | bytes 12296 | tf_op jit(solution)/shard_map/ppermute | solution.py:147
  68.3 4.5 %collective-permute-start.20 = (f32[8,128]{1,0:T(8,128)S(1)}, f32[8,128]{1,0:T(8,128)S(1)}, u32[]{:S(2)}, u32[]{:S(2)}) collective-permute-start(f32[8,128]{1,0:T(8,128)S(1)} %maximum_maximum_fusion.refs_2_), channel_id=1, source_target_pairs={{8,0},{12,4},{0,8},{4,12},{9,1},{13,5},{1,9},{5,13},{10,2},{14,6},... | collective-permute-start | bytes 12296 | tf_op jit(solution)/shard_map/ppermute | solution.py:147
  69.3 5.4 %collective-permute-start.21 = (f32[8,128]{1,0:T(8,128)S(1)}, f32[8,128]{1,0:T(8,128)S(1)}, u32[]{:S(2)}, u32[]{:S(2)}) collective-permute-start(f32[8,128]{1,0:T(8,128)S(1)} %maximum_maximum_fusion.refs_2_), channel_id=1, source_target_pairs={{12,0},{8,4},{4,8},{0,12},{13,1},{9,5},{5,9},{1,13},{14,2},{10,6},... | collective-permute-start | bytes 12296 | tf_op jit(solution)/shard_map/ppermute | solution.py:147
  71.3 3.5 %collective-permute-start.22 = (bf16[2,17,32,128]{3,2,1,0:T(8,128)(2,1)S(1)}, bf16[2,17,32,128]{3,2,1,0:T(8,128)(2,1)S(1)}, u32[]{:S(2)}, u32[]{:S(2)}) collective-permute-start(bf16[2,17,32,128]{3,2,1,0:T(8,128)(2,1)S(1)} %collective-permute-done.18.refs_10_), channel_id=1, source_target_pairs={{1,0},{0,1},{3,2},{2,3},{5,4},{4,5},{7,6},{6,7},{9,8},{8,9},{11,10... | collective-permute-start | bytes 835592 | tf_op jit(solution)/shard_map/ppermute | solution.py:36
  86.3 2.7 %collective-permute-start.24 = (bf16[4,32,128]{2,1,0:T(8,128)(2,1)}, bf16[4,32,128]{2,1,0:T(8,128)(2,1)S(1)}, u32[]{:S(2)}, u32[]{:S(2)}) collective-permute-start(bf16[4,32,128]{2,1,0:T(8,128)(2,1)} %get-tuple-element.49), channel_id=1, source_target_pairs={{1,0},{0,1},{3,2},{2,3},{5,4},{4,5},{7,6},{6,7},{9,8},{8,9},{11,10... | collective-permute-start | bytes 98312 | tf_op jit(solution)/shard_map/ppermute | solution.py:36
  86.6 4.1 %collective-permute-start.25 = (bf16[4,32,128]{2,1,0:T(8,128)(2,1)}, bf16[4,32,128]{2,1,0:T(8,128)(2,1)S(1)}, u32[]{:S(2)}, u32[]{:S(2)}) collective-permute-start(bf16[4,32,128]{2,1,0:T(8,128)(2,1)} %get-tuple-element.50), channel_id=1, source_target_pairs={{2,0},{3,1},{0,2},{1,3},{6,4},{7,5},{4,6},{5,7},{10,8},{11,9},{8,1... | collective-permute-start | bytes 98312 | tf_op jit(solution)/shard_map/ppermute | solution.py:36
  87.8 3.6 %collective-permute-start.26 = (bf16[4,32,128]{2,1,0:T(8,128)(2,1)}, bf16[4,32,128]{2,1,0:T(8,128)(2,1)S(1)}, u32[]{:S(2)}, u32[]{:S(2)}) collective-permute-start(bf16[4,32,128]{2,1,0:T(8,128)(2,1)} %get-tuple-element.51), channel_id=1, source_target_pairs={{3,0},{2,1},{1,2},{0,3},{7,4},{6,5},{5,6},{4,7},{11,8},{10,9},{9,1... | collective-permute-start | bytes 98312 | tf_op jit(solution)/shard_map/ppermute | solution.py:36
  (29 other events, 159.5 us)

commit v6 on v5

--- a/solution.py
+++ b/solution.py
@@ -45,7 +45,7 @@
     return bits
 
 
-def exchange(own, cross_last):
+def exchange(own):
     n_bond, n_mpo = lax.axis_size("bond"), lax.axis_size("mpo")
     pairs = [
         (i * n_mpo + j, (i + 1 - 2 * (j % 2)) * n_mpo + j)
@@ -53,35 +53,56 @@
         for j in range(n_mpo)
         if 0 <= i + 1 - 2 * (j % 2) < n_bond
     ]
+    here = own_sector(own)
+    first = jnp.stack([here[0], here[1]])
+    mine = {}
+    for r in range(0, n_mpo, 2):
+        pair = jnp.stack([here[r], here[r ^ 1]]) if r else first
+        mine[r] = lax.ppermute(pair, ("bond", "mpo"), pairs)
+    return here, first, mine
+
+
+def own_sector(own):
     here = {0: own, 1: from_near(own, 0, 1)}
     for bit in mpo_bits()[:-1]:
         here.update({r ^ bit: from_near(here[r], 0, bit) for r in sorted(here) if r % 2 == 0})
-    for r in range(2, n_mpo, 2):
+    for r in range(2, len(here) * 2 - 2, 2):
         here[r ^ 1] = from_near(here[r], 0, 1)
-    mine = {}
-    for r in range(0, n_mpo, 2):
-        if r == 0 or not cross_last:
-            mine[r] = lax.ppermute(jnp.stack([here[r], here[r ^ 1]]), ("bond", "mpo"), pairs)
-    if cross_last:
-        for bit in mpo_bits()[:-1]:
-            mine.update({r ^ bit: from_near(pair, 0, bit) for r, pair in list(mine.items())})
-    return here, mine
+    return here
+
+
+def exchange_all(own, before):
+    n_mpo = lax.axis_size("mpo")
+    low, high = from_near(own, -1, 0), from_near(own, 1, 0)
+    here = own_sector(own)
+    (low, high), _, before = lax.optimization_barrier(((low, high), here[n_mpo // 2], before))
+    both = {0: jnp.stack([low, high])}
+    for bit in mpo_bits():
+        both.update({r ^ bit: from_near(pair, 0, bit) for r, pair in list(both.items())})
+    rest = [here[r] for r in range(2, n_mpo)]
+    return [jnp.stack([here[0], here[1]])] + rest + [both[r] for r in range(n_mpo)], before
+
+
+def all_places(n_mpo):
+    places = [(0, 0, 0, 0), (0, 1, 1, 0)] + [(r - 1, None, r, 0) for r in range(2, n_mpo)]
+    return places + [(n_mpo - 1 + r, side, r, 3 + side) for r in range(n_mpo) for side in range(2)]
 
 
 def handed_pairs(mine):
     return {r: from_near(pair, 0, 1) for r, pair in mine.items()}
 
 
-def by_place(here, mine, other):
+def by_place(here, first, mine, other):
     evens = sorted(mine)
-    return [here[r] for r in sorted(here)] + [mine[r] for r in evens] + [other[r] for r in evens]
+    rest = [here[r] for r in sorted(here) if r > 1]
+    return [first] + rest + [mine[r] for r in evens] + [other[r] for r in evens]
 
 
 def block_places(n_mpo):
-    places = [(r, None, r, 0) for r in range(n_mpo)]
+    places = [(0, 0, 0, 0), (0, 1, 1, 0)] + [(r - 1, None, r, 0) for r in range(2, n_mpo)]
     for kind in (1, 2):
         for r in range(0, n_mpo, 2):
-            array = n_mpo + (kind - 1) * (n_mpo // 2) + r // 2
+            array = n_mpo - 1 + (kind - 1) * (n_mpo // 2) + r // 2
             order = (r, r ^ 1) if kind == 1 else (r ^ 1, r)
             places += [(array, index, member, kind) for index, member in enumerate(order)]
     return places
@@ -91,6 +112,8 @@
     odd = lax.rem(lax.axis_index("mpo"), 2)
     if kind == 0:
         return 0, 0
+    if kind > 2:
+        return kind - 2, 2 * kind - 7
     above = odd if kind == 1 else 1 - odd
     return 1 + above, 2 * above - 1
 
@@ -151,9 +174,25 @@
     return parts
 
 
-def sector_limits(sizes_ref, sector, count):
+def far_sums(sums):
+    n_bond, n_mpo = lax.axis_size("bond"), lax.axis_size("mpo")
+    pairs = [((i ^ (2 + j % 2)) * n_mpo + j, i * n_mpo + j) for i in range(n_bond) for j in range(n_mpo)]
+    return [sums, lax.ppermute(sums, ("bond", "mpo"), pairs)]
+
+
+def near_sums(plan, image_near):
+    here = lax.axis_index("bond")
+    parts = []
+    for place, (_, _, _, kind) in enumerate(block_places(plan.n_mpo)):
+        if kind > 0:
+            wanted = here + sector_of(kind)[1] == lax.bitwise_xor(here, 1)
+            parts.append(sums_of(image_near[place]) * jnp.where(wanted, 1.0, 0.0).astype(F32))
+    return parts
+
+
+def sector_limits(sizes_ref, first, sector, count):
     inside = (sector >= 0) & (sector < count)
-    return jnp.where(inside, sizes_ref[jnp.clip(sector, 0, count - 1)], 0)
+    return jnp.where(inside, sizes_ref[first + jnp.clip(sector, 0, count - 1)], 0)
 
 
 def state_charge(state):
@@ -171,10 +210,11 @@
         self.rows = width // n_mpo
         self.y_step = self.rows + 8
         self.far = min(RIM, n_bond - 1)
+        self.n_near = 2 * n_mpo - 1
         self.n_far = 2 * ((self.far + 1) // 2)
 
 
-def fill_left(plan, charge_ref, left_near, wide, ls):
+def fill_left(plan, sizes_ref, left_near, wide, ls):
     me = lax.axis_index("mpo")
     wide[...] = jnp.zeros_like(wide)
     for r in range(plan.n_mpo):
@@ -183,26 +223,26 @@
             w = owner * plan.w_here + t
             block = left_near[r, t].astype(F32)
             for c, charge in enumerate((0, 1, -1)):
-                factor = jnp.where(charge_ref[w] == charge, 1.0, 0.0).astype(F32)
+                factor = jnp.where(sizes_ref[w] == charge, 1.0, 0.0).astype(F32)
                 wide[c, pl.ds(w, plan.rows, stride=plan.w_pad), :] = block * factor
     for c in range(3):
         ls[:, c * plan.width : (c + 1) * plan.width] = wide[c].astype(BF16)
 
 
-def fill_vector(plan, left_ref, right_ref, psi_near, fs):
+def fill_vector(plan, sizes_ref, psi_near, fs):
     me = lax.axis_index("mpo")
     here = lax.axis_index("bond")
     row = lax.broadcasted_iota(jnp.int32, (plan.width, plan.width), 0)
     column = lax.broadcasted_iota(jnp.int32, (plan.width, plan.width), 1)
-    for place, (_, _, r, kind) in enumerate(block_places(plan.n_mpo)):
+    for place, (_, _, r, kind) in enumerate(all_places(plan.n_mpo)):
         slot, step = sector_of(kind)
         sector = here + step
         first = lax.bitwise_xor(me, r)
-        row_ok = row < sector_limits(left_ref, sector, plan.n_bond)
+        row_ok = row < sector_limits(sizes_ref, plan.w, sector, plan.n_bond)
         where = pl.ds(pl.multiple_of(slot * plan.width, plan.width), plan.width)
         for second in range(STATES):
             target = sector + state_charge(first) + STATE_CHARGES[second]
-            ok = row_ok & (column < sector_limits(right_ref, target, plan.n_bond))
+            ok = row_ok & (column < sector_limits(sizes_ref, plan.w + plan.n_bond, target, plan.n_bond))
             block = psi_near[place, second].astype(F32)
             fs[first * STATES + second, where, :] = jnp.where(ok, block, 0.0).astype(BF16)
 
@@ -219,7 +259,7 @@
     lax.fori_loop(0, PAIRS // 2, step, 0, unroll=8)
 
 
-def site_matrices(plan, charge_ref, sites_ref, first_out, second_out):
+def site_matrices(plan, sizes_ref, sites_ref, first_out, second_out):
     w, pad = plan.w, plan.w_pad
     size = STATES * w
 
@@ -229,7 +269,7 @@
     def charges(bond):
         total = jnp.zeros(bond.shape, jnp.int32)
         for v in range(w):
-            total = jnp.where(bond == v, charge_ref[v], total)
+            total = jnp.where(bond == v, sizes_ref[v], total)
         return total
 
     row, column = index((size, size), 0), index((size, size), 1)
@@ -328,30 +368,48 @@
     return result
 
 
+class RightCopy:
+    def __init__(self, plan, source, right_near, slot, sem):
+        self.copy = pltpu.make_async_copy(source.at[:, 0], right_near.at[slot], sem)
+        self.there = None if isinstance(slot, int) else slot <= plan.far
+
+    def start(self):
+        self.do(self.copy.start)
+
+    def wait(self):
+        self.do(self.copy.wait)
+
+    def do(self, action):
+        if self.there is None:
+            action()
+        else:
+            pl.when(self.there)(action)
+
+
 def right_copies(plan, own_ref, far_refs, right_near, sems):
     odd = lax.rem(lax.axis_index("mpo"), 2)
     copies = [[] for _ in range(plan.far + 1)]
-    copies[0].append(pltpu.make_async_copy(own_ref.at[:, 0], right_near.at[0], sems.at[0]))
+    copies[0].append(RightCopy(plan, own_ref, right_near, 0, sems.at[0]))
     for place, source in enumerate(far_refs):
         first, other = 1 + 2 * (place // 2), place % 2
         slot = first + (1 - odd if other else odd)
-        copies[first].append(pltpu.make_async_copy(source.at[:, 0], right_near.at[slot], sems.at[1 + place]))
+        copies[first].append(RightCopy(plan, source, right_near, slot, sems.at[1 + place]))
     return copies
 
 
-def masked_rows(plan, left_ref, right_ref, result):
+def masked_rows(plan, sizes_ref, result):
     me = lax.axis_index("mpo")
     here = lax.axis_index("bond")
     shape = (plan.rows, plan.width)
     row = lax.broadcasted_iota(jnp.int32, shape, 0) + me * plan.rows
     column = lax.broadcasted_iota(jnp.int32, shape, 1)
-    row_ok = row < sector_limits(left_ref, here, plan.n_bond)
+    row_ok = row < sector_limits(sizes_ref, plan.w, here, plan.n_bond)
     blocks = []
     for p, charge in enumerate(pair_charges()):
         if result[p] is None:
             blocks.append(jnp.zeros(shape, BF16))
             continue
-        ok = row_ok & (column < sector_limits(right_ref, here + charge, plan.n_bond))
+        ok = row_ok & (column < sector_limits(sizes_ref, plan.w + plan.n_bond, here + charge, plan.n_bond))
         blocks.append(jnp.where(ok, result[p], 0.0).astype(BF16))
     return blocks
 
@@ -360,40 +418,38 @@
     return jnp.sum(jnp.sum(values, axis=1, keepdims=True), axis=0, keepdims=True)
 
 
-def near_copies(plan, refs, near, sems, count):
+def near_copies(places, refs, near, sems, count):
     copies = []
-    for place, (array, index, _, _) in enumerate(block_places(plan.n_mpo)):
+    for place, (array, index, _, _) in enumerate(places):
         source = refs[array] if index is None else refs[array].at[index]
         copies.append(pltpu.make_async_copy(source.at[pl.ds(0, count)], near.at[place], sems.at[place]))
     return copies
 
 
 def first_kernel(plan, *refs):
-    charge_ref, left_ref, right_ref = refs[:3]
-    psi_refs = refs[3 : 3 + 2 * plan.n_mpo]
-    left_refs = refs[3 + 2 * plan.n_mpo : 3 + 3 * plan.n_mpo]
-    refs = refs[3 + 3 * plan.n_mpo :]
+    sizes_ref, refs = refs[0], refs[1:]
+    psi_refs, refs = refs[: plan.n_near], refs[plan.n_near :]
+    left_refs, refs = refs[: plan.n_mpo], refs[plan.n_mpo :]
     sites_ref, ys_out, fs_out, ls_out, first_out, second_out = refs[:6]
     fs, ls, wide, xs, ys, left_near, psi_near, left_sem, psi_sem, out_sem, y_sem = refs[6:]
     me = lax.axis_index("mpo")
-    rows_here = pl.ds(pl.multiple_of(me * plan.rows, plan.rows), plan.rows)
     odd_rows = pl.ds(pl.multiple_of(lax.rem(me, 2) * plan.rows, plan.rows), plan.rows)
     left_copies = [
-        pltpu.make_async_copy(source.at[:, odd_rows if r > 1 else rows_here, :], left_near.at[r], left_sem.at[r])
+        pltpu.make_async_copy(source.at[:, odd_rows, :], left_near.at[r], left_sem.at[r])
         for r, source in enumerate(left_refs)
     ]
-    psi_copies = near_copies(plan, psi_refs, psi_near, psi_sem, STATES)
+    psi_copies = near_copies(all_places(plan.n_mpo), psi_refs, psi_near, psi_sem, STATES)
     for copy in left_copies + psi_copies:
         copy.start()
-    site_matrices(plan, charge_ref, sites_ref, first_out, second_out)
+    site_matrices(plan, sizes_ref, sites_ref, first_out, second_out)
     for copy in left_copies:
         copy.wait()
-    fill_left(plan, charge_ref, left_near, wide, ls)
+    fill_left(plan, sizes_ref, left_near, wide, ls)
     ls_copy = pltpu.make_async_copy(ls, ls_out, out_sem.at[0])
     ls_copy.start()
     for copy in psi_copies:
         copy.wait()
-    fill_vector(plan, left_ref, right_ref, psi_near, fs)
+    fill_vector(plan, sizes_ref, psi_near, fs)
     fs_copy = pltpu.make_async_copy(fs, fs_out, out_sem.at[1])
     fs_copy.start()
     left_phase(plan, fs, ls, xs)
@@ -412,7 +468,7 @@
     fs_copy.wait()
 
 
-def image_kernel(plan, left_ref, right_ref, ys_ref, vector_ref, own_ref, *refs):
+def image_kernel(plan, sizes_ref, ys_ref, vector_ref, own_ref, *refs):
     far_refs, (image, ys, right_near, vector, y_sem, right_sem, v_sem) = refs[: plan.n_far], refs[plan.n_far :]
     me = lax.axis_index("mpo")
     rows_here = pl.ds(pl.multiple_of(me * plan.rows, plan.rows), plan.rows)
@@ -422,17 +478,18 @@
     }
     r_copies = right_copies(plan, own_ref, far_refs, right_near, right_sem)
     v_copy = pltpu.make_async_copy(vector_ref.at[:, rows_here, :], vector, v_sem)
-    for n in range(plan.far + 1):
-        for copy in r_copies[n] + [y_copies[p] for p in range(PAIRS) if charges[p] == n]:
+    stages = [r_copies[n] + [y_copies[p] for p in range(PAIRS) if charges[p] == n] for n in range(plan.far + 1)]
+    for copy in [copy for some in stages[:AHEAD] for copy in some] + [v_copy]:
+        copy.start()
+
+    def ready(n):
+        for copy in [copy for some in stages[n + AHEAD : n + AHEAD + 1] for copy in some]:
             copy.start()
-    v_copy.start()
-
-    def ready(n):
-        for copy in r_copies[n] + [y_copies[p] for p in range(PAIRS) if charges[p] == n]:
+        for copy in stages[n]:
             copy.wait()
 
     result = right_phase(plan, True, ys, plan.rows, right_near, ready)
-    blocks = masked_rows(plan, left_ref, right_ref, result)
+    blocks = masked_rows(plan, sizes_ref, result)
     v_copy.wait()
     along = jnp.zeros((plan.rows, plan.width), F32)
     norm = jnp.zeros((plan.rows, plan.width), F32)
@@ -464,27 +521,28 @@
     return block[0:8] + block[8:16] + block[16:24]
 
 
-def second_kernel(plan, count_all, n_parts, *refs):
-    left_ref, right_ref = refs[:2]
-    parts, refs = refs[2 : 2 + n_parts], refs[2 + n_parts :]
-    image_refs, refs = refs[: 2 * plan.n_mpo], refs[2 * plan.n_mpo :]
+def second_kernel(plan, count_all, n_parts, near, *refs):
+    sizes_ref = refs[0]
+    parts, refs = refs[1 : 1 + n_parts], refs[1 + n_parts :]
+    image_refs, refs = refs[: plan.n_near], refs[plan.n_near :]
     vector_ref, ls_ref, first_ref, second_ref, own_ref = refs[:5]
     far_refs, refs = refs[5 : 5 + plan.n_far], refs[5 + plan.n_far :]
     outs, image_out = refs[: plan.n_mpo], refs[plan.n_mpo]
     fs, xs, ys, image_near, vector, ls, right_near, image_sem, field_sem, right_sem, out_sem = refs[plan.n_mpo + 1 :]
     me = lax.axis_index("mpo")
-    image_copies = near_copies(plan, image_refs, image_near, image_sem, PAIRS)
+    image_copies = near_copies(block_places(plan.n_mpo), image_refs, image_near, image_sem, PAIRS + 1)
     v_copy = pltpu.make_async_copy(vector_ref, vector, field_sem.at[0])
     l_copy = pltpu.make_async_copy(ls_ref, ls, field_sem.at[1])
     r_copies = right_copies(plan, own_ref, far_refs, right_near, right_sem)
     for copy in [v_copy] + image_copies + [l_copy]:
         copy.start()
-    sums = merged([part[...] for part in parts])
+    for copy in image_copies:
+        copy.wait()
+    sums = merged([part[...] for part in parts] + (near_sums(plan, image_near) if near else []))
     rayleigh = sums[0:1, :] / sums[1:2, :]
     scale = lax.rsqrt(sums[2:3, :] / count_all + EPSILON)
     v_copy.wait()
     for place, (_, _, r, kind) in enumerate(block_places(plan.n_mpo)):
-        image_copies[place].wait()
         slot, _ = sector_of(kind)
         start = slot * plan.width + lax.bitwise_xor(me, r) * plan.rows
         where = pl.ds(pl.multiple_of(start, plan.rows), plan.rows)
@@ -512,7 +570,7 @@
             copy.wait()
 
     result = right_phase(plan, False, ys, plan.y_step, right_near, ready)
-    rows = masked_rows(plan, left_ref, right_ref, result)
+    rows = masked_rows(plan, sizes_ref, result)
     for p in range(PAIRS):
         ys[p, : plan.rows, :] = rows[p].astype(F32)
     for r, out in enumerate(outs):
@@ -524,12 +582,14 @@
 
 
 Y_BLOCK = 8
+AHEAD = 2
 COST_A = 1_000
 COST_B = 4_000_000_000
 VMEM = pl.BlockSpec(memory_space=pltpu.VMEM)
 ANY = pl.BlockSpec(memory_space=pl.ANY)
 SMEM = pl.BlockSpec(memory_space=pltpu.SMEM)
-PARAMS = pltpu.CompilerParams(vmem_limit_bytes=59 * 1024 * 1024)
+PARAMS = pltpu.CompilerParams(vmem_limit_bytes=52 * 1024 * 1024)
+PARAMS_B = pltpu.CompilerParams(vmem_limit_bytes=52 * 1024 * 1024)
 
 
 def shape_of(shape, dtype):
@@ -546,18 +606,20 @@
     sites = jnp.transpose(jnp.stack([site_one, site_two]), (0, 3, 2, 4, 1))
     sites = sites.reshape(2, STATES * plan.w, STATES * plan.w)
 
-    psi_here, psi_mine = exchange(psi[0], True)
-    psi_mine, sites = lax.optimization_barrier((psi_mine, sites))
-    psi_other = handed_pairs(psi_mine)
+    sizes = jnp.concatenate([mpo_charge, left_sizes, right_sizes])
 
     left_mine = left_env[:, 0]
-    left_pieces = [left_mine, from_near(left_mine, 0, 1)]
-    for r in range(2, n_mpo, 2):
+    left_halves = []
+    for r in range(0, n_mpo, 2):
         start = lax.bitwise_xor(me - lax.rem(me, 2), r) * plan.rows
-        both = from_near(lax.dynamic_slice_in_dim(left_mine, start, 2 * plan.rows, 1), 0, r)
-        left_pieces += [both, from_near(both, 0, 1)]
-
-    right_far = right_exchange(right_env, plan.far)
+        left_halves.append(lax.dynamic_slice_in_dim(left_mine, start, 2 * plan.rows, 1))
+    right_here, left_halves[0] = lax.optimization_barrier((right_env, left_halves[0]))
+    left_halves = [from_near(both, 0, 2 * r) if r else both for r, both in enumerate(left_halves)]
+    psi_arrays, before = exchange_all(psi[0], (left_halves, sites, sizes))
+    left_halves, sites, sizes = before
+    left_pieces = [piece for both in left_halves for piece in (both, from_near(both, 0, 1))]
+
+    right_far = right_exchange(right_here, plan.far)
 
     field_shape = (PAIRS, 3 * width, width)
     left_shape = (plan.rows * plan.w_pad, 3 * width)
@@ -577,7 +639,7 @@
             shape_of(first_shape, BF16),
             shape_of(second_shape, BF16),
         ),
-        in_specs=[SMEM] * 3 + [ANY] * (3 * n_mpo) + [VMEM],
+        in_specs=[SMEM] + [ANY] * (plan.n_near + n_mpo) + [VMEM],
         out_specs=(ANY, ANY, ANY, VMEM, VMEM),
         scratch_shapes=[
             pltpu.VMEM(field_shape, BF16),
@@ -596,7 +658,7 @@
         cost_estimate=pl.CostEstimate(flops=COST_A, bytes_accessed=0, transcendentals=0),
         name="states_of_vector",
     )(
-        mpo_charge, left_sizes, right_sizes, *by_place(psi_here, psi_mine, psi_other), *left_pieces, sites,
+        sizes, *psi_arrays, *left_pieces, sites,
     )
 
     right_far, ys = lax.optimization_barrier((right_far, ys))
@@ -606,7 +668,7 @@
     image_rows = pl.pallas_call(
         functools.partial(image_kernel, plan),
         out_shape=shape_of(image_shape, BF16),
-        in_specs=[SMEM] * 2 + [ANY] * (3 + plan.n_far),
+        in_specs=[SMEM] + [ANY] * (3 + plan.n_far),
         out_specs=VMEM,
         scratch_shapes=[
             pltpu.VMEM((PAIRS, plan.w * plan.rows, width), F32),
@@ -616,29 +678,33 @@
             pltpu.SemaphoreType.DMA((1 + plan.n_far,)),
             pltpu.SemaphoreType.DMA,
         ],
-        compiler_params=PARAMS,
+        compiler_params=PARAMS_B,
         cost_estimate=pl.CostEstimate(flops=COST_B, bytes_accessed=0, transcendentals=0),
         name="image_rows",
-    )(left_sizes, right_sizes, ys.reshape(PAIRS, plan.w * plan.rows, width), vector, right_env, *right_pieces)
-
-    image_here, image_mine = exchange(image_rows, False)
+    )(sizes, ys.reshape(PAIRS, plan.w * plan.rows, width), vector, right_env, *right_pieces)
+
+    image_here, image_first, image_mine = exchange(image_rows)
     blocks, _ = lax.optimization_barrier((image_here, image_mine[0]))
-    sums = summed_over_bond(merged([sums_of(blocks[r]) for r in range(n_mpo)]))
+    sums = merged([sums_of(blocks[r]) for r in range(n_mpo)])
+    near = n_bond == 4
+    sums = far_sums(sums) if near else summed_over_bond(sums)
     last = max(image_mine)
     image_mine[last], sums = lax.optimization_barrier((image_mine[last], sums))
     image_other = handed_pairs(image_mine)
+    if near:
+        sums = sums + [from_near(sums[1], 0, 1)]
 
     count_all = n_bond * PAIRS * width * width
     *second_rows, image = pl.pallas_call(
-        functools.partial(second_kernel, plan, float(count_all), len(sums)),
+        functools.partial(second_kernel, plan, float(count_all), len(sums), near),
         out_shape=(shape_of((STATES,) + row_shape[1:], BF16),) * n_mpo + (shape_of(psi.shape, BF16),),
-        in_specs=[SMEM] * 2 + [VMEM] * len(sums) + [ANY] * (2 * n_mpo + 2) + [VMEM] * 2 + [ANY] * (1 + plan.n_far),
+        in_specs=[SMEM] + [VMEM] * len(sums) + [ANY] * (plan.n_near + 2) + [VMEM] * 2 + [ANY] * (1 + plan.n_far),
         out_specs=(VMEM,) * n_mpo + (ANY,),
         scratch_shapes=[
             pltpu.VMEM(field_shape, BF16),
             pltpu.VMEM(x_shape, F32),
             pltpu.VMEM(y_shape, F32),
-            pltpu.VMEM((3 * n_mpo,) + row_shape, BF16),
+            pltpu.VMEM((3 * n_mpo,) + image_shape, BF16),
             pltpu.VMEM(field_shape, BF16),
             pltpu.VMEM(left_shape, BF16),
             right_scratch,
@@ -651,7 +717,7 @@
         cost_estimate=pl.CostEstimate(flops=COST_A, bytes_accessed=0, transcendentals=0),
         name="correction_image_rows",
     )(
-        left_sizes, right_sizes, *sums, *by_place(image_here, image_mine, image_other), vector, left_rows,
+        sizes, *sums, *by_place(image_here, image_first, image_mine, image_other), vector, left_rows,
         first, second, right_env, *right_pieces,
     )
 

time: 92.8 us -> 86.2 us (0.929)
  waiting for transfers between devices: 20.7 us -> 18.9 us
  local copies, waits for them, and re-layouts: 6.53 us -> 4.93 us
  Pallas kernels: 28.7 us -> 27.5 us
  other arithmetic: 3.9 us -> 2.97 us
    ppermute x6 -> x3, starting transfers between devices: 17.1 us -> 10.3 us  [the longest x2 9.17 us: exchange(): mine[r] = lax.ppermute(pair, ('bond', 'mpo'), pairs)]
    ppermute x17 -> x20, starting transfers between devices: 9.11 us -> 13.6 us  [from_near(): return lax.ppermute(value, ('bond', 'mpo'), pairs)]
    ppermute x2, starting transfers between devices: 2.51 us -> 4.04 us  [handed_over(): result += [array, lax.ppermute(array, ('bond', 'mpo'), pairs)]]
    pallas_call x1, Pallas kernels: 6.4 us -> 5.16 us  [shards(): pl.pallas_call(functools.partial(image_kernel, plan), out_shape=shape_of(...]
    ppermute x6 -> x3, waiting for transfers between devices: 4.68 us -> 3.45 us  [the longest x1 3.44 us: far_sums(): return [sums, lax.ppermute(sums, ('bond', 'mpo'), pairs)]]
    another operation x3 -> x4, other arithmetic: 1.99 us -> 1.01 us  [the longest x1 0.93 us: exchange_all(): jnp.stack([here[0], here[1]])]
    ppermute x17 -> x20, waiting for transfers between devices: 14.4 us -> 13.8 us  [from_near(): return lax.ppermute(value, ('bond', 'mpo'), pairs)]
    unnamed x52 -> x14, local copies, waits for them, and re-layouts: 3.65 us -> 3.36 us
  transfers between devices with their start and end apart: 27 -> 27, of which waited for: 11 -> 13; matrix products, arithmetic and copies ran while one was open for 6% -> 5% of each run, Pallas kernels for 14% -> 15%
where the time goes in v6:
time: 86.2 us; the launch traced here: 85.8 us
  starting transfers between devices  30.6 us (35%)
  Pallas kernels  27.5 us (32%)
  waiting for transfers between devices  18.9 us (22%)
  local copies, waits for them, and re-layouts  4.93 us (6%)
  other arithmetic  2.97 us (3%)
  between operations  0.94 us (1%)
    ppermute x20, waiting for transfers between devices, from_near(): return lax.ppermute(value, ('bond', 'mpo'), pairs)  13.8 us
    ppermute x20, starting transfers between devices, from_near(): return lax.ppermute(value, ('bond', 'mpo'), pairs)  13.6 us
    pallas_call x1, Pallas kernels, shards(): pl.pallas_call(functools.partial(first_kernel, plan), out_shape=(shape_of...  13.1 us
    pallas_call x1, Pallas kernels, shards(): pl.pallas_call(functools.partial(second_kernel, plan, float(count_all), l...  9.23 us
    ppermute x2, starting transfers between devices, exchange(): mine[r] = lax.ppermute(pair, ('bond', 'mpo'), pairs)  9.17 us
    pallas_call x1, Pallas kernels, shards(): pl.pallas_call(functools.partial(image_kernel, plan), out_shape=shape_of(...  5.16 us
    ppermute x2, starting transfers between devices, handed_over(): result += [array, lax.ppermute(array, ('bond', 'mpo'), pairs)]  4.04 us
    ppermute x1, waiting for transfers between devices, far_sums(): return [sums, lax.ppermute(sums, ('bond', 'mpo'), pairs)]  3.44 us
  transfers between devices with their start and end apart: 27, of which 13 were waited for; matrix products, arithmetic and copies ran while one was open for 5% of the time, Pallas kernels for 15%

profile of v6, /device:TPU:0, one launch (start us, length us, event | category | flops | bytes accessed | tf_op | source)
XLA Modules:
  0.0 85.8 jit_solution(769122006226075497)
XLA Ops:
  0.6 3.0 %collective-permute-start.2 = (bf16[4,128,128]{2,1,0:T(8,128)(2,1)}, bf16[4,128,128]{2,1,0:T(8,128)(2,1)S(1)}, u32[]{:S(2)}, u32[]{:S(2)}) collective-permute-start(bf16[4,128,128]{2,1,0:T(8,128)(2,1)} %bitcast.117), channel_id=1, source_target_pairs={{2,0},{3,1},{0,2},{1,3},{6,4},{7,5},{4,6},{5,7},{10,8},{11,9},{8,1... | collective-permute-start | bytes 393224 | tf_op jit(solution)/shard_map/ppermute | solution.py:36
  3.6 3.5 %collective-permute-start = (bf16[4,128,128]{2,1,0:T(8,128)(2,1)}, bf16[4,128,128]{2,1,0:T(8,128)(2,1)S(1)}, u32[]{:S(2)}, u32[]{:S(2)}) collective-permute-start(bf16[4,128,128]{2,1,0:T(8,128)(2,1)} %bitcast.118), channel_id=1, source_target_pairs={{0,4},{1,5},{2,6},{3,7},{4,8},{5,9},{6,10},{7,11},{8,12},{9,13},{1... | collective-permute-start | bytes 393224 | tf_op jit(solution)/shard_map/ppermute | solution.py:36
  7.1 1.3 %collective-permute-start.1 = (bf16[4,128,128]{2,1,0:T(8,128)(2,1)}, bf16[4,128,128]{2,1,0:T(8,128)(2,1)S(1)}, u32[]{:S(2)}, u32[]{:S(2)}) collective-permute-start(bf16[4,128,128]{2,1,0:T(8,128)(2,1)} %bitcast.119), channel_id=1, source_target_pairs={{4,0},{5,1},{6,2},{7,3},{8,4},{9,5},{10,6},{11,7},{12,8},{13,9},{1... | collective-permute-start | bytes 393224 | tf_op jit(solution)/shard_map/ppermute | solution.py:36
  10.0 1.3 %collective-permute-start.4 = (bf16[20,1,128,128]{3,2,1,0:T(8,128)(2,1)}, bf16[20,1,128,128]{3,2,1,0:T(8,128)(2,1)S(1)}, u32[]{:S(2)}, u32[]{:S(2)}) collective-permute-start(bf16[20,1,128,128]{3,2,1,0:T(8,128)(2,1)} %refs_15_.1), channel_id=1, source_target_pairs={{4,0},{9,1},{6,2},{11,3},{8,4},{13,5},{10,6},{15,7},{12,8},{14,10}... | collective-permute-start | bytes 1966088 | tf_op jit(solution)/shard_map/ppermute | solution.py:131
  11.3 1.1 %maximum_bitcast_fusion = bf16[2,4,20,4,20]{2,3,1,4,0:T(4,128)(2,1)S(1)} fusion(bf16[1,20,20,4,4]{2,4,3,1,0:T(4,128)(2,1)} %bitcast.124, bf16[1,20,20,4,4]{2,4,3,1,0:T(4,128)(2,1)} %bitcast.125), kind=kLoop, calls=%fused_computation.4 | loop fusion | flops 12800 | bytes 51200 | tf_op jit(solution)/shard_map/transpose | solution.py:606
  12.3 1.6 %collective-permute-done.3.refs_10_ = bf16[5,64,128]{2,1,0:T(8,128)(2,1)S(1)} collective-permute-done((bf16[5,64,128]{2,1,0:T(8,128)(2,1)S(1)}, bf16[5,64,128]{2,1,0:T(8,128)(2,1)S(1)}, u32[]{:S(2)}, u32[]{:S(2)}) %collective-permute-start.3) | collective-permute-done | bytes 81952 | tf_op jit(solution)/shard_map/ppermute | solution.py:36
  13.9 1.3 %collective-permute-start.5 = (bf16[20,1,128,128]{3,2,1,0:T(8,128)(2,1)}, bf16[20,1,128,128]{3,2,1,0:T(8,128)(2,1)S(1)}, u32[]{:S(2)}, u32[]{:S(2)}) collective-permute-start(bf16[20,1,128,128]{3,2,1,0:T(8,128)(2,1)} %refs_15_.1), channel_id=1, source_target_pairs={{12,0},{14,2},{28,16},{30,18}} | collective-permute-start | bytes 1966088 | tf_op jit(solution)/shard_map/ppermute | solution.py:131
  17.6 1.2 %collective-permute-done.6 = bf16[4,128,128]{2,1,0:T(8,128)(2,1)S(1)} collective-permute-done((bf16[4,128,128]{2,1,0:T(8,128)(2,1)}, bf16[4,128,128]{2,1,0:T(8,128)(2,1)S(1)}, u32[]{:S(2)}, u32[]{:S(2)}) %collective-permute-start.6) | collective-permute-done | bytes 131104 | tf_op jit(solution)/shard_map/ppermute | solution.py:36
  18.9 4.0 %collective-permute-done.9.refs_6_ = bf16[2,4,128,128]{3,2,1,0:T(8,128)(2,1)S(1)} collective-permute-done((bf16[2,4,128,128]{3,2,1,0:T(8,128)(2,1)S(1)}, bf16[2,4,128,128]{3,2,1,0:T(8,128)(2,1)S(1)}, u32[]{:S(2)}, u32[]{:S(2)}) %collective-permute-start.9) | collective-permute-done | bytes 262176 | tf_op jit(solution)/shard_map/ppermute | solution.py:36
  23.4 1.1 %collective-permute-done.12.refs_11_ = bf16[5,64,128]{2,1,0:T(8,128)(2,1)S(1)} collective-permute-done((bf16[5,64,128]{2,1,0:T(8,128)(2,1)S(1)}, bf16[5,64,128]{2,1,0:T(8,128)(2,1)S(1)}, u32[]{:S(2)}, u32[]{:S(2)}) %collective-permute-start.12) | collective-permute-done | bytes 81952 | tf_op jit(solution)/shard_map/ppermute | solution.py:36
  26.6 13.1 %states_of_vector.1 = (f32[16,20,32,128]{3,2,1,0:T(8,128)}, bf16[16,384,128]{2,1,0:T(8,128)(2,1)}, bf16[768,384]{1,0:T(8,128)(2,1)}, bf16[80,96]{1,0:T(8,128)(2,1)S(1)}, bf16[160,160]{1,0:T(8,128)(2,1)S(1)}) custom-call(s32[28]{0:T(128)S(1)} %pad_add_fusion.refs_0_.sizes_ref, bf16[2,4,128,128]{3,2,1,0:T(8,128)(2,1)S(1)} %pad_maximum_fusion.2.refs_1_, ...), custom_call_target="tpu_custom_call" | custom-call | flops 1000 | tf_op jit(solution)/shard_map/states_of_vector/pallas_call | solution.py:633
  39.8 2.1 %collective-permute-start.13 = (bf16[20,1,128,128]{3,2,1,0:T(8,128)(2,1)S(1)}, bf16[20,1,128,128]{3,2,1,0:T(8,128)(2,1)S(1)}, u32[]{:S(2)}, u32[]{:S(2)}) collective-permute-start(bf16[20,1,128,128]{3,2,1,0:T(8,128)(2,1)S(1)} %collective-permute-done.4.refs_0_.refs_16_), channel_id=1, source_target_pairs={{0,1},{1,0},{2,3},{3,2},{4,5},{5,4},{6,7},{7,6},{8,9},{9,8},{10,11... | collective-permute-start | bytes 1966088 | tf_op jit(solution)/shard_map/ppermute | solution.py:145
  41.8 2.0 %collective-permute-start.14 = (bf16[20,1,128,128]{3,2,1,0:T(8,128)(2,1)S(1)}, bf16[20,1,128,128]{3,2,1,0:T(8,128)(2,1)S(1)}, u32[]{:S(2)}, u32[]{:S(2)}) collective-permute-start(bf16[20,1,128,128]{3,2,1,0:T(8,128)(2,1)S(1)} %collective-permute-done.5.refs_2_.refs_18_), channel_id=1, source_target_pairs={{0,1},{2,3},{4,5},{6,7},{8,9},{10,11},{12,13},{14,15},{16,17},{18,... | collective-permute-start | bytes 1966088 | tf_op jit(solution)/shard_map/ppermute | solution.py:145
  43.8 1.6 %collective-permute-done.14.refs_3_.refs_19_ = bf16[20,1,128,128]{3,2,1,0:T(8,128)(2,1)S(1)} collective-permute-done((bf16[20,1,128,128]{3,2,1,0:T(8,128)(2,1)S(1)}, bf16[20,1,128,128]{3,2,1,0:T(8,128)(2,1)S(1)}, u32[]{:S(2)}, u32[]{:S(2)}) %collective-permute-start.14) | collective-permute-done | bytes 655392 | tf_op jit(solution)/shard_map/ppermute | solution.py:145
  46.4 1.1 %copy-done = bf16[20,1,128,128]{3,2,1,0:T(8,128)(2,1)S(1)} copy-done((bf16[20,1,128,128]{3,2,1,0:T(8,128)(2,1)S(1)}, bf16[20,1,128,128]{3,2,1,0:T(8,128)(2,1)}, u32[]{:S(2)}) %copy-start) | copy-done | bytes 655384
  47.5 5.2 %image_rows.1 = bf16[17,32,128]{2,1,0:T(8,128)(2,1)S(1)} custom-call(s32[28]{0:T(128)S(1)} %pad_add_fusion.refs_0_.sizes_ref, f32[16,640,128]{2,1,0:T(8,128)} %bitcast.126, bf16[16,384,128]{2,1,0:T(8,128)(2,1)} %get-tuple-element.40.vector_ref.refs_11_, bf16[20,1,128,128]{3,2,1,0:T(8,128)(2,1)S(1)} %copy-done, ...), custom_call_target="tpu_custom_call" | custom-call | flops 4000000000 | tf_op jit(solution)/shard_map/image_rows/pallas_call | solution.py:668
  54.2 4.5 %collective-permute-start.19 = (bf16[2,17,32,128]{3,2,1,0:T(8,128)(2,1)S(1)}, bf16[2,17,32,128]{3,2,1,0:T(8,128)(2,1)S(1)}, u32[]{:S(2)}, u32[]{:S(2)}) collective-permute-start(bf16[2,17,32,128]{3,2,1,0:T(8,128)(2,1)S(1)} %pad_maximum_fusion.1.refs_4_), channel_id=1, source_target_pairs={{0,4},{2,6},{4,8},{5,1},{6,10},{7,3},{8,12},{9,5},{10,14},{11,7},{... | collective-permute-start | bytes 835592 | tf_op jit(solution)/shard_map/ppermute | solution.py:61
  58.9 1.3 %collective-permute-done.16.refs_6_ = bf16[17,32,128]{2,1,0:T(8,128)(2,1)S(1)} collective-permute-done((bf16[17,32,128]{2,1,0:T(8,128)(2,1)S(1)}, bf16[17,32,128]{2,1,0:T(8,128)(2,1)S(1)}, u32[]{:S(2)}, u32[]{:S(2)}) %collective-permute-start.16) | collective-permute-done | bytes 139296 | tf_op jit(solution)/shard_map/ppermute | solution.py:36
  60.2 4.7 %collective-permute-start.17 = (bf16[2,17,32,128]{3,2,1,0:T(8,128)(2,1)S(1)}, bf16[2,17,32,128]{3,2,1,0:T(8,128)(2,1)S(1)}, u32[]{:S(2)}, u32[]{:S(2)}) collective-permute-start(bf16[2,17,32,128]{3,2,1,0:T(8,128)(2,1)S(1)} %pad_maximum_fusion), channel_id=1, source_target_pairs={{0,4},{2,6},{4,8},{5,1},{6,10},{7,3},{8,12},{9,5},{10,14},{11,7},{... | collective-permute-start | bytes 835592 | tf_op jit(solution)/shard_map/ppermute | solution.py:61
  65.1 1.2 %collective-permute-start.20 = (f32[8,128]{1,0:T(8,128)S(1)}, f32[8,128]{1,0:T(8,128)S(1)}, u32[]{:S(2)}, u32[]{:S(2)}) collective-permute-start(f32[8,128]{1,0:T(8,128)S(1)} %maximum_maximum_fusion.refs_1_), channel_id=1, source_target_pairs={{8,0},{13,1},{10,2},{15,3},{12,4},{9,5},{14,6},{11,7},{0,8},{5,9},... | collective-permute-start | bytes 12296 | tf_op jit(solution)/shard_map/ppermute | solution.py:180
  66.3 3.4 %collective-permute-done.20.refs_2_ = f32[8,128]{1,0:T(8,128)S(1)} collective-permute-done((f32[8,128]{1,0:T(8,128)S(1)}, f32[8,128]{1,0:T(8,128)S(1)}, u32[]{:S(2)}, u32[]{:S(2)}) %collective-permute-start.20) | collective-permute-done | bytes 4128 | tf_op jit(solution)/shard_map/ppermute | solution.py:180
  70.2 1.1 %collective-permute-done.21.refs_3_ = f32[8,128]{1,0:T(8,128)S(1)} collective-permute-done((f32[8,128]{1,0:T(8,128)S(1)}, f32[8,128]{1,0:T(8,128)S(1)}, u32[]{:S(2)}, u32[]{:S(2)}) %collective-permute-start.21) | collective-permute-done | bytes 4128 | tf_op jit(solution)/shard_map/ppermute | solution.py:36
  71.3 9.2 %correction_image_rows.1 = (bf16[4,32,128]{2,1,0:T(8,128)(2,1)S(1)}, bf16[4,32,128]{2,1,0:T(8,128)(2,1)S(1)}, bf16[4,32,128]{2,1,0:T(8,128)(2,1)S(1)}, bf16[4,32...) custom-call(s32[28]{0:T(128)S(1)} %pad_add_fusion.refs_0_.sizes_ref, f32[8,128]{1,0:T(8,128)S(1)} %maximum_maximum_fusion.refs_1_, ...), custom_call_target="tpu_custom_call" | custom-call | flops 1000 | tf_op jit(solution)/shard_map/correction_image_rows/pallas_call | solution.py:698
  82.5 2.1 %collective-permute-done.25 = bf16[4,32,128]{2,1,0:T(8,128)(2,1)S(1)} collective-permute-done((bf16[4,32,128]{2,1,0:T(8,128)(2,1)S(1)}, bf16[4,32,128]{2,1,0:T(8,128)(2,1)S(1)}, u32[]{:S(2)}, u32[]{:S(2)}) %collective-permute-start.25) | collective-permute-done | bytes 32800 | tf_op jit(solution)/shard_map/ppermute | solution.py:36
  (71 shorter events, 13.1 us)
Async XLA Ops:
  0.6 15.8 %collective-permute-start.2 = (bf16[4,128,128]{2,1,0:T(8,128)(2,1)}, bf16[4,128,128]{2,1,0:T(8,128)(2,1)S(1)}, u32[]{:S(2)}, u32[]{:S(2)}) collective-permute-start(bf16[4,128,128]{2,1,0:T(8,128)(2,1)} %bitcast.117), channel_id=1, source_target_pairs={{2,0},{3,1},{0,2},{1,3},{6,4},{7,5},{4,6},{5,7},{10,8},{11,9},{8,1... | collective-permute-start | bytes 393224 | tf_op jit(solution)/shard_map/ppermute | solution.py:36
  3.6 12.8 %collective-permute-start = (bf16[4,128,128]{2,1,0:T(8,128)(2,1)}, bf16[4,128,128]{2,1,0:T(8,128)(2,1)S(1)}, u32[]{:S(2)}, u32[]{:S(2)}) collective-permute-start(bf16[4,128,128]{2,1,0:T(8,128)(2,1)} %bitcast.118), channel_id=1, source_target_pairs={{0,4},{1,5},{2,6},{3,7},{4,8},{5,9},{6,10},{7,11},{8,12},{9,13},{1... | collective-permute-start | bytes 393224 | tf_op jit(solution)/shard_map/ppermute | solution.py:36
  7.1 9.3 %collective-permute-start.1 = (bf16[4,128,128]{2,1,0:T(8,128)(2,1)}, bf16[4,128,128]{2,1,0:T(8,128)(2,1)S(1)}, u32[]{:S(2)}, u32[]{:S(2)}) collective-permute-start(bf16[4,128,128]{2,1,0:T(8,128)(2,1)} %bitcast.119), channel_id=1, source_target_pairs={{4,0},{5,1},{6,2},{7,3},{8,4},{9,5},{10,6},{11,7},{12,8},{13,9},{1... | collective-permute-start | bytes 393224 | tf_op jit(solution)/shard_map/ppermute | solution.py:36
  9.4 4.5 %collective-permute-start.3 = (bf16[5,64,128]{2,1,0:T(8,128)(2,1)S(1)}, bf16[5,64,128]{2,1,0:T(8,128)(2,1)S(1)}, u32[]{:S(2)}, u32[]{:S(2)}) collective-permute-start(bf16[5,64,128]{2,1,0:T(8,128)(2,1)S(1)} %get-tuple-element.61), channel_id=1, source_target_pairs={{2,0},{3,1},{0,2},{1,3},{6,4},{7,5},{4,6},{5,7},{10,8},{11,9},{8,1... | collective-permute-start | bytes 245768 | tf_op jit(solution)/shard_map/ppermute | solution.py:36
  10.0 29.7 %collective-permute-start.4 = (bf16[20,1,128,128]{3,2,1,0:T(8,128)(2,1)}, bf16[20,1,128,128]{3,2,1,0:T(8,128)(2,1)S(1)}, u32[]{:S(2)}, u32[]{:S(2)}) collective-permute-start(bf16[20,1,128,128]{3,2,1,0:T(8,128)(2,1)} %refs_15_.1), channel_id=1, source_target_pairs={{4,0},{9,1},{6,2},{11,3},{8,4},{13,5},{10,6},{15,7},{12,8},{14,10}... | collective-permute-start | bytes 1966088 | tf_op jit(solution)/shard_map/ppermute | solution.py:131
  13.9 25.9 %collective-permute-start.5 = (bf16[20,1,128,128]{3,2,1,0:T(8,128)(2,1)}, bf16[20,1,128,128]{3,2,1,0:T(8,128)(2,1)S(1)}, u32[]{:S(2)}, u32[]{:S(2)}) collective-permute-start(bf16[20,1,128,128]{3,2,1,0:T(8,128)(2,1)} %refs_15_.1), channel_id=1, source_target_pairs={{12,0},{14,2},{28,16},{30,18}} | collective-permute-start | bytes 1966088 | tf_op jit(solution)/shard_map/ppermute | solution.py:131
  16.5 6.4 %collective-permute-start.9 = (bf16[2,4,128,128]{3,2,1,0:T(8,128)(2,1)S(1)}, bf16[2,4,128,128]{3,2,1,0:T(8,128)(2,1)S(1)}, u32[]{:S(2)}, u32[]{:S(2)}) collective-permute-start(bf16[2,4,128,128]{3,2,1,0:T(8,128)(2,1)S(1)} %pad_maximum_fusion.3.refs_4_), channel_id=1, source_target_pairs={{2,0},{3,1},{0,2},{1,3},{6,4},{7,5},{4,6},{5,7},{10,8},{11,9},{8,1... | collective-permute-start | bytes 786440 | tf_op jit(solution)/shard_map/ppermute | solution.py:36
  17.1 1.7 %collective-permute-start.6 = (bf16[4,128,128]{2,1,0:T(8,128)(2,1)}, bf16[4,128,128]{2,1,0:T(8,128)(2,1)S(1)}, u32[]{:S(2)}, u32[]{:S(2)}) collective-permute-start(bf16[4,128,128]{2,1,0:T(8,128)(2,1)} %bitcast.120), channel_id=1, source_target_pairs={{1,0},{0,1},{3,2},{2,3},{5,4},{4,5},{7,6},{6,7},{9,8},{8,9},{11,10... | collective-permute-start | bytes 393224 | tf_op jit(solution)/shard_map/ppermute | solution.py:36
  17.1 5.8 %collective-permute-start.11 = (bf16[5,64,128]{2,1,0:T(8,128)(2,1)S(1)}, bf16[5,64,128]{2,1,0:T(8,128)(2,1)S(1)}, u32[]{:S(2)}, u32[]{:S(2)}) collective-permute-start(bf16[5,64,128]{2,1,0:T(8,128)(2,1)S(1)} %get-tuple-element.35.refs_8_), channel_id=1, source_target_pairs={{1,0},{0,1},{3,2},{2,3},{5,4},{4,5},{7,6},{6,7},{9,8},{8,9},{11,10... | collective-permute-start | bytes 245768 | tf_op jit(solution)/shard_map/ppermute | solution.py:36
  18.8 7.2 %collective-permute-start.8 = (bf16[2,4,128,128]{3,2,1,0:T(8,128)(2,1)S(1)}, bf16[2,4,128,128]{3,2,1,0:T(8,128)(2,1)S(1)}, u32[]{:S(2)}, u32[]{:S(2)}) collective-permute-start(bf16[2,4,128,128]{3,2,1,0:T(8,128)(2,1)S(1)} %pad_maximum_fusion.3.refs_4_), channel_id=1, source_target_pairs={{1,0},{0,1},{3,2},{2,3},{5,4},{4,5},{7,6},{6,7},{9,8},{8,9},{11,10... | collective-permute-start | bytes 786440 | tf_op jit(solution)/shard_map/ppermute | solution.py:36
  22.9 3.0 %collective-permute-start.10 = (bf16[2,4,128,128]{3,2,1,0:T(8,128)(2,1)S(1)}, bf16[2,4,128,128]{3,2,1,0:T(8,128)(2,1)S(1)}, u32[]{:S(2)}, u32[]{:S(2)}) collective-permute-start(bf16[2,4,128,128]{3,2,1,0:T(8,128)(2,1)S(1)} %collective-permute-done.9.refs_6_), channel_id=1, source_target_pairs={{1,0},{0,1},{3,2},{2,3},{5,4},{4,5},{7,6},{6,7},{9,8},{8,9},{11,10... | collective-permute-start | bytes 786440 | tf_op jit(solution)/shard_map/ppermute | solution.py:36
  22.9 1.6 %collective-permute-start.12 = (bf16[5,64,128]{2,1,0:T(8,128)(2,1)S(1)}, bf16[5,64,128]{2,1,0:T(8,128)(2,1)S(1)}, u32[]{:S(2)}, u32[]{:S(2)}) collective-permute-start(bf16[5,64,128]{2,1,0:T(8,128)(2,1)S(1)} %collective-permute-done.3.refs_10_), channel_id=1, source_target_pairs={{1,0},{0,1},{3,2},{2,3},{5,4},{4,5},{7,6},{6,7},{9,8},{8,9},{11,10... | collective-permute-start | bytes 245768 | tf_op jit(solution)/shard_map/ppermute | solution.py:36
  39.8 4.0 %collective-permute-start.13 = (bf16[20,1,128,128]{3,2,1,0:T(8,128)(2,1)S(1)}, bf16[20,1,128,128]{3,2,1,0:T(8,128)(2,1)S(1)}, u32[]{:S(2)}, u32[]{:S(2)}) collective-permute-start(bf16[20,1,128,128]{3,2,1,0:T(8,128)(2,1)S(1)} %collective-permute-done.4.refs_0_.refs_16_), channel_id=1, source_target_pairs={{0,1},{1,0},{2,3},{3,2},{4,5},{5,4},{6,7},{7,6},{8,9},{9,8},{10,11... | collective-permute-start | bytes 1966088 | tf_op jit(solution)/shard_map/ppermute | solution.py:145
  41.8 3.6 %collective-permute-start.14 = (bf16[20,1,128,128]{3,2,1,0:T(8,128)(2,1)S(1)}, bf16[20,1,128,128]{3,2,1,0:T(8,128)(2,1)S(1)}, u32[]{:S(2)}, u32[]{:S(2)}) collective-permute-start(bf16[20,1,128,128]{3,2,1,0:T(8,128)(2,1)S(1)} %collective-permute-done.5.refs_2_.refs_18_), channel_id=1, source_target_pairs={{0,1},{2,3},{4,5},{6,7},{8,9},{10,11},{12,13},{14,15},{16,17},{18,... | collective-permute-start | bytes 1966088 | tf_op jit(solution)/shard_map/ppermute | solution.py:145
  53.1 5.7 %collective-permute-start.15 = (bf16[17,32,128]{2,1,0:T(8,128)(2,1)S(1)}, bf16[17,32,128]{2,1,0:T(8,128)(2,1)S(1)}, u32[]{:S(2)}, u32[]{:S(2)}) collective-permute-start(bf16[17,32,128]{2,1,0:T(8,128)(2,1)S(1)} %image_rows.1), channel_id=1, source_target_pairs={{2,0},{3,1},{0,2},{1,3},{6,4},{7,5},{4,6},{5,7},{10,8},{11,9},{8,1... | collective-permute-start | bytes 417800 | tf_op jit(solution)/shard_map/ppermute | solution.py:36
  54.2 10.8 %collective-permute-start.19 = (bf16[2,17,32,128]{3,2,1,0:T(8,128)(2,1)S(1)}, bf16[2,17,32,128]{3,2,1,0:T(8,128)(2,1)S(1)}, u32[]{:S(2)}, u32[]{:S(2)}) collective-permute-start(bf16[2,17,32,128]{3,2,1,0:T(8,128)(2,1)S(1)} %pad_maximum_fusion.1.refs_4_), channel_id=1, source_target_pairs={{0,4},{2,6},{4,8},{5,1},{6,10},{7,3},{8,12},{9,5},{10,14},{11,7},{... | collective-permute-start | bytes 835592 | tf_op jit(solution)/shard_map/ppermute | solution.py:61
  60.2 9.5 %collective-permute-start.17 = (bf16[2,17,32,128]{3,2,1,0:T(8,128)(2,1)S(1)}, bf16[2,17,32,128]{3,2,1,0:T(8,128)(2,1)S(1)}, u32[]{:S(2)}, u32[]{:S(2)}) collective-permute-start(bf16[2,17,32,128]{3,2,1,0:T(8,128)(2,1)S(1)} %pad_maximum_fusion), channel_id=1, source_target_pairs={{0,4},{2,6},{4,8},{5,1},{6,10},{7,3},{8,12},{9,5},{10,14},{11,7},{... | collective-permute-start | bytes 835592 | tf_op jit(solution)/shard_map/ppermute | solution.py:61
  65.1 4.6 %collective-permute-start.20 = (f32[8,128]{1,0:T(8,128)S(1)}, f32[8,128]{1,0:T(8,128)S(1)}, u32[]{:S(2)}, u32[]{:S(2)}) collective-permute-start(f32[8,128]{1,0:T(8,128)S(1)} %maximum_maximum_fusion.refs_1_), channel_id=1, source_target_pairs={{8,0},{13,1},{10,2},{15,3},{12,4},{9,5},{14,6},{11,7},{0,8},{5,9},... | collective-permute-start | bytes 12296 | tf_op jit(solution)/shard_map/ppermute | solution.py:180
  66.3 5.0 %collective-permute-start.22 = (bf16[2,17,32,128]{3,2,1,0:T(8,128)(2,1)S(1)}, bf16[2,17,32,128]{3,2,1,0:T(8,128)(2,1)S(1)}, u32[]{:S(2)}, u32[]{:S(2)}) collective-permute-start(bf16[2,17,32,128]{3,2,1,0:T(8,128)(2,1)S(1)} %collective-permute-done.19.refs_7_), channel_id=1, source_target_pairs={{1,0},{0,1},{3,2},{2,3},{5,4},{4,5},{7,6},{6,7},{9,8},{8,9},{11,10... | collective-permute-start | bytes 835592 | tf_op jit(solution)/shard_map/ppermute | solution.py:36
  69.7 1.6 %collective-permute-start.23 = (bf16[2,17,32,128]{3,2,1,0:T(8,128)(2,1)S(1)}, bf16[2,17,32,128]{3,2,1,0:T(8,128)(2,1)S(1)}, u32[]{:S(2)}, u32[]{:S(2)}) collective-permute-start(bf16[2,17,32,128]{3,2,1,0:T(8,128)(2,1)S(1)} %collective-permute-done.17.refs_8_), channel_id=1, source_target_pairs={{1,0},{0,1},{3,2},{2,3},{5,4},{4,5},{7,6},{6,7},{9,8},{8,9},{11,10... | collective-permute-start | bytes 835592 | tf_op jit(solution)/shard_map/ppermute | solution.py:36
  69.7 1.6 %collective-permute-start.21 = (f32[8,128]{1,0:T(8,128)S(1)}, f32[8,128]{1,0:T(8,128)S(1)}, u32[]{:S(2)}, u32[]{:S(2)}) collective-permute-start(f32[8,128]{1,0:T(8,128)S(1)} %collective-permute-done.20.refs_2_), channel_id=1, source_target_pairs={{1,0},{0,1},{3,2},{2,3},{5,4},{4,5},{7,6},{6,7},{9,8},{8,9},{11,10... | collective-permute-start | bytes 12296 | tf_op jit(solution)/shard_map/ppermute | solution.py:36
  80.5 2.0 %collective-permute-start.24 = (bf16[4,32,128]{2,1,0:T(8,128)(2,1)S(1)}, bf16[4,32,128]{2,1,0:T(8,128)(2,1)S(1)}, u32[]{:S(2)}, u32[]{:S(2)}) collective-permute-start(bf16[4,32,128]{2,1,0:T(8,128)(2,1)S(1)} %get-tuple-element.55), channel_id=1, source_target_pairs={{1,0},{0,1},{3,2},{2,3},{5,4},{4,5},{7,6},{6,7},{9,8},{8,9},{11,10... | collective-permute-start | bytes 98312 | tf_op jit(solution)/shard_map/ppermute | solution.py:36
  80.7 3.9 %collective-permute-start.25 = (bf16[4,32,128]{2,1,0:T(8,128)(2,1)S(1)}, bf16[4,32,128]{2,1,0:T(8,128)(2,1)S(1)}, u32[]{:S(2)}, u32[]{:S(2)}) collective-permute-start(bf16[4,32,128]{2,1,0:T(8,128)(2,1)S(1)} %get-tuple-element.56), channel_id=1, source_target_pairs={{2,0},{3,1},{0,2},{1,3},{6,4},{7,5},{4,6},{5,7},{10,8},{11,9},{8,1... | collective-permute-start | bytes 98312 | tf_op jit(solution)/shard_map/ppermute | solution.py:36
  81.7 3.4 %collective-permute-start.26 = (bf16[4,32,128]{2,1,0:T(8,128)(2,1)S(1)}, bf16[4,32,128]{2,1,0:T(8,128)(2,1)S(1)}, u32[]{:S(2)}, u32[]{:S(2)}) collective-permute-start(bf16[4,32,128]{2,1,0:T(8,128)(2,1)S(1)} %get-tuple-element.57), channel_id=1, source_target_pairs={{3,0},{2,1},{1,2},{0,3},{7,4},{6,5},{5,6},{4,7},{11,8},{10,9},{9,1... | collective-permute-start | bytes 98312 | tf_op jit(solution)/shard_map/ppermute | solution.py:36
  (10 other events, 27.8 us)

commit v7 on v6

--- a/solution.py
+++ b/solution.py
@@ -180,13 +180,13 @@
     return [sums, lax.ppermute(sums, ("bond", "mpo"), pairs)]
 
 
-def near_sums(plan, image_near):
+def near_sums(plan, blocks):
     here = lax.axis_index("bond")
     parts = []
     for place, (_, _, _, kind) in enumerate(block_places(plan.n_mpo)):
         if kind > 0:
             wanted = here + sector_of(kind)[1] == lax.bitwise_xor(here, 1)
-            parts.append(sums_of(image_near[place]) * jnp.where(wanted, 1.0, 0.0).astype(F32))
+            parts.append(sums_of(blocks[place]) * jnp.where(wanted, 1.0, 0.0).astype(F32))
     return parts
 
 
@@ -214,14 +214,15 @@
         self.n_far = 2 * ((self.far + 1) // 2)
 
 
-def fill_left(plan, sizes_ref, left_near, wide, ls):
+def fill_left(plan, sizes_ref, left_refs, wide, ls):
     me = lax.axis_index("mpo")
+    odd_rows = pl.ds(pl.multiple_of(lax.rem(me, 2) * plan.rows, plan.rows), plan.rows)
     wide[...] = jnp.zeros_like(wide)
     for r in range(plan.n_mpo):
         owner = lax.bitwise_xor(me, r)
         for t in range(plan.w_here):
             w = owner * plan.w_here + t
-            block = left_near[r, t].astype(F32)
+            block = left_refs[r][t, odd_rows, :].astype(F32)
             for c, charge in enumerate((0, 1, -1)):
                 factor = jnp.where(sizes_ref[w] == charge, 1.0, 0.0).astype(F32)
                 wide[c, pl.ds(w, plan.rows, stride=plan.w_pad), :] = block * factor
@@ -229,7 +230,7 @@
         ls[:, c * plan.width : (c + 1) * plan.width] = wide[c].astype(BF16)
 
 
-def fill_vector(plan, sizes_ref, psi_near, fs):
+def fill_vector(plan, sizes_ref, psi_blocks, fs):
     me = lax.axis_index("mpo")
     here = lax.axis_index("bond")
     row = lax.broadcasted_iota(jnp.int32, (plan.width, plan.width), 0)
@@ -243,7 +244,7 @@
         for second in range(STATES):
             target = sector + state_charge(first) + STATE_CHARGES[second]
             ok = row_ok & (column < sector_limits(sizes_ref, plan.w + plan.n_bond, target, plan.n_bond))
-            block = psi_near[place, second].astype(F32)
+            block = psi_blocks[place][second].astype(F32)
             fs[first * STATES + second, where, :] = jnp.where(ok, block, 0.0).astype(BF16)
 
 
@@ -418,12 +419,8 @@
     return jnp.sum(jnp.sum(values, axis=1, keepdims=True), axis=0, keepdims=True)
 
 
-def near_copies(places, refs, near, sems, count):
-    copies = []
-    for place, (array, index, _, _) in enumerate(places):
-        source = refs[array] if index is None else refs[array].at[index]
-        copies.append(pltpu.make_async_copy(source.at[pl.ds(0, count)], near.at[place], sems.at[place]))
-    return copies
+def near_blocks(places, refs):
+    return [refs[array] if index is None else refs[array].at[index] for array, index, _, _ in places]
 
 
 def first_kernel(plan, *refs):
@@ -431,25 +428,12 @@
     psi_refs, refs = refs[: plan.n_near], refs[plan.n_near :]
     left_refs, refs = refs[: plan.n_mpo], refs[plan.n_mpo :]
     sites_ref, ys_out, fs_out, ls_out, first_out, second_out = refs[:6]
-    fs, ls, wide, xs, ys, left_near, psi_near, left_sem, psi_sem, out_sem, y_sem = refs[6:]
-    me = lax.axis_index("mpo")
-    odd_rows = pl.ds(pl.multiple_of(lax.rem(me, 2) * plan.rows, plan.rows), plan.rows)
-    left_copies = [
-        pltpu.make_async_copy(source.at[:, odd_rows, :], left_near.at[r], left_sem.at[r])
-        for r, source in enumerate(left_refs)
-    ]
-    psi_copies = near_copies(all_places(plan.n_mpo), psi_refs, psi_near, psi_sem, STATES)
-    for copy in left_copies + psi_copies:
-        copy.start()
+    fs, ls, wide, xs, ys, out_sem, y_sem = refs[6:]
     site_matrices(plan, sizes_ref, sites_ref, first_out, second_out)
-    for copy in left_copies:
-        copy.wait()
-    fill_left(plan, sizes_ref, left_near, wide, ls)
+    fill_left(plan, sizes_ref, left_refs, wide, ls)
     ls_copy = pltpu.make_async_copy(ls, ls_out, out_sem.at[0])
     ls_copy.start()
-    for copy in psi_copies:
-        copy.wait()
-    fill_vector(plan, sizes_ref, psi_near, fs)
+    fill_vector(plan, sizes_ref, near_blocks(all_places(plan.n_mpo), psi_refs), fs)
     fs_copy = pltpu.make_async_copy(fs, fs_out, out_sem.at[1])
     fs_copy.start()
     left_phase(plan, fs, ls, xs)
@@ -528,17 +512,15 @@
     vector_ref, ls_ref, first_ref, second_ref, own_ref = refs[:5]
     far_refs, refs = refs[5 : 5 + plan.n_far], refs[5 + plan.n_far :]
     outs, image_out = refs[: plan.n_mpo], refs[plan.n_mpo]
-    fs, xs, ys, image_near, vector, ls, right_near, image_sem, field_sem, right_sem, out_sem = refs[plan.n_mpo + 1 :]
+    fs, xs, ys, vector, ls, right_near, field_sem, right_sem, out_sem = refs[plan.n_mpo + 1 :]
     me = lax.axis_index("mpo")
-    image_copies = near_copies(block_places(plan.n_mpo), image_refs, image_near, image_sem, PAIRS + 1)
+    blocks = near_blocks(block_places(plan.n_mpo), image_refs)
     v_copy = pltpu.make_async_copy(vector_ref, vector, field_sem.at[0])
     l_copy = pltpu.make_async_copy(ls_ref, ls, field_sem.at[1])
     r_copies = right_copies(plan, own_ref, far_refs, right_near, right_sem)
-    for copy in [v_copy] + image_copies + [l_copy]:
+    for copy in [v_copy, l_copy]:
         copy.start()
-    for copy in image_copies:
-        copy.wait()
-    sums = merged([part[...] for part in parts] + (near_sums(plan, image_near) if near else []))
+    sums = merged([part[...] for part in parts] + (near_sums(plan, blocks) if near else []))
     rayleigh = sums[0:1, :] / sums[1:2, :]
     scale = lax.rsqrt(sums[2:3, :] / count_all + EPSILON)
     v_copy.wait()
@@ -547,7 +529,7 @@
         start = slot * plan.width + lax.bitwise_xor(me, r) * plan.rows
         where = pl.ds(pl.multiple_of(start, plan.rows), plan.rows)
         for p in range(PAIRS):
-            block = image_near[place, p].astype(F32)
+            block = blocks[place][p].astype(F32)
             residual = block - rayleigh * vector[p, where, :].astype(F32)
             fs[p, where, :] = (residual * scale).astype(BF16)
     out_copies = []
@@ -557,7 +539,7 @@
             start = lax.bitwise_xor(me, r) * plan.rows
             rows = pl.ds(pl.multiple_of(start, plan.rows), plan.rows)
             out_copies.append(
-                pltpu.make_async_copy(image_near.at[place, pairs_here], image_out.at[0, :, rows, :], out_sem.at[r])
+                pltpu.make_async_copy(blocks[place].at[pairs_here], image_out.at[0, :, rows, :], out_sem.at[r])
             )
     for copy in out_copies + [copy for some in r_copies for copy in some]:
         copy.start()
@@ -639,7 +621,7 @@
             shape_of(first_shape, BF16),
             shape_of(second_shape, BF16),
         ),
-        in_specs=[SMEM] + [ANY] * (plan.n_near + n_mpo) + [VMEM],
+        in_specs=[SMEM] + [VMEM] * (plan.n_near + n_mpo + 1),
         out_specs=(ANY, ANY, ANY, VMEM, VMEM),
         scratch_shapes=[
             pltpu.VMEM(field_shape, BF16),
@@ -647,10 +629,6 @@
             pltpu.VMEM((3, left_shape[0], width), F32),
             pltpu.VMEM(x_shape, F32),
             pltpu.VMEM(y_shape, F32),
-            pltpu.VMEM((n_mpo, plan.w_here, plan.rows, width), BF16),
-            pltpu.VMEM((3 * n_mpo,) + psi.shape[1:], BF16),
-            pltpu.SemaphoreType.DMA((n_mpo,)),
-            pltpu.SemaphoreType.DMA((3 * n_mpo,)),
             pltpu.SemaphoreType.DMA((2,)),
             pltpu.SemaphoreType.DMA((plan.rows // Y_BLOCK,)),
         ],
@@ -698,17 +676,15 @@
     *second_rows, image = pl.pallas_call(
         functools.partial(second_kernel, plan, float(count_all), len(sums), near),
         out_shape=(shape_of((STATES,) + row_shape[1:], BF16),) * n_mpo + (shape_of(psi.shape, BF16),),
-        in_specs=[SMEM] + [VMEM] * len(sums) + [ANY] * (plan.n_near + 2) + [VMEM] * 2 + [ANY] * (1 + plan.n_far),
+        in_specs=[SMEM] + [VMEM] * (len(sums) + plan.n_near) + [ANY] * 2 + [VMEM] * 2 + [ANY] * (1 + plan.n_far),
         out_specs=(VMEM,) * n_mpo + (ANY,),
         scratch_shapes=[
             pltpu.VMEM(field_shape, BF16),
             pltpu.VMEM(x_shape, F32),
             pltpu.VMEM(y_shape, F32),
-            pltpu.VMEM((3 * n_mpo,) + image_shape, BF16),
             pltpu.VMEM(field_shape, BF16),
             pltpu.VMEM(left_shape, BF16),
             right_scratch,
-            pltpu.SemaphoreType.DMA((3 * n_mpo,)),
             pltpu.SemaphoreType.DMA((2,)),
             pltpu.SemaphoreType.DMA((1 + plan.n_far,)),
             pltpu.SemaphoreType.DMA((n_mpo,)),

time: 86.2 us -> 84.6 us (0.981)
  Pallas kernels: 27.5 us -> 23.7 us
  waiting for transfers between devices: 18.9 us -> 20 us
  starting transfers between devices: 30.6 us -> 31.6 us
    ppermute x2, starting transfers between devices: 4.04 us -> 6.16 us  [handed_over(): result += [array, lax.ppermute(array, ('bond', 'mpo'), pairs)]]
    pallas_call x1, Pallas kernels: 13.1 us -> 11 us  [shards(): pl.pallas_call(functools.partial(first_kernel, plan), out_shape=(shape_of...]
    pallas_call x1, Pallas kernels: 9.23 us -> 7.57 us  [shards(): pl.pallas_call(functools.partial(second_kernel, plan, float(count_all), l...]
    ppermute x1, starting transfers between devices: 1.17 us -> 0.02 us  [far_sums(): return [sums, lax.ppermute(sums, ('bond', 'mpo'), pairs)]]
    ppermute x1, waiting for transfers between devices: 3.44 us -> 4.52 us  [far_sums(): return [sums, lax.ppermute(sums, ('bond', 'mpo'), pairs)]]
  transfers between devices with their start and end apart: 27 -> 27, of which waited for: 13 -> 13; matrix products, arithmetic and copies ran while one was open for 5% -> 5% of each run, Pallas kernels for 15% -> 13%
where the time goes in v7:
time: 84.6 us; the launch traced here: 84.1 us
  starting transfers between devices  31.6 us (37%)
  Pallas kernels  23.7 us (28%)
  waiting for transfers between devices  20 us (24%)
  local copies, waits for them, and re-layouts  4.93 us (6%)
  other arithmetic  2.97 us (4%)
  between operations  0.96 us (1%)
    ppermute x20, waiting for transfers between devices, from_near(): return lax.ppermute(value, ('bond', 'mpo'), pairs)  13.8 us
    ppermute x20, starting transfers between devices, from_near(): return lax.ppermute(value, ('bond', 'mpo'), pairs)  13.7 us
    pallas_call x1, Pallas kernels, shards(): pl.pallas_call(functools.partial(first_kernel, plan), out_shape=(shape_of...  11 us
    ppermute x2, starting transfers between devices, exchange(): mine[r] = lax.ppermute(pair, ('bond', 'mpo'), pairs)  9.17 us
    pallas_call x1, Pallas kernels, shards(): pl.pallas_call(functools.partial(second_kernel, plan, float(count_all), l...  7.57 us
    ppermute x2, starting transfers between devices, handed_over(): result += [array, lax.ppermute(array, ('bond', 'mpo'), pairs)]  6.16 us
    pallas_call x1, Pallas kernels, shards(): pl.pallas_call(functools.partial(image_kernel, plan), out_shape=shape_of(...  5.16 us
    ppermute x1, waiting for transfers between devices, far_sums(): return [sums, lax.ppermute(sums, ('bond', 'mpo'), pairs)]  4.52 us
  transfers between devices with their start and end apart: 27, of which 13 were waited for; matrix products, arithmetic and copies ran while one was open for 5% of the time, Pallas kernels for 13%

profile of v7, /device:TPU:0, one launch (start us, length us, event | category | flops | bytes accessed | tf_op | source)
XLA Modules:
  0.0 84.1 jit_solution(2796440871744062348)
XLA Ops:
  0.6 3.0 %collective-permute-start.2 = (bf16[4,128,128]{2,1,0:T(8,128)(2,1)}, bf16[4,128,128]{2,1,0:T(8,128)(2,1)S(1)}, u32[]{:S(2)}, u32[]{:S(2)}) collective-permute-start(bf16[4,128,128]{2,1,0:T(8,128)(2,1)} %bitcast.117), channel_id=1, source_target_pairs={{2,0},{3,1},{0,2},{1,3},{6,4},{7,5},{4,6},{5,7},{10,8},{11,9},{8,1... | collective-permute-start | bytes 393224 | tf_op jit(solution)/shard_map/ppermute | solution.py:36
  3.6 3.5 %collective-permute-start = (bf16[4,128,128]{2,1,0:T(8,128)(2,1)}, bf16[4,128,128]{2,1,0:T(8,128)(2,1)S(1)}, u32[]{:S(2)}, u32[]{:S(2)}) collective-permute-start(bf16[4,128,128]{2,1,0:T(8,128)(2,1)} %bitcast.118), channel_id=1, source_target_pairs={{0,4},{1,5},{2,6},{3,7},{4,8},{5,9},{6,10},{7,11},{8,12},{9,13},{1... | collective-permute-start | bytes 393224 | tf_op jit(solution)/shard_map/ppermute | solution.py:36
  7.1 1.3 %collective-permute-start.1 = (bf16[4,128,128]{2,1,0:T(8,128)(2,1)}, bf16[4,128,128]{2,1,0:T(8,128)(2,1)S(1)}, u32[]{:S(2)}, u32[]{:S(2)}) collective-permute-start(bf16[4,128,128]{2,1,0:T(8,128)(2,1)} %bitcast.119), channel_id=1, source_target_pairs={{4,0},{5,1},{6,2},{7,3},{8,4},{9,5},{10,6},{11,7},{12,8},{13,9},{1... | collective-permute-start | bytes 393224 | tf_op jit(solution)/shard_map/ppermute | solution.py:36
  10.0 1.3 %collective-permute-start.4 = (bf16[20,1,128,128]{3,2,1,0:T(8,128)(2,1)}, bf16[20,1,128,128]{3,2,1,0:T(8,128)(2,1)S(1)}, u32[]{:S(2)}, u32[]{:S(2)}) collective-permute-start(bf16[20,1,128,128]{3,2,1,0:T(8,128)(2,1)} %refs_15_.1), channel_id=1, source_target_pairs={{4,0},{9,1},{6,2},{11,3},{8,4},{13,5},{10,6},{15,7},{12,8},{14,10}... | collective-permute-start | bytes 1966088 | tf_op jit(solution)/shard_map/ppermute | solution.py:131
  11.3 1.1 %maximum_bitcast_fusion = bf16[2,4,20,4,20]{2,3,1,4,0:T(4,128)(2,1)S(1)} fusion(bf16[1,20,20,4,4]{2,4,3,1,0:T(4,128)(2,1)} %bitcast.124, bf16[1,20,20,4,4]{2,4,3,1,0:T(4,128)(2,1)} %bitcast.125), kind=kLoop, calls=%fused_computation.4 | loop fusion | flops 12800 | bytes 51200 | tf_op jit(solution)/shard_map/transpose | solution.py:588
  12.3 1.6 %collective-permute-done.3.refs_10_ = bf16[5,64,128]{2,1,0:T(8,128)(2,1)S(1)} collective-permute-done((bf16[5,64,128]{2,1,0:T(8,128)(2,1)S(1)}, bf16[5,64,128]{2,1,0:T(8,128)(2,1)S(1)}, u32[]{:S(2)}, u32[]{:S(2)}) %collective-permute-start.3) | collective-permute-done | bytes 81952 | tf_op jit(solution)/shard_map/ppermute | solution.py:36
  13.9 1.3 %collective-permute-start.5 = (bf16[20,1,128,128]{3,2,1,0:T(8,128)(2,1)}, bf16[20,1,128,128]{3,2,1,0:T(8,128)(2,1)S(1)}, u32[]{:S(2)}, u32[]{:S(2)}) collective-permute-start(bf16[20,1,128,128]{3,2,1,0:T(8,128)(2,1)} %refs_15_.1), channel_id=1, source_target_pairs={{12,0},{14,2},{28,16},{30,18}} | collective-permute-start | bytes 1966088 | tf_op jit(solution)/shard_map/ppermute | solution.py:131
  17.6 1.2 %collective-permute-done.6 = bf16[4,128,128]{2,1,0:T(8,128)(2,1)S(1)} collective-permute-done((bf16[4,128,128]{2,1,0:T(8,128)(2,1)}, bf16[4,128,128]{2,1,0:T(8,128)(2,1)S(1)}, u32[]{:S(2)}, u32[]{:S(2)}) %collective-permute-start.6) | collective-permute-done | bytes 131104 | tf_op jit(solution)/shard_map/ppermute | solution.py:36
  18.9 4.0 %collective-permute-done.9.refs_6_ = bf16[2,4,128,128]{3,2,1,0:T(8,128)(2,1)S(1)} collective-permute-done((bf16[2,4,128,128]{3,2,1,0:T(8,128)(2,1)S(1)}, bf16[2,4,128,128]{3,2,1,0:T(8,128)(2,1)S(1)}, u32[]{:S(2)}, u32[]{:S(2)}) %collective-permute-start.9) | collective-permute-done | bytes 262176 | tf_op jit(solution)/shard_map/ppermute | solution.py:36
  23.4 1.1 %collective-permute-done.12.refs_11_ = bf16[5,64,128]{2,1,0:T(8,128)(2,1)S(1)} collective-permute-done((bf16[5,64,128]{2,1,0:T(8,128)(2,1)S(1)}, bf16[5,64,128]{2,1,0:T(8,128)(2,1)S(1)}, u32[]{:S(2)}, u32[]{:S(2)}) %collective-permute-start.12) | collective-permute-done | bytes 81952 | tf_op jit(solution)/shard_map/ppermute | solution.py:36
  26.6 11.0 %states_of_vector.1 = (f32[16,20,32,128]{3,2,1,0:T(8,128)}, bf16[16,384,128]{2,1,0:T(8,128)(2,1)}, bf16[768,384]{1,0:T(8,128)(2,1)}, bf16[80,96]{1,0:T(8,128)(2,1)S(1)}, bf16[160,160]{1,0:T(8,128)(2,1)S(1)}) custom-call(s32[28]{0:T(128)S(1)} %pad_add_fusion.refs_0_.sizes_ref, bf16[2,4,128,128]{3,2,1,0:T(8,128)(2,1)S(1)} %pad_maximum_fusion.2.refs_1_, ...), custom_call_target="tpu_custom_call" | custom-call | flops 1000 | tf_op jit(solution)/shard_map/states_of_vector/pallas_call | solution.py:615
  37.6 4.2 %collective-permute-start.13 = (bf16[20,1,128,128]{3,2,1,0:T(8,128)(2,1)S(1)}, bf16[20,1,128,128]{3,2,1,0:T(8,128)(2,1)S(1)}, u32[]{:S(2)}, u32[]{:S(2)}) collective-permute-start(bf16[20,1,128,128]{3,2,1,0:T(8,128)(2,1)S(1)} %collective-permute-done.4.refs_0_.refs_16_), channel_id=1, source_target_pairs={{0,1},{1,0},{2,3},{3,2},{4,5},{5,4},{6,7},{7,6},{8,9},{9,8},{10,11... | collective-permute-start | bytes 1966088 | tf_op jit(solution)/shard_map/ppermute | solution.py:145
  41.8 2.0 %collective-permute-start.14 = (bf16[20,1,128,128]{3,2,1,0:T(8,128)(2,1)S(1)}, bf16[20,1,128,128]{3,2,1,0:T(8,128)(2,1)S(1)}, u32[]{:S(2)}, u32[]{:S(2)}) collective-permute-start(bf16[20,1,128,128]{3,2,1,0:T(8,128)(2,1)S(1)} %collective-permute-done.5.refs_2_.refs_18_), channel_id=1, source_target_pairs={{0,1},{2,3},{4,5},{6,7},{8,9},{10,11},{12,13},{14,15},{16,17},{18,... | collective-permute-start | bytes 1966088 | tf_op jit(solution)/shard_map/ppermute | solution.py:145
  43.8 1.6 %collective-permute-done.14.refs_3_.refs_19_ = bf16[20,1,128,128]{3,2,1,0:T(8,128)(2,1)S(1)} collective-permute-done((bf16[20,1,128,128]{3,2,1,0:T(8,128)(2,1)S(1)}, bf16[20,1,128,128]{3,2,1,0:T(8,128)(2,1)S(1)}, u32[]{:S(2)}, u32[]{:S(2)}) %collective-permute-start.14) | collective-permute-done | bytes 655392 | tf_op jit(solution)/shard_map/ppermute | solution.py:145
  46.4 1.1 %copy-done = bf16[20,1,128,128]{3,2,1,0:T(8,128)(2,1)S(1)} copy-done((bf16[20,1,128,128]{3,2,1,0:T(8,128)(2,1)S(1)}, bf16[20,1,128,128]{3,2,1,0:T(8,128)(2,1)}, u32[]{:S(2)}) %copy-start) | copy-done | bytes 655384
  47.5 5.2 %image_rows.1 = bf16[17,32,128]{2,1,0:T(8,128)(2,1)S(1)} custom-call(s32[28]{0:T(128)S(1)} %pad_add_fusion.refs_0_.sizes_ref, f32[16,640,128]{2,1,0:T(8,128)} %bitcast.126, bf16[16,384,128]{2,1,0:T(8,128)(2,1)} %get-tuple-element.40.vector_ref.refs_11_, bf16[20,1,128,128]{3,2,1,0:T(8,128)(2,1)S(1)} %copy-done, ...), custom_call_target="tpu_custom_call" | custom-call | flops 4000000000 | tf_op jit(solution)/shard_map/image_rows/pallas_call | solution.py:646
  54.2 4.5 %collective-permute-start.19 = (bf16[2,17,32,128]{3,2,1,0:T(8,128)(2,1)S(1)}, bf16[2,17,32,128]{3,2,1,0:T(8,128)(2,1)S(1)}, u32[]{:S(2)}, u32[]{:S(2)}) collective-permute-start(bf16[2,17,32,128]{3,2,1,0:T(8,128)(2,1)S(1)} %pad_maximum_fusion.1.refs_4_), channel_id=1, source_target_pairs={{0,4},{2,6},{4,8},{5,1},{6,10},{7,3},{8,12},{9,5},{10,14},{11,7},{... | collective-permute-start | bytes 835592 | tf_op jit(solution)/shard_map/ppermute | solution.py:61
  58.9 1.3 %collective-permute-done.16.refs_6_ = bf16[17,32,128]{2,1,0:T(8,128)(2,1)S(1)} collective-permute-done((bf16[17,32,128]{2,1,0:T(8,128)(2,1)S(1)}, bf16[17,32,128]{2,1,0:T(8,128)(2,1)S(1)}, u32[]{:S(2)}, u32[]{:S(2)}) %collective-permute-start.16) | collective-permute-done | bytes 139296 | tf_op jit(solution)/shard_map/ppermute | solution.py:36
  60.2 4.7 %collective-permute-start.17 = (bf16[2,17,32,128]{3,2,1,0:T(8,128)(2,1)S(1)}, bf16[2,17,32,128]{3,2,1,0:T(8,128)(2,1)S(1)}, u32[]{:S(2)}, u32[]{:S(2)}) collective-permute-start(bf16[2,17,32,128]{3,2,1,0:T(8,128)(2,1)S(1)} %pad_maximum_fusion), channel_id=1, source_target_pairs={{0,4},{2,6},{4,8},{5,1},{6,10},{7,3},{8,12},{9,5},{10,14},{11,7},{... | collective-permute-start | bytes 835592 | tf_op jit(solution)/shard_map/ppermute | solution.py:61
  65.2 4.5 %collective-permute-done.20.refs_2_ = f32[8,128]{1,0:T(8,128)S(1)} collective-permute-done((f32[8,128]{1,0:T(8,128)S(1)}, f32[8,128]{1,0:T(8,128)S(1)}, u32[]{:S(2)}, u32[]{:S(2)}) %collective-permute-start.20) | collective-permute-done | bytes 4128 | tf_op jit(solution)/shard_map/ppermute | solution.py:180
  70.2 1.1 %collective-permute-done.21.refs_3_ = f32[8,128]{1,0:T(8,128)S(1)} collective-permute-done((f32[8,128]{1,0:T(8,128)S(1)}, f32[8,128]{1,0:T(8,128)S(1)}, u32[]{:S(2)}, u32[]{:S(2)}) %collective-permute-start.21) | collective-permute-done | bytes 4128 | tf_op jit(solution)/shard_map/ppermute | solution.py:36
  71.3 7.6 %correction_image_rows.1 = (bf16[4,32,128]{2,1,0:T(8,128)(2,1)S(1)}, bf16[4,32,128]{2,1,0:T(8,128)(2,1)S(1)}, bf16[4,32,128]{2,1,0:T(8,128)(2,1)S(1)}, bf16[4,32...) custom-call(s32[28]{0:T(128)S(1)} %pad_add_fusion.refs_0_.sizes_ref, f32[8,128]{1,0:T(8,128)S(1)} %maximum_maximum_fusion.refs_1_, ...), custom_call_target="tpu_custom_call" | custom-call | flops 1000 | tf_op jit(solution)/shard_map/correction_image_rows/pallas_call | solution.py:676
  79.1 1.0 %collective-permute-start.25 = (bf16[4,32,128]{2,1,0:T(8,128)(2,1)S(1)}, bf16[4,32,128]{2,1,0:T(8,128)(2,1)S(1)}, u32[]{:S(2)}, u32[]{:S(2)}) collective-permute-start(bf16[4,32,128]{2,1,0:T(8,128)(2,1)S(1)} %get-tuple-element.56), channel_id=1, source_target_pairs={{2,0},{3,1},{0,2},{1,3},{6,4},{7,5},{4,6},{5,7},{10,8},{11,9},{8,1... | collective-permute-start | bytes 98312 | tf_op jit(solution)/shard_map/ppermute | solution.py:36
  80.9 2.1 %collective-permute-done.25 = bf16[4,32,128]{2,1,0:T(8,128)(2,1)S(1)} collective-permute-done((bf16[4,32,128]{2,1,0:T(8,128)(2,1)S(1)}, bf16[4,32,128]{2,1,0:T(8,128)(2,1)S(1)}, u32[]{:S(2)}, u32[]{:S(2)}) %collective-permute-start.25) | collective-permute-done | bytes 32800 | tf_op jit(solution)/shard_map/ppermute | solution.py:36
  (71 shorter events, 12.2 us)
Async XLA Ops:
  0.6 15.8 %collective-permute-start.2 = (bf16[4,128,128]{2,1,0:T(8,128)(2,1)}, bf16[4,128,128]{2,1,0:T(8,128)(2,1)S(1)}, u32[]{:S(2)}, u32[]{:S(2)}) collective-permute-start(bf16[4,128,128]{2,1,0:T(8,128)(2,1)} %bitcast.117), channel_id=1, source_target_pairs={{2,0},{3,1},{0,2},{1,3},{6,4},{7,5},{4,6},{5,7},{10,8},{11,9},{8,1... | collective-permute-start | bytes 393224 | tf_op jit(solution)/shard_map/ppermute | solution.py:36
  3.6 12.8 %collective-permute-start = (bf16[4,128,128]{2,1,0:T(8,128)(2,1)}, bf16[4,128,128]{2,1,0:T(8,128)(2,1)S(1)}, u32[]{:S(2)}, u32[]{:S(2)}) collective-permute-start(bf16[4,128,128]{2,1,0:T(8,128)(2,1)} %bitcast.118), channel_id=1, source_target_pairs={{0,4},{1,5},{2,6},{3,7},{4,8},{5,9},{6,10},{7,11},{8,12},{9,13},{1... | collective-permute-start | bytes 393224 | tf_op jit(solution)/shard_map/ppermute | solution.py:36
  7.1 9.3 %collective-permute-start.1 = (bf16[4,128,128]{2,1,0:T(8,128)(2,1)}, bf16[4,128,128]{2,1,0:T(8,128)(2,1)S(1)}, u32[]{:S(2)}, u32[]{:S(2)}) collective-permute-start(bf16[4,128,128]{2,1,0:T(8,128)(2,1)} %bitcast.119), channel_id=1, source_target_pairs={{4,0},{5,1},{6,2},{7,3},{8,4},{9,5},{10,6},{11,7},{12,8},{13,9},{1... | collective-permute-start | bytes 393224 | tf_op jit(solution)/shard_map/ppermute | solution.py:36
  9.4 4.5 %collective-permute-start.3 = (bf16[5,64,128]{2,1,0:T(8,128)(2,1)S(1)}, bf16[5,64,128]{2,1,0:T(8,128)(2,1)S(1)}, u32[]{:S(2)}, u32[]{:S(2)}) collective-permute-start(bf16[5,64,128]{2,1,0:T(8,128)(2,1)S(1)} %get-tuple-element.61), channel_id=1, source_target_pairs={{2,0},{3,1},{0,2},{1,3},{6,4},{7,5},{4,6},{5,7},{10,8},{11,9},{8,1... | collective-permute-start | bytes 245768 | tf_op jit(solution)/shard_map/ppermute | solution.py:36
  10.0 27.6 %collective-permute-start.4 = (bf16[20,1,128,128]{3,2,1,0:T(8,128)(2,1)}, bf16[20,1,128,128]{3,2,1,0:T(8,128)(2,1)S(1)}, u32[]{:S(2)}, u32[]{:S(2)}) collective-permute-start(bf16[20,1,128,128]{3,2,1,0:T(8,128)(2,1)} %refs_15_.1), channel_id=1, source_target_pairs={{4,0},{9,1},{6,2},{11,3},{8,4},{13,5},{10,6},{15,7},{12,8},{14,10}... | collective-permute-start | bytes 1966088 | tf_op jit(solution)/shard_map/ppermute | solution.py:131
  13.9 23.7 %collective-permute-start.5 = (bf16[20,1,128,128]{3,2,1,0:T(8,128)(2,1)}, bf16[20,1,128,128]{3,2,1,0:T(8,128)(2,1)S(1)}, u32[]{:S(2)}, u32[]{:S(2)}) collective-permute-start(bf16[20,1,128,128]{3,2,1,0:T(8,128)(2,1)} %refs_15_.1), channel_id=1, source_target_pairs={{12,0},{14,2},{28,16},{30,18}} | collective-permute-start | bytes 1966088 | tf_op jit(solution)/shard_map/ppermute | solution.py:131
  16.5 6.4 %collective-permute-start.9 = (bf16[2,4,128,128]{3,2,1,0:T(8,128)(2,1)S(1)}, bf16[2,4,128,128]{3,2,1,0:T(8,128)(2,1)S(1)}, u32[]{:S(2)}, u32[]{:S(2)}) collective-permute-start(bf16[2,4,128,128]{3,2,1,0:T(8,128)(2,1)S(1)} %pad_maximum_fusion.3.refs_4_), channel_id=1, source_target_pairs={{2,0},{3,1},{0,2},{1,3},{6,4},{7,5},{4,6},{5,7},{10,8},{11,9},{8,1... | collective-permute-start | bytes 786440 | tf_op jit(solution)/shard_map/ppermute | solution.py:36
  17.1 1.7 %collective-permute-start.6 = (bf16[4,128,128]{2,1,0:T(8,128)(2,1)}, bf16[4,128,128]{2,1,0:T(8,128)(2,1)S(1)}, u32[]{:S(2)}, u32[]{:S(2)}) collective-permute-start(bf16[4,128,128]{2,1,0:T(8,128)(2,1)} %bitcast.120), channel_id=1, source_target_pairs={{1,0},{0,1},{3,2},{2,3},{5,4},{4,5},{7,6},{6,7},{9,8},{8,9},{11,10... | collective-permute-start | bytes 393224 | tf_op jit(solution)/shard_map/ppermute | solution.py:36
  17.1 5.8 %collective-permute-start.11 = (bf16[5,64,128]{2,1,0:T(8,128)(2,1)S(1)}, bf16[5,64,128]{2,1,0:T(8,128)(2,1)S(1)}, u32[]{:S(2)}, u32[]{:S(2)}) collective-permute-start(bf16[5,64,128]{2,1,0:T(8,128)(2,1)S(1)} %get-tuple-element.35.refs_8_), channel_id=1, source_target_pairs={{1,0},{0,1},{3,2},{2,3},{5,4},{4,5},{7,6},{6,7},{9,8},{8,9},{11,10... | collective-permute-start | bytes 245768 | tf_op jit(solution)/shard_map/ppermute | solution.py:36
  18.8 7.2 %collective-permute-start.8 = (bf16[2,4,128,128]{3,2,1,0:T(8,128)(2,1)S(1)}, bf16[2,4,128,128]{3,2,1,0:T(8,128)(2,1)S(1)}, u32[]{:S(2)}, u32[]{:S(2)}) collective-permute-start(bf16[2,4,128,128]{3,2,1,0:T(8,128)(2,1)S(1)} %pad_maximum_fusion.3.refs_4_), channel_id=1, source_target_pairs={{1,0},{0,1},{3,2},{2,3},{5,4},{4,5},{7,6},{6,7},{9,8},{8,9},{11,10... | collective-permute-start | bytes 786440 | tf_op jit(solution)/shard_map/ppermute | solution.py:36
  22.9 3.0 %collective-permute-start.10 = (bf16[2,4,128,128]{3,2,1,0:T(8,128)(2,1)S(1)}, bf16[2,4,128,128]{3,2,1,0:T(8,128)(2,1)S(1)}, u32[]{:S(2)}, u32[]{:S(2)}) collective-permute-start(bf16[2,4,128,128]{3,2,1,0:T(8,128)(2,1)S(1)} %collective-permute-done.9.refs_6_), channel_id=1, source_target_pairs={{1,0},{0,1},{3,2},{2,3},{5,4},{4,5},{7,6},{6,7},{9,8},{8,9},{11,10... | collective-permute-start | bytes 786440 | tf_op jit(solution)/shard_map/ppermute | solution.py:36
  22.9 1.6 %collective-permute-start.12 = (bf16[5,64,128]{2,1,0:T(8,128)(2,1)S(1)}, bf16[5,64,128]{2,1,0:T(8,128)(2,1)S(1)}, u32[]{:S(2)}, u32[]{:S(2)}) collective-permute-start(bf16[5,64,128]{2,1,0:T(8,128)(2,1)S(1)} %collective-permute-done.3.refs_10_), channel_id=1, source_target_pairs={{1,0},{0,1},{3,2},{2,3},{5,4},{4,5},{7,6},{6,7},{9,8},{8,9},{11,10... | collective-permute-start | bytes 245768 | tf_op jit(solution)/shard_map/ppermute | solution.py:36
  37.6 6.2 %collective-permute-start.13 = (bf16[20,1,128,128]{3,2,1,0:T(8,128)(2,1)S(1)}, bf16[20,1,128,128]{3,2,1,0:T(8,128)(2,1)S(1)}, u32[]{:S(2)}, u32[]{:S(2)}) collective-permute-start(bf16[20,1,128,128]{3,2,1,0:T(8,128)(2,1)S(1)} %collective-permute-done.4.refs_0_.refs_16_), channel_id=1, source_target_pairs={{0,1},{1,0},{2,3},{3,2},{4,5},{5,4},{6,7},{7,6},{8,9},{9,8},{10,11... | collective-permute-start | bytes 1966088 | tf_op jit(solution)/shard_map/ppermute | solution.py:145
  41.8 3.6 %collective-permute-start.14 = (bf16[20,1,128,128]{3,2,1,0:T(8,128)(2,1)S(1)}, bf16[20,1,128,128]{3,2,1,0:T(8,128)(2,1)S(1)}, u32[]{:S(2)}, u32[]{:S(2)}) collective-permute-start(bf16[20,1,128,128]{3,2,1,0:T(8,128)(2,1)S(1)} %collective-permute-done.5.refs_2_.refs_18_), channel_id=1, source_target_pairs={{0,1},{2,3},{4,5},{6,7},{8,9},{10,11},{12,13},{14,15},{16,17},{18,... | collective-permute-start | bytes 1966088 | tf_op jit(solution)/shard_map/ppermute | solution.py:145
  53.1 5.7 %collective-permute-start.15 = (bf16[17,32,128]{2,1,0:T(8,128)(2,1)S(1)}, bf16[17,32,128]{2,1,0:T(8,128)(2,1)S(1)}, u32[]{:S(2)}, u32[]{:S(2)}) collective-permute-start(bf16[17,32,128]{2,1,0:T(8,128)(2,1)S(1)} %image_rows.1), channel_id=1, source_target_pairs={{2,0},{3,1},{0,2},{1,3},{6,4},{7,5},{4,6},{5,7},{10,8},{11,9},{8,1... | collective-permute-start | bytes 417800 | tf_op jit(solution)/shard_map/ppermute | solution.py:36
  54.2 10.8 %collective-permute-start.19 = (bf16[2,17,32,128]{3,2,1,0:T(8,128)(2,1)S(1)}, bf16[2,17,32,128]{3,2,1,0:T(8,128)(2,1)S(1)}, u32[]{:S(2)}, u32[]{:S(2)}) collective-permute-start(bf16[2,17,32,128]{3,2,1,0:T(8,128)(2,1)S(1)} %pad_maximum_fusion.1.refs_4_), channel_id=1, source_target_pairs={{0,4},{2,6},{4,8},{5,1},{6,10},{7,3},{8,12},{9,5},{10,14},{11,7},{... | collective-permute-start | bytes 835592 | tf_op jit(solution)/shard_map/ppermute | solution.py:61
  60.2 9.5 %collective-permute-start.17 = (bf16[2,17,32,128]{3,2,1,0:T(8,128)(2,1)S(1)}, bf16[2,17,32,128]{3,2,1,0:T(8,128)(2,1)S(1)}, u32[]{:S(2)}, u32[]{:S(2)}) collective-permute-start(bf16[2,17,32,128]{3,2,1,0:T(8,128)(2,1)S(1)} %pad_maximum_fusion), channel_id=1, source_target_pairs={{0,4},{2,6},{4,8},{5,1},{6,10},{7,3},{8,12},{9,5},{10,14},{11,7},{... | collective-permute-start | bytes 835592 | tf_op jit(solution)/shard_map/ppermute | solution.py:61
  65.1 4.6 %collective-permute-start.20 = (f32[8,128]{1,0:T(8,128)S(1)}, f32[8,128]{1,0:T(8,128)S(1)}, u32[]{:S(2)}, u32[]{:S(2)}) collective-permute-start(f32[8,128]{1,0:T(8,128)S(1)} %maximum_maximum_fusion.refs_1_), channel_id=1, source_target_pairs={{8,0},{13,1},{10,2},{15,3},{12,4},{9,5},{14,6},{11,7},{0,8},{5,9},... | collective-permute-start | bytes 12296 | tf_op jit(solution)/shard_map/ppermute | solution.py:180
  65.1 6.2 %collective-permute-start.22 = (bf16[2,17,32,128]{3,2,1,0:T(8,128)(2,1)S(1)}, bf16[2,17,32,128]{3,2,1,0:T(8,128)(2,1)S(1)}, u32[]{:S(2)}, u32[]{:S(2)}) collective-permute-start(bf16[2,17,32,128]{3,2,1,0:T(8,128)(2,1)S(1)} %collective-permute-done.19.refs_7_), channel_id=1, source_target_pairs={{1,0},{0,1},{3,2},{2,3},{5,4},{4,5},{7,6},{6,7},{9,8},{8,9},{11,10... | collective-permute-start | bytes 835592 | tf_op jit(solution)/shard_map/ppermute | solution.py:36
  69.7 1.6 %collective-permute-start.23 = (bf16[2,17,32,128]{3,2,1,0:T(8,128)(2,1)S(1)}, bf16[2,17,32,128]{3,2,1,0:T(8,128)(2,1)S(1)}, u32[]{:S(2)}, u32[]{:S(2)}) collective-permute-start(bf16[2,17,32,128]{3,2,1,0:T(8,128)(2,1)S(1)} %collective-permute-done.17.refs_8_), channel_id=1, source_target_pairs={{1,0},{0,1},{3,2},{2,3},{5,4},{4,5},{7,6},{6,7},{9,8},{8,9},{11,10... | collective-permute-start | bytes 835592 | tf_op jit(solution)/shard_map/ppermute | solution.py:36
  69.7 1.6 %collective-permute-start.21 = (f32[8,128]{1,0:T(8,128)S(1)}, f32[8,128]{1,0:T(8,128)S(1)}, u32[]{:S(2)}, u32[]{:S(2)}) collective-permute-start(f32[8,128]{1,0:T(8,128)S(1)} %collective-permute-done.20.refs_2_), channel_id=1, source_target_pairs={{1,0},{0,1},{3,2},{2,3},{5,4},{4,5},{7,6},{6,7},{9,8},{8,9},{11,10... | collective-permute-start | bytes 12296 | tf_op jit(solution)/shard_map/ppermute | solution.py:36
  78.9 2.0 %collective-permute-start.24 = (bf16[4,32,128]{2,1,0:T(8,128)(2,1)S(1)}, bf16[4,32,128]{2,1,0:T(8,128)(2,1)S(1)}, u32[]{:S(2)}, u32[]{:S(2)}) collective-permute-start(bf16[4,32,128]{2,1,0:T(8,128)(2,1)S(1)} %get-tuple-element.55), channel_id=1, source_target_pairs={{1,0},{0,1},{3,2},{2,3},{5,4},{4,5},{7,6},{6,7},{9,8},{8,9},{11,10... | collective-permute-start | bytes 98312 | tf_op jit(solution)/shard_map/ppermute | solution.py:36
  79.1 3.9 %collective-permute-start.25 = (bf16[4,32,128]{2,1,0:T(8,128)(2,1)S(1)}, bf16[4,32,128]{2,1,0:T(8,128)(2,1)S(1)}, u32[]{:S(2)}, u32[]{:S(2)}) collective-permute-start(bf16[4,32,128]{2,1,0:T(8,128)(2,1)S(1)} %get-tuple-element.56), channel_id=1, source_target_pairs={{2,0},{3,1},{0,2},{1,3},{6,4},{7,5},{4,6},{5,7},{10,8},{11,9},{8,1... | collective-permute-start | bytes 98312 | tf_op jit(solution)/shard_map/ppermute | solution.py:36
  80.1 3.4 %collective-permute-start.26 = (bf16[4,32,128]{2,1,0:T(8,128)(2,1)S(1)}, bf16[4,32,128]{2,1,0:T(8,128)(2,1)S(1)}, u32[]{:S(2)}, u32[]{:S(2)}) collective-permute-start(bf16[4,32,128]{2,1,0:T(8,128)(2,1)S(1)} %get-tuple-element.57), channel_id=1, source_target_pairs={{3,0},{2,1},{1,2},{0,3},{7,4},{6,5},{5,6},{4,7},{11,8},{10,9},{9,1... | collective-permute-start | bytes 98312 | tf_op jit(solution)/shard_map/ppermute | solution.py:36
  (10 other events, 32.1 us)

commit v8 on v7

--- a/solution.py
+++ b/solution.py
@@ -120,30 +120,20 @@
 
 def right_exchange(own, far):
     n_bond, n_mpo = lax.axis_size("bond"), lax.axis_size("mpo")
-    arrays = []
-    for first in range(1, far + 1, 2):
-        pairs = [
-            ((i + first + j % 2) * n_mpo + j, i * n_mpo + j)
-            for i in range(n_bond)
-            for j in range(n_mpo)
-            if first + j % 2 <= far and i + first + j % 2 < n_bond
-        ]
-        arrays.append(lax.ppermute(own, ("bond", "mpo"), pairs))
-    return arrays
-
-
-def handed_over(arrays, far):
-    n_bond, n_mpo = lax.axis_size("bond"), lax.axis_size("mpo")
-    result = []
-    for place, array in enumerate(arrays):
-        pairs = [
-            (i * n_mpo + j, i * n_mpo + (j ^ 1))
-            for i in range(n_bond)
-            for j in range(n_mpo)
-            if 1 + 2 * place + j % 2 <= far
-        ]
-        result += [array, lax.ppermute(array, ("bond", "mpo"), pairs)]
-    return result
+    pairs = [
+        ((i + 1 + j % 2) * n_mpo + j, i * n_mpo + j)
+        for i in range(n_bond)
+        for j in range(n_mpo)
+        if 1 + j % 2 <= far and i + 1 + j % 2 < n_bond
+    ]
+    arrays = [lax.ppermute(own, ("bond", "mpo"), pairs)]
+    half = own.shape[0] // 2
+    part = lax.dynamic_slice_in_dim(own, lax.rem(lax.axis_index("mpo"), 2) * half, half, 0)
+    return arrays + [from_near(part, d, 0) for d in range(3, far + 1)]
+
+
+def handed_over(arrays):
+    return [piece for array in arrays for piece in (array, from_near(array, 0, 1))]
 
 
 def merged(parts):
@@ -211,7 +201,8 @@
         self.y_step = self.rows + 8
         self.far = min(RIM, n_bond - 1)
         self.n_near = 2 * n_mpo - 1
-        self.n_far = 2 * ((self.far + 1) // 2)
+        self.slots = max(3, self.far + 1)
+        self.n_far = 2 * max(1, self.far - 1)
 
 
 def fill_left(plan, sizes_ref, left_refs, wide, ls):
@@ -370,9 +361,9 @@
 
 
 class RightCopy:
-    def __init__(self, plan, source, right_near, slot, sem):
-        self.copy = pltpu.make_async_copy(source.at[:, 0], right_near.at[slot], sem)
-        self.there = None if isinstance(slot, int) else slot <= plan.far
+    def __init__(self, plan, source, target, sem, slot=None):
+        self.copy = pltpu.make_async_copy(source.at[:, 0], target, sem)
+        self.there = None if slot is None else slot <= plan.far
 
     def start(self):
         self.do(self.copy.start)
@@ -389,12 +380,17 @@
 
 def right_copies(plan, own_ref, far_refs, right_near, sems):
     odd = lax.rem(lax.axis_index("mpo"), 2)
+    half = plan.w // 2
     copies = [[] for _ in range(plan.far + 1)]
-    copies[0].append(RightCopy(plan, own_ref, right_near, 0, sems.at[0]))
+    copies[0].append(RightCopy(plan, own_ref, right_near.at[0], sems.at[0]))
     for place, source in enumerate(far_refs):
-        first, other = 1 + 2 * (place // 2), place % 2
-        slot = first + (1 - odd if other else odd)
-        copies[first].append(RightCopy(plan, source, right_near, slot, sems.at[1 + place]))
+        side = 1 - odd if place % 2 else odd
+        sem = sems.at[1 + place]
+        if place < 2:
+            copies[1].append(RightCopy(plan, source, right_near.at[1 + side], sem, 1 + side))
+        else:
+            n = 2 + place // 2
+            copies[n].append(RightCopy(plan, source, right_near.at[n, pl.ds(side * half, half)], sem))
     return copies
 
 
@@ -640,8 +636,8 @@
     )
 
     right_far, ys = lax.optimization_barrier((right_far, ys))
-    right_pieces = handed_over(right_far, plan.far)
-    right_scratch = pltpu.VMEM((plan.n_far + 1, plan.w, width, width), BF16)
+    right_pieces = handed_over(right_far)
+    right_scratch = pltpu.VMEM((plan.slots, plan.w, width, width), BF16)
     image_shape = (PAIRS + 1,) + row_shape[1:]
     image_rows = pl.pallas_call(
         functools.partial(image_kernel, plan),

time: 84.6 us -> 83.2 us (0.983)
  starting transfers between devices: 31.6 us -> 30 us
  local copies, waits for them, and re-layouts: 4.93 us -> 5.92 us
    ppermute x4 -> x1, starting transfers between devices: 8.72 us -> 1.28 us  [right_exchange(): arrays = [lax.ppermute(own, ('bond', 'mpo'), pairs)]]
    ppermute x20 -> x23, starting transfers between devices: 13.7 us -> 19.7 us  [from_near(): return lax.ppermute(value, ('bond', 'mpo'), pairs)]
    ppermute x4 -> x1, waiting for transfers between devices: 1.65 us -> 0.01 us  [right_exchange(): arrays = [lax.ppermute(own, ('bond', 'mpo'), pairs)]]
    dynamic_slice x0 -> x1, local copies, waits for them, and re-layouts: none -> 0.99 us  [right_exchange(): lax.dynamic_slice_in_dim(own, lax.rem(lax.axis_index('mpo'), 2) * half, h...]
    ppermute x20 -> x23, waiting for transfers between devices: 13.8 us -> 14.7 us  [from_near(): return lax.ppermute(value, ('bond', 'mpo'), pairs)]
  transfers between devices with their start and end apart: 27 -> 27, of which waited for: 13 -> 14; matrix products, arithmetic and copies ran while one was open for 5% -> 7% of each run, Pallas kernels for 13% -> 13%
where the time goes in v8:
time: 83.2 us; the launch traced here: 82.7 us
  starting transfers between devices  30 us (36%)
  Pallas kernels  23.8 us (29%)
  waiting for transfers between devices  19.2 us (23%)
  local copies, waits for them, and re-layouts  5.92 us (7%)
  other arithmetic  2.97 us (4%)
  between operations  0.89 us (1%)
    ppermute x23, starting transfers between devices, from_near(): return lax.ppermute(value, ('bond', 'mpo'), pairs)  19.7 us
    ppermute x23, waiting for transfers between devices, from_near(): return lax.ppermute(value, ('bond', 'mpo'), pairs)  14.7 us
    pallas_call x1, Pallas kernels, shards(): pl.pallas_call(functools.partial(first_kernel, plan), out_shape=(shape_of...  11 us
    ppermute x2, starting transfers between devices, exchange(): mine[r] = lax.ppermute(pair, ('bond', 'mpo'), pairs)  8.93 us
    pallas_call x1, Pallas kernels, shards(): pl.pallas_call(functools.partial(second_kernel, plan, float(count_all), l...  7.57 us
    pallas_call x1, Pallas kernels, shards(): pl.pallas_call(functools.partial(image_kernel, plan), out_shape=shape_of(...  5.25 us
    ppermute x1, waiting for transfers between devices, far_sums(): return [sums, lax.ppermute(sums, ('bond', 'mpo'), pairs)]  4.48 us
    unnamed x14, local copies, waits for them, and re-layouts  3.36 us
  transfers between devices with their start and end apart: 27, of which 14 were waited for; matrix products, arithmetic and copies ran while one was open for 7% of the time, Pallas kernels for 13%

profile of v8, /device:TPU:0, one launch (start us, length us, event | category | flops | bytes accessed | tf_op | source)
XLA Modules:
  0.0 82.7 jit_solution(904277520356509348)
XLA Ops:
  0.6 3.0 %collective-permute-start.2 = (bf16[4,128,128]{2,1,0:T(8,128)(2,1)}, bf16[4,128,128]{2,1,0:T(8,128)(2,1)S(1)}, u32[]{:S(2)}, u32[]{:S(2)}) collective-permute-start(bf16[4,128,128]{2,1,0:T(8,128)(2,1)} %bitcast.117), channel_id=1, source_target_pairs={{2,0},{3,1},{0,2},{1,3},{6,4},{7,5},{4,6},{5,7},{10,8},{11,9},{8,1... | collective-permute-start | bytes 393224 | tf_op jit(solution)/shard_map/ppermute | solution.py:36
  3.6 3.5 %collective-permute-start = (bf16[4,128,128]{2,1,0:T(8,128)(2,1)}, bf16[4,128,128]{2,1,0:T(8,128)(2,1)S(1)}, u32[]{:S(2)}, u32[]{:S(2)}) collective-permute-start(bf16[4,128,128]{2,1,0:T(8,128)(2,1)} %bitcast.118), channel_id=1, source_target_pairs={{0,4},{1,5},{2,6},{3,7},{4,8},{5,9},{6,10},{7,11},{8,12},{9,13},{1... | collective-permute-start | bytes 393224 | tf_op jit(solution)/shard_map/ppermute | solution.py:36
  7.1 1.3 %collective-permute-start.1 = (bf16[4,128,128]{2,1,0:T(8,128)(2,1)}, bf16[4,128,128]{2,1,0:T(8,128)(2,1)S(1)}, u32[]{:S(2)}, u32[]{:S(2)}) collective-permute-start(bf16[4,128,128]{2,1,0:T(8,128)(2,1)} %bitcast.119), channel_id=1, source_target_pairs={{4,0},{5,1},{6,2},{7,3},{8,4},{9,5},{10,6},{11,7},{12,8},{13,9},{1... | collective-permute-start | bytes 393224 | tf_op jit(solution)/shard_map/ppermute | solution.py:36
  10.0 1.3 %collective-permute-start.4 = (bf16[20,1,128,128]{3,2,1,0:T(8,128)(2,1)}, bf16[20,1,128,128]{3,2,1,0:T(8,128)(2,1)S(1)}, u32[]{:S(2)}, u32[]{:S(2)}) collective-permute-start(bf16[20,1,128,128]{3,2,1,0:T(8,128)(2,1)} %refs_15_.1), channel_id=1, source_target_pairs={{4,0},{9,1},{6,2},{11,3},{8,4},{13,5},{10,6},{15,7},{12,8},{14,10}... | collective-permute-start | bytes 1966088 | tf_op jit(solution)/shard_map/ppermute | solution.py:129
  11.3 1.1 %maximum_bitcast_fusion = bf16[2,4,20,4,20]{2,3,1,4,0:T(4,128)(2,1)S(1)} fusion(bf16[1,20,20,4,4]{2,4,3,1,0:T(4,128)(2,1)} %bitcast.124, bf16[1,20,20,4,4]{2,4,3,1,0:T(4,128)(2,1)} %bitcast.125), kind=kLoop, calls=%fused_computation.4 | loop fusion | flops 12800 | bytes 51200 | tf_op jit(solution)/shard_map/transpose | solution.py:584
  14.2 1.0 %collective-permute-start.9 = (bf16[2,4,128,128]{3,2,1,0:T(8,128)(2,1)S(1)}, bf16[2,4,128,128]{3,2,1,0:T(8,128)(2,1)S(1)}, u32[]{:S(2)}, u32[]{:S(2)}) collective-permute-start(bf16[2,4,128,128]{3,2,1,0:T(8,128)(2,1)S(1)} %pad_maximum_fusion.3.refs_4_), channel_id=1, source_target_pairs={{2,0},{3,1},{0,2},{1,3},{6,4},{7,5},{4,6},{5,7},{10,8},{11,9},{8,1... | collective-permute-start | bytes 786440 | tf_op jit(solution)/shard_map/ppermute | solution.py:36
  15.2 1.0 %constant_dynamic-slice_fusion = bf16[10,1,128,128]{3,2,1,0:T(8,128)(2,1)S(1)} fusion(bf16[20,1,128,128]{3,2,1,0:T(8,128)(2,1)} %refs_15_.1, s32[]{:T(128)S(6)} %select_n.54), kind=kLoop, calls=%fused_computation.34 | loop fusion | bytes 655364 | tf_op jit(solution)/shard_map/dynamic_slice | solution.py:131
  16.2 1.3 %collective-permute-start.5 = (bf16[10,1,128,128]{3,2,1,0:T(8,128)(2,1)S(1)}, bf16[10,1,128,128]{3,2,1,0:T(8,128)(2,1)S(1)}, u32[]{:S(2)}, u32[]{:S(2)}) collective-permute-start(bf16[10,1,128,128]{3,2,1,0:T(8,128)(2,1)S(1)} %constant_dynamic-slice_fusion), channel_id=1, source_target_pairs={{12,0},{13,1},{14,2},{15,3},{28,16},{29,17},{30,18},{31,19}} | collective-permute-start | bytes 983048 | tf_op jit(solution)/shard_map/ppermute | solution.py:36
  18.2 2.8 %collective-permute-done.9.refs_6_ = bf16[2,4,128,128]{3,2,1,0:T(8,128)(2,1)S(1)} collective-permute-done((bf16[2,4,128,128]{3,2,1,0:T(8,128)(2,1)S(1)}, bf16[2,4,128,128]{3,2,1,0:T(8,128)(2,1)S(1)}, u32[]{:S(2)}, u32[]{:S(2)}) %collective-permute-start.9) | collective-permute-done | bytes 262176 | tf_op jit(solution)/shard_map/ppermute | solution.py:36
  21.5 1.1 %collective-permute-done.12.refs_11_ = bf16[5,64,128]{2,1,0:T(8,128)(2,1)S(1)} collective-permute-done((bf16[5,64,128]{2,1,0:T(8,128)(2,1)S(1)}, bf16[5,64,128]{2,1,0:T(8,128)(2,1)S(1)}, u32[]{:S(2)}, u32[]{:S(2)}) %collective-permute-start.12) | collective-permute-done | bytes 81952 | tf_op jit(solution)/shard_map/ppermute | solution.py:36
  24.6 11.0 %states_of_vector.1 = (f32[16,20,32,128]{3,2,1,0:T(8,128)}, bf16[16,384,128]{2,1,0:T(8,128)(2,1)}, bf16[768,384]{1,0:T(8,128)(2,1)}, bf16[80,96]{1,0:T(8,128)(2,1)S(1)}, bf16[160,160]{1,0:T(8,128)(2,1)S(1)}) custom-call(s32[28]{0:T(128)S(1)} %pad_add_fusion.refs_0_.sizes_ref, bf16[2,4,128,128]{3,2,1,0:T(8,128)(2,1)S(1)} %pad_maximum_fusion.2.refs_1_, ...), custom_call_target="tpu_custom_call" | custom-call | flops 1000 | tf_op jit(solution)/shard_map/states_of_vector/pallas_call | solution.py:611
  35.6 1.9 %collective-permute-done.5.refs_2_.refs_18_ = bf16[10,1,128,128]{3,2,1,0:T(8,128)(2,1)S(1)} collective-permute-done((bf16[10,1,128,128]{3,2,1,0:T(8,128)(2,1)S(1)}, bf16[10,1,128,128]{3,2,1,0:T(8,128)(2,1)S(1)}, u32[]{:S(2)}, u32[]{:S(2)}) %collective-permute-start.5) | collective-permute-done | bytes 327712 | tf_op jit(solution)/shard_map/ppermute | solution.py:36
  37.5 4.3 %collective-permute-start.13 = (bf16[20,1,128,128]{3,2,1,0:T(8,128)(2,1)S(1)}, bf16[20,1,128,128]{3,2,1,0:T(8,128)(2,1)S(1)}, u32[]{:S(2)}, u32[]{:S(2)}) collective-permute-start(bf16[20,1,128,128]{3,2,1,0:T(8,128)(2,1)S(1)} %collective-permute-done.4.refs_0_.refs_16_), channel_id=1, source_target_pairs={{1,0},{0,1},{3,2},{2,3},{5,4},{4,5},{7,6},{6,7},{9,8},{8,9},{11,10... | collective-permute-start | bytes 1966088 | tf_op jit(solution)/shard_map/ppermute | solution.py:36
  41.8 2.2 %collective-permute-done.14.refs_3_.refs_19_ = bf16[10,1,128,128]{3,2,1,0:T(8,128)(2,1)S(1)} collective-permute-done((bf16[10,1,128,128]{3,2,1,0:T(8,128)(2,1)S(1)}, bf16[10,1,128,128]{3,2,1,0:T(8,128)(2,1)S(1)}, u32[]{:S(2)}, u32[]{:S(2)}) %collective-permute-start.14) | collective-permute-done | bytes 327712 | tf_op jit(solution)/shard_map/ppermute | solution.py:36
  44.9 1.1 %copy-done = bf16[20,1,128,128]{3,2,1,0:T(8,128)(2,1)S(1)} copy-done((bf16[20,1,128,128]{3,2,1,0:T(8,128)(2,1)S(1)}, bf16[20,1,128,128]{3,2,1,0:T(8,128)(2,1)}, u32[]{:S(2)}) %copy-start) | copy-done | bytes 655384
  46.0 5.2 %image_rows.1 = bf16[17,32,128]{2,1,0:T(8,128)(2,1)S(1)} custom-call(s32[28]{0:T(128)S(1)} %pad_add_fusion.refs_0_.sizes_ref, f32[16,640,128]{2,1,0:T(8,128)} %bitcast.126, bf16[16,384,128]{2,1,0:T(8,128)(2,1)} %get-tuple-element.40.vector_ref.refs_11_, bf16[20,1,128,128]{3,2,1,0:T(8,128)(2,1)S(1)} %copy-done, bf16[20,1,128,128]{3,2,1,0:T(8,128)(2,1)} %copy-done.3, ...), custom_call_target="tpu_custom_call" | custom-call | flops 4000000000 | tf_op jit(solution)/shard_map/image_rows/pallas_call | solution.py:642
  52.7 4.4 %collective-permute-start.19 = (bf16[2,17,32,128]{3,2,1,0:T(8,128)(2,1)S(1)}, bf16[2,17,32,128]{3,2,1,0:T(8,128)(2,1)S(1)}, u32[]{:S(2)}, u32[]{:S(2)}) collective-permute-start(bf16[2,17,32,128]{3,2,1,0:T(8,128)(2,1)S(1)} %pad_maximum_fusion.1.refs_4_), channel_id=1, source_target_pairs={{0,4},{2,6},{4,8},{5,1},{6,10},{7,3},{8,12},{9,5},{10,14},{11,7},{... | collective-permute-start | bytes 835592 | tf_op jit(solution)/shard_map/ppermute | solution.py:61
  57.5 1.3 %collective-permute-done.16.refs_6_ = bf16[17,32,128]{2,1,0:T(8,128)(2,1)S(1)} collective-permute-done((bf16[17,32,128]{2,1,0:T(8,128)(2,1)S(1)}, bf16[17,32,128]{2,1,0:T(8,128)(2,1)S(1)}, u32[]{:S(2)}, u32[]{:S(2)}) %collective-permute-start.16) | collective-permute-done | bytes 139296 | tf_op jit(solution)/shard_map/ppermute | solution.py:36
  58.8 4.6 %collective-permute-start.17 = (bf16[2,17,32,128]{3,2,1,0:T(8,128)(2,1)S(1)}, bf16[2,17,32,128]{3,2,1,0:T(8,128)(2,1)S(1)}, u32[]{:S(2)}, u32[]{:S(2)}) collective-permute-start(bf16[2,17,32,128]{3,2,1,0:T(8,128)(2,1)S(1)} %pad_maximum_fusion), channel_id=1, source_target_pairs={{0,4},{2,6},{4,8},{5,1},{6,10},{7,3},{8,12},{9,5},{10,14},{11,7},{... | collective-permute-start | bytes 835592 | tf_op jit(solution)/shard_map/ppermute | solution.py:61
  63.7 4.5 %collective-permute-done.20.refs_2_ = f32[8,128]{1,0:T(8,128)S(1)} collective-permute-done((f32[8,128]{1,0:T(8,128)S(1)}, f32[8,128]{1,0:T(8,128)S(1)}, u32[]{:S(2)}, u32[]{:S(2)}) %collective-permute-start.20) | collective-permute-done | bytes 4128 | tf_op jit(solution)/shard_map/ppermute | solution.py:170
  68.7 1.1 %collective-permute-done.21.refs_3_ = f32[8,128]{1,0:T(8,128)S(1)} collective-permute-done((f32[8,128]{1,0:T(8,128)S(1)}, f32[8,128]{1,0:T(8,128)S(1)}, u32[]{:S(2)}, u32[]{:S(2)}) %collective-permute-start.21) | collective-permute-done | bytes 4128 | tf_op jit(solution)/shard_map/ppermute | solution.py:36
  69.8 7.6 %correction_image_rows.1 = (bf16[4,32,128]{2,1,0:T(8,128)(2,1)S(1)}, bf16[4,32,128]{2,1,0:T(8,128)(2,1)S(1)}, bf16[4,32,128]{2,1,0:T(8,128)(2,1)S(1)}, bf16[4,32...) custom-call(s32[28]{0:T(128)S(1)} %pad_add_fusion.refs_0_.sizes_ref, f32[8,128]{1,0:T(8,128)S(1)} %maximum_maximum_fusion.refs_1_, ...), custom_call_target="tpu_custom_call" | custom-call | flops 1000 | tf_op jit(solution)/shard_map/correction_image_rows/pallas_call | solution.py:672
  77.6 1.0 %collective-permute-start.25 = (bf16[4,32,128]{2,1,0:T(8,128)(2,1)S(1)}, bf16[4,32,128]{2,1,0:T(8,128)(2,1)S(1)}, u32[]{:S(2)}, u32[]{:S(2)}) collective-permute-start(bf16[4,32,128]{2,1,0:T(8,128)(2,1)S(1)} %get-tuple-element.56), channel_id=1, source_target_pairs={{2,0},{3,1},{0,2},{1,3},{6,4},{7,5},{4,6},{5,7},{10,8},{11,9},{8,1... | collective-permute-start | bytes 98312 | tf_op jit(solution)/shard_map/ppermute | solution.py:36
  79.3 2.1 %collective-permute-done.25 = bf16[4,32,128]{2,1,0:T(8,128)(2,1)S(1)} collective-permute-done((bf16[4,32,128]{2,1,0:T(8,128)(2,1)S(1)}, bf16[4,32,128]{2,1,0:T(8,128)(2,1)S(1)}, u32[]{:S(2)}, u32[]{:S(2)}) %collective-permute-start.25) | collective-permute-done | bytes 32800 | tf_op jit(solution)/shard_map/ppermute | solution.py:36
  (72 shorter events, 12.4 us)
Async XLA Ops:
  0.6 13.3 %collective-permute-start.2 = (bf16[4,128,128]{2,1,0:T(8,128)(2,1)}, bf16[4,128,128]{2,1,0:T(8,128)(2,1)S(1)}, u32[]{:S(2)}, u32[]{:S(2)}) collective-permute-start(bf16[4,128,128]{2,1,0:T(8,128)(2,1)} %bitcast.117), channel_id=1, source_target_pairs={{2,0},{3,1},{0,2},{1,3},{6,4},{7,5},{4,6},{5,7},{10,8},{11,9},{8,1... | collective-permute-start | bytes 393224 | tf_op jit(solution)/shard_map/ppermute | solution.py:36
  3.6 10.3 %collective-permute-start = (bf16[4,128,128]{2,1,0:T(8,128)(2,1)}, bf16[4,128,128]{2,1,0:T(8,128)(2,1)S(1)}, u32[]{:S(2)}, u32[]{:S(2)}) collective-permute-start(bf16[4,128,128]{2,1,0:T(8,128)(2,1)} %bitcast.118), channel_id=1, source_target_pairs={{0,4},{1,5},{2,6},{3,7},{4,8},{5,9},{6,10},{7,11},{8,12},{9,13},{1... | collective-permute-start | bytes 393224 | tf_op jit(solution)/shard_map/ppermute | solution.py:36
  7.1 7.1 %collective-permute-start.1 = (bf16[4,128,128]{2,1,0:T(8,128)(2,1)}, bf16[4,128,128]{2,1,0:T(8,128)(2,1)S(1)}, u32[]{:S(2)}, u32[]{:S(2)}) collective-permute-start(bf16[4,128,128]{2,1,0:T(8,128)(2,1)} %bitcast.119), channel_id=1, source_target_pairs={{4,0},{5,1},{6,2},{7,3},{8,4},{9,5},{10,6},{11,7},{12,8},{13,9},{1... | collective-permute-start | bytes 393224 | tf_op jit(solution)/shard_map/ppermute | solution.py:36
  9.4 4.5 %collective-permute-start.3 = (bf16[5,64,128]{2,1,0:T(8,128)(2,1)S(1)}, bf16[5,64,128]{2,1,0:T(8,128)(2,1)S(1)}, u32[]{:S(2)}, u32[]{:S(2)}) collective-permute-start(bf16[5,64,128]{2,1,0:T(8,128)(2,1)S(1)} %get-tuple-element.61), channel_id=1, source_target_pairs={{2,0},{3,1},{0,2},{1,3},{6,4},{7,5},{4,6},{5,7},{10,8},{11,9},{8,1... | collective-permute-start | bytes 245768 | tf_op jit(solution)/shard_map/ppermute | solution.py:36
  10.0 27.5 %collective-permute-start.4 = (bf16[20,1,128,128]{3,2,1,0:T(8,128)(2,1)}, bf16[20,1,128,128]{3,2,1,0:T(8,128)(2,1)S(1)}, u32[]{:S(2)}, u32[]{:S(2)}) collective-permute-start(bf16[20,1,128,128]{3,2,1,0:T(8,128)(2,1)} %refs_15_.1), channel_id=1, source_target_pairs={{4,0},{9,1},{6,2},{11,3},{8,4},{13,5},{10,6},{15,7},{12,8},{14,10}... | collective-permute-start | bytes 1966088 | tf_op jit(solution)/shard_map/ppermute | solution.py:129
  14.2 6.7 %collective-permute-start.9 = (bf16[2,4,128,128]{3,2,1,0:T(8,128)(2,1)S(1)}, bf16[2,4,128,128]{3,2,1,0:T(8,128)(2,1)S(1)}, u32[]{:S(2)}, u32[]{:S(2)}) collective-permute-start(bf16[2,4,128,128]{3,2,1,0:T(8,128)(2,1)S(1)} %pad_maximum_fusion.3.refs_4_), channel_id=1, source_target_pairs={{2,0},{3,1},{0,2},{1,3},{6,4},{7,5},{4,6},{5,7},{10,8},{11,9},{8,1... | collective-permute-start | bytes 786440 | tf_op jit(solution)/shard_map/ppermute | solution.py:36
  15.2 2.9 %collective-permute-start.6 = (bf16[4,128,128]{2,1,0:T(8,128)(2,1)}, bf16[4,128,128]{2,1,0:T(8,128)(2,1)S(1)}, u32[]{:S(2)}, u32[]{:S(2)}) collective-permute-start(bf16[4,128,128]{2,1,0:T(8,128)(2,1)} %bitcast.120), channel_id=1, source_target_pairs={{1,0},{0,1},{3,2},{2,3},{5,4},{4,5},{7,6},{6,7},{9,8},{8,9},{11,10... | collective-permute-start | bytes 393224 | tf_op jit(solution)/shard_map/ppermute | solution.py:36
  16.2 21.3 %collective-permute-start.5 = (bf16[10,1,128,128]{3,2,1,0:T(8,128)(2,1)S(1)}, bf16[10,1,128,128]{3,2,1,0:T(8,128)(2,1)S(1)}, u32[]{:S(2)}, u32[]{:S(2)}) collective-permute-start(bf16[10,1,128,128]{3,2,1,0:T(8,128)(2,1)S(1)} %constant_dynamic-slice_fusion), channel_id=1, source_target_pairs={{12,0},{13,1},{14,2},{15,3},{28,16},{29,17},{30,18},{31,19}} | collective-permute-start | bytes 983048 | tf_op jit(solution)/shard_map/ppermute | solution.py:36
  17.5 3.4 %collective-permute-start.11 = (bf16[5,64,128]{2,1,0:T(8,128)(2,1)S(1)}, bf16[5,64,128]{2,1,0:T(8,128)(2,1)S(1)}, u32[]{:S(2)}, u32[]{:S(2)}) collective-permute-start(bf16[5,64,128]{2,1,0:T(8,128)(2,1)S(1)} %get-tuple-element.35.refs_8_), channel_id=1, source_target_pairs={{1,0},{0,1},{3,2},{2,3},{5,4},{4,5},{7,6},{6,7},{9,8},{8,9},{11,10... | collective-permute-start | bytes 245768 | tf_op jit(solution)/shard_map/ppermute | solution.py:36
  18.1 5.8 %collective-permute-start.8 = (bf16[2,4,128,128]{3,2,1,0:T(8,128)(2,1)S(1)}, bf16[2,4,128,128]{3,2,1,0:T(8,128)(2,1)S(1)}, u32[]{:S(2)}, u32[]{:S(2)}) collective-permute-start(bf16[2,4,128,128]{3,2,1,0:T(8,128)(2,1)S(1)} %pad_maximum_fusion.3.refs_4_), channel_id=1, source_target_pairs={{1,0},{0,1},{3,2},{2,3},{5,4},{4,5},{7,6},{6,7},{9,8},{8,9},{11,10... | collective-permute-start | bytes 786440 | tf_op jit(solution)/shard_map/ppermute | solution.py:36
  20.9 3.0 %collective-permute-start.10 = (bf16[2,4,128,128]{3,2,1,0:T(8,128)(2,1)S(1)}, bf16[2,4,128,128]{3,2,1,0:T(8,128)(2,1)S(1)}, u32[]{:S(2)}, u32[]{:S(2)}) collective-permute-start(bf16[2,4,128,128]{3,2,1,0:T(8,128)(2,1)S(1)} %collective-permute-done.9.refs_6_), channel_id=1, source_target_pairs={{1,0},{0,1},{3,2},{2,3},{5,4},{4,5},{7,6},{6,7},{9,8},{8,9},{11,10... | collective-permute-start | bytes 786440 | tf_op jit(solution)/shard_map/ppermute | solution.py:36
  20.9 1.6 %collective-permute-start.12 = (bf16[5,64,128]{2,1,0:T(8,128)(2,1)S(1)}, bf16[5,64,128]{2,1,0:T(8,128)(2,1)S(1)}, u32[]{:S(2)}, u32[]{:S(2)}) collective-permute-start(bf16[5,64,128]{2,1,0:T(8,128)(2,1)S(1)} %collective-permute-done.3.refs_10_), channel_id=1, source_target_pairs={{1,0},{0,1},{3,2},{2,3},{5,4},{4,5},{7,6},{6,7},{9,8},{8,9},{11,10... | collective-permute-start | bytes 245768 | tf_op jit(solution)/shard_map/ppermute | solution.py:36
  37.5 6.5 %collective-permute-start.13 = (bf16[20,1,128,128]{3,2,1,0:T(8,128)(2,1)S(1)}, bf16[20,1,128,128]{3,2,1,0:T(8,128)(2,1)S(1)}, u32[]{:S(2)}, u32[]{:S(2)}) collective-permute-start(bf16[20,1,128,128]{3,2,1,0:T(8,128)(2,1)S(1)} %collective-permute-done.4.refs_0_.refs_16_), channel_id=1, source_target_pairs={{1,0},{0,1},{3,2},{2,3},{5,4},{4,5},{7,6},{6,7},{9,8},{8,9},{11,10... | collective-permute-start | bytes 1966088 | tf_op jit(solution)/shard_map/ppermute | solution.py:36
  41.8 2.2 %collective-permute-start.14 = (bf16[10,1,128,128]{3,2,1,0:T(8,128)(2,1)S(1)}, bf16[10,1,128,128]{3,2,1,0:T(8,128)(2,1)S(1)}, u32[]{:S(2)}, u32[]{:S(2)}) collective-permute-start(bf16[10,1,128,128]{3,2,1,0:T(8,128)(2,1)S(1)} %collective-permute-done.5.refs_2_.refs_18_), channel_id=1, source_target_pairs={{1,0},{0,1},{3,2},{2,3},{5,4},{4,5},{7,6},{6,7},{9,8},{8,9},{11,10... | collective-permute-start | bytes 983048 | tf_op jit(solution)/shard_map/ppermute | solution.py:36
  51.7 5.7 %collective-permute-start.15 = (bf16[17,32,128]{2,1,0:T(8,128)(2,1)S(1)}, bf16[17,32,128]{2,1,0:T(8,128)(2,1)S(1)}, u32[]{:S(2)}, u32[]{:S(2)}) collective-permute-start(bf16[17,32,128]{2,1,0:T(8,128)(2,1)S(1)} %image_rows.1), channel_id=1, source_target_pairs={{2,0},{3,1},{0,2},{1,3},{6,4},{7,5},{4,6},{5,7},{10,8},{11,9},{8,1... | collective-permute-start | bytes 417800 | tf_op jit(solution)/shard_map/ppermute | solution.py:36
  52.7 10.7 %collective-permute-start.19 = (bf16[2,17,32,128]{3,2,1,0:T(8,128)(2,1)S(1)}, bf16[2,17,32,128]{3,2,1,0:T(8,128)(2,1)S(1)}, u32[]{:S(2)}, u32[]{:S(2)}) collective-permute-start(bf16[2,17,32,128]{3,2,1,0:T(8,128)(2,1)S(1)} %pad_maximum_fusion.1.refs_4_), channel_id=1, source_target_pairs={{0,4},{2,6},{4,8},{5,1},{6,10},{7,3},{8,12},{9,5},{10,14},{11,7},{... | collective-permute-start | bytes 835592 | tf_op jit(solution)/shard_map/ppermute | solution.py:61
  58.8 9.4 %collective-permute-start.17 = (bf16[2,17,32,128]{3,2,1,0:T(8,128)(2,1)S(1)}, bf16[2,17,32,128]{3,2,1,0:T(8,128)(2,1)S(1)}, u32[]{:S(2)}, u32[]{:S(2)}) collective-permute-start(bf16[2,17,32,128]{3,2,1,0:T(8,128)(2,1)S(1)} %pad_maximum_fusion), channel_id=1, source_target_pairs={{0,4},{2,6},{4,8},{5,1},{6,10},{7,3},{8,12},{9,5},{10,14},{11,7},{... | collective-permute-start | bytes 835592 | tf_op jit(solution)/shard_map/ppermute | solution.py:61
  63.6 4.6 %collective-permute-start.20 = (f32[8,128]{1,0:T(8,128)S(1)}, f32[8,128]{1,0:T(8,128)S(1)}, u32[]{:S(2)}, u32[]{:S(2)}) collective-permute-start(f32[8,128]{1,0:T(8,128)S(1)} %maximum_maximum_fusion.refs_1_), channel_id=1, source_target_pairs={{8,0},{13,1},{10,2},{15,3},{12,4},{9,5},{14,6},{11,7},{0,8},{5,9},... | collective-permute-start | bytes 12296 | tf_op jit(solution)/shard_map/ppermute | solution.py:170
  63.6 6.2 %collective-permute-start.22 = (bf16[2,17,32,128]{3,2,1,0:T(8,128)(2,1)S(1)}, bf16[2,17,32,128]{3,2,1,0:T(8,128)(2,1)S(1)}, u32[]{:S(2)}, u32[]{:S(2)}) collective-permute-start(bf16[2,17,32,128]{3,2,1,0:T(8,128)(2,1)S(1)} %collective-permute-done.19.refs_7_), channel_id=1, source_target_pairs={{1,0},{0,1},{3,2},{2,3},{5,4},{4,5},{7,6},{6,7},{9,8},{8,9},{11,10... | collective-permute-start | bytes 835592 | tf_op jit(solution)/shard_map/ppermute | solution.py:36
  68.2 1.6 %collective-permute-start.23 = (bf16[2,17,32,128]{3,2,1,0:T(8,128)(2,1)S(1)}, bf16[2,17,32,128]{3,2,1,0:T(8,128)(2,1)S(1)}, u32[]{:S(2)}, u32[]{:S(2)}) collective-permute-start(bf16[2,17,32,128]{3,2,1,0:T(8,128)(2,1)S(1)} %collective-permute-done.17.refs_8_), channel_id=1, source_target_pairs={{1,0},{0,1},{3,2},{2,3},{5,4},{4,5},{7,6},{6,7},{9,8},{8,9},{11,10... | collective-permute-start | bytes 835592 | tf_op jit(solution)/shard_map/ppermute | solution.py:36
  68.2 1.6 %collective-permute-start.21 = (f32[8,128]{1,0:T(8,128)S(1)}, f32[8,128]{1,0:T(8,128)S(1)}, u32[]{:S(2)}, u32[]{:S(2)}) collective-permute-start(f32[8,128]{1,0:T(8,128)S(1)} %collective-permute-done.20.refs_2_), channel_id=1, source_target_pairs={{1,0},{0,1},{3,2},{2,3},{5,4},{4,5},{7,6},{6,7},{9,8},{8,9},{11,10... | collective-permute-start | bytes 12296 | tf_op jit(solution)/shard_map/ppermute | solution.py:36
  77.3 2.0 %collective-permute-start.24 = (bf16[4,32,128]{2,1,0:T(8,128)(2,1)S(1)}, bf16[4,32,128]{2,1,0:T(8,128)(2,1)S(1)}, u32[]{:S(2)}, u32[]{:S(2)}) collective-permute-start(bf16[4,32,128]{2,1,0:T(8,128)(2,1)S(1)} %get-tuple-element.55), channel_id=1, source_target_pairs={{1,0},{0,1},{3,2},{2,3},{5,4},{4,5},{7,6},{6,7},{9,8},{8,9},{11,10... | collective-permute-start | bytes 98312 | tf_op jit(solution)/shard_map/ppermute | solution.py:36
  77.6 3.9 %collective-permute-start.25 = (bf16[4,32,128]{2,1,0:T(8,128)(2,1)S(1)}, bf16[4,32,128]{2,1,0:T(8,128)(2,1)S(1)}, u32[]{:S(2)}, u32[]{:S(2)}) collective-permute-start(bf16[4,32,128]{2,1,0:T(8,128)(2,1)S(1)} %get-tuple-element.56), channel_id=1, source_target_pairs={{2,0},{3,1},{0,2},{1,3},{6,4},{7,5},{4,6},{5,7},{10,8},{11,9},{8,1... | collective-permute-start | bytes 98312 | tf_op jit(solution)/shard_map/ppermute | solution.py:36
  78.6 3.4 %collective-permute-start.26 = (bf16[4,32,128]{2,1,0:T(8,128)(2,1)S(1)}, bf16[4,32,128]{2,1,0:T(8,128)(2,1)S(1)}, u32[]{:S(2)}, u32[]{:S(2)}) collective-permute-start(bf16[4,32,128]{2,1,0:T(8,128)(2,1)S(1)} %get-tuple-element.57), channel_id=1, source_target_pairs={{3,0},{2,1},{1,2},{0,3},{7,4},{6,5},{5,6},{4,7},{11,8},{10,9},{9,1... | collective-permute-start | bytes 98312 | tf_op jit(solution)/shard_map/ppermute | solution.py:36
  (10 other events, 35.1 us)

commit v9 on v8

--- a/solution.py
+++ b/solution.py
@@ -133,7 +133,17 @@
 
 
 def handed_over(arrays):
-    return [piece for array in arrays for piece in (array, from_near(array, 0, 1))]
+    n_bond, n_mpo = lax.axis_size("bond"), lax.axis_size("mpo")
+    result = []
+    for place, array in enumerate(arrays):
+        pairs = [
+            (i * n_mpo + j, i * n_mpo + (j ^ 1))
+            for i in range(n_bond)
+            for j in range(n_mpo)
+            if i + (2 + place if place else 1 + j % 2) < n_bond
+        ]
+        result += [array, lax.ppermute(array, ("bond", "mpo"), pairs)]
+    return result
 
 
 def merged(parts):

time: 83.2 us -> 84.6 us (1.017)
  waiting for transfers between devices: 19.2 us -> 20.7 us
    ppermute x0 -> x2, starting transfers between devices: none -> 8.11 us  [handed_over(): result += [array, lax.ppermute(array, ('bond', 'mpo'), pairs)]]
    ppermute x23 -> x21, starting transfers between devices: 19.7 us -> 15.2 us  [from_near(): return lax.ppermute(value, ('bond', 'mpo'), pairs)]
    ppermute x2, starting transfers between devices: 8.93 us -> 5.21 us  [exchange(): mine[r] = lax.ppermute(pair, ('bond', 'mpo'), pairs)]
    ppermute x0 -> x2, waiting for transfers between devices: none -> 1.6 us  [handed_over(): result += [array, lax.ppermute(array, ('bond', 'mpo'), pairs)]]
    ppermute x23 -> x21, waiting for transfers between devices: 14.7 us -> 14.5 us  [from_near(): return lax.ppermute(value, ('bond', 'mpo'), pairs)]
where the time goes in v9:
time: 84.6 us; the launch traced here: 84 us
  starting transfers between devices  29.8 us (35%)
  Pallas kernels  23.8 us (28%)
  waiting for transfers between devices  20.7 us (24%)
  local copies, waits for them, and re-layouts  5.92 us (7%)
  other arithmetic  2.97 us (4%)
  between operations  0.91 us (1%)
    ppermute x21, starting transfers between devices, from_near(): return lax.ppermute(value, ('bond', 'mpo'), pairs)  15.2 us
    ppermute x21, waiting for transfers between devices, from_near(): return lax.ppermute(value, ('bond', 'mpo'), pairs)  14.5 us
    pallas_call x1, Pallas kernels, shards(): pl.pallas_call(functools.partial(first_kernel, plan), out_shape=(shape_of...  11 us
    ppermute x2, starting transfers between devices, handed_over(): result += [array, lax.ppermute(array, ('bond', 'mpo'), pairs)]  8.11 us
    pallas_call x1, Pallas kernels, shards(): pl.pallas_call(functools.partial(second_kernel, plan, float(count_all), l...  7.57 us
    pallas_call x1, Pallas kernels, shards(): pl.pallas_call(functools.partial(image_kernel, plan), out_shape=shape_of(...  5.26 us
    ppermute x2, starting transfers between devices, exchange(): mine[r] = lax.ppermute(pair, ('bond', 'mpo'), pairs)  5.21 us
    ppermute x1, waiting for transfers between devices, far_sums(): return [sums, lax.ppermute(sums, ('bond', 'mpo'), pairs)]  4.52 us
  transfers between devices with their start and end apart: 27, of which 14 were waited for; matrix products, arithmetic and copies ran while one was open for 7% of the time, Pallas kernels for 13%

profile of v9, /device:TPU:0, one launch (start us, length us, event | category | flops | bytes accessed | tf_op | source)
XLA Modules:
  0.0 84.0 jit_solution(3821428436247541066)
XLA Ops:
  0.6 3.0 %collective-permute-start.2 = (bf16[4,128,128]{2,1,0:T(8,128)(2,1)}, bf16[4,128,128]{2,1,0:T(8,128)(2,1)S(1)}, u32[]{:S(2)}, u32[]{:S(2)}) collective-permute-start(bf16[4,128,128]{2,1,0:T(8,128)(2,1)} %bitcast.117), channel_id=1, source_target_pairs={{2,0},{3,1},{0,2},{1,3},{6,4},{7,5},{4,6},{5,7},{10,8},{11,9},{8,1... | collective-permute-start | bytes 393224 | tf_op jit(solution)/shard_map/ppermute | solution.py:36
  3.6 3.5 %collective-permute-start = (bf16[4,128,128]{2,1,0:T(8,128)(2,1)}, bf16[4,128,128]{2,1,0:T(8,128)(2,1)S(1)}, u32[]{:S(2)}, u32[]{:S(2)}) collective-permute-start(bf16[4,128,128]{2,1,0:T(8,128)(2,1)} %bitcast.118), channel_id=1, source_target_pairs={{0,4},{1,5},{2,6},{3,7},{4,8},{5,9},{6,10},{7,11},{8,12},{9,13},{1... | collective-permute-start | bytes 393224 | tf_op jit(solution)/shard_map/ppermute | solution.py:36
  7.1 1.3 %collective-permute-start.1 = (bf16[4,128,128]{2,1,0:T(8,128)(2,1)}, bf16[4,128,128]{2,1,0:T(8,128)(2,1)S(1)}, u32[]{:S(2)}, u32[]{:S(2)}) collective-permute-start(bf16[4,128,128]{2,1,0:T(8,128)(2,1)} %bitcast.119), channel_id=1, source_target_pairs={{4,0},{5,1},{6,2},{7,3},{8,4},{9,5},{10,6},{11,7},{12,8},{13,9},{1... | collective-permute-start | bytes 393224 | tf_op jit(solution)/shard_map/ppermute | solution.py:36
  10.0 1.3 %collective-permute-start.4 = (bf16[20,1,128,128]{3,2,1,0:T(8,128)(2,1)}, bf16[20,1,128,128]{3,2,1,0:T(8,128)(2,1)S(1)}, u32[]{:S(2)}, u32[]{:S(2)}) collective-permute-start(bf16[20,1,128,128]{3,2,1,0:T(8,128)(2,1)} %refs_15_.1), channel_id=1, source_target_pairs={{4,0},{9,1},{6,2},{11,3},{8,4},{13,5},{10,6},{15,7},{12,8},{14,10}... | collective-permute-start | bytes 1966088 | tf_op jit(solution)/shard_map/ppermute | solution.py:129
  11.3 1.1 %maximum_bitcast_fusion = bf16[2,4,20,4,20]{2,3,1,4,0:T(4,128)(2,1)S(1)} fusion(bf16[1,20,20,4,4]{2,4,3,1,0:T(4,128)(2,1)} %bitcast.124, bf16[1,20,20,4,4]{2,4,3,1,0:T(4,128)(2,1)} %bitcast.125), kind=kLoop, calls=%fused_computation.4 | loop fusion | flops 12800 | bytes 51200 | tf_op jit(solution)/shard_map/transpose | solution.py:594
  14.2 1.0 %collective-permute-start.9 = (bf16[2,4,128,128]{3,2,1,0:T(8,128)(2,1)S(1)}, bf16[2,4,128,128]{3,2,1,0:T(8,128)(2,1)S(1)}, u32[]{:S(2)}, u32[]{:S(2)}) collective-permute-start(bf16[2,4,128,128]{3,2,1,0:T(8,128)(2,1)S(1)} %pad_maximum_fusion.3.refs_4_), channel_id=1, source_target_pairs={{2,0},{3,1},{0,2},{1,3},{6,4},{7,5},{4,6},{5,7},{10,8},{11,9},{8,1... | collective-permute-start | bytes 786440 | tf_op jit(solution)/shard_map/ppermute | solution.py:36
  16.2 1.3 %collective-permute-start.5 = (bf16[10,1,128,128]{3,2,1,0:T(8,128)(2,1)S(1)}, bf16[10,1,128,128]{3,2,1,0:T(8,128)(2,1)S(1)}, u32[]{:S(2)}, u32[]{:S(2)}) collective-permute-start(bf16[10,1,128,128]{3,2,1,0:T(8,128)(2,1)S(1)} %constant_dynamic-slice_fusion), channel_id=1, source_target_pairs={{12,0},{13,1},{14,2},{15,3},{28,16},{29,17},{30,18},{31,19}} | collective-permute-start | bytes 983048 | tf_op jit(solution)/shard_map/ppermute | solution.py:36
  18.2 2.8 %collective-permute-done.9.refs_6_ = bf16[2,4,128,128]{3,2,1,0:T(8,128)(2,1)S(1)} collective-permute-done((bf16[2,4,128,128]{3,2,1,0:T(8,128)(2,1)S(1)}, bf16[2,4,128,128]{3,2,1,0:T(8,128)(2,1)S(1)}, u32[]{:S(2)}, u32[]{:S(2)}) %collective-permute-start.9) | collective-permute-done | bytes 262176 | tf_op jit(solution)/shard_map/ppermute | solution.py:36
  21.5 1.1 %collective-permute-done.12.refs_11_ = bf16[5,64,128]{2,1,0:T(8,128)(2,1)S(1)} collective-permute-done((bf16[5,64,128]{2,1,0:T(8,128)(2,1)S(1)}, bf16[5,64,128]{2,1,0:T(8,128)(2,1)S(1)}, u32[]{:S(2)}, u32[]{:S(2)}) %collective-permute-start.12) | collective-permute-done | bytes 81952 | tf_op jit(solution)/shard_map/ppermute | solution.py:36
  24.6 11.0 %states_of_vector.1 = (f32[16,20,32,128]{3,2,1,0:T(8,128)}, bf16[16,384,128]{2,1,0:T(8,128)(2,1)}, bf16[768,384]{1,0:T(8,128)(2,1)}, bf16[80,96]{1,0:T(8,128)(2,1)S(1)}, bf16[160,160]{1,0:T(8,128)(2,1)S(1)}) custom-call(s32[28]{0:T(128)S(1)} %pad_add_fusion.refs_0_.sizes_ref, bf16[2,4,128,128]{3,2,1,0:T(8,128)(2,1)S(1)} %pad_maximum_fusion.2.refs_1_, ...), custom_call_target="tpu_custom_call" | custom-call | flops 1000 | tf_op jit(solution)/shard_map/states_of_vector/pallas_call | solution.py:621
  35.6 1.9 %collective-permute-done.5.refs_2_.refs_18_ = bf16[10,1,128,128]{3,2,1,0:T(8,128)(2,1)S(1)} collective-permute-done((bf16[10,1,128,128]{3,2,1,0:T(8,128)(2,1)S(1)}, bf16[10,1,128,128]{3,2,1,0:T(8,128)(2,1)S(1)}, u32[]{:S(2)}, u32[]{:S(2)}) %collective-permute-start.5) | collective-permute-done | bytes 327712 | tf_op jit(solution)/shard_map/ppermute | solution.py:36
  37.5 6.2 %collective-permute-start.13 = (bf16[20,1,128,128]{3,2,1,0:T(8,128)(2,1)S(1)}, bf16[20,1,128,128]{3,2,1,0:T(8,128)(2,1)S(1)}, u32[]{:S(2)}, u32[]{:S(2)}) collective-permute-start(bf16[20,1,128,128]{3,2,1,0:T(8,128)(2,1)S(1)} %collective-permute-done.4.refs_0_.refs_16_), channel_id=1, source_target_pairs={{0,1},{1,0},{2,3},{3,2},{4,5},{5,4},{6,7},{7,6},{8,9},{10,11},{16,... | collective-permute-start | bytes 1966088 | tf_op jit(solution)/shard_map/ppermute | solution.py:145
  43.7 1.9 %collective-permute-start.14 = (bf16[10,1,128,128]{3,2,1,0:T(8,128)(2,1)S(1)}, bf16[10,1,128,128]{3,2,1,0:T(8,128)(2,1)S(1)}, u32[]{:S(2)}, u32[]{:S(2)}) collective-permute-start(bf16[10,1,128,128]{3,2,1,0:T(8,128)(2,1)S(1)} %collective-permute-done.5.refs_2_.refs_18_), channel_id=1, source_target_pairs={{0,1},{1,0},{2,3},{3,2},{16,17},{17,16},{18,19},{19,18}} | collective-permute-start | bytes 983048 | tf_op jit(solution)/shard_map/ppermute | solution.py:145
  45.6 1.6 %collective-permute-done.14.refs_3_.refs_19_ = bf16[10,1,128,128]{3,2,1,0:T(8,128)(2,1)S(1)} collective-permute-done((bf16[10,1,128,128]{3,2,1,0:T(8,128)(2,1)S(1)}, bf16[10,1,128,128]{3,2,1,0:T(8,128)(2,1)S(1)}, u32[]{:S(2)}, u32[]{:S(2)}) %collective-permute-start.14) | collective-permute-done | bytes 327712 | tf_op jit(solution)/shard_map/ppermute | solution.py:145
  48.1 1.1 %copy-done = bf16[20,1,128,128]{3,2,1,0:T(8,128)(2,1)S(1)} copy-done((bf16[20,1,128,128]{3,2,1,0:T(8,128)(2,1)S(1)}, bf16[20,1,128,128]{3,2,1,0:T(8,128)(2,1)}, u32[]{:S(2)}) %copy-start) | copy-done | bytes 655384
  49.2 5.3 %image_rows.1 = bf16[17,32,128]{2,1,0:T(8,128)(2,1)S(1)} custom-call(s32[28]{0:T(128)S(1)} %pad_add_fusion.refs_0_.sizes_ref, f32[16,640,128]{2,1,0:T(8,128)} %bitcast.126, bf16[16,384,128]{2,1,0:T(8,128)(2,1)} %get-tuple-element.40.vector_ref.refs_11_, bf16[20,1,128,128]{3,2,1,0:T(8,128)(2,1)S(1)} %copy-done, bf16[20,1,128,128]{3,2,1,0:T(8,128)(2,1)} %copy-done.3, ...), custom_call_target="tpu_custom_call" | custom-call | flops 4000000000 | tf_op jit(solution)/shard_map/image_rows/pallas_call | solution.py:652
  56.0 2.5 %collective-permute-start.19 = (bf16[2,17,32,128]{3,2,1,0:T(8,128)(2,1)S(1)}, bf16[2,17,32,128]{3,2,1,0:T(8,128)(2,1)S(1)}, u32[]{:S(2)}, u32[]{:S(2)}) collective-permute-start(bf16[2,17,32,128]{3,2,1,0:T(8,128)(2,1)S(1)} %pad_maximum_fusion.1.refs_4_), channel_id=1, source_target_pairs={{0,4},{2,6},{4,8},{5,1},{6,10},{7,3},{8,12},{9,5},{10,14},{11,7},{... | collective-permute-start | bytes 835592 | tf_op jit(solution)/shard_map/ppermute | solution.py:61
  58.5 2.2 %collective-permute-done.15.refs_5_ = bf16[17,32,128]{2,1,0:T(8,128)(2,1)S(1)} collective-permute-done((bf16[17,32,128]{2,1,0:T(8,128)(2,1)S(1)}, bf16[17,32,128]{2,1,0:T(8,128)(2,1)S(1)}, u32[]{:S(2)}, u32[]{:S(2)}) %collective-permute-start.15) | collective-permute-done | bytes 139296 | tf_op jit(solution)/shard_map/ppermute | solution.py:36
  60.7 1.3 %collective-permute-done.16.refs_6_ = bf16[17,32,128]{2,1,0:T(8,128)(2,1)S(1)} collective-permute-done((bf16[17,32,128]{2,1,0:T(8,128)(2,1)S(1)}, bf16[17,32,128]{2,1,0:T(8,128)(2,1)S(1)}, u32[]{:S(2)}, u32[]{:S(2)}) %collective-permute-start.16) | collective-permute-done | bytes 139296 | tf_op jit(solution)/shard_map/ppermute | solution.py:36
  62.1 2.7 %collective-permute-start.17 = (bf16[2,17,32,128]{3,2,1,0:T(8,128)(2,1)S(1)}, bf16[2,17,32,128]{3,2,1,0:T(8,128)(2,1)S(1)}, u32[]{:S(2)}, u32[]{:S(2)}) collective-permute-start(bf16[2,17,32,128]{3,2,1,0:T(8,128)(2,1)S(1)} %pad_maximum_fusion), channel_id=1, source_target_pairs={{0,4},{2,6},{4,8},{5,1},{6,10},{7,3},{8,12},{9,5},{10,14},{11,7},{... | collective-permute-start | bytes 835592 | tf_op jit(solution)/shard_map/ppermute | solution.py:61
  65.0 4.5 %collective-permute-done.20.refs_2_ = f32[8,128]{1,0:T(8,128)S(1)} collective-permute-done((f32[8,128]{1,0:T(8,128)S(1)}, f32[8,128]{1,0:T(8,128)S(1)}, u32[]{:S(2)}, u32[]{:S(2)}) %collective-permute-start.20) | collective-permute-done | bytes 4128 | tf_op jit(solution)/shard_map/ppermute | solution.py:180
  70.1 1.1 %collective-permute-done.21.refs_3_ = f32[8,128]{1,0:T(8,128)S(1)} collective-permute-done((f32[8,128]{1,0:T(8,128)S(1)}, f32[8,128]{1,0:T(8,128)S(1)}, u32[]{:S(2)}, u32[]{:S(2)}) %collective-permute-start.21) | collective-permute-done | bytes 4128 | tf_op jit(solution)/shard_map/ppermute | solution.py:36
  71.1 7.6 %correction_image_rows.1 = (bf16[4,32,128]{2,1,0:T(8,128)(2,1)S(1)}, bf16[4,32,128]{2,1,0:T(8,128)(2,1)S(1)}, bf16[4,32,128]{2,1,0:T(8,128)(2,1)S(1)}, bf16[4,32...) custom-call(s32[28]{0:T(128)S(1)} %pad_add_fusion.refs_0_.sizes_ref, f32[8,128]{1,0:T(8,128)S(1)} %maximum_maximum_fusion.refs_1_, ...), custom_call_target="tpu_custom_call" | custom-call | flops 1000 | tf_op jit(solution)/shard_map/correction_image_rows/pallas_call | solution.py:682
  80.7 2.1 %collective-permute-done.25 = bf16[4,32,128]{2,1,0:T(8,128)(2,1)S(1)} collective-permute-done((bf16[4,32,128]{2,1,0:T(8,128)(2,1)S(1)}, bf16[4,32,128]{2,1,0:T(8,128)(2,1)S(1)}, u32[]{:S(2)}, u32[]{:S(2)}) %collective-permute-start.25) | collective-permute-done | bytes 32800 | tf_op jit(solution)/shard_map/ppermute | solution.py:36
  (72 shorter events, 14.0 us)
Async XLA Ops:
  0.6 13.3 %collective-permute-start.2 = (bf16[4,128,128]{2,1,0:T(8,128)(2,1)}, bf16[4,128,128]{2,1,0:T(8,128)(2,1)S(1)}, u32[]{:S(2)}, u32[]{:S(2)}) collective-permute-start(bf16[4,128,128]{2,1,0:T(8,128)(2,1)} %bitcast.117), channel_id=1, source_target_pairs={{2,0},{3,1},{0,2},{1,3},{6,4},{7,5},{4,6},{5,7},{10,8},{11,9},{8,1... | collective-permute-start | bytes 393224 | tf_op jit(solution)/shard_map/ppermute | solution.py:36
  3.6 10.3 %collective-permute-start = (bf16[4,128,128]{2,1,0:T(8,128)(2,1)}, bf16[4,128,128]{2,1,0:T(8,128)(2,1)S(1)}, u32[]{:S(2)}, u32[]{:S(2)}) collective-permute-start(bf16[4,128,128]{2,1,0:T(8,128)(2,1)} %bitcast.118), channel_id=1, source_target_pairs={{0,4},{1,5},{2,6},{3,7},{4,8},{5,9},{6,10},{7,11},{8,12},{9,13},{1... | collective-permute-start | bytes 393224 | tf_op jit(solution)/shard_map/ppermute | solution.py:36
  7.1 7.1 %collective-permute-start.1 = (bf16[4,128,128]{2,1,0:T(8,128)(2,1)}, bf16[4,128,128]{2,1,0:T(8,128)(2,1)S(1)}, u32[]{:S(2)}, u32[]{:S(2)}) collective-permute-start(bf16[4,128,128]{2,1,0:T(8,128)(2,1)} %bitcast.119), channel_id=1, source_target_pairs={{4,0},{5,1},{6,2},{7,3},{8,4},{9,5},{10,6},{11,7},{12,8},{13,9},{1... | collective-permute-start | bytes 393224 | tf_op jit(solution)/shard_map/ppermute | solution.py:36
  9.4 4.5 %collective-permute-start.3 = (bf16[5,64,128]{2,1,0:T(8,128)(2,1)S(1)}, bf16[5,64,128]{2,1,0:T(8,128)(2,1)S(1)}, u32[]{:S(2)}, u32[]{:S(2)}) collective-permute-start(bf16[5,64,128]{2,1,0:T(8,128)(2,1)S(1)} %get-tuple-element.61), channel_id=1, source_target_pairs={{2,0},{3,1},{0,2},{1,3},{6,4},{7,5},{4,6},{5,7},{10,8},{11,9},{8,1... | collective-permute-start | bytes 245768 | tf_op jit(solution)/shard_map/ppermute | solution.py:36
  10.0 27.5 %collective-permute-start.4 = (bf16[20,1,128,128]{3,2,1,0:T(8,128)(2,1)}, bf16[20,1,128,128]{3,2,1,0:T(8,128)(2,1)S(1)}, u32[]{:S(2)}, u32[]{:S(2)}) collective-permute-start(bf16[20,1,128,128]{3,2,1,0:T(8,128)(2,1)} %refs_15_.1), channel_id=1, source_target_pairs={{4,0},{9,1},{6,2},{11,3},{8,4},{13,5},{10,6},{15,7},{12,8},{14,10}... | collective-permute-start | bytes 1966088 | tf_op jit(solution)/shard_map/ppermute | solution.py:129
  14.2 6.7 %collective-permute-start.9 = (bf16[2,4,128,128]{3,2,1,0:T(8,128)(2,1)S(1)}, bf16[2,4,128,128]{3,2,1,0:T(8,128)(2,1)S(1)}, u32[]{:S(2)}, u32[]{:S(2)}) collective-permute-start(bf16[2,4,128,128]{3,2,1,0:T(8,128)(2,1)S(1)} %pad_maximum_fusion.3.refs_4_), channel_id=1, source_target_pairs={{2,0},{3,1},{0,2},{1,3},{6,4},{7,5},{4,6},{5,7},{10,8},{11,9},{8,1... | collective-permute-start | bytes 786440 | tf_op jit(solution)/shard_map/ppermute | solution.py:36
  15.2 2.9 %collective-permute-start.6 = (bf16[4,128,128]{2,1,0:T(8,128)(2,1)}, bf16[4,128,128]{2,1,0:T(8,128)(2,1)S(1)}, u32[]{:S(2)}, u32[]{:S(2)}) collective-permute-start(bf16[4,128,128]{2,1,0:T(8,128)(2,1)} %bitcast.120), channel_id=1, source_target_pairs={{1,0},{0,1},{3,2},{2,3},{5,4},{4,5},{7,6},{6,7},{9,8},{8,9},{11,10... | collective-permute-start | bytes 393224 | tf_op jit(solution)/shard_map/ppermute | solution.py:36
  16.2 21.3 %collective-permute-start.5 = (bf16[10,1,128,128]{3,2,1,0:T(8,128)(2,1)S(1)}, bf16[10,1,128,128]{3,2,1,0:T(8,128)(2,1)S(1)}, u32[]{:S(2)}, u32[]{:S(2)}) collective-permute-start(bf16[10,1,128,128]{3,2,1,0:T(8,128)(2,1)S(1)} %constant_dynamic-slice_fusion), channel_id=1, source_target_pairs={{12,0},{13,1},{14,2},{15,3},{28,16},{29,17},{30,18},{31,19}} | collective-permute-start | bytes 983048 | tf_op jit(solution)/shard_map/ppermute | solution.py:36
  17.5 3.4 %collective-permute-start.11 = (bf16[5,64,128]{2,1,0:T(8,128)(2,1)S(1)}, bf16[5,64,128]{2,1,0:T(8,128)(2,1)S(1)}, u32[]{:S(2)}, u32[]{:S(2)}) collective-permute-start(bf16[5,64,128]{2,1,0:T(8,128)(2,1)S(1)} %get-tuple-element.35.refs_8_), channel_id=1, source_target_pairs={{1,0},{0,1},{3,2},{2,3},{5,4},{4,5},{7,6},{6,7},{9,8},{8,9},{11,10... | collective-permute-start | bytes 245768 | tf_op jit(solution)/shard_map/ppermute | solution.py:36
  18.1 5.8 %collective-permute-start.8 = (bf16[2,4,128,128]{3,2,1,0:T(8,128)(2,1)S(1)}, bf16[2,4,128,128]{3,2,1,0:T(8,128)(2,1)S(1)}, u32[]{:S(2)}, u32[]{:S(2)}) collective-permute-start(bf16[2,4,128,128]{3,2,1,0:T(8,128)(2,1)S(1)} %pad_maximum_fusion.3.refs_4_), channel_id=1, source_target_pairs={{1,0},{0,1},{3,2},{2,3},{5,4},{4,5},{7,6},{6,7},{9,8},{8,9},{11,10... | collective-permute-start | bytes 786440 | tf_op jit(solution)/shard_map/ppermute | solution.py:36
  20.9 3.0 %collective-permute-start.10 = (bf16[2,4,128,128]{3,2,1,0:T(8,128)(2,1)S(1)}, bf16[2,4,128,128]{3,2,1,0:T(8,128)(2,1)S(1)}, u32[]{:S(2)}, u32[]{:S(2)}) collective-permute-start(bf16[2,4,128,128]{3,2,1,0:T(8,128)(2,1)S(1)} %collective-permute-done.9.refs_6_), channel_id=1, source_target_pairs={{1,0},{0,1},{3,2},{2,3},{5,4},{4,5},{7,6},{6,7},{9,8},{8,9},{11,10... | collective-permute-start | bytes 786440 | tf_op jit(solution)/shard_map/ppermute | solution.py:36
  20.9 1.6 %collective-permute-start.12 = (bf16[5,64,128]{2,1,0:T(8,128)(2,1)S(1)}, bf16[5,64,128]{2,1,0:T(8,128)(2,1)S(1)}, u32[]{:S(2)}, u32[]{:S(2)}) collective-permute-start(bf16[5,64,128]{2,1,0:T(8,128)(2,1)S(1)} %collective-permute-done.3.refs_10_), channel_id=1, source_target_pairs={{1,0},{0,1},{3,2},{2,3},{5,4},{4,5},{7,6},{6,7},{9,8},{8,9},{11,10... | collective-permute-start | bytes 245768 | tf_op jit(solution)/shard_map/ppermute | solution.py:36
  37.5 9.7 %collective-permute-start.13 = (bf16[20,1,128,128]{3,2,1,0:T(8,128)(2,1)S(1)}, bf16[20,1,128,128]{3,2,1,0:T(8,128)(2,1)S(1)}, u32[]{:S(2)}, u32[]{:S(2)}) collective-permute-start(bf16[20,1,128,128]{3,2,1,0:T(8,128)(2,1)S(1)} %collective-permute-done.4.refs_0_.refs_16_), channel_id=1, source_target_pairs={{0,1},{1,0},{2,3},{3,2},{4,5},{5,4},{6,7},{7,6},{8,9},{10,11},{16,... | collective-permute-start | bytes 1966088 | tf_op jit(solution)/shard_map/ppermute | solution.py:145
  43.7 3.5 %collective-permute-start.14 = (bf16[10,1,128,128]{3,2,1,0:T(8,128)(2,1)S(1)}, bf16[10,1,128,128]{3,2,1,0:T(8,128)(2,1)S(1)}, u32[]{:S(2)}, u32[]{:S(2)}) collective-permute-start(bf16[10,1,128,128]{3,2,1,0:T(8,128)(2,1)S(1)} %collective-permute-done.5.refs_2_.refs_18_), channel_id=1, source_target_pairs={{0,1},{1,0},{2,3},{3,2},{16,17},{17,16},{18,19},{19,18}} | collective-permute-start | bytes 983048 | tf_op jit(solution)/shard_map/ppermute | solution.py:145
  54.7 6.0 %collective-permute-start.15 = (bf16[17,32,128]{2,1,0:T(8,128)(2,1)S(1)}, bf16[17,32,128]{2,1,0:T(8,128)(2,1)S(1)}, u32[]{:S(2)}, u32[]{:S(2)}) collective-permute-start(bf16[17,32,128]{2,1,0:T(8,128)(2,1)S(1)} %image_rows.1), channel_id=1, source_target_pairs={{2,0},{3,1},{0,2},{1,3},{6,4},{7,5},{4,6},{5,7},{10,8},{11,9},{8,1... | collective-permute-start | bytes 417800 | tf_op jit(solution)/shard_map/ppermute | solution.py:36
  56.0 8.8 %collective-permute-start.19 = (bf16[2,17,32,128]{3,2,1,0:T(8,128)(2,1)S(1)}, bf16[2,17,32,128]{3,2,1,0:T(8,128)(2,1)S(1)}, u32[]{:S(2)}, u32[]{:S(2)}) collective-permute-start(bf16[2,17,32,128]{3,2,1,0:T(8,128)(2,1)S(1)} %pad_maximum_fusion.1.refs_4_), channel_id=1, source_target_pairs={{0,4},{2,6},{4,8},{5,1},{6,10},{7,3},{8,12},{9,5},{10,14},{11,7},{... | collective-permute-start | bytes 835592 | tf_op jit(solution)/shard_map/ppermute | solution.py:61
  62.1 7.5 %collective-permute-start.17 = (bf16[2,17,32,128]{3,2,1,0:T(8,128)(2,1)S(1)}, bf16[2,17,32,128]{3,2,1,0:T(8,128)(2,1)S(1)}, u32[]{:S(2)}, u32[]{:S(2)}) collective-permute-start(bf16[2,17,32,128]{3,2,1,0:T(8,128)(2,1)S(1)} %pad_maximum_fusion), channel_id=1, source_target_pairs={{0,4},{2,6},{4,8},{5,1},{6,10},{7,3},{8,12},{9,5},{10,14},{11,7},{... | collective-permute-start | bytes 835592 | tf_op jit(solution)/shard_map/ppermute | solution.py:61
  64.9 4.6 %collective-permute-start.20 = (f32[8,128]{1,0:T(8,128)S(1)}, f32[8,128]{1,0:T(8,128)S(1)}, u32[]{:S(2)}, u32[]{:S(2)}) collective-permute-start(f32[8,128]{1,0:T(8,128)S(1)} %maximum_maximum_fusion.refs_1_), channel_id=1, source_target_pairs={{8,0},{13,1},{10,2},{15,3},{12,4},{9,5},{14,6},{11,7},{0,8},{5,9},... | collective-permute-start | bytes 12296 | tf_op jit(solution)/shard_map/ppermute | solution.py:180
  65.0 6.2 %collective-permute-start.22 = (bf16[2,17,32,128]{3,2,1,0:T(8,128)(2,1)S(1)}, bf16[2,17,32,128]{3,2,1,0:T(8,128)(2,1)S(1)}, u32[]{:S(2)}, u32[]{:S(2)}) collective-permute-start(bf16[2,17,32,128]{3,2,1,0:T(8,128)(2,1)S(1)} %collective-permute-done.19.refs_7_), channel_id=1, source_target_pairs={{1,0},{0,1},{3,2},{2,3},{5,4},{4,5},{7,6},{6,7},{9,8},{8,9},{11,10... | collective-permute-start | bytes 835592 | tf_op jit(solution)/shard_map/ppermute | solution.py:36
  69.6 1.6 %collective-permute-start.23 = (bf16[2,17,32,128]{3,2,1,0:T(8,128)(2,1)S(1)}, bf16[2,17,32,128]{3,2,1,0:T(8,128)(2,1)S(1)}, u32[]{:S(2)}, u32[]{:S(2)}) collective-permute-start(bf16[2,17,32,128]{3,2,1,0:T(8,128)(2,1)S(1)} %collective-permute-done.17.refs_8_), channel_id=1, source_target_pairs={{1,0},{0,1},{3,2},{2,3},{5,4},{4,5},{7,6},{6,7},{9,8},{8,9},{11,10... | collective-permute-start | bytes 835592 | tf_op jit(solution)/shard_map/ppermute | solution.py:36
  69.7 1.5 %collective-permute-start.21 = (f32[8,128]{1,0:T(8,128)S(1)}, f32[8,128]{1,0:T(8,128)S(1)}, u32[]{:S(2)}, u32[]{:S(2)}) collective-permute-start(f32[8,128]{1,0:T(8,128)S(1)} %collective-permute-done.20.refs_2_), channel_id=1, source_target_pairs={{1,0},{0,1},{3,2},{2,3},{5,4},{4,5},{7,6},{6,7},{9,8},{8,9},{11,10... | collective-permute-start | bytes 12296 | tf_op jit(solution)/shard_map/ppermute | solution.py:36
  78.7 2.0 %collective-permute-start.24 = (bf16[4,32,128]{2,1,0:T(8,128)(2,1)S(1)}, bf16[4,32,128]{2,1,0:T(8,128)(2,1)S(1)}, u32[]{:S(2)}, u32[]{:S(2)}) collective-permute-start(bf16[4,32,128]{2,1,0:T(8,128)(2,1)S(1)} %get-tuple-element.55), channel_id=1, source_target_pairs={{1,0},{0,1},{3,2},{2,3},{5,4},{4,5},{7,6},{6,7},{9,8},{8,9},{11,10... | collective-permute-start | bytes 98312 | tf_op jit(solution)/shard_map/ppermute | solution.py:36
  78.9 3.9 %collective-permute-start.25 = (bf16[4,32,128]{2,1,0:T(8,128)(2,1)S(1)}, bf16[4,32,128]{2,1,0:T(8,128)(2,1)S(1)}, u32[]{:S(2)}, u32[]{:S(2)}) collective-permute-start(bf16[4,32,128]{2,1,0:T(8,128)(2,1)S(1)} %get-tuple-element.56), channel_id=1, source_target_pairs={{2,0},{3,1},{0,2},{1,3},{6,4},{7,5},{4,6},{5,7},{10,8},{11,9},{8,1... | collective-permute-start | bytes 98312 | tf_op jit(solution)/shard_map/ppermute | solution.py:36
  79.9 3.4 %collective-permute-start.26 = (bf16[4,32,128]{2,1,0:T(8,128)(2,1)S(1)}, bf16[4,32,128]{2,1,0:T(8,128)(2,1)S(1)}, u32[]{:S(2)}, u32[]{:S(2)}) collective-permute-start(bf16[4,32,128]{2,1,0:T(8,128)(2,1)S(1)} %get-tuple-element.57), channel_id=1, source_target_pairs={{3,0},{2,1},{1,2},{0,3},{7,4},{6,5},{5,6},{4,7},{11,8},{10,9},{9,1... | collective-permute-start | bytes 98312 | tf_op jit(solution)/shard_map/ppermute | solution.py:36
  (10 other events, 41.5 us)
